TPU v7x, 128 devices: a whole 4x4x4 slice. The times are simulated.
128 devices in a mesh: samp: 16 (over z_hi, y, core), feat: 8 (over z_lo, x).
Axes of the slice: x: 4, y: 4, z: 4 (z_hi: 2, z_lo: 2; z = z_hi * 2 + z_lo), core: 2. Of those that a mesh axis runs over, the one named last changes fastest.
Arguments:
- noise: bfloat16 [4096, 32768], P('samp', 'feat'), may hold values from -24 to 24
- data: bfloat16 [4096, 32768], P('samp', 'feat'), may hold values from -6 to 6
Outputs:
- targets: bfloat16 [4096, 32768], P('samp', 'feat')
- column_potential: float32 [4096], P('feat')
All inputs are finite; a program needn't handle non-finite values.
Results may differ from a plain program's by a relative error of at most 0.0065.
Values may be sent and summed in bfloat16 or wider, within the bound.
No kernel may reach another device: no remote copies, remote signals or barrier semaphores. Data moves between devices by JAX's collectives and lax.ppermute only.
A program may use at most 128 MiB of HBM per device.

v0:
```python
import math

import jax
import jax.numpy as jnp
from jax import lax
from jax.sharding import PartitionSpec as P

F = 32768
ITERS = 3


def column_lse(values):
    peak = lax.pmax(jnp.max(values, axis=0), "samp")
    total = lax.psum(jnp.sum(jnp.exp(values - peak[None, :]), axis=0), "samp")
    return peak + jnp.log(total)


def row_stats(values):
    peak = jnp.max(values, axis=1)
    total = jnp.sum(jnp.exp(values - peak[:, None]), axis=1)
    return (peak, total)


def local(noise, data):
    temper = 0.5 / math.sqrt(F)
    everything = lax.all_gather(data, "samp", axis=0, tiled=True)
    inner = lax.dot_general(
        noise, everything, (((1,), (1,)), ((), ())), preferred_element_type=jnp.float32
    )
    noise_square = jnp.sum(jnp.square(noise.astype(jnp.float32)), axis=1)
    data_square = jnp.sum(jnp.square(everything.astype(jnp.float32)), axis=1)
    partial_cost = (noise_square[:, None] + data_square[None, :] - 2.0 * inner) / F
    cost = lax.psum(partial_cost, "feat")
    column_potential = jnp.zeros((cost.shape[1],), jnp.float32)
    for step in range(ITERS):
        peak, total = row_stats((column_potential[None, :] - cost) / temper)
        row_potential = -temper * (peak + jnp.log(total))
        column_potential = -temper * column_lse((row_potential[:, None] - cost) / temper)
    logits = (column_potential[None, :] - cost) / temper
    peak, total = row_stats(logits)
    weights = (jnp.exp(logits - peak[:, None]) / total[:, None]).astype(jnp.bfloat16)
    share = cost.shape[1] // lax.axis_size("feat")
    start = lax.axis_index("feat") * share
    column_out = lax.dynamic_slice_in_dim(column_potential, start, share, 0)
    targets = jnp.dot(weights, everything, preferred_element_type=jnp.float32).astype(jnp.bfloat16)
    return (targets, column_out)


def solution(mesh):
    in_specs = (P("samp", "feat"), P("samp", "feat"))
    out_specs = (P("samp", "feat"), P("feat"))
    return jax.shard_map(local, mesh=mesh, in_specs=in_specs, out_specs=out_specs, check_vma=False)
```

profile of v0, /device:TPU:0, one launch (start us, length us, event | category | flops | bytes accessed | tf_op | source)
XLA Modules:
  0.0 777.7 jit_solution(11729898805615150538)
XLA Ops:
  7.2 0.7 all-gather.2.cloned.1.call-update
  7.9 0.0 all-reduce.2.cloned.1.call-start
  7.9 2.1 multiply_reduce_fusion.1
  10.0 190.7 %all-gather.2.cloned.1.call-done = bf16[4096,4096]{1,0:T(8,128)(2,1)} async-done(((bf16[256,4096]{1,0:T(8,128)(2,1)}), bf16[4096,4096]{1,0:T(8,128)(2,1)}) %all-gather.2.cloned.1.call-update) | async-done | bytes 33554448 | tf_op jit(solution)/shard_map/all_gather | solution.py:26
  200.7 11.3 %multiply_reduce_fusion = f32[4096]{0:T(1024)S(1)} fusion(bf16[4096,4096]{1,0:T(8,128)(2,1)} %all-gather.2.cloned.1.call-done), kind=kLoop, calls=%fused_computation | loop fusion | flops 50327552 | bytes 33570816 | tf_op jit(solution)/shard_map/reduce_sum | solution.py:31
  212.1 16.7 %fusion.1 = f32[256,4096]{1,0:T(8,128)} fusion(bf16[256,4096]{1,0:T(8,128)(2,1)S(1)} %copy-done.4, bf16[4096,4096]{1,0:T(8,128)(2,1)} %all-gather.2.cloned.1.call-done, f32[4096]{0:T(1024)S(1)} %multiply_reduce_fusion, f32[256]{0:T(256)S(1)} %multiply_reduce_fusion.1), kind=kOutput, calls=%fused_computation.3 | convolution fusion | flops 8594128896 | bytes 39863296 | tf_op jit(solution)/shard_map/dot_general | solution.py:27
  228.8 102.8 %all-reduce.2.cloned.1.call-done = f32[256,4096]{1,0:T(8,128)} async-done(((f32[256,4096]{1,0:T(8,128)}), f32[256,4096]{1,0:T(8,128)}) %all-reduce.2.cloned.1.call-update) | async-done | bytes 4194320 | tf_op jit(solution)/shard_map/psum | solution.py:33
  331.6 2.8 fusion.2
  334.4 0.6 copy-done
  335.0 0.9 exponential_reduce_fusion.5
  336.0 0.6 fusion.3
  336.6 69.3 %pmax.21 = f32[4096]{0:T(1024)S(1)} all-reduce(f32[4096]{0:T(1024)S(1)} %fusion.3), channel_id=1, replica_groups=mesh['samp'=16,'feat'=8] {'samp'}, use_global_device_ids=true, to_apply=%region_6.0 | all-reduce | flops 4096 | bytes 32768 | tf_op jit(solution)/shard_map/pmax | solution.py:13
  405.9 3.1 exponential_reduce_fusion.4
  408.9 64.9 %psum.29 = f32[4096]{0:T(1024)S(1)} all-reduce(f32[4096]{0:T(1024)S(1)} %exponential_reduce_fusion.4), channel_id=1, replica_groups=mesh['samp'=16,'feat'=8] {'samp'}, use_global_device_ids=true, to_apply=%region_8.0 | all-reduce | flops 4096 | bytes 32768 | tf_op jit(solution)/shard_map/psum | solution.py:14
  473.9 2.9 fusion.4
  476.7 0.6 copy-done.1
  477.3 0.9 exponential_reduce_fusion.3
  478.3 0.6 fusion.5
  478.9 64.9 %pmax.22 = f32[4096]{0:T(1024)S(1)} all-reduce(f32[4096]{0:T(1024)S(1)} %fusion.5), channel_id=1, replica_groups=mesh['samp'=16,'feat'=8] {'samp'}, use_global_device_ids=true, to_apply=%region_12.0 | all-reduce | flops 4096 | bytes 32768 | tf_op jit(solution)/shard_map/pmax | solution.py:13
  543.8 3.1 exponential_reduce_fusion.2
  546.9 65.1 %psum.30 = f32[4096]{0:T(1024)S(1)} all-reduce(f32[4096]{0:T(1024)S(1)} %exponential_reduce_fusion.2), channel_id=1, replica_groups=mesh['samp'=16,'feat'=8] {'samp'}, use_global_device_ids=true, to_apply=%region_14.0 | all-reduce | flops 4096 | bytes 32768 | tf_op jit(solution)/shard_map/psum | solution.py:14
  612.0 2.9 fusion.6
  614.9 0.6 copy-done.2
  615.4 0.9 exponential_reduce_fusion.1
  616.4 0.6 fusion.7
  617.0 64.9 %pmax.23 = f32[4096]{0:T(1024)S(1)} all-reduce(f32[4096]{0:T(1024)S(1)} %fusion.7), channel_id=1, replica_groups=mesh['samp'=16,'feat'=8] {'samp'}, use_global_device_ids=true, to_apply=%region_18.0 | all-reduce | flops 4096 | bytes 32768 | tf_op jit(solution)/shard_map/pmax | solution.py:13
  681.9 3.1 exponential_reduce_fusion
  685.0 64.9 %psum.31 = f32[4096]{0:T(1024)S(1)} all-reduce(f32[4096]{0:T(1024)S(1)} %exponential_reduce_fusion), channel_id=1, replica_groups=mesh['samp'=16,'feat'=8] {'samp'}, use_global_device_ids=true, to_apply=%region_20.0 | all-reduce | flops 4096 | bytes 32768 | tf_op jit(solution)/shard_map/psum | solution.py:14
  750.0 0.7 dynamic_slice.3
  750.6 3.1 fusion.8
  753.7 0.9 fusion.9
  754.6 16.2 %convolution_convert_fusion = bf16[256,4096]{1,0:T(8,128)(2,1)} fusion(bf16[4096,4096]{1,0:T(8,128)(2,1)} %all-gather.2.cloned.1.call-done, f32[256,4096]{1,0:T(8,128)S(1)} %copy-done.3, f32[256]{0:T(256)S(1)} %fusion.9, f32[256]{0:T(256)S(1)} %fusion.8, f32[4096]{0:T(1024)S(1)} %add_multiply_fusion), kind=kOutput, calls=%fused_computation.4 | convolution fusion | flops 8596226048 | bytes 39864320 | tf_op jit(solution)/shard_map/dot_general | solution.py:45
  (15 shorter events, 0.1 us)
Async XLA Ops:
  7.2 193.5 %all-gather.2.cloned.1.call-start = ((), (), s32[]{:S(2)}) async-start(), calls=%async_computation | async-start | bytes 35651584 | tf_op jit(solution)/shard_map/all_gather | solution.py:26
  7.9 323.7 %all-reduce.2.cloned.1.call-start = ((), (), s32[]{:S(2)}) async-start(), calls=%async_computation.1 | async-start | bytes 8388608 | tf_op jit(solution)/shard_map/psum | solution.py:33
  10.0 202.0 %copy-start.4 = (bf16[256,4096]{1,0:T(8,128)(2,1)S(1)}, bf16[256,4096]{1,0:T(8,128)(2,1)}, u32[]{:S(2)}) copy-start(bf16[256,4096]{1,0:T(8,128)(2,1)} %param.2) | copy-start | bytes 6291460
  331.6 3.4 copy-start
  473.9 3.4 copy-start.1
  612.0 3.4 copy-start.2
  749.9 3.7 copy-start.3
Sparse Core Ops, SparseCore 0:
  10.4 190.2 all-gather.1
  228.9 102.6 all-reduce.1
where the time goes:
time: 778 us
  blocking collectives  394 us (51%)
  waiting for transfers between devices  294 us (38%)
  other arithmetic  39.9 us (5%)
  matrix products  32.9 us (4%)
  between operations  14.1 us (2%)
    pmax x3, blocking collectives, column_lse(): peak = lax.pmax(jnp.max(values, axis=0), 'samp')  199 us
    psum x3, blocking collectives, column_lse(): total = lax.psum(jnp.sum(jnp.exp(values - peak[None, :]), axis=0), 'samp')  195 us
    all_gather x1, waiting for transfers between devices, local(): everything = lax.all_gather(data, 'samp', axis=0, tiled=True)  191 us
    psum x1, waiting for transfers between devices, local(): cost = lax.psum(partial_cost, 'feat')  103 us
    dot_general x1, matrix products, local(): lax.dot_general(noise, everything, (((1,), (1,)), ((), ())), preferred_el...  16.7 us
    dot_general x1, matrix products, local(): jnp.dot(weights, everything, preferred_element_type=jnp.float32)  16.2 us
  transfers between devices with their start and end apart: 2, of which 2 were waited for; matrix products, arithmetic and copies ran while one was open for 0% of the time, Pallas kernels for 0%

commit v1 on v0

v1 whole, which is shorter than its diff:
```python
import functools
import math

import jax
import jax.numpy as jnp
from jax import lax
from jax.experimental import pallas as pl
from jax.experimental.pallas import tpu as pltpu
from jax.sharding import PartitionSpec as P

F = 32768
ITERS = 3
SAMPLES = 4096
LANES = 128
ROWS = 32
GROUP = 4


def tile_list(shapes):
    return [
        (k, g, n)
        for k, (_, groups, _, width) in enumerate(shapes)
        for g in range(groups)
        for n in range(0, width, LANES)
    ]


def row_pass(tiles, blocks, logits, c_ref, peak_ref, row_ref):
    def tile(f, t):
        k, g, n = tiles[t]
        return logits[k][f, g, :, n:n + LANES] + c_ref[:, t * LANES:(t + 1) * LANES]

    def maxima(f, _):
        acc = tile(f, 0)
        for t in range(1, len(tiles)):
            acc = jnp.maximum(acc, tile(f, t))
        peak_ref[pl.ds(f * ROWS, ROWS), :] = acc
        return 0

    lax.fori_loop(0, blocks, maxima, 0)
    peak = jnp.max(peak_ref[...], axis=1, keepdims=True)
    peak_ref[...] = jnp.broadcast_to(peak, peak_ref.shape)

    def totals(f, _):
        top = peak_ref[pl.ds(f * ROWS, ROWS), :]
        acc = jnp.exp(tile(f, 0) - top)
        for t in range(1, len(tiles)):
            acc = acc + jnp.exp(tile(f, t) - top)
        row_ref[pl.ds(f * ROWS, ROWS), :] = acc
        return 0

    lax.fori_loop(0, blocks, totals, 0)
    return jnp.sum(row_ref[...], axis=1, keepdims=True)


def sinkhorn_kernel(shapes, *refs):
    logits, (c_ref, out_ref, peak_ref, row_ref) = refs[:len(shapes)], refs[len(shapes):]
    tiles = tile_list(shapes)
    blocks = shapes[0][0]
    total = row_pass(tiles, blocks, logits, c_ref, peak_ref, row_ref)
    row_ref[...] = jnp.broadcast_to(-(peak_ref[:, 0:1] + jnp.log(total)), row_ref.shape)
    for first in range(0, len(tiles), GROUP):
        group = range(first, first + GROUP)

        def values(f, r, t):
            k, g, n = tiles[t]
            rows = row_ref[pl.ds(f * ROWS + r * 8, 8), :]
            return logits[k][f, g, r * 8:(r + 1) * 8, n:n + LANES] + rows

        def maxima(f, acc):
            for r in range(ROWS // 8):
                acc = [jnp.maximum(a, values(f, r, t)) for a, t in zip(acc, group)]
            return acc

        start = [jnp.full((8, LANES), -jnp.inf, jnp.float32) for _ in group]
        acc = lax.fori_loop(0, blocks, maxima, start)
        peaks = [jnp.max(a, axis=0, keepdims=True) for a in acc]

        def totals(f, acc):
            for r in range(ROWS // 8):
                acc = [a + jnp.exp(values(f, r, t) - p) for a, p, t in zip(acc, peaks, group)]
            return acc

        start = [jnp.zeros((8, LANES), jnp.float32) for _ in group]
        acc = lax.fori_loop(0, blocks, totals, start)
        for a, p, t in zip(acc, peaks, group):
            out_ref[0:1, t * LANES:(t + 1) * LANES] = p
            out_ref[1:2, t * LANES:(t + 1) * LANES] = jnp.sum(a, axis=0, keepdims=True)


def weights_kernel(shapes, *refs):
    logits, (c_ref, out_ref, peak_ref, row_ref) = refs[:len(shapes)], refs[len(shapes):]
    tiles = tile_list(shapes)
    blocks = shapes[0][0]
    total = row_pass(tiles, blocks, logits, c_ref, peak_ref, row_ref)
    row_ref[...] = jnp.broadcast_to(total, row_ref.shape)

    def write(f, _):
        rows = pl.ds(f * ROWS, ROWS)
        top, scale = peak_ref[rows, :], 1.0 / row_ref[rows, :]
        for t, (k, g, n) in enumerate(tiles):
            lanes = slice(t * LANES, (t + 1) * LANES)
            x = logits[k][f, g, :, n:n + LANES] + c_ref[:, lanes]
            out_ref[rows, lanes] = (jnp.exp(x - top) * scale).astype(jnp.bfloat16)
        return 0

    lax.fori_loop(0, blocks, write, 0)


def row_call(kernel, out_shape, logits, c):
    shapes = tuple(a.shape for a in logits)
    rows = shapes[0][0] * ROWS
    vmem = pl.BlockSpec(memory_space=pltpu.VMEM)
    return pl.pallas_call(
        functools.partial(kernel, shapes),
        out_shape=out_shape,
        in_specs=[vmem] * (len(logits) + 1),
        out_specs=vmem,
        scratch_shapes=[pltpu.VMEM((rows, LANES), jnp.float32)] * 2,
        compiler_params=pltpu.CompilerParams(vmem_limit_bytes=32 * 2**20),
    )(*logits, c)


def combine(a, b):
    peak = jnp.maximum(a[0], b[0])
    total = a[1] * jnp.exp(a[0] - peak) + b[1] * jnp.exp(b[0] - peak)
    return jnp.stack([peak, total])


def column_update(stats, n):
    step = 1
    while step < n:
        pairs = [(i, i ^ step) for i in range(n)]
        stats = combine(stats, lax.ppermute(stats, "samp", pairs))
        step *= 2
    return -(stats[0] + jnp.log(stats[1]))[None, :]


def local(noise, data):
    temper = 0.5 / math.sqrt(F)
    everything = lax.all_gather(data, "samp", axis=0, tiled=True)
    inner = lax.dot_general(
        noise, everything, (((1,), (1,)), ((), ())), preferred_element_type=jnp.float32
    )
    noise_square = jnp.sum(jnp.square(noise.astype(jnp.float32)), axis=1)
    data_square = jnp.sum(jnp.square(everything.astype(jnp.float32)), axis=1)
    partial = (noise_square[:, None] + data_square[None, :] - 2.0 * inner) * (-1.0 / (F * temper))
    logits = lax.psum(partial, "feat")
    rows = noise.shape[0]
    logits = [logits.reshape(rows // ROWS, 1, ROWS, SAMPLES)]
    c = jnp.zeros((1, SAMPLES), jnp.float32)
    for _ in range(ITERS):
        stats = row_call(sinkhorn_kernel, jax.ShapeDtypeStruct((2, SAMPLES), jnp.float32), logits, c)
        c = column_update(stats, lax.axis_size("samp"))
    weights = row_call(weights_kernel, jax.ShapeDtypeStruct((rows, SAMPLES), jnp.bfloat16), logits, c)
    share = SAMPLES // lax.axis_size("feat")
    start = lax.axis_index("feat") * share
    column_out = lax.dynamic_slice_in_dim(c[0] * temper, start, share, 0)
    targets = jnp.dot(weights, everything, preferred_element_type=jnp.float32).astype(jnp.bfloat16)
    return (targets, column_out)


def solution(mesh):
    in_specs = (P("samp", "feat"), P("samp", "feat"))
    out_specs = (P("samp", "feat"), P("feat"))
    return jax.shard_map(local, mesh=mesh, in_specs=in_specs, out_specs=out_specs, check_vma=False)
```

time: 778 us -> 424 us (0.54)
  blocking collectives: 394 us -> 0 us
  waiting for transfers between devices: 294 us -> 320 us
  other arithmetic: 39.9 us -> 15.1 us
  starting transfers between devices: 0.08 us -> 23.3 us
  Pallas kernels: 0 us -> 13.2 us
    pmax x3 -> x0, blocking collectives: 199 us -> none  [column_lse(): peak = lax.pmax(jnp.max(values, axis=0), 'samp')]
    psum x3 -> x0, blocking collectives: 195 us -> none  [column_lse(): total = lax.psum(jnp.sum(jnp.exp(values - peak[None, :]), axis=0), 'samp')]
    ppermute x0 -> x12, waiting for transfers between devices: none -> 25.8 us  [column_update(): stats = combine(stats, lax.ppermute(stats, 'samp', pairs))]
    ppermute x0 -> x12, starting transfers between devices: none -> 23.2 us  [column_update(): stats = combine(stats, lax.ppermute(stats, 'samp', pairs))]
    reduce_max x7 -> x0, other arithmetic: 13.4 us -> none  [the longest x4 11.6 us: row_stats(): peak = jnp.max(values, axis=1)]
    pallas_call x0 -> x4, Pallas kernels: none -> 13.2 us  [row_call(): pl.pallas_call(functools.partial(kernel, shapes), out_shape=out_shape, in...]
    reduce_sum x7 -> x0, other arithmetic: 13 us -> none  [the longest x3 9.28 us: column_lse(): total = lax.psum(jnp.sum(jnp.exp(values - peak[None, :]), axis=0), 'samp')]
  transfers between devices with their start and end apart: 2 -> 14, of which waited for: 2 -> 14; matrix products, arithmetic and copies ran while one was open for 0% -> 0% of each run, Pallas kernels for 0% -> 0%
where the time goes in v1:
time: 424 us
  waiting for transfers between devices  320 us (75%)
  matrix products  33.5 us (8%)
  starting transfers between devices  23.3 us (5%)
  other arithmetic  15.1 us (4%)
  between operations  14.2 us (3%)
  Pallas kernels  13.2 us (3%)
  local copies, waits for them, and re-layouts  4.38 us (1%)
    all_gather x1, waiting for transfers between devices, local(): everything = lax.all_gather(data, 'samp', axis=0, tiled=True)  191 us
    psum x1, waiting for transfers between devices, local(): logits = lax.psum(partial, 'feat')  103 us
    ppermute x12, waiting for transfers between devices, column_update(): stats = combine(stats, lax.ppermute(stats, 'samp', pairs))  25.8 us
    ppermute x12, starting transfers between devices, column_update(): stats = combine(stats, lax.ppermute(stats, 'samp', pairs))  23.2 us
    dot_general x1, matrix products, local(): lax.dot_general(noise, everything, (((1,), (1,)), ((), ())), preferred_el...  16.8 us
    dot_general x1, matrix products, local(): jnp.dot(weights, everything, preferred_element_type=jnp.float32)  16.7 us
    pallas_call x4, Pallas kernels, row_call(): pl.pallas_call(functools.partial(kernel, shapes), out_shape=out_shape, in...  13.2 us
    reduce_sum x1, other arithmetic, local(): data_square = jnp.sum(jnp.square(everything.astype(jnp.float32)), axis=1)  11.3 us
  transfers between devices with their start and end apart: 14, of which 14 were waited for; matrix products, arithmetic and copies ran while one was open for 0% of the time, Pallas kernels for 0%

profile of v1, /device:TPU:0, one launch (start us, length us, event | category | flops | bytes accessed | tf_op | source)
XLA Modules:
  0.0 423.6 jit_solution(97614047017711457)
XLA Ops:
  7.9 2.1 multiply_reduce_fusion.1
  10.0 190.7 %all-gather.2.cloned.1.call-done = bf16[4096,4096]{1,0:T(8,128)(2,1)} async-done(((bf16[256,4096]{1,0:T(8,128)(2,1)}), bf16[4096,4096]{1,0:T(8,128)(2,1)}) %all-gather.2.cloned.1.call-update) | async-done | bytes 33554448 | tf_op jit(solution)/shard_map/all_gather | solution.py:141
  200.7 11.3 %multiply_reduce_fusion = f32[4096]{0:T(1024)S(1)} fusion(bf16[4096,4096]{1,0:T(8,128)(2,1)} %all-gather.2.cloned.1.call-done), kind=kLoop, calls=%fused_computation | loop fusion | flops 50327552 | bytes 33570816 | tf_op jit(solution)/shard_map/reduce_sum | solution.py:146
  212.0 16.8 %fusion.1 = f32[256,4096]{1,0:T(8,128)} fusion(bf16[256,4096]{1,0:T(8,128)(2,1)S(1)} %copy-done.2, bf16[4096,4096]{1,0:T(8,128)(2,1)} %all-gather.2.cloned.1.call-done, f32[4096]{0:T(1024)S(1)} %multiply_reduce_fusion, f32[256]{0:T(256)S(1)} %multiply_reduce_fusion.1), kind=kOutput, calls=%fused_computation.3 | convolution fusion | flops 8594128896 | bytes 39863296 | tf_op jit(solution)/shard_map/dot_general | solution.py:142
  228.8 102.8 %all-reduce.2.cloned.1.call-done.refs_0_ = f32[8,1,32,4096]{3,2,1,0:T(8,128)} async-done(((f32[8,1,32,4096]{3,2,1,0:T(8,128)}), f32[8,1,32,4096]{3,2,1,0:T(8,128)}) %all-reduce.2.cloned.1.call-update) | async-done | bytes 4194320 | tf_op jit(solution)/shard_map/psum | solution.py:148
  331.6 2.2 copy-done
  333.8 3.6 shard_map.41
  337.5 1.2 collective-permute-done
  338.8 1.6 collective-permute-start.1
  340.4 2.4 collective-permute-done.1
  342.9 3.1 collective-permute-start.2
  346.0 2.4 collective-permute-done.2
  348.5 2.9 collective-permute-start.3
  351.5 2.6 collective-permute-done.3
  354.1 3.6 shard_map.42
  357.8 1.2 collective-permute-done.4
  359.1 1.6 collective-permute-start.5
  360.7 2.4 collective-permute-done.5
  363.2 3.1 collective-permute-start.6
  366.3 2.4 collective-permute-done.6
  368.8 2.9 collective-permute-start.7
  371.8 2.6 collective-permute-done.7
  374.4 3.6 shard_map.43
  379.4 1.6 collective-permute-start.9
  381.0 2.4 collective-permute-done.9
  383.5 3.1 collective-permute-start.10
  386.6 2.4 collective-permute-done.10
  389.1 3.1 collective-permute-start.11
  392.2 2.6 collective-permute-done.11
  395.5 2.2 copy-done.1
  397.7 2.4 shard_map.44
  400.1 16.7 %convolution_convert_fusion = bf16[256,4096]{1,0:T(8,128)(2,1)} fusion(bf16[256,4096]{1,0:T(8,128)(2,1)S(1)} %shard_map.44, bf16[4096,4096]{1,0:T(8,128)(2,1)} %all-gather.2.cloned.1.call-done), kind=kOutput, calls=%fused_computation.4 | convolution fusion | flops 8590983168 | bytes 37748736 | tf_op jit(solution)/shard_map/dot_general | solution.py:159
  (35 shorter events, 4.0 us)
Async XLA Ops:
  7.2 193.5 %all-gather.2.cloned.1.call-start = ((), (), s32[]{:S(2)}) async-start(), calls=%async_computation | async-start | bytes 35651584 | tf_op jit(solution)/shard_map/all_gather | solution.py:141
  7.9 323.7 %all-reduce.2.cloned.1.call-start = ((), (), s32[]{:S(2)}) async-start(), calls=%async_computation.1 | async-start | bytes 8388608 | tf_op jit(solution)/shard_map/psum | solution.py:148
  10.0 202.0 %copy-start.2 = (bf16[256,4096]{1,0:T(8,128)(2,1)S(1)}, bf16[256,4096]{1,0:T(8,128)(2,1)}, u32[]{:S(2)}) copy-start(bf16[256,4096]{1,0:T(8,128)(2,1)} %param.2) | copy-start | bytes 6291460
  331.6 2.2 copy-start
  337.4 1.3 collective-permute-start
  338.8 4.0 collective-permute-start.1
  342.9 5.5 %collective-permute-start.2 = (f32[2,4096]{1,0:T(2,128)S(1)}, f32[2,4096]{1,0:T(2,128)S(1)}, u32[]{:S(2)}, u32[]{:S(2)}) collective-permute-start(f32[2,4096]{1,0:T(2,128)S(1)} %pad_maximum_fusion.1), channel_id=1, source_target_pairs={{0,32},{8,40},{16,48},{24,56},{32,0},{40,8},{48,16},{56,24},{64,96... | collective-permute-start | bytes 98312 | tf_op jit(solution)/shard_map/ppermute | solution.py:134
  348.5 5.5 %collective-permute-start.3 = (f32[2,4096]{1,0:T(2,128)S(1)}, f32[2,4096]{1,0:T(2,128)S(1)}, u32[]{:S(2)}, u32[]{:S(2)}) collective-permute-start(f32[2,4096]{1,0:T(2,128)S(1)} %pad_maximum_fusion.2), channel_id=1, source_target_pairs={{0,64},{8,72},{16,80},{24,88},{32,96},{40,104},{48,112},{56,120},{... | collective-permute-start | bytes 98312 | tf_op jit(solution)/shard_map/ppermute | solution.py:134
  357.7 1.3 collective-permute-start.4
  359.1 4.0 collective-permute-start.5
  363.2 5.5 %collective-permute-start.6 = (f32[2,4096]{1,0:T(2,128)S(1)}, f32[2,4096]{1,0:T(2,128)S(1)}, u32[]{:S(2)}, u32[]{:S(2)}) collective-permute-start(f32[2,4096]{1,0:T(2,128)S(1)} %pad_maximum_fusion.4), channel_id=1, source_target_pairs={{0,32},{8,40},{16,48},{24,56},{32,0},{40,8},{48,16},{56,24},{64,96... | collective-permute-start | bytes 98312 | tf_op jit(solution)/shard_map/ppermute | solution.py:134
  368.8 5.5 %collective-permute-start.7 = (f32[2,4096]{1,0:T(2,128)S(1)}, f32[2,4096]{1,0:T(2,128)S(1)}, u32[]{:S(2)}, u32[]{:S(2)}) collective-permute-start(f32[2,4096]{1,0:T(2,128)S(1)} %pad_maximum_fusion.5), channel_id=1, source_target_pairs={{0,64},{8,72},{16,80},{24,88},{32,96},{40,104},{48,112},{56,120},{... | collective-permute-start | bytes 98312 | tf_op jit(solution)/shard_map/ppermute | solution.py:134
  378.0 1.3 collective-permute-start.8
  379.4 4.0 collective-permute-start.9
  383.5 5.5 %collective-permute-start.10 = (f32[2,4096]{1,0:T(2,128)S(1)}, f32[2,4096]{1,0:T(2,128)S(1)}, u32[]{:S(2)}, u32[]{:S(2)}) collective-permute-start(f32[2,4096]{1,0:T(2,128)S(1)} %pad_maximum_fusion.7), channel_id=1, source_target_pairs={{0,32},{8,40},{16,48},{24,56},{32,0},{40,8},{48,16},{56,24},{64,96... | collective-permute-start | bytes 98312 | tf_op jit(solution)/shard_map/ppermute | solution.py:134
  389.1 5.7 %collective-permute-start.11 = (f32[2,4096]{1,0:T(2,128)S(1)}, f32[2,4096]{1,0:T(2,128)S(1)}, u32[]{:S(2)}, u32[]{:S(2)}) collective-permute-start(f32[2,4096]{1,0:T(2,128)S(1)} %pad_maximum_fusion.8), channel_id=1, source_target_pairs={{0,64},{8,72},{16,80},{24,88},{32,96},{40,104},{48,112},{56,120},{... | collective-permute-start | bytes 98312 | tf_op jit(solution)/shard_map/ppermute | solution.py:134
  395.5 2.2 copy-start.1
Sparse Core Ops, SparseCore 0:
  10.4 190.2 all-gather.1
  229.0 102.6 all-reduce.1

commit v2 on v1

v2 whole, which is shorter than its diff:
```python
import functools
import math

import jax
import jax.numpy as jnp
from jax import lax
from jax.experimental import pallas as pl
from jax.experimental.pallas import tpu as pltpu
from jax.sharding import Mesh, PartitionSpec as P

F = 32768
ITERS = 3
SAMPLES = 4096
LANES = 128
ROWS = 32
GROUP = 4
DEPTH = 1024
FEAT = ("zl", "x")


def tile_list(shapes):
    return [
        (k, g, n)
        for k, (_, groups, _, width) in enumerate(shapes)
        for g in range(groups)
        for n in range(0, width, LANES)
    ]


def row_pass(tiles, blocks, logits, where, c_ref, peak_ref, row_ref):
    def tile(f, t):
        k, g, n = tiles[t]
        return logits[k][f, g, :, n:n + LANES] + c_ref[:, lanes(where[0, t])]

    def maxima(f, _):
        acc = tile(f, 0)
        for t in range(1, len(tiles)):
            acc = jnp.maximum(acc, tile(f, t))
        peak_ref[pl.ds(f * ROWS, ROWS), :] = acc
        return 0

    lax.fori_loop(0, blocks, maxima, 0)
    peak = jnp.max(peak_ref[...], axis=1, keepdims=True)
    peak_ref[...] = jnp.broadcast_to(peak, peak_ref.shape)

    def totals(f, _):
        top = peak_ref[pl.ds(f * ROWS, ROWS), :]
        acc = jnp.exp(tile(f, 0) - top)
        for t in range(1, len(tiles)):
            acc = acc + jnp.exp(tile(f, t) - top)
        row_ref[pl.ds(f * ROWS, ROWS), :] = acc
        return 0

    lax.fori_loop(0, blocks, totals, 0)
    return jnp.sum(row_ref[...], axis=1, keepdims=True)


def lanes(tile):
    return pl.ds(pl.multiple_of(tile * LANES, LANES), LANES)


def sinkhorn_kernel(shapes, where, *refs):
    logits, (c_ref, out_ref, peak_ref, row_ref) = refs[:len(shapes)], refs[len(shapes):]
    tiles = tile_list(shapes)
    blocks = shapes[0][0]
    total = row_pass(tiles, blocks, logits, where, c_ref, peak_ref, row_ref)
    row_ref[...] = jnp.broadcast_to(-(peak_ref[:, 0:1] + jnp.log(total)), row_ref.shape)
    for first in range(0, len(tiles), GROUP):
        group = range(first, first + GROUP)

        def values(f, r, t):
            k, g, n = tiles[t]
            rows = row_ref[pl.ds(f * ROWS + r * 8, 8), :]
            return logits[k][f, g, r * 8:(r + 1) * 8, n:n + LANES] + rows

        def maxima(f, acc):
            for r in range(ROWS // 8):
                acc = [jnp.maximum(a, values(f, r, t)) for a, t in zip(acc, group)]
            return acc

        start = [jnp.full((8, LANES), -jnp.inf, jnp.float32) for _ in group]
        acc = lax.fori_loop(0, blocks, maxima, start)
        peaks = [jnp.max(a, axis=0, keepdims=True) for a in acc]

        def totals(f, acc):
            for r in range(ROWS // 8):
                acc = [a + jnp.exp(values(f, r, t) - p) for a, p, t in zip(acc, peaks, group)]
            return acc

        start = [jnp.zeros((8, LANES), jnp.float32) for _ in group]
        acc = lax.fori_loop(0, blocks, totals, start)
        for a, p, t in zip(acc, peaks, group):
            out_ref[0:1, lanes(where[0, t])] = p
            out_ref[1:2, lanes(where[0, t])] = jnp.sum(a, axis=0, keepdims=True)


def weights_kernel(shapes, where, *refs):
    logits, (c_ref, out_ref, peak_ref, row_ref) = refs[:len(shapes)], refs[len(shapes):]
    tiles = tile_list(shapes)
    blocks = shapes[0][0]
    total = row_pass(tiles, blocks, logits, where, c_ref, peak_ref, row_ref)
    row_ref[...] = jnp.broadcast_to(total, row_ref.shape)

    def write(f, _):
        rows = pl.ds(f * ROWS, ROWS)
        top, scale = peak_ref[rows, :], 1.0 / row_ref[rows, :]
        for t, (k, g, n) in enumerate(tiles):
            x = logits[k][f, g, :, n:n + LANES] + c_ref[:, lanes(where[0, t])]
            out_ref[rows, lanes(where[1, t])] = (jnp.exp(x - top) * scale).astype(jnp.bfloat16)
        return 0

    lax.fori_loop(0, blocks, write, 0)


def row_call(kernel, out_shape, where, logits, c):
    shapes = tuple(a.shape for a in logits)
    rows = shapes[0][0] * ROWS
    vmem = pl.BlockSpec(memory_space=pltpu.VMEM)
    return pl.pallas_call(
        functools.partial(kernel, shapes),
        out_shape=out_shape,
        in_specs=[pl.BlockSpec(memory_space=pltpu.SMEM)] + [vmem] * (len(logits) + 1),
        out_specs=vmem,
        scratch_shapes=[pltpu.VMEM((rows, LANES), jnp.float32)] * 2,
        compiler_params=pltpu.CompilerParams(vmem_limit_bytes=32 * 2**20),
    )(where, *logits, c)


def combine(a, b):
    peak = jnp.maximum(a[0], b[0])
    total = a[1] * jnp.exp(a[0] - peak) + b[1] * jnp.exp(b[0] - peak)
    return jnp.stack([peak, total])


def column_update(stats):
    for axis, n, step in (("core", 2, 1), ("y", 4, 1), ("y", 4, 2), ("zh", 2, 1)):
        pairs = [(i, i ^ step) for i in range(n)]
        stats = combine(stats, lax.ppermute(stats, axis, pairs))
    return -(stats[0] + jnp.log(stats[1]))[None, :]


def lane_sums(x):
    acc = None
    for n in range(0, x.shape[1], LANES):
        v = x[:, n:n + LANES].astype(jnp.float32)
        acc = v * v if acc is None else acc + v * v
    return acc


def partial_kernel(nq, widths, scale, *refs):
    n_refs, x_refs = refs[:nq], refs[nq:nq + len(widths)]
    out_ref, noise_sq, data_sq = refs[nq + len(widths):]
    step = pl.program_id(0)
    rows = n_refs[0].shape[0]
    parts = out_ref.shape[0]
    share = rows // parts

    @pl.when(step == 0)
    def _():
        out_ref[...] = jnp.zeros_like(out_ref)
        noise_sq[...] = jnp.zeros_like(noise_sq)
        data_sq[...] = jnp.zeros_like(data_sq)

    for q in range(nq):
        block = n_refs[q][...]
        noise_sq[q] += lane_sums(block)
        first = 0
        for x, width in zip(x_refs, widths):
            inner = lax.dot_general(
                block, x[...], (((1,), (1,)), ((), ())), preferred_element_type=jnp.float32
            )
            out_ref[:, q, :, first:first + width] += inner.reshape(parts, share, width)
            first += width
    first = 0
    for x, width in zip(x_refs, widths):
        data_sq[first:first + width, :] += lane_sums(x[...])
        first += width

    @pl.when(step == pl.num_programs(0) - 1)
    def _():
        columns = lax.dot_general(
            jnp.ones((8, LANES), jnp.float32), data_sq[...], (((1,), (1,)), ((), ())),
            precision=lax.Precision.HIGHEST, preferred_element_type=jnp.float32,
        )[0:1]
        for q in range(nq):
            square = jnp.sum(noise_sq[q], axis=1, keepdims=True)
            for f in range(parts):
                own = square[f * share:(f + 1) * share]
                out_ref[f, q] = (own + columns - 2.0 * out_ref[f, q]) * scale


def partial_call(scale, parts, noises, datas):
    nq, widths = len(noises), tuple(d.shape[0] for d in datas)
    rows, depth = noises[0].shape
    shape = (parts, nq, rows // parts, sum(widths))
    block = DEPTH
    return pl.pallas_call(
        functools.partial(partial_kernel, nq, widths, scale),
        out_shape=jax.ShapeDtypeStruct(shape, jnp.float32),
        grid=(depth // block,),
        in_specs=[pl.BlockSpec((a.shape[0], block), lambda k: (0, k)) for a in (*noises, *datas)],
        out_specs=pl.BlockSpec(shape, lambda k: (0, 0, 0, 0)),
        scratch_shapes=[
            pltpu.VMEM((nq, rows, LANES), jnp.float32),
            pltpu.VMEM((sum(widths), LANES), jnp.float32),
        ],
        compiler_params=pltpu.CompilerParams(vmem_limit_bytes=48 * 2**20),
    )(*noises, *datas)


def targets_kernel(widths, w_ref, *refs):
    x_refs, out_ref = refs[:-1], refs[-1]
    first, acc = 0, None
    for x, width in zip(x_refs, widths):
        part = jnp.dot(w_ref[:, first:first + width], x[...], preferred_element_type=jnp.float32)
        acc = part if acc is None else acc + part
        first += width
    out_ref[...] = acc.astype(out_ref.dtype)


def targets_call(weights, datas):
    widths = tuple(d.shape[0] for d in datas)
    rows, depth = weights.shape[0], datas[0].shape[1]
    block = 512
    return pl.pallas_call(
        functools.partial(targets_kernel, widths),
        out_shape=jax.ShapeDtypeStruct((rows, depth), jnp.bfloat16),
        grid=(depth // block,),
        in_specs=[pl.BlockSpec(weights.shape, lambda n: (0, 0))]
        + [pl.BlockSpec((w, block), lambda n: (0, n)) for w in widths],
        out_specs=pl.BlockSpec((rows, block), lambda n: (0, n)),
        compiler_params=pltpu.CompilerParams(vmem_limit_bytes=48 * 2**20),
    )(weights, *datas)


def ring(x, shift):
    return lax.ppermute(x, "y", [(i, (i + shift) % 4) for i in range(4)])


def swap(x, dz, dc):
    if dz and dc:
        return lax.ppermute(x, ("zh", "core"), [(i, 3 - i) for i in range(4)])
    if dz or dc:
        return lax.ppermute(x, "zh" if dz else "core", [(0, 1), (1, 0)])
    return x


def ring_gather(x):
    half = x.shape[0] // 2
    a, b = x[:half], x[half:]
    u1, w1 = ring(a, 1), ring(a, -1)
    u2, w2 = ring(b, 1), ring(b, -1)
    u3, w3 = ring(u1, 1), ring(w2, -1)
    return [x, u1, w1, u2, w2, u3, w3]


SOURCES = [(0, 0), (0, 1), (-1, 0), (1, 0), (-1, 1), (1, 1), (-2, 0), (2, 1)]
QUARTERS = [(0, 0), (0, 1), (1, 0), (1, 1)]


def sum_and_share(part, quarters):
    own = lax.psum_scatter(part, FEAT, scatter_dimension=0, tiled=False)
    own = jnp.stack([swap(own[i], *q) for i, q in enumerate(quarters)])
    return lax.all_gather(own, FEAT, axis=0, tiled=False)


def tables(chunks):
    zh, y, core = (lax.axis_index(a) for a in ("zh", "y", "core"))
    where, place = [], []
    for quarters, sources in chunks:
        for dz, dc in quarters:
            for s in sources:
                dy, half = SOURCES[s]
                inside = ((y + dy + 4) % 4 * 2 + (core + dc) % 2) * 2 + half
                where.append((zh + dz) % 2 * 16 + inside)
                place.append(16 + inside if dz else jnp.int32(dc * 8 + s))
    return jnp.stack([jnp.stack(where), jnp.stack(place)]).astype(jnp.int32)


def local(noise, data):
    temper = 0.5 / math.sqrt(F)
    scale = -1.0 / (F * temper)
    parts = 8
    near = [noise, swap(noise, 0, 1)]
    far = swap(noise, 1, 0)
    blocks = ring_gather(data)
    far = [far, swap(far, 0, 1)]
    data, far[0] = lax.optimization_barrier((data, far[0]))
    other = swap(data, 1, 0)

    first, second, third = blocks[:3], blocks[3:5], blocks[5:]
    everyone = near + far
    p1 = partial_call(scale, parts, near, first)
    p2 = partial_call(scale, parts, far, first)
    p3 = partial_call(scale, parts, everyone, second)
    p4 = partial_call(scale, parts, everyone, third)
    chunks = [
        (QUARTERS[:2], (0, 1, 2, 3)),
        (QUARTERS[2:], (0, 1, 2, 3)),
        (QUARTERS, (4, 5)),
        (QUARTERS, (6, 7)),
    ]
    logits = [sum_and_share(p, q) for p, (q, _) in zip((p1, p2, p3, p4), chunks)]
    where = tables(chunks)

    others = lax.all_gather(other, ("y", "core"), axis=0, tiled=True)
    gathered = blocks + [swap(b, 0, 1) for b in blocks] + [others]

    c = jnp.zeros((1, SAMPLES), jnp.float32)
    for _ in range(ITERS):
        out = jax.ShapeDtypeStruct((2, SAMPLES), jnp.float32)
        c = column_update(row_call(sinkhorn_kernel, out, where, logits, c))
    out = jax.ShapeDtypeStruct((noise.shape[0], SAMPLES), jnp.bfloat16)
    weights = row_call(weights_kernel, out, where, logits, c)
    share = SAMPLES // parts
    start = (lax.axis_index("zl") * 4 + lax.axis_index("x")) * share
    column_out = lax.dynamic_slice_in_dim(c[0] * temper, start, share, 0)
    return (targets_call(weights, gathered), column_out)


def solution(mesh):
    fine = Mesh(mesh.devices.reshape(2, 4, 2, 2, 4), ("zh", "y", "core", "zl", "x"))
    samp, feat = ("zh", "y", "core"), FEAT
    in_specs = (P(samp, feat), P(samp, feat))
    out_specs = (P(samp, feat), P(feat))
    return jax.shard_map(local, mesh=fine, in_specs=in_specs, out_specs=out_specs, check_vma=False)
```

time: 424 us -> 508 us (1.20)
  Pallas kernels: 13.2 us -> 66.2 us
  matrix products: 33.5 us -> 0 us
  starting transfers between devices: 23.3 us -> 50.9 us
  waiting for transfers between devices: 320 us -> 345 us
  local copies, waits for them, and re-layouts: 4.38 us -> 24.7 us
  other arithmetic: 15.1 us -> 4.35 us
    ppermute x12 -> x38, waiting for transfers between devices: 25.8 us -> 160 us  [the longest x17 81.1 us: swap(): return lax.ppermute(x, 'zh' if dz else 'core', [(0, 1), (1, 0)])]
    psum x1 -> x0, waiting for transfers between devices: 103 us -> none  [local(): logits = lax.psum(partial, 'feat')]
    all_gather x1 -> x5, waiting for transfers between devices: 191 us -> 126 us  [the longest x4 116 us: sum_and_share(): return lax.all_gather(own, FEAT, axis=0, tiled=False)]
    reduce_scatter x0 -> x4, waiting for transfers between devices: none -> 58.8 us  [sum_and_share(): own = lax.psum_scatter(part, FEAT, scatter_dimension=0, tiled=False)]
    pallas_call x0 -> x5, Pallas kernels: none -> 49.2 us  [the longest x4 30.2 us: partial_call(): pl.pallas_call(functools.partial(partial_kernel, nq, widths, scale), out_...]
    dot_general x2 -> x0, matrix products: 33.5 us -> none  [the longest x1 16.8 us: local(): lax.dot_general(noise, everything, (((1,), (1,)), ((), ())), preferred_el...]
    ppermute x12 -> x38, starting transfers between devices: 23.2 us -> 50.6 us  [the longest x12 23.7 us: column_update(): stats = combine(stats, lax.ppermute(stats, axis, pairs))]
    unnamed x6 -> x48, local copies, waits for them, and re-layouts: 4.37 us -> 18.4 us
  transfers between devices with their start and end apart: 14 -> 47, of which waited for: 14 -> 28; matrix products, arithmetic and copies ran while one was open for 0% -> 2% of each run, Pallas kernels for 0% -> 9%
where the time goes in v2:
time: 508 us; the launch traced here: 506 us
  waiting for transfers between devices  345 us (68%)
  Pallas kernels  66.2 us (13%)
  starting transfers between devices  50.9 us (10%)
  local copies, waits for them, and re-layouts  24.7 us (5%)
  between operations  14.4 us (3%)
    all_gather x4, waiting for transfers between devices, sum_and_share(): return lax.all_gather(own, FEAT, axis=0, tiled=False)  116 us
    ppermute x17, waiting for transfers between devices, swap(): return lax.ppermute(x, 'zh' if dz else 'core', [(0, 1), (1, 0)])  81.1 us
    reduce_scatter x4, waiting for transfers between devices, sum_and_share(): own = lax.psum_scatter(part, FEAT, scatter_dimension=0, tiled=False)  58.8 us
    ppermute x6, waiting for transfers between devices, ring(): return lax.ppermute(x, 'y', [(i, (i + shift) % 4) for i in range(4)])  48.6 us
    pallas_call x4, Pallas kernels, partial_call(): pl.pallas_call(functools.partial(partial_kernel, nq, widths, scale), out_...  30.2 us
    ppermute x12, waiting for transfers between devices, column_update(): stats = combine(stats, lax.ppermute(stats, axis, pairs))  25.5 us
    ppermute x12, starting transfers between devices, column_update(): stats = combine(stats, lax.ppermute(stats, axis, pairs))  23.7 us
    pallas_call x1, Pallas kernels, targets_call(): pl.pallas_call(functools.partial(targets_kernel, widths), out_shape=jax.S...  19 us
  transfers between devices with their start and end apart: 47, of which 28 were waited for; matrix products, arithmetic and copies ran while one was open for 2% of the time, Pallas kernels for 9%

profile of v2, /device:TPU:0, one launch (start us, length us, event | category | flops | bytes accessed | tf_op | source)
XLA Modules:
  0.0 506.0 jit_solution(11908738718086549624)
XLA Ops:
  7.2 4.0 collective-permute-start.4
  19.0 38.2 %collective-permute-done.4.refs_0_.refs_2_ = bf16[256,4096]{1,0:T(8,128)(2,1)} collective-permute-done((bf16[256,4096]{1,0:T(8,128)(2,1)}, bf16[256,4096]{1,0:T(8,128)(2,1)}, u32[]{:S(2)}, u32[]{:S(2)}) %collective-permute-start.4) | collective-permute-done | bytes 2097184 | tf_op jit(solution)/shard_map/ppermute | solution.py:244
  58.6 6.8 %shard_map.41 = f32[8,2,32,512]{3,2,1,0:T(8,128)S(1)} custom-call(bf16[256,4096]{1,0:T(8,128)(2,1)S(1)} %copy-done, bf16[256,4096]{1,0:T(8,128)(2,1)} %copy-done.20, bf16[256,4096]{1,0:T(8,128)(2,1)} %refs_0_.7, bf16[128,4096]{1,0:T(8,128)(2,1)S(1)} %collective-permute-done.1.refs_3_.refs_1_, bf16[128,4096]{1,0:T(8,128)(2,1)S(1)} %collective-permute-done.2.refs_4_.refs_2_), custom_call_target="tpu_custom_call" | custom-call | tf_op jit(solution)/shard_map/pallas_call | solution.py:197
  70.7 23.7 %collective-permute-done.13.refs_4_.refs_5_ = bf16[128,4096]{1,0:T(8,128)(2,1)} collective-permute-done((bf16[128,4096]{1,0:T(8,128)(2,1)S(1)}, bf16[128,4096]{1,0:T(8,128)(2,1)}, u32[]{:S(2)}, u32[]{:S(2)}) %collective-permute-start.13) | collective-permute-done | bytes 1048608 | tf_op jit(solution)/shard_map/ppermute | solution.py:237
  94.6 7.7 %shard_map.44 = f32[8,4,32,256]{3,2,1,0:T(8,128)S(1)} custom-call(bf16[256,4096]{1,0:T(8,128)(2,1)S(1)} %copy-done, bf16[256,4096]{1,0:T(8,128)(2,1)} %copy-done.20, bf16[256,4096]{1,0:T(8,128)(2,1)} %collective-permute-done.4.refs_0_.refs_2_, bf16[256,4096]{1,0:T(8,128)(2,1)} %collective-permute-done.5.refs_1_.refs_3_, ...), custom_call_target="tpu_custom_call" | custom-call | tf_op jit(solution)/shard_map/pallas_call | solution.py:197
  105.1 24.6 %collective-permute-done.8.refs_4_.refs_3_ = bf16[128,4096]{1,0:T(8,128)(2,1)} collective-permute-done((bf16[128,4096]{1,0:T(8,128)(2,1)}, bf16[128,4096]{1,0:T(8,128)(2,1)}, u32[]{:S(2)}, u32[]{:S(2)}) %collective-permute-start.8) | collective-permute-done | bytes 1048608 | tf_op jit(solution)/shard_map/ppermute | solution.py:237
  129.7 7.7 %shard_map.43 = f32[8,4,32,256]{3,2,1,0:T(8,128)S(1)} custom-call(bf16[256,4096]{1,0:T(8,128)(2,1)S(1)} %copy-done, bf16[256,4096]{1,0:T(8,128)(2,1)} %copy-done.20, bf16[256,4096]{1,0:T(8,128)(2,1)} %collective-permute-done.4.refs_0_.refs_2_, bf16[256,4096]{1,0:T(8,128)(2,1)} %collective-permute-done.5.refs_1_.refs_3_, ...), custom_call_target="tpu_custom_call" | custom-call | tf_op jit(solution)/shard_map/pallas_call | solution.py:197
  139.8 7.9 %shard_map.42 = f32[8,2,32,512]{3,2,1,0:T(8,128)} custom-call(bf16[256,4096]{1,0:T(8,128)(2,1)} %collective-permute-done.4.refs_0_.refs_2_, bf16[256,4096]{1,0:T(8,128)(2,1)} %collective-permute-done.5.refs_1_.refs_3_, bf16[256,4096]{1,0:T(8,128)(2,1)} %refs_0_.7, bf16[128,4096]{1,0:T(8,128)(2,1)S(1)} %collective-permute-done.1.refs_3_.refs_1_, ...), custom_call_target="tpu_custom_call" | custom-call | tf_op jit(solution)/shard_map/pallas_call | solution.py:197
  151.8 3.2 collective-permute-start.16
  160.8 28.4 %reduce-scatter.9.cloned.1.call-done = f32[1,4,32,256]{3,2,1,0:T(8,128)} async-done(((f32[8,4,32,256]{3,2,1,0:T(8,128)}), f32[1,4,32,256]{3,2,1,0:T(8,128)}) %reduce-scatter.9.cloned.1.call-update) | async-done | bytes 131088 | tf_op jit(solution)/shard_map/reduce_scatter | solution.py:262
  190.0 3.0 collective-permute-start.11
  199.7 30.4 %reduce-scatter.7.cloned.1.call-done = f32[1,2,32,512]{3,2,1,0:T(8,128)} async-done(((f32[8,2,32,512]{3,2,1,0:T(8,128)}), f32[1,2,32,512]{3,2,1,0:T(8,128)}) %reduce-scatter.7.cloned.1.call-update) | async-done | bytes 131088 | tf_op jit(solution)/shard_map/reduce_scatter | solution.py:262
  230.9 3.0 collective-permute-start.6
  233.9 35.9 %collective-permute-done.6 = f32[32,512]{1,0:T(8,128)S(1)} collective-permute-done((f32[32,512]{1,0:T(8,128)S(1)}, f32[32,512]{1,0:T(8,128)S(1)}, u32[]{:S(2)}, u32[]{:S(2)}) %collective-permute-start.6) | collective-permute-done | bytes 65568 | tf_op jit(solution)/shard_map/ppermute | solution.py:244
  272.2 37.1 %all-gather.18.cloned.1.call-done = f32[32,32,256]{2,1,0:T(8,128)} async-done(((f32[4,32,256]{2,1,0:T(8,128)}), f32[32,32,256]{2,1,0:T(8,128)}) %all-gather.18.cloned.1.call-update) | async-done | bytes 1048592 | tf_op jit(solution)/shard_map/all_gather | solution.py:264
  309.3 39.6 %all-gather.16.cloned.1.call-done = f32[32,32,256]{2,1,0:T(8,128)} async-done(((f32[4,32,256]{2,1,0:T(8,128)}), f32[32,32,256]{2,1,0:T(8,128)}) %all-gather.16.cloned.1.call-update) | async-done | bytes 1048592 | tf_op jit(solution)/shard_map/all_gather | solution.py:264
  348.9 39.6 %all-gather.14.cloned.1.call-done = f32[16,32,512]{2,1,0:T(8,128)} async-done(((f32[2,32,512]{2,1,0:T(8,128)}), f32[16,32,512]{2,1,0:T(8,128)}) %all-gather.14.cloned.1.call-update) | async-done | bytes 1048592 | tf_op jit(solution)/shard_map/all_gather | solution.py:264
  393.5 4.6 shard_map.45
  403.6 3.1 collective-permute-start.20
  406.7 3.1 collective-permute-done.20
  409.8 2.9 collective-permute-start.21
  415.4 4.6 shard_map.46
  426.4 3.0 collective-permute-start.24
  429.4 3.1 collective-permute-done.24
  432.6 2.9 collective-permute-start.25
  438.3 4.6 shard_map.47
  446.3 2.8 collective-permute-done.27
  449.2 3.0 collective-permute-start.28
  455.4 2.8 collective-permute-start.29
  463.0 3.2 shard_map.48.w_ref
  468.2 9.8 %all-gather.10.cloned.1.call-done.refs_14_ = bf16[2048,4096]{1,0:T(8,128)(2,1)} async-done(((bf16[256,4096]{1,0:T(8,128)(2,1)}), bf16[2048,4096]{1,0:T(8,128)(2,1)}) %all-gather.10.cloned.1.call-update) | async-done | bytes 16777232 | tf_op jit(solution)/shard_map/all_gather | solution.py:306
  480.4 19.0 %shard_map.49 = bf16[256,4096]{1,0:T(8,128)(2,1)} custom-call(bf16[256,4096]{1,0:T(8,128)(2,1)} %copy-done.16, bf16[256,4096]{1,0:T(8,128)(2,1)} %refs_0_.7, bf16[128,4096]{1,0:T(8,128)(2,1)S(1)} %copy-done.11, bf16[128,4096]{1,0:T(8,128)(2,1)S(1)} %copy-done.15, bf16[128,4096]{1,0:T(8,128)(2,1)} %collective-permute-done.8.refs_4_.refs_3_, ...), custom_call_target="tpu_custom_call" | custom-call | tf_op jit(solution)/shard_map/pallas_call | solution.py:225
  (163 shorter events, 78.1 us)
Async XLA Ops:
  7.2 140.6 %reduce-scatter.5.cloned.1.call-start = ((), (), s32[]{:S(2)}) async-start(), calls=%async_computation.4 | async-start | bytes 1179648 | tf_op jit(solution)/shard_map/reduce_scatter | solution.py:262
  7.2 50.0 %collective-permute-start.4 = (bf16[256,4096]{1,0:T(8,128)(2,1)}, bf16[256,4096]{1,0:T(8,128)(2,1)}, u32[]{:S(2)}, u32[]{:S(2)}) collective-permute-start(bf16[256,4096]{1,0:T(8,128)(2,1)} %refs_0_.6), channel_id=1, source_target_pairs={{0,64},{64,0},{1,65},{65,1},{2,66},{66,2},{3,67},{67,3},{4,68},{68... | collective-permute-start | bytes 6291464 | tf_op jit(solution)/shard_map/ppermute | solution.py:244
  11.3 46.0 %collective-permute-start = (bf16[256,4096]{1,0:T(8,128)(2,1)}, bf16[256,4096]{1,0:T(8,128)(2,1)S(1)}, u32[]{:S(2)}, u32[]{:S(2)}) collective-permute-start(bf16[256,4096]{1,0:T(8,128)(2,1)} %refs_0_.6), channel_id=1, source_target_pairs={{0,8},{8,0},{1,9},{9,1},{2,10},{10,2},{3,11},{11,3},{4,12},{12,4},... | collective-permute-start | bytes 6291464 | tf_op jit(solution)/shard_map/ppermute | solution.py:244
  14.0 43.2 %collective-permute-start.1 = (bf16[128,4096]{1,0:T(8,128)(2,1)S(1)}, bf16[128,4096]{1,0:T(8,128)(2,1)S(1)}, u32[]{:S(2)}, u32[]{:S(2)}) collective-permute-start(bf16[128,4096]{1,0:T(8,128)(2,1)S(1)} %get-tuple-element.25), channel_id=1, source_target_pairs={{0,16},{16,32},{32,48},{48,0},{1,17},{17,33},{33,49},{49,1},{2,18}... | collective-permute-start | bytes 3145736 | tf_op jit(solution)/shard_map/ppermute | solution.py:237
  15.6 41.7 %collective-permute-start.2 = (bf16[128,4096]{1,0:T(8,128)(2,1)S(1)}, bf16[128,4096]{1,0:T(8,128)(2,1)S(1)}, u32[]{:S(2)}, u32[]{:S(2)}) collective-permute-start(bf16[128,4096]{1,0:T(8,128)(2,1)S(1)} %get-tuple-element.25), channel_id=1, source_target_pairs={{0,48},{16,0},{32,16},{48,32},{1,49},{17,1},{33,17},{49,33},{2,50}... | collective-permute-start | bytes 3145736 | tf_op jit(solution)/shard_map/ppermute | solution.py:237
  17.2 51.8 %collective-permute-start.9 = (bf16[128,4096]{1,0:T(8,128)(2,1)}, bf16[128,4096]{1,0:T(8,128)(2,1)}, u32[]{:S(2)}, u32[]{:S(2)}) collective-permute-start(bf16[128,4096]{1,0:T(8,128)(2,1)} %get-tuple-element.24), channel_id=1, source_target_pairs={{0,48},{16,0},{32,16},{48,32},{1,49},{17,1},{33,17},{49,33},{2,50}... | collective-permute-start | bytes 3145736 | tf_op jit(solution)/shard_map/ppermute | solution.py:237
  57.2 37.4 %collective-permute-start.5 = (bf16[256,4096]{1,0:T(8,128)(2,1)}, bf16[256,4096]{1,0:T(8,128)(2,1)}, u32[]{:S(2)}, u32[]{:S(2)}) collective-permute-start(bf16[256,4096]{1,0:T(8,128)(2,1)} %collective-permute-done.4.refs_0_.refs_2_), channel_id=1, source_target_pairs={{0,8},{8,0},{1,9},{9,1},{2,10},{10,2},{3,11},{11,3},{4,12},{12,4},... | collective-permute-start | bytes 6291464 | tf_op jit(solution)/shard_map/ppermute | solution.py:244
  67.3 83.4 %reduce-scatter.11.cloned.1.call-start = ((), (), s32[]{:S(2)}) async-start(), calls=%async_computation.7 | async-start | bytes 1179648 | tf_op jit(solution)/shard_map/reduce_scatter | solution.py:262
  67.4 27.0 %collective-permute-start.13 = (bf16[128,4096]{1,0:T(8,128)(2,1)S(1)}, bf16[128,4096]{1,0:T(8,128)(2,1)}, u32[]{:S(2)}, u32[]{:S(2)}) collective-permute-start(bf16[128,4096]{1,0:T(8,128)(2,1)S(1)} %collective-permute-done.1.refs_3_.refs_1_), channel_id=1, source_target_pairs={{0,16},{16,32},{32,48},{48,0},{1,17},{17,33},{33,49},{49,1},{2,18}... | collective-permute-start | bytes 3145736 | tf_op jit(solution)/shard_map/ppermute | solution.py:237
  69.0 25.6 %collective-permute-start.14 = (bf16[128,4096]{1,0:T(8,128)(2,1)}, bf16[128,4096]{1,0:T(8,128)(2,1)}, u32[]{:S(2)}, u32[]{:S(2)}) collective-permute-start(bf16[128,4096]{1,0:T(8,128)(2,1)} %collective-permute-done.9.refs_5_.refs_4_), channel_id=1, source_target_pairs={{0,48},{16,0},{32,16},{48,32},{1,49},{17,1},{33,17},{49,33},{2,50}... | collective-permute-start | bytes 3145736 | tf_op jit(solution)/shard_map/ppermute | solution.py:237
  103.4 85.7 %reduce-scatter.9.cloned.1.call-start = ((), (), s32[]{:S(2)}) async-start(), calls=%async_computation.6 | async-start | bytes 1179648 | tf_op jit(solution)/shard_map/reduce_scatter | solution.py:262
  103.5 26.3 %collective-permute-start.8 = (bf16[128,4096]{1,0:T(8,128)(2,1)}, bf16[128,4096]{1,0:T(8,128)(2,1)}, u32[]{:S(2)}, u32[]{:S(2)}) collective-permute-start(bf16[128,4096]{1,0:T(8,128)(2,1)} %get-tuple-element.24), channel_id=1, source_target_pairs={{0,16},{16,32},{32,48},{48,0},{1,17},{17,33},{33,49},{49,1},{2,18}... | collective-permute-start | bytes 3145736 | tf_op jit(solution)/shard_map/ppermute | solution.py:237
  138.5 91.6 %reduce-scatter.7.cloned.1.call-start = ((), (), s32[]{:S(2)}) async-start(), calls=%async_computation.5 | async-start | bytes 1179648 | tf_op jit(solution)/shard_map/reduce_scatter | solution.py:262
  147.7 124.5 %all-gather.12.cloned.1.call-start = ((), (), s32[]{:S(2)}) async-start(), calls=%async_computation.9 | async-start | bytes 1179648 | tf_op jit(solution)/shard_map/all_gather | solution.py:264
  150.7 158.6 %all-gather.18.cloned.1.call-start = ((), (), s32[]{:S(2)}) async-start(), calls=%async_computation.12 | async-start | bytes 1179648 | tf_op jit(solution)/shard_map/all_gather | solution.py:264
  160.7 188.2 %all-gather.16.cloned.1.call-start = ((), (), s32[]{:S(2)}) async-start(), calls=%async_computation.11 | async-start | bytes 1179648 | tf_op jit(solution)/shard_map/all_gather | solution.py:264
  198.6 189.9 %all-gather.14.cloned.1.call-start = ((), (), s32[]{:S(2)}) async-start(), calls=%async_computation.10 | async-start | bytes 1179648 | tf_op jit(solution)/shard_map/all_gather | solution.py:264
  198.7 71.8 %collective-permute-start.37 = (bf16[256,4096]{1,0:T(8,128)(2,1)}, bf16[256,4096]{1,0:T(8,128)(2,1)S(1)}, u32[]{:S(2)}, u32[]{:S(2)}) collective-permute-start(bf16[256,4096]{1,0:T(8,128)(2,1)} %refs_0_.7), channel_id=1, source_target_pairs={{0,64},{64,0},{1,65},{65,1},{2,66},{66,2},{3,67},{67,3},{4,68},{68... | collective-permute-start | bytes 6291464 | tf_op jit(solution)/shard_map/ppermute | solution.py:244
  230.9 38.8 %collective-permute-start.6 = (f32[32,512]{1,0:T(8,128)S(1)}, f32[32,512]{1,0:T(8,128)S(1)}, u32[]{:S(2)}, u32[]{:S(2)}) collective-permute-start(f32[32,512]{1,0:T(8,128)S(1)} %get-tuple-element.34), channel_id=1, source_target_pairs={{0,64},{64,0},{1,65},{65,1},{2,66},{66,2},{3,67},{67,3},{4,68},{68... | collective-permute-start | bytes 196616 | tf_op jit(solution)/shard_map/ppermute | solution.py:244
  233.9 35.9 %collective-permute-start.7 = (f32[32,512]{1,0:T(8,128)S(1)}, f32[32,512]{1,0:T(8,128)S(1)}, u32[]{:S(2)}, u32[]{:S(2)}) collective-permute-start(f32[32,512]{1,0:T(8,128)S(1)} %get-tuple-element.35), channel_id=1, source_target_pairs={{0,72},{8,64},{64,8},{72,0},{1,73},{9,65},{65,9},{73,1},{2,74},{10... | collective-permute-start | bytes 196616 | tf_op jit(solution)/shard_map/ppermute | solution.py:242
  270.4 207.5 %all-gather.10.cloned.1.call-start = ((), (), s32[]{:S(2)}) async-start(), calls=%async_computation.8 | async-start | bytes 18874368 | tf_op jit(solution)/shard_map/all_gather | solution.py:306
  403.6 6.2 %collective-permute-start.20 = (f32[2,4096]{1,0:T(2,128)S(1)}, f32[2,4096]{1,0:T(2,128)S(1)}, u32[]{:S(2)}, u32[]{:S(2)}) collective-permute-start(f32[2,4096]{1,0:T(2,128)S(1)} %pad_maximum_fusion.5), channel_id=1, source_target_pairs={{0,32},{16,48},{32,0},{48,16},{1,33},{17,49},{33,1},{49,17},{2,34}... | collective-permute-start | bytes 98312 | tf_op jit(solution)/shard_map/ppermute | solution.py:138
  426.4 6.2 %collective-permute-start.24 = (f32[2,4096]{1,0:T(2,128)S(1)}, f32[2,4096]{1,0:T(2,128)S(1)}, u32[]{:S(2)}, u32[]{:S(2)}) collective-permute-start(f32[2,4096]{1,0:T(2,128)S(1)} %pad_maximum_fusion.8), channel_id=1, source_target_pairs={{0,32},{16,48},{32,0},{48,16},{1,33},{17,49},{33,1},{49,17},{2,34}... | collective-permute-start | bytes 98312 | tf_op jit(solution)/shard_map/ppermute | solution.py:138
  449.2 6.2 %collective-permute-start.28 = (f32[2,4096]{1,0:T(2,128)S(1)}, f32[2,4096]{1,0:T(2,128)S(1)}, u32[]{:S(2)}, u32[]{:S(2)}) collective-permute-start(f32[2,4096]{1,0:T(2,128)S(1)} %pad_maximum_fusion.11), channel_id=1, source_target_pairs={{0,32},{16,48},{32,0},{48,16},{1,33},{17,49},{33,1},{49,17},{2,34}... | collective-permute-start | bytes 98312 | tf_op jit(solution)/shard_map/ppermute | solution.py:138
  452.2 16.0 %collective-permute-start.30 = (bf16[256,4096]{1,0:T(8,128)(2,1)}, bf16[256,4096]{1,0:T(8,128)(2,1)}, u32[]{:S(2)}, u32[]{:S(2)}) collective-permute-start(bf16[256,4096]{1,0:T(8,128)(2,1)} %refs_0_.7), channel_id=1, source_target_pairs={{0,8},{8,0},{1,9},{9,1},{2,10},{10,2},{3,11},{11,3},{4,12},{12,4},... | collective-permute-start | bytes 6291464 | tf_op jit(solution)/shard_map/ppermute | solution.py:244
  452.2 6.1 %collective-permute-start.31 = (bf16[128,4096]{1,0:T(8,128)(2,1)S(1)}, bf16[128,4096]{1,0:T(8,128)(2,1)S(1)}, u32[]{:S(2)}, u32[]{:S(2)}) collective-permute-start(bf16[128,4096]{1,0:T(8,128)(2,1)S(1)} %copy-done.10), channel_id=1, source_target_pairs={{0,8},{8,0},{1,9},{9,1},{2,10},{10,2},{3,11},{11,3},{4,12},{12,4},... | collective-permute-start | bytes 3145736 | tf_op jit(solution)/shard_map/ppermute | solution.py:244
  452.7 7.6 %collective-permute-start.32 = (bf16[128,4096]{1,0:T(8,128)(2,1)S(1)}, bf16[128,4096]{1,0:T(8,128)(2,1)S(1)}, u32[]{:S(2)}, u32[]{:S(2)}) collective-permute-start(bf16[128,4096]{1,0:T(8,128)(2,1)S(1)} %copy-done.14), channel_id=1, source_target_pairs={{0,8},{8,0},{1,9},{9,1},{2,10},{10,2},{3,11},{11,3},{4,12},{12,4},... | collective-permute-start | bytes 3145736 | tf_op jit(solution)/shard_map/ppermute | solution.py:244
  455.4 5.9 %collective-permute-start.29 = (f32[2,4096]{1,0:T(2,128)S(1)}, f32[2,4096]{1,0:T(2,128)S(1)}, u32[]{:S(2)}, u32[]{:S(2)}) collective-permute-start(f32[2,4096]{1,0:T(2,128)S(1)} %pad_maximum_fusion.12), channel_id=1, source_target_pairs={{0,64},{64,0},{1,65},{65,1},{2,66},{66,2},{3,67},{67,3},{4,68},{68... | collective-permute-start | bytes 98312 | tf_op jit(solution)/shard_map/ppermute | solution.py:138
  458.3 9.9 %collective-permute-start.34 = (bf16[128,4096]{1,0:T(8,128)(2,1)}, bf16[128,4096]{1,0:T(8,128)(2,1)}, u32[]{:S(2)}, u32[]{:S(2)}) collective-permute-start(bf16[128,4096]{1,0:T(8,128)(2,1)} %collective-permute-done.9.refs_5_.refs_4_), channel_id=1, source_target_pairs={{0,8},{8,0},{1,9},{9,1},{2,10},{10,2},{3,11},{11,3},{4,12},{12,4},... | collective-permute-start | bytes 3145736 | tf_op jit(solution)/shard_map/ppermute | solution.py:244
  458.3 9.9 %collective-permute-start.33 = (bf16[128,4096]{1,0:T(8,128)(2,1)}, bf16[128,4096]{1,0:T(8,128)(2,1)}, u32[]{:S(2)}, u32[]{:S(2)}) collective-permute-start(bf16[128,4096]{1,0:T(8,128)(2,1)} %collective-permute-done.8.refs_4_.refs_3_), channel_id=1, source_target_pairs={{0,8},{8,0},{1,9},{9,1},{2,10},{10,2},{3,11},{11,3},{4,12},{12,4},... | collective-permute-start | bytes 3145736 | tf_op jit(solution)/shard_map/ppermute | solution.py:244
  460.3 7.9 %collective-permute-start.35 = (bf16[128,4096]{1,0:T(8,128)(2,1)}, bf16[128,4096]{1,0:T(8,128)(2,1)}, u32[]{:S(2)}, u32[]{:S(2)}) collective-permute-start(bf16[128,4096]{1,0:T(8,128)(2,1)} %collective-permute-done.13.refs_4_.refs_5_), channel_id=1, source_target_pairs={{0,8},{8,0},{1,9},{9,1},{2,10},{10,2},{3,11},{11,3},{4,12},{12,4},... | collective-permute-start | bytes 3145736 | tf_op jit(solution)/shard_map/ppermute | solution.py:244
  461.3 6.9 %collective-permute-start.36 = (bf16[128,4096]{1,0:T(8,128)(2,1)}, bf16[128,4096]{1,0:T(8,128)(2,1)}, u32[]{:S(2)}, u32[]{:S(2)}) collective-permute-start(bf16[128,4096]{1,0:T(8,128)(2,1)} %collective-permute-done.14.refs_5_.refs_6_), channel_id=1, source_target_pairs={{0,8},{8,0},{1,9},{9,1},{2,10},{10,2},{3,11},{11,3},{4,12},{12,4},... | collective-permute-start | bytes 3145736 | tf_op jit(solution)/shard_map/ppermute | solution.py:244
  (39 other events, 332.8 us)
Sparse Core Ops, SparseCore 0:
  67.5 41.0 reduce-scatter.4
  110.9 37.7 reduce-scatter.10
  151.2 37.8 reduce-scatter.8
  191.9 38.0 reduce-scatter.6
  231.5 37.9 all-gather.11
  271.0 38.2 all-gather.17
  310.9 37.9 all-gather.15
  350.6 37.9 all-gather.13
  390.8 87.0 all-gather.9

commit v3 on v2

--- a/solution.py
+++ b/solution.py
@@ -14,6 +14,7 @@
 LANES = 128
 ROWS = 32
 GROUP = 4
+SPREAD = 2
 DEPTH = 1024
 FEAT = ("zl", "x")
 
@@ -132,8 +133,12 @@
     return jnp.stack([peak, total])
 
 
-def column_update(stats):
-    for axis, n, step in (("core", 2, 1), ("y", 4, 1), ("y", 4, 2), ("zh", 2, 1)):
+SAMP_STEPS = (("core", 2, 1), ("y", 4, 1), ("y", 4, 2), ("zh", 2, 1))
+FEAT_STEPS = (("zl", 2, 1), ("x", 4, 1), ("x", 4, 2))
+
+
+def column_update(stats, steps):
+    for axis, n, step in steps:
         pairs = [(i, i ^ step) for i in range(n)]
         stats = combine(stats, lax.ppermute(stats, axis, pairs))
     return -(stats[0] + jnp.log(stats[1]))[None, :]
@@ -147,65 +152,79 @@
     return acc
 
 
-def partial_kernel(nq, widths, scale, *refs):
-    n_refs, x_refs = refs[:nq], refs[nq:nq + len(widths)]
-    out_ref, noise_sq, data_sq = refs[nq + len(widths):]
+def partial_kernel(jobs, scale, *refs):
+    n_count = 1 + max(q for qs, _ in jobs for q in qs)
+    x_count = 1 + max(x for _, xs in jobs for x in xs)
+    where, refs = refs[0], refs[1:]
+    n_refs, n_sq, x_refs = refs[:n_count], refs[n_count:2 * n_count], refs[2 * n_count:2 * n_count + x_count]
+    outs, (acc, x_sq) = refs[2 * n_count + x_count:-2], refs[-2:]
     step = pl.program_id(0)
     rows = n_refs[0].shape[0]
-    parts = out_ref.shape[0]
-    share = rows // parts
+    parts, share, _ = acc.shape
 
     @pl.when(step == 0)
     def _():
-        out_ref[...] = jnp.zeros_like(out_ref)
-        noise_sq[...] = jnp.zeros_like(noise_sq)
-        data_sq[...] = jnp.zeros_like(data_sq)
-
-    for q in range(nq):
-        block = n_refs[q][...]
-        noise_sq[q] += lane_sums(block)
-        first = 0
-        for x, width in zip(x_refs, widths):
+        acc[...] = jnp.zeros_like(acc)
+        x_sq[...] = jnp.zeros_like(x_sq)
+
+    places, first = [], 0
+    for qs, xs in jobs:
+        widths = [x_refs[x].shape[0] for x in xs]
+        block = jnp.concatenate([n_refs[q][...] for q in qs], axis=0)
+        offset = first
+        for x, width in zip(xs, widths):
             inner = lax.dot_general(
-                block, x[...], (((1,), (1,)), ((), ())), preferred_element_type=jnp.float32
+                block, x_refs[x][...], (((1,), (1,)), ((), ())), preferred_element_type=jnp.float32
             )
-            out_ref[:, q, :, first:first + width] += inner.reshape(parts, share, width)
-            first += width
-    first = 0
-    for x, width in zip(x_refs, widths):
-        data_sq[first:first + width, :] += lane_sums(x[...])
-        first += width
+            for i, q in enumerate(qs):
+                at = offset + i * sum(widths)
+                part = inner[i * rows:(i + 1) * rows].reshape(parts, share, width)
+                acc[:, :, at:at + width] += part
+                places.append((q, x, at))
+            offset += width
+        first += len(qs) * sum(widths)
+    starts = [sum(r.shape[0] for r in x_refs[:x]) for x in range(x_count)]
+    for x, start in zip(x_refs, starts):
+        x_sq[start:start + x.shape[0], :] += lane_sums(x[...])
 
     @pl.when(step == pl.num_programs(0) - 1)
     def _():
         columns = lax.dot_general(
-            jnp.ones((8, LANES), jnp.float32), data_sq[...], (((1,), (1,)), ((), ())),
+            jnp.ones((8, LANES), jnp.float32), x_sq[...], (((1,), (1,)), ((), ())),
             precision=lax.Precision.HIGHEST, preferred_element_type=jnp.float32,
         )[0:1]
-        for q in range(nq):
-            square = jnp.sum(noise_sq[q], axis=1, keepdims=True)
-            for f in range(parts):
-                own = square[f * share:(f + 1) * share]
-                out_ref[f, q] = (own + columns - 2.0 * out_ref[f, q]) * scale
-
-
-def partial_call(scale, parts, noises, datas):
-    nq, widths = len(noises), tuple(d.shape[0] for d in datas)
+        for d, out in zip((0, 1, -1, 2), outs):
+            for z in range(2):
+                f = (where[1] + z) % 2 * 4 + (where[0] + d + 4) % 4
+                for q, x, at in places:
+                    width = x_refs[x].shape[0]
+                    own = n_sq[q][pl.ds(f * share, share), :]
+                    other = columns[:, starts[x]:starts[x] + width]
+                    inner = acc[f, :, at:at + width]
+                    out[z, :, at:at + width] = (own + other - 2.0 * inner) * scale
+
+
+def partial_call(scale, parts, where, noises, squares, datas, jobs):
     rows, depth = noises[0].shape
-    shape = (parts, nq, rows // parts, sum(widths))
+    total = sum(len(qs) * sum(datas[x].shape[0] for x in xs) for qs, xs in jobs)
+    share = rows // parts
     block = DEPTH
+    out = (2, share, total)
     return pl.pallas_call(
-        functools.partial(partial_kernel, nq, widths, scale),
-        out_shape=jax.ShapeDtypeStruct(shape, jnp.float32),
+        functools.partial(partial_kernel, jobs, scale),
+        out_shape=[jax.ShapeDtypeStruct(out, jnp.float32)] * 4,
         grid=(depth // block,),
-        in_specs=[pl.BlockSpec((a.shape[0], block), lambda k: (0, k)) for a in (*noises, *datas)],
-        out_specs=pl.BlockSpec(shape, lambda k: (0, 0, 0, 0)),
+        in_specs=[pl.BlockSpec(memory_space=pltpu.SMEM)]
+        + [pl.BlockSpec((rows, block), lambda k: (0, k)) for _ in noises]
+        + [pl.BlockSpec((rows, 1), lambda k: (0, 0)) for _ in noises]
+        + [pl.BlockSpec((d.shape[0], block), lambda k: (0, k)) for d in datas],
+        out_specs=[pl.BlockSpec(out, lambda k: (0, 0, 0))] * 4,
         scratch_shapes=[
-            pltpu.VMEM((nq, rows, LANES), jnp.float32),
-            pltpu.VMEM((sum(widths), LANES), jnp.float32),
+            pltpu.VMEM((parts, share, total), jnp.float32),
+            pltpu.VMEM((sum(d.shape[0] for d in datas), LANES), jnp.float32),
         ],
         compiler_params=pltpu.CompilerParams(vmem_limit_bytes=48 * 2**20),
-    )(*noises, *datas)
+    )(where, *noises, *squares, *datas)
 
 
 def targets_kernel(widths, w_ref, *refs):
@@ -258,23 +277,26 @@
 QUARTERS = [(0, 0), (0, 1), (1, 0), (1, 1)]
 
 
-def sum_and_share(part, quarters):
-    own = lax.psum_scatter(part, FEAT, scatter_dimension=0, tiled=False)
-    own = jnp.stack([swap(own[i], *q) for i, q in enumerate(quarters)])
-    return lax.all_gather(own, FEAT, axis=0, tiled=False)
-
-
-def tables(chunks):
+def sum_over_feat(pieces):
+    own, right, left, across = pieces
+    for piece, step in ((right, 1), (left, -1), (across, 2)):
+        own = own + lax.ppermute(piece, "x", [(i, (i + step) % 4) for i in range(4)])
+    return own[0] + lax.ppermute(own[1], "zl", [(0, 1), (1, 0)])
+
+
+def tables(parts):
     zh, y, core = (lax.axis_index(a) for a in ("zh", "y", "core"))
     where, place = [], []
-    for quarters, sources in chunks:
-        for dz, dc in quarters:
-            for s in sources:
-                dy, half = SOURCES[s]
-                inside = ((y + dy + 4) % 4 * 2 + (core + dc) % 2) * 2 + half
-                where.append((zh + dz) % 2 * 16 + inside)
-                place.append(16 + inside if dz else jnp.int32(dc * 8 + s))
+    for dz, dc in QUARTERS:
+        for s, (dy, half) in enumerate(SOURCES):
+            inside = ((y + dy + 4) % 4 * 2 + (core + dc) % 2) * 2 + half
+            where.append((zh + dz) % 2 * 16 + inside)
+            place.append(16 + inside if dz else jnp.int32(dc * 8 + s))
     return jnp.stack([jnp.stack(where), jnp.stack(place)]).astype(jnp.int32)
+
+
+def row_squares(x):
+    return jnp.sum(jnp.square(x.astype(jnp.float32)), axis=1, keepdims=True)
 
 
 def local(noise, data):
@@ -288,30 +310,37 @@
     data, far[0] = lax.optimization_barrier((data, far[0]))
     other = swap(data, 1, 0)
 
-    first, second, third = blocks[:3], blocks[3:5], blocks[5:]
     everyone = near + far
-    p1 = partial_call(scale, parts, near, first)
-    p2 = partial_call(scale, parts, far, first)
-    p3 = partial_call(scale, parts, everyone, second)
-    p4 = partial_call(scale, parts, everyone, third)
-    chunks = [
-        (QUARTERS[:2], (0, 1, 2, 3)),
-        (QUARTERS[2:], (0, 1, 2, 3)),
-        (QUARTERS, (4, 5)),
-        (QUARTERS, (6, 7)),
-    ]
-    logits = [sum_and_share(p, q) for p, (q, _) in zip((p1, p2, p3, p4), chunks)]
-    where = tables(chunks)
-
+    squares = [row_squares(n) for n in everyone]
+    here = jnp.stack([lax.axis_index("x"), lax.axis_index("zl")]).astype(jnp.int32)
+    call = functools.partial(partial_call, scale, parts, here)
+    pieces = call(near, squares[:2], blocks[:3], (((0, 1), (0, 1, 2)),))
+    sum1 = sum_over_feat(pieces)
+    pieces = call(everyone, squares, blocks[:5], (((2, 3), (0, 1, 2)), ((0, 1, 2, 3), (3, 4))))
+    sum2 = sum_over_feat(pieces)
+    pieces = call(everyone, squares, blocks[5:], (((0, 1, 2, 3), (0, 1)),))
+    sum3 = sum_over_feat(pieces)
+    quarters = []
+    for i, q in enumerate(QUARTERS):
+        head = sum2[:, (i - 2) * 512:(i - 1) * 512] if i >= 2 else sum1[:, i * 512:(i + 1) * 512]
+        middle = sum2[:, 1024 + i * 256:1280 + i * 256]
+        quarters.append(swap(jnp.concatenate([head, middle, sum3[:, i * 256:(i + 1) * 256]], axis=1), *q))
+    own = jnp.stack(quarters)
+    where = tables(parts)
+
+    shared = lax.all_gather(own, FEAT, axis=0, tiled=False)
     others = lax.all_gather(other, ("y", "core"), axis=0, tiled=True)
     gathered = blocks + [swap(b, 0, 1) for b in blocks] + [others]
 
     c = jnp.zeros((1, SAMPLES), jnp.float32)
-    for _ in range(ITERS):
+    for i in range(ITERS):
         out = jax.ShapeDtypeStruct((2, SAMPLES), jnp.float32)
-        c = column_update(row_call(sinkhorn_kernel, out, where, logits, c))
+        if i < SPREAD:
+            c = column_update(row_call(sinkhorn_kernel, out, where, [own[None]], c), SAMP_STEPS + FEAT_STEPS)
+        else:
+            c = column_update(row_call(sinkhorn_kernel, out, where, [shared], c), SAMP_STEPS)
     out = jax.ShapeDtypeStruct((noise.shape[0], SAMPLES), jnp.bfloat16)
-    weights = row_call(weights_kernel, out, where, logits, c)
+    weights = row_call(weights_kernel, out, where, [shared], c)
     share = SAMPLES // parts
     start = (lax.axis_index("zl") * 4 + lax.axis_index("x")) * share
     column_out = lax.dynamic_slice_in_dim(c[0] * temper, start, share, 0)

time: 508 us -> 419 us (0.82)
  waiting for transfers between devices: 345 us -> 249 us
  starting transfers between devices: 50.9 us -> 71.5 us
  local copies, waits for them, and re-layouts: 24.7 us -> 12.6 us
  Pallas kernels: 66.2 us -> 56.7 us
  other arithmetic: 4.35 us -> 12.5 us
    all_gather x4 -> x1, waiting for transfers between devices: 116 us -> 0.02 us  [local(): shared = lax.all_gather(own, FEAT, axis=0, tiled=False)]
    reduce_scatter x4 -> x0, waiting for transfers between devices: 58.8 us -> none  [sum_and_share(): own = lax.psum_scatter(part, FEAT, scatter_dimension=0, tiled=False)]
    ppermute x17 -> x13, waiting for transfers between devices: 81.1 us -> 137 us  [swap(): return lax.ppermute(x, 'zh' if dz else 'core', [(0, 1), (1, 0)])]
    ppermute x0 -> x12, waiting for transfers between devices: none -> 27.7 us  [the longest x9 22.6 us: sum_over_feat(): lax.ppermute(piece, 'x', [(i, (i + step) % 4) for i in range(4)])]
    ppermute x12 -> x18, waiting for transfers between devices: 25.5 us -> 45.2 us  [column_update(): stats = combine(stats, lax.ppermute(stats, axis, pairs))]
    ppermute x0 -> x12, starting transfers between devices: none -> 19.2 us  [the longest x9 15.2 us: sum_over_feat(): lax.ppermute(piece, 'x', [(i, (i + step) % 4) for i in range(4)])]
    ppermute x6, waiting for transfers between devices: 48.6 us -> 35.7 us  [ring(): return lax.ppermute(x, 'y', [(i, (i + shift) % 4) for i in range(4)])]
    unnamed x48 -> x22, local copies, waits for them, and re-layouts: 18.4 us -> 7.35 us
  transfers between devices with their start and end apart: 47 -> 52, of which waited for: 28 -> 29; matrix products, arithmetic and copies ran while one was open for 2% -> 4% of each run, Pallas kernels for 9% -> 9%
where the time goes in v3:
time: 419 us; the launch traced here: 417 us
  waiting for transfers between devices  249 us (59%)
  starting transfers between devices  71.5 us (17%)
  Pallas kernels  56.7 us (14%)
  between operations  14.7 us (4%)
  local copies, waits for them, and re-layouts  12.6 us (3%)
  other arithmetic  12.5 us (3%)
    ppermute x13, waiting for transfers between devices, swap(): return lax.ppermute(x, 'zh' if dz else 'core', [(0, 1), (1, 0)])  137 us
    ppermute x18, waiting for transfers between devices, column_update(): stats = combine(stats, lax.ppermute(stats, axis, pairs))  45.2 us
    ppermute x6, waiting for transfers between devices, ring(): return lax.ppermute(x, 'y', [(i, (i + shift) % 4) for i in range(4)])  35.7 us
    ppermute x18, starting transfers between devices, column_update(): stats = combine(stats, lax.ppermute(stats, axis, pairs))  30.8 us
    pallas_call x3, Pallas kernels, partial_call(): pl.pallas_call(functools.partial(partial_kernel, jobs, scale), out_shape=...  27.7 us
    ppermute x9, waiting for transfers between devices, sum_over_feat(): lax.ppermute(piece, 'x', [(i, (i + step) % 4) for i in range(4)])  22.6 us
    pallas_call x1, Pallas kernels, targets_call(): pl.pallas_call(functools.partial(targets_kernel, widths), out_shape=jax.S...  19.2 us
    ppermute x9, starting transfers between devices, sum_over_feat(): lax.ppermute(piece, 'x', [(i, (i + step) % 4) for i in range(4)])  15.2 us
  transfers between devices with their start and end apart: 52, of which 29 were waited for; matrix products, arithmetic and copies ran while one was open for 4% of the time, Pallas kernels for 9%

profile of v3, /device:TPU:0, one launch (start us, length us, event | category | flops | bytes accessed | tf_op | source)
XLA Modules:
  0.0 417.2 jit_solution(4428183874857206314)
XLA Ops:
  7.2 4.0 collective-permute-start.7
  11.3 45.9 %collective-permute-done.7.refs_3_ = bf16[256,4096]{1,0:T(8,128)(2,1)} collective-permute-done((bf16[256,4096]{1,0:T(8,128)(2,1)}, bf16[256,4096]{1,0:T(8,128)(2,1)}, u32[]{:S(2)}, u32[]{:S(2)}) %collective-permute-start.7) | collective-permute-done | bytes 2097184 | tf_op jit(solution)/shard_map/ppermute | solution.py:263
  57.2 3.1 fusion.28
  68.3 19.1 %collective-permute-done.1.refs_6_.refs_10_.refs_1_ = bf16[128,4096]{1,0:T(8,128)(2,1)S(1)} collective-permute-done((bf16[128,4096]{1,0:T(8,128)(2,1)}, bf16[128,4096]{1,0:T(8,128)(2,1)S(1)}, u32[]{:S(2)}, u32[]{:S(2)}) %collective-permute-start.1) | collective-permute-done | bytes 1048608 | tf_op jit(solution)/shard_map/ppermute | solution.py:256
  88.2 7.5 %shard_map.41 = (f32[2,32,1024]{2,1,0:T(8,128)S(1)}, f32[2,32,1024]{2,1,0:T(8,128)S(1)}, f32[2,32,1024]{2,1,0:T(8,128)S(1)}, f32[2,32,1024]{2,1,0:T(8,128)}) custom-call(s32[2]{0:T(128)S(1)} %pad_add_fusion.1.refs_0_, bf16[256,4096]{1,0:T(8,128)(2,1)S(1)} %copy-done, bf16[256,4096]{1,0:T(8,128)(2,1)} %collective-permute-done.refs_2_, ...), custom_call_target="tpu_custom_call" | custom-call | tf_op jit(solution)/shard_map/pallas_call | solution.py:213
  100.5 9.4 %collective-permute-done.10.refs_13_.refs_4_ = bf16[128,4096]{1,0:T(8,128)(2,1)} collective-permute-done((bf16[128,4096]{1,0:T(8,128)(2,1)}, bf16[128,4096]{1,0:T(8,128)(2,1)}, u32[]{:S(2)}, u32[]{:S(2)}) %collective-permute-start.10) | collective-permute-done | bytes 1048608 | tf_op jit(solution)/shard_map/ppermute | solution.py:256
  110.0 2.9 collective-permute-start.16
  112.9 3.0 collective-permute-start.5
  118.3 3.8 collective-permute-done.5
  128.9 6.4 %collective-permute-done.16.refs_10_.refs_6_ = bf16[128,4096]{1,0:T(8,128)(2,1)} collective-permute-done((bf16[128,4096]{1,0:T(8,128)(2,1)}, bf16[128,4096]{1,0:T(8,128)(2,1)}, u32[]{:S(2)}, u32[]{:S(2)}) %collective-permute-start.16) | collective-permute-done | bytes 1048608 | tf_op jit(solution)/shard_map/ppermute | solution.py:256
  136.2 7.7 %shard_map.43 = (f32[2,32,1024]{2,1,0:T(8,128)S(1)}, f32[2,32,1024]{2,1,0:T(8,128)S(1)}, f32[2,32,1024]{2,1,0:T(8,128)S(1)}, f32[2,32,1024]{2,1,0:T(8,128)S(1)}) custom-call(s32[2]{0:T(128)S(1)} %pad_add_fusion.1.refs_0_, bf16[256,4096]{1,0:T(8,128)(2,1)S(1)} %copy-done, bf16[256,4096]{1,0:T(8,128)(2,1)} %collective-permute-done.refs_2_, ...), custom_call_target="tpu_custom_call" | custom-call | tf_op jit(solution)/shard_map/pallas_call | solution.py:213
  149.9 12.5 %shard_map.42 = (f32[2,32,2048]{2,1,0:T(8,128)S(1)}, f32[2,32,2048]{2,1,0:T(8,128)S(1)}, f32[2,32,2048]{2,1,0:T(8,128)S(1)}, f32[2,32,2048]{2,1,0:T(8,128)S(1)}) custom-call(s32[2]{0:T(128)S(1)} %pad_add_fusion.1.refs_0_, bf16[256,4096]{1,0:T(8,128)(2,1)} %refs_1_.5, bf16[256,4096]{1,0:T(8,128)(2,1)} %collective-permute-done.refs_2_, ...), custom_call_target="tpu_custom_call" | custom-call | tf_op jit(solution)/shard_map/pallas_call | solution.py:213
  167.7 18.8 %collective-permute-done.11 = f32[2,32,2048]{2,1,0:T(8,128)S(1)} collective-permute-done((f32[2,32,2048]{2,1,0:T(8,128)S(1)}, f32[2,32,2048]{2,1,0:T(8,128)S(1)}, u32[]{:S(2)}, u32[]{:S(2)}) %collective-permute-start.11) | collective-permute-done | bytes 524320 | tf_op jit(solution)/shard_map/ppermute | solution.py:283
  188.0 5.1 %collective-permute-done.14 = f32[32,2048]{1,0:T(8,128)S(1)} collective-permute-done((f32[32,2048]{1,0:T(8,128)S(1)}, f32[32,2048]{1,0:T(8,128)S(1)}, u32[]{:S(2)}, u32[]{:S(2)}) %collective-permute-start.14) | collective-permute-done | bytes 262176 | tf_op jit(solution)/shard_map/ppermute | solution.py:284
  193.3 3.3 collective-permute-start.22
  196.8 3.9 collective-permute-done.22
  207.5 86.1 %collective-permute-done.49 = bf16[256,4096]{1,0:T(8,128)(2,1)} collective-permute-done((bf16[256,4096]{1,0:T(8,128)(2,1)}, bf16[256,4096]{1,0:T(8,128)(2,1)}, u32[]{:S(2)}, u32[]{:S(2)}) %collective-permute-start.49) | collective-permute-done | bytes 2097184 | tf_op jit(solution)/shard_map/ppermute | solution.py:263
  297.5 2.9 collective-permute-done.25
  300.5 3.2 collective-permute-start.26
  315.9 3.9 collective-permute-done.29
  322.4 3.0 collective-permute-done.30
  329.1 3.6 collective-permute-done.32
  332.8 3.5 collective-permute-start.33
  339.1 3.1 collective-permute-start.34
  349.4 3.6 collective-permute-done.36
  355.6 3.0 collective-permute-done.37
  361.0 4.6 %shard_map.46 = f32[2,4096]{1,0:T(2,128)S(1)} custom-call(s32[2,32]{1,0:T(2,128)S(1)} %pad_add_fusion.where, f32[8,4,32,1024]{3,2,1,0:T(8,128)S(1)} %bitcast.83, f32[1,4096]{1,0:T(1,128)S(1)} %add_negate_fusion.1.refs_1_), custom_call_target="tpu_custom_call" | custom-call | tf_op jit(solution)/shard_map/pallas_call | solution.py:120
  368.3 3.5 collective-permute-done.39
  371.8 3.5 collective-permute-start.40
  378.1 3.1 collective-permute-start.41
  386.0 3.1 shard_map.47.w_ref
  391.1 19.2 %shard_map.48 = bf16[256,4096]{1,0:T(8,128)(2,1)} custom-call(bf16[256,4096]{1,0:T(8,128)(2,1)} %copy-done.3, bf16[256,4096]{1,0:T(8,128)(2,1)} %refs_0_.1, bf16[128,4096]{1,0:T(8,128)(2,1)S(1)} %collective-permute-done.1.refs_6_.refs_10_.refs_1_, bf16[128,4096]{1,0:T(8,128)(2,1)} %collective-permute-done.2.refs_7_.refs_11_.refs_2_, ...), custom_call_target="tpu_custom_call" | custom-call | tf_op jit(solution)/shard_map/pallas_call | solution.py:244
  (170 shorter events, 92.9 us)
Async XLA Ops:
  7.2 351.6 %all-gather.6.cloned.1.call-start = ((), (), s32[]{:S(2)}) async-start(), calls=%async_computation.1 | async-start | bytes 4718592 | tf_op jit(solution)/shard_map/all_gather | solution.py:331
  7.2 50.0 %collective-permute-start.7 = (bf16[256,4096]{1,0:T(8,128)(2,1)}, bf16[256,4096]{1,0:T(8,128)(2,1)}, u32[]{:S(2)}, u32[]{:S(2)}) collective-permute-start(bf16[256,4096]{1,0:T(8,128)(2,1)} %refs_1_.5), channel_id=1, source_target_pairs={{0,64},{64,0},{1,65},{65,1},{2,66},{66,2},{3,67},{67,3},{4,68},{68... | collective-permute-start | bytes 6291464 | tf_op jit(solution)/shard_map/ppermute | solution.py:263
  11.3 54.8 %collective-permute-start = (bf16[256,4096]{1,0:T(8,128)(2,1)}, bf16[256,4096]{1,0:T(8,128)(2,1)}, u32[]{:S(2)}, u32[]{:S(2)}) collective-permute-start(bf16[256,4096]{1,0:T(8,128)(2,1)} %refs_1_.5), channel_id=1, source_target_pairs={{0,8},{8,0},{1,9},{9,1},{2,10},{10,2},{3,11},{11,3},{4,12},{12,4},... | collective-permute-start | bytes 6291464 | tf_op jit(solution)/shard_map/ppermute | solution.py:263
  57.2 68.8 %collective-permute-start.8 = (bf16[256,4096]{1,0:T(8,128)(2,1)}, bf16[256,4096]{1,0:T(8,128)(2,1)}, u32[]{:S(2)}, u32[]{:S(2)}) collective-permute-start(bf16[256,4096]{1,0:T(8,128)(2,1)} %collective-permute-done.7.refs_3_), channel_id=1, source_target_pairs={{0,8},{8,0},{1,9},{9,1},{2,10},{10,2},{3,11},{11,3},{4,12},{12,4},... | collective-permute-start | bytes 6291464 | tf_op jit(solution)/shard_map/ppermute | solution.py:263
  60.3 27.1 %collective-permute-start.1 = (bf16[128,4096]{1,0:T(8,128)(2,1)}, bf16[128,4096]{1,0:T(8,128)(2,1)S(1)}, u32[]{:S(2)}, u32[]{:S(2)}) collective-permute-start(bf16[128,4096]{1,0:T(8,128)(2,1)} %get-tuple-element.61), channel_id=1, source_target_pairs={{0,16},{16,32},{32,48},{48,0},{1,17},{17,33},{33,49},{49,1},{2,18}... | collective-permute-start | bytes 3145736 | tf_op jit(solution)/shard_map/ppermute | solution.py:256
  61.9 26.3 %collective-permute-start.2 = (bf16[128,4096]{1,0:T(8,128)(2,1)}, bf16[128,4096]{1,0:T(8,128)(2,1)}, u32[]{:S(2)}, u32[]{:S(2)}) collective-permute-start(bf16[128,4096]{1,0:T(8,128)(2,1)} %get-tuple-element.61), channel_id=1, source_target_pairs={{0,48},{16,0},{32,16},{48,32},{1,49},{17,1},{33,17},{49,33},{2,50}... | collective-permute-start | bytes 3145736 | tf_op jit(solution)/shard_map/ppermute | solution.py:256
  63.6 46.4 %collective-permute-start.10 = (bf16[128,4096]{1,0:T(8,128)(2,1)}, bf16[128,4096]{1,0:T(8,128)(2,1)}, u32[]{:S(2)}, u32[]{:S(2)}) collective-permute-start(bf16[128,4096]{1,0:T(8,128)(2,1)} %get-tuple-element.60), channel_id=1, source_target_pairs={{0,48},{16,0},{32,16},{48,32},{1,49},{17,1},{33,17},{49,33},{2,50}... | collective-permute-start | bytes 3145736 | tf_op jit(solution)/shard_map/ppermute | solution.py:256
  95.7 17.2 %collective-permute-start.3 = (f32[2,32,1024]{2,1,0:T(8,128)S(1)}, f32[2,32,1024]{2,1,0:T(8,128)S(1)}, u32[]{:S(2)}, u32[]{:S(2)}) collective-permute-start(f32[2,32,1024]{2,1,0:T(8,128)S(1)} %get-tuple-element.17), channel_id=1, source_target_pairs={{0,1},{1,2},{2,3},{3,0},{4,5},{5,6},{6,7},{7,4},{8,9},{9,10},{10,1... | collective-permute-start | bytes 786440 | tf_op jit(solution)/shard_map/ppermute | solution.py:283
  97.2 18.7 %collective-permute-start.4 = (f32[2,32,1024]{2,1,0:T(8,128)S(1)}, f32[2,32,1024]{2,1,0:T(8,128)S(1)}, u32[]{:S(2)}, u32[]{:S(2)}) collective-permute-start(f32[2,32,1024]{2,1,0:T(8,128)S(1)} %get-tuple-element.18), channel_id=1, source_target_pairs={{0,3},{1,0},{2,1},{3,2},{4,7},{5,4},{6,5},{7,6},{8,11},{9,8},{10,9... | collective-permute-start | bytes 786440 | tf_op jit(solution)/shard_map/ppermute | solution.py:283
  99.0 29.9 %collective-permute-start.15 = (bf16[128,4096]{1,0:T(8,128)(2,1)S(1)}, bf16[128,4096]{1,0:T(8,128)(2,1)}, u32[]{:S(2)}, u32[]{:S(2)}) collective-permute-start(bf16[128,4096]{1,0:T(8,128)(2,1)S(1)} %collective-permute-done.1.refs_6_.refs_10_.refs_1_), channel_id=1, source_target_pairs={{0,16},{16,32},{32,48},{48,0},{1,17},{17,33},{33,49},{49,1},{2,18}... | collective-permute-start | bytes 3145736 | tf_op jit(solution)/shard_map/ppermute | solution.py:256
  110.0 25.3 %collective-permute-start.16 = (bf16[128,4096]{1,0:T(8,128)(2,1)}, bf16[128,4096]{1,0:T(8,128)(2,1)}, u32[]{:S(2)}, u32[]{:S(2)}) collective-permute-start(bf16[128,4096]{1,0:T(8,128)(2,1)} %collective-permute-done.10.refs_13_.refs_4_), channel_id=1, source_target_pairs={{0,48},{16,0},{32,16},{48,32},{1,49},{17,1},{33,17},{49,33},{2,50}... | collective-permute-start | bytes 3145736 | tf_op jit(solution)/shard_map/ppermute | solution.py:256
  112.9 9.2 %collective-permute-start.5 = (f32[2,32,1024]{2,1,0:T(8,128)}, f32[2,32,1024]{2,1,0:T(8,128)}, u32[]{:S(2)}, u32[]{:S(2)}) collective-permute-start(f32[2,32,1024]{2,1,0:T(8,128)} %get-tuple-element.19), channel_id=1, source_target_pairs={{0,2},{1,3},{2,0},{3,1},{4,6},{5,7},{6,4},{7,5},{8,10},{9,11},{10,... | collective-permute-start | bytes 786440 | tf_op jit(solution)/shard_map/ppermute | solution.py:283
  116.0 34.0 %collective-permute-start.9 = (bf16[128,4096]{1,0:T(8,128)(2,1)}, bf16[128,4096]{1,0:T(8,128)(2,1)}, u32[]{:S(2)}, u32[]{:S(2)}) collective-permute-start(bf16[128,4096]{1,0:T(8,128)(2,1)} %get-tuple-element.60), channel_id=1, source_target_pairs={{0,16},{16,32},{32,48},{48,0},{1,17},{17,33},{33,49},{49,1},{2,18}... | collective-permute-start | bytes 3145736 | tf_op jit(solution)/shard_map/ppermute | solution.py:256
  124.7 24.3 %collective-permute-start.6 = (f32[32,1024]{1,0:T(8,128)}, f32[32,1024]{1,0:T(8,128)}, u32[]{:S(2)}, u32[]{:S(2)}) collective-permute-start(f32[32,1024]{1,0:T(8,128)} %slice_bitcast_fusion.4), channel_id=1, source_target_pairs={{0,4},{4,0},{1,5},{5,1},{2,6},{6,2},{3,7},{7,3},{8,12},{12,8},{9,1... | collective-permute-start | bytes 393224 | tf_op jit(solution)/shard_map/ppermute | solution.py:284
  143.9 21.8 %collective-permute-start.17 = (f32[2,32,1024]{2,1,0:T(8,128)S(1)}, f32[2,32,1024]{2,1,0:T(8,128)S(1)}, u32[]{:S(2)}, u32[]{:S(2)}) collective-permute-start(f32[2,32,1024]{2,1,0:T(8,128)S(1)} %get-tuple-element.26), channel_id=1, source_target_pairs={{0,1},{1,2},{2,3},{3,0},{4,5},{5,6},{6,7},{7,4},{8,9},{9,10},{10,1... | collective-permute-start | bytes 786440 | tf_op jit(solution)/shard_map/ppermute | solution.py:283
  145.4 20.8 %collective-permute-start.18 = (f32[2,32,1024]{2,1,0:T(8,128)S(1)}, f32[2,32,1024]{2,1,0:T(8,128)S(1)}, u32[]{:S(2)}, u32[]{:S(2)}) collective-permute-start(f32[2,32,1024]{2,1,0:T(8,128)S(1)} %get-tuple-element.27), channel_id=1, source_target_pairs={{0,3},{1,0},{2,1},{3,2},{4,7},{5,4},{6,5},{7,6},{8,11},{9,8},{10,9... | collective-permute-start | bytes 786440 | tf_op jit(solution)/shard_map/ppermute | solution.py:283
  147.2 19.1 %collective-permute-start.19 = (f32[2,32,1024]{2,1,0:T(8,128)S(1)}, f32[2,32,1024]{2,1,0:T(8,128)S(1)}, u32[]{:S(2)}, u32[]{:S(2)}) collective-permute-start(f32[2,32,1024]{2,1,0:T(8,128)S(1)} %get-tuple-element.28), channel_id=1, source_target_pairs={{0,2},{1,3},{2,0},{3,1},{4,6},{5,7},{6,4},{7,5},{8,10},{9,11},{10,... | collective-permute-start | bytes 786440 | tf_op jit(solution)/shard_map/ppermute | solution.py:283
  162.4 24.1 %collective-permute-start.11 = (f32[2,32,2048]{2,1,0:T(8,128)S(1)}, f32[2,32,2048]{2,1,0:T(8,128)S(1)}, u32[]{:S(2)}, u32[]{:S(2)}) collective-permute-start(f32[2,32,2048]{2,1,0:T(8,128)S(1)} %get-tuple-element.22), channel_id=1, source_target_pairs={{0,1},{1,2},{2,3},{3,0},{4,5},{5,6},{6,7},{7,4},{8,9},{9,10},{10,1... | collective-permute-start | bytes 1572872 | tf_op jit(solution)/shard_map/ppermute | solution.py:283
  163.1 23.4 %collective-permute-start.12 = (f32[2,32,2048]{2,1,0:T(8,128)S(1)}, f32[2,32,2048]{2,1,0:T(8,128)S(1)}, u32[]{:S(2)}, u32[]{:S(2)}) collective-permute-start(f32[2,32,2048]{2,1,0:T(8,128)S(1)} %get-tuple-element.23), channel_id=1, source_target_pairs={{0,3},{1,0},{2,1},{3,2},{4,7},{5,4},{6,5},{7,6},{8,11},{9,8},{10,9... | collective-permute-start | bytes 1572872 | tf_op jit(solution)/shard_map/ppermute | solution.py:283
  165.7 20.8 %collective-permute-start.13 = (f32[2,32,2048]{2,1,0:T(8,128)S(1)}, f32[2,32,2048]{2,1,0:T(8,128)S(1)}, u32[]{:S(2)}, u32[]{:S(2)}) collective-permute-start(f32[2,32,2048]{2,1,0:T(8,128)S(1)} %get-tuple-element.24), channel_id=1, source_target_pairs={{0,2},{1,3},{2,0},{3,1},{4,6},{5,7},{6,4},{7,5},{8,10},{9,11},{10,... | collective-permute-start | bytes 1572872 | tf_op jit(solution)/shard_map/ppermute | solution.py:283
  166.4 21.6 %collective-permute-start.20 = (f32[32,1024]{1,0:T(8,128)S(1)}, f32[32,1024]{1,0:T(8,128)S(1)}, u32[]{:S(2)}, u32[]{:S(2)}) collective-permute-start(f32[32,1024]{1,0:T(8,128)S(1)} %slice_bitcast_fusion.2), channel_id=1, source_target_pairs={{0,4},{4,0},{1,5},{5,1},{2,6},{6,2},{3,7},{7,3},{8,12},{12,8},{9,1... | collective-permute-start | bytes 393224 | tf_op jit(solution)/shard_map/ppermute | solution.py:284
  186.6 6.5 %collective-permute-start.14 = (f32[32,2048]{1,0:T(8,128)S(1)}, f32[32,2048]{1,0:T(8,128)S(1)}, u32[]{:S(2)}, u32[]{:S(2)}) collective-permute-start(f32[32,2048]{1,0:T(8,128)S(1)} %slice_bitcast_fusion), channel_id=1, source_target_pairs={{0,4},{4,0},{1,5},{5,1},{2,6},{6,2},{3,7},{7,3},{8,12},{12,8},{9,1... | collective-permute-start | bytes 786440 | tf_op jit(solution)/shard_map/ppermute | solution.py:284
  193.3 7.5 %collective-permute-start.22 = (f32[32,1024]{1,0:T(8,128)S(1)}, f32[32,1024]{1,0:T(8,128)S(1)}, u32[]{:S(2)}, u32[]{:S(2)}) collective-permute-start(f32[32,1024]{1,0:T(8,128)S(1)} %pad_maximum_fusion.2), channel_id=1, source_target_pairs={{0,64},{64,0},{1,65},{65,1},{2,66},{66,2},{3,67},{67,3},{4,68},{68... | collective-permute-start | bytes 393224 | tf_op jit(solution)/shard_map/ppermute | solution.py:263
  196.6 7.1 %collective-permute-start.23 = (f32[32,1024]{1,0:T(8,128)S(1)}, f32[32,1024]{1,0:T(8,128)S(1)}, u32[]{:S(2)}, u32[]{:S(2)}) collective-permute-start(f32[32,1024]{1,0:T(8,128)S(1)} %pad_maximum_fusion.3), channel_id=1, source_target_pairs={{0,72},{8,64},{64,8},{72,0},{1,73},{9,65},{65,9},{73,1},{2,74},{10... | collective-permute-start | bytes 393224 | tf_op jit(solution)/shard_map/ppermute | solution.py:261
  204.6 186.4 %all-gather.4.cloned.1.call-start = ((), (), s32[]{:S(2)}) async-start(), calls=%async_computation | async-start | bytes 18874368 | tf_op jit(solution)/shard_map/all_gather | solution.py:332
  204.7 88.9 %collective-permute-start.49 = (bf16[256,4096]{1,0:T(8,128)(2,1)}, bf16[256,4096]{1,0:T(8,128)(2,1)}, u32[]{:S(2)}, u32[]{:S(2)}) collective-permute-start(bf16[256,4096]{1,0:T(8,128)(2,1)} %refs_0_.1), channel_id=1, source_target_pairs={{0,64},{64,0},{1,65},{65,1},{2,66},{66,2},{3,67},{67,3},{4,68},{68... | collective-permute-start | bytes 6291464 | tf_op jit(solution)/shard_map/ppermute | solution.py:263
  375.3 15.7 %collective-permute-start.42 = (bf16[256,4096]{1,0:T(8,128)(2,1)}, bf16[256,4096]{1,0:T(8,128)(2,1)}, u32[]{:S(2)}, u32[]{:S(2)}) collective-permute-start(bf16[256,4096]{1,0:T(8,128)(2,1)} %refs_0_.1), channel_id=1, source_target_pairs={{0,8},{8,0},{1,9},{9,1},{2,10},{10,2},{3,11},{11,3},{4,12},{12,4},... | collective-permute-start | bytes 6291464 | tf_op jit(solution)/shard_map/ppermute | solution.py:263
  375.8 7.4 %collective-permute-start.44 = (bf16[128,4096]{1,0:T(8,128)(2,1)}, bf16[128,4096]{1,0:T(8,128)(2,1)}, u32[]{:S(2)}, u32[]{:S(2)}) collective-permute-start(bf16[128,4096]{1,0:T(8,128)(2,1)} %collective-permute-done.2.refs_7_.refs_11_.refs_2_), channel_id=1, source_target_pairs={{0,8},{8,0},{1,9},{9,1},{2,10},{10,2},{3,11},{11,3},{4,12},{12,4},... | collective-permute-start | bytes 3145736 | tf_op jit(solution)/shard_map/ppermute | solution.py:263
  381.2 9.8 %collective-permute-start.46 = (bf16[128,4096]{1,0:T(8,128)(2,1)}, bf16[128,4096]{1,0:T(8,128)(2,1)}, u32[]{:S(2)}, u32[]{:S(2)}) collective-permute-start(bf16[128,4096]{1,0:T(8,128)(2,1)} %collective-permute-done.10.refs_13_.refs_4_), channel_id=1, source_target_pairs={{0,8},{8,0},{1,9},{9,1},{2,10},{10,2},{3,11},{11,3},{4,12},{12,4},... | collective-permute-start | bytes 3145736 | tf_op jit(solution)/shard_map/ppermute | solution.py:263
  381.2 9.8 %collective-permute-start.45 = (bf16[128,4096]{1,0:T(8,128)(2,1)}, bf16[128,4096]{1,0:T(8,128)(2,1)}, u32[]{:S(2)}, u32[]{:S(2)}) collective-permute-start(bf16[128,4096]{1,0:T(8,128)(2,1)} %collective-permute-done.9.refs_12_.refs_3_), channel_id=1, source_target_pairs={{0,8},{8,0},{1,9},{9,1},{2,10},{10,2},{3,11},{11,3},{4,12},{12,4},... | collective-permute-start | bytes 3145736 | tf_op jit(solution)/shard_map/ppermute | solution.py:263
  383.2 7.8 %collective-permute-start.47 = (bf16[128,4096]{1,0:T(8,128)(2,1)}, bf16[128,4096]{1,0:T(8,128)(2,1)}, u32[]{:S(2)}, u32[]{:S(2)}) collective-permute-start(bf16[128,4096]{1,0:T(8,128)(2,1)} %collective-permute-done.15.refs_9_.refs_5_), channel_id=1, source_target_pairs={{0,8},{8,0},{1,9},{9,1},{2,10},{10,2},{3,11},{11,3},{4,12},{12,4},... | collective-permute-start | bytes 3145736 | tf_op jit(solution)/shard_map/ppermute | solution.py:263
  383.6 7.4 %collective-permute-start.48 = (bf16[128,4096]{1,0:T(8,128)(2,1)}, bf16[128,4096]{1,0:T(8,128)(2,1)}, u32[]{:S(2)}, u32[]{:S(2)}) collective-permute-start(bf16[128,4096]{1,0:T(8,128)(2,1)} %collective-permute-done.16.refs_10_.refs_6_), channel_id=1, source_target_pairs={{0,8},{8,0},{1,9},{9,1},{2,10},{10,2},{3,11},{11,3},{4,12},{12,4},... | collective-permute-start | bytes 3145736 | tf_op jit(solution)/shard_map/ppermute | solution.py:263
  (31 other events, 204.5 us)
Sparse Core Ops, SparseCore 0:
  204.8 54.3 all-gather.5
  293.7 90.1 all-gather.3

commit v4 on v3

--- a/solution.py
+++ b/solution.py
@@ -95,22 +95,73 @@
             out_ref[1:2, lanes(where[0, t])] = jnp.sum(a, axis=0, keepdims=True)
 
 
+def exponentials_kernel(shapes, where, *refs):
+    logits, (c_ref, out_ref, peak_ref, _) = refs[:len(shapes)], refs[len(shapes):]
+    tiles = tile_list(shapes)
+    acc = None
+    for t, (k, g, n) in enumerate(tiles):
+        x = logits[k][0, g, :, n:n + LANES] + c_ref[:, lanes(where[0, t])]
+        acc = x if acc is None else jnp.maximum(acc, x)
+    peak_ref[...] = jnp.broadcast_to(jnp.max(acc, axis=1, keepdims=True), peak_ref.shape)
+    top = peak_ref[...]
+    for t, (k, g, n) in enumerate(tiles):
+        x = logits[k][0, g, :, n:n + LANES] + c_ref[:, lanes(where[0, t])]
+        out_ref[g, :, n:n + LANES] = jnp.exp(x - top).astype(jnp.bfloat16)
+
+
+def scaled_rows(tiles, kernels, where, v_ref, row_ref):
+    for d, k_ref in enumerate(kernels):
+        for z in range(k_ref.shape[0]):
+            acc = None
+            for t, (_, g, n) in enumerate(tiles):
+                x = k_ref[z, g, :, n:n + LANES].astype(jnp.float32) * v_ref[:, lanes(where[0, t])]
+                acc = x if acc is None else acc + x
+            first = (d * k_ref.shape[0] + z) * ROWS
+            row_ref[first:first + ROWS, :] = acc
+    return jnp.sum(row_ref[...], axis=1, keepdims=True)
+
+
+def balance_kernel(shapes, where, *refs):
+    kernels, (v_ref, out_ref, row_ref) = refs[:len(shapes)], refs[len(shapes):]
+    tiles = tile_list(((1,) + shapes[0][1:],))
+    total = scaled_rows(tiles, kernels, where, v_ref, row_ref)
+    row_ref[...] = jnp.broadcast_to(1.0 / total, row_ref.shape)
+    for t, (_, g, n) in enumerate(tiles):
+        acc = jnp.zeros((ROWS, LANES), jnp.float32)
+        for d, k_ref in enumerate(kernels):
+            for z in range(k_ref.shape[0]):
+                first = (d * k_ref.shape[0] + z) * ROWS
+                acc = acc + k_ref[z, g, :, n:n + LANES].astype(jnp.float32) * row_ref[first:first + ROWS, :]
+        out_ref[0:1, lanes(where[0, t])] = jnp.sum(acc, axis=0, keepdims=True)
+
+
 def weights_kernel(shapes, where, *refs):
-    logits, (c_ref, out_ref, peak_ref, row_ref) = refs[:len(shapes)], refs[len(shapes):]
-    tiles = tile_list(shapes)
-    blocks = shapes[0][0]
-    total = row_pass(tiles, blocks, logits, where, c_ref, peak_ref, row_ref)
-    row_ref[...] = jnp.broadcast_to(total, row_ref.shape)
-
-    def write(f, _):
-        rows = pl.ds(f * ROWS, ROWS)
-        top, scale = peak_ref[rows, :], 1.0 / row_ref[rows, :]
-        for t, (k, g, n) in enumerate(tiles):
-            x = logits[k][f, g, :, n:n + LANES] + c_ref[:, lanes(where[0, t])]
-            out_ref[rows, lanes(where[1, t])] = (jnp.exp(x - top) * scale).astype(jnp.bfloat16)
-        return 0
-
-    lax.fori_loop(0, blocks, write, 0)
+    kernels, (v_ref, out_ref, row_ref) = refs[:len(shapes)], refs[len(shapes):]
+    tiles = tile_list(((1,) + shapes[0][1:],))
+    total = scaled_rows(tiles, kernels, where, v_ref, row_ref)
+    row_ref[...] = jnp.broadcast_to(1.0 / total, row_ref.shape)
+    for d, k_ref in enumerate(kernels):
+        for z in range(k_ref.shape[0]):
+            first = (d * k_ref.shape[0] + z) * ROWS
+            scale = row_ref[first:first + ROWS, :]
+            rows = pl.ds(pl.multiple_of(where[2, d * k_ref.shape[0] + z] * ROWS, ROWS), ROWS)
+            for t, (_, g, n) in enumerate(tiles):
+                x = k_ref[z, g, :, n:n + LANES].astype(jnp.float32) * v_ref[:, lanes(where[0, t])]
+                out_ref[rows, lanes(where[1, t])] = (x * scale).astype(jnp.bfloat16)
+
+
+def balance_call(kernel, out_shape, where, kernels, v):
+    shapes = tuple(a.shape for a in kernels)
+    rows = sum(s[0] for s in shapes) * ROWS
+    vmem = pl.BlockSpec(memory_space=pltpu.VMEM)
+    return pl.pallas_call(
+        functools.partial(kernel, shapes),
+        out_shape=out_shape,
+        in_specs=[pl.BlockSpec(memory_space=pltpu.SMEM)] + [vmem] * (len(kernels) + 1),
+        out_specs=vmem,
+        scratch_shapes=[pltpu.VMEM((rows, LANES), jnp.float32)],
+        compiler_params=pltpu.CompilerParams(vmem_limit_bytes=32 * 2**20),
+    )(where, *kernels, v)
 
 
 def row_call(kernel, out_shape, where, logits, c):
@@ -137,6 +188,12 @@
 FEAT_STEPS = (("zl", 2, 1), ("x", 4, 1), ("x", 4, 2))
 
 
+def column_sum(x):
+    for axis, n, step in SAMP_STEPS:
+        x = x + lax.ppermute(x, axis, [(i, i ^ step) for i in range(n)])
+    return x
+
+
 def column_update(stats, steps):
     for axis, n, step in steps:
         pairs = [(i, i ^ step) for i in range(n)]
@@ -152,15 +209,16 @@
     return acc
 
 
-def partial_kernel(jobs, scale, *refs):
-    n_count = 1 + max(q for qs, _ in jobs for q in qs)
+def partial_kernel(noise_parts, jobs, scale, *refs):
+    n_count = sum(noise_parts)
     x_count = 1 + max(x for _, xs in jobs for x in xs)
-    where, refs = refs[0], refs[1:]
-    n_refs, n_sq, x_refs = refs[:n_count], refs[n_count:2 * n_count], refs[2 * n_count:2 * n_count + x_count]
-    outs, (acc, x_sq) = refs[2 * n_count + x_count:-2], refs[-2:]
+    where, n_sq = refs[0], refs[1]
+    n_refs, x_refs = refs[2:2 + n_count], refs[2 + n_count:2 + n_count + x_count]
+    outs, (acc, x_sq) = refs[2 + n_count + x_count:-2], refs[-2:]
     step = pl.program_id(0)
-    rows = n_refs[0].shape[0]
     parts, share, _ = acc.shape
+    rows = parts * share
+    starts = [sum(noise_parts[:q]) for q in range(len(noise_parts))]
 
     @pl.when(step == 0)
     def _():
@@ -170,7 +228,9 @@
     places, first = [], 0
     for qs, xs in jobs:
         widths = [x_refs[x].shape[0] for x in xs]
-        block = jnp.concatenate([n_refs[q][...] for q in qs], axis=0)
+        block = jnp.concatenate(
+            [n_refs[starts[q] + p][...] for q in qs for p in range(noise_parts[q])], axis=0
+        )
         offset = first
         for x, width in zip(xs, widths):
             inner = lax.dot_general(
@@ -183,8 +243,8 @@
                 places.append((q, x, at))
             offset += width
         first += len(qs) * sum(widths)
-    starts = [sum(r.shape[0] for r in x_refs[:x]) for x in range(x_count)]
-    for x, start in zip(x_refs, starts):
+    x_starts = [sum(r.shape[0] for r in x_refs[:x]) for x in range(x_count)]
+    for x, start in zip(x_refs, x_starts):
         x_sq[start:start + x.shape[0], :] += lane_sums(x[...])
 
     @pl.when(step == pl.num_programs(0) - 1)
@@ -198,33 +258,35 @@
                 f = (where[1] + z) % 2 * 4 + (where[0] + d + 4) % 4
                 for q, x, at in places:
                     width = x_refs[x].shape[0]
-                    own = n_sq[q][pl.ds(f * share, share), :]
-                    other = columns[:, starts[x]:starts[x] + width]
+                    own = n_sq[pl.ds(q * rows + f * share, share), :]
+                    other = columns[:, x_starts[x]:x_starts[x] + width]
                     inner = acc[f, :, at:at + width]
                     out[z, :, at:at + width] = (own + other - 2.0 * inner) * scale
 
 
-def partial_call(scale, parts, where, noises, squares, datas, jobs):
-    rows, depth = noises[0].shape
+def partial_call(scale, parts, where, squares, noises, datas, jobs):
+    noise_parts = tuple(len(n) for n in noises)
+    flat = [a for n in noises for a in n]
+    rows, depth = sum(a.shape[0] for a in noises[0]), flat[0].shape[1]
     total = sum(len(qs) * sum(datas[x].shape[0] for x in xs) for qs, xs in jobs)
     share = rows // parts
     block = DEPTH
     out = (2, share, total)
     return pl.pallas_call(
-        functools.partial(partial_kernel, jobs, scale),
+        functools.partial(partial_kernel, noise_parts, jobs, scale),
+        cost_estimate=pl.CostEstimate(flops=0, bytes_accessed=0, transcendentals=0),
         out_shape=[jax.ShapeDtypeStruct(out, jnp.float32)] * 4,
         grid=(depth // block,),
         in_specs=[pl.BlockSpec(memory_space=pltpu.SMEM)]
-        + [pl.BlockSpec((rows, block), lambda k: (0, k)) for _ in noises]
-        + [pl.BlockSpec((rows, 1), lambda k: (0, 0)) for _ in noises]
-        + [pl.BlockSpec((d.shape[0], block), lambda k: (0, k)) for d in datas],
+        + [pl.BlockSpec(squares.shape, lambda k: (0, 0))]
+        + [pl.BlockSpec((a.shape[0], block), lambda k: (0, k)) for a in (*flat, *datas)],
         out_specs=[pl.BlockSpec(out, lambda k: (0, 0, 0))] * 4,
         scratch_shapes=[
             pltpu.VMEM((parts, share, total), jnp.float32),
             pltpu.VMEM((sum(d.shape[0] for d in datas), LANES), jnp.float32),
         ],
         compiler_params=pltpu.CompilerParams(vmem_limit_bytes=48 * 2**20),
-    )(where, *noises, *squares, *datas)
+    )(where, squares, *flat, *datas)
 
 
 def targets_kernel(widths, w_ref, *refs):
@@ -264,24 +326,13 @@
     return x
 
 
-def ring_gather(x):
-    half = x.shape[0] // 2
-    a, b = x[:half], x[half:]
-    u1, w1 = ring(a, 1), ring(a, -1)
-    u2, w2 = ring(b, 1), ring(b, -1)
-    u3, w3 = ring(u1, 1), ring(w2, -1)
-    return [x, u1, w1, u2, w2, u3, w3]
-
-
-SOURCES = [(0, 0), (0, 1), (-1, 0), (1, 0), (-1, 1), (1, 1), (-2, 0), (2, 1)]
+SOURCES = [(0, 0), (0, 1), (-1, 0), (-1, 1), (1, 0), (1, 1), (-2, 0), (2, 1)]
+ALONG_X = (0, 1, -1, 2)
 QUARTERS = [(0, 0), (0, 1), (1, 0), (1, 1)]
 
 
-def sum_over_feat(pieces):
-    own, right, left, across = pieces
-    for piece, step in ((right, 1), (left, -1), (across, 2)):
-        own = own + lax.ppermute(piece, "x", [(i, (i + step) % 4) for i in range(4)])
-    return own[0] + lax.ppermute(own[1], "zl", [(0, 1), (1, 0)])
+def along_x(x, step):
+    return lax.ppermute(x, "x", [(i, (i + step) % 4) for i in range(4)])
 
 
 def tables(parts):
@@ -292,7 +343,10 @@
             inside = ((y + dy + 4) % 4 * 2 + (core + dc) % 2) * 2 + half
             where.append((zh + dz) % 2 * 16 + inside)
             place.append(16 + inside if dz else jnp.int32(dc * 8 + s))
-    return jnp.stack([jnp.stack(where), jnp.stack(place)]).astype(jnp.int32)
+    x, zl = lax.axis_index("x"), lax.axis_index("zl")
+    rows = [(zl + z) % 2 * 4 + (x + d + 4) % 4 for d in ALONG_X for z in range(2)]
+    rows = jnp.pad(jnp.stack(rows), (0, len(where) - len(rows)))
+    return jnp.stack([jnp.stack(where), jnp.stack(place), rows]).astype(jnp.int32)
 
 
 def row_squares(x):
@@ -303,48 +357,79 @@
     temper = 0.5 / math.sqrt(F)
     scale = -1.0 / (F * temper)
     parts = 8
-    near = [noise, swap(noise, 0, 1)]
+    half = noise.shape[0] // 2
+    call = functools.partial(partial_call, scale, parts)
+    where = tables(parts)
+    here = jnp.stack([lax.axis_index("x"), lax.axis_index("zl")]).astype(jnp.int32)
+    hold = lax.optimization_barrier
+
+    near = swap(noise, 0, 1)
+    u, w = ring(data, 1), ring(data, -1)
     far = swap(noise, 1, 0)
-    blocks = ring_gather(data)
-    far = [far, swap(far, 0, 1)]
-    data, far[0] = lax.optimization_barrier((data, far[0]))
+    squares = jnp.concatenate([row_squares(n) for n in (noise, near)], axis=0)
+    u, w, far, data, squares = hold((u, w, far, data, squares))
+
+    u3, w3 = ring(u[:half], 1), ring(w[half:], -1)
     other = swap(data, 1, 0)
-
-    everyone = near + far
-    squares = [row_squares(n) for n in everyone]
-    here = jnp.stack([lax.axis_index("x"), lax.axis_index("zl")]).astype(jnp.int32)
-    call = functools.partial(partial_call, scale, parts, here)
-    pieces = call(near, squares[:2], blocks[:3], (((0, 1), (0, 1, 2)),))
-    sum1 = sum_over_feat(pieces)
-    pieces = call(everyone, squares, blocks[:5], (((2, 3), (0, 1, 2)), ((0, 1, 2, 3), (3, 4))))
-    sum2 = sum_over_feat(pieces)
-    pieces = call(everyone, squares, blocks[5:], (((0, 1, 2, 3), (0, 1)),))
-    sum3 = sum_over_feat(pieces)
-    quarters = []
-    for i, q in enumerate(QUARTERS):
-        head = sum2[:, (i - 2) * 512:(i - 1) * 512] if i >= 2 else sum1[:, i * 512:(i + 1) * 512]
-        middle = sum2[:, 1024 + i * 256:1280 + i * 256]
-        quarters.append(swap(jnp.concatenate([head, middle, sum3[:, i * 256:(i + 1) * 256]], axis=1), *q))
-    own = jnp.stack(quarters)
-    where = tables(parts)
-
-    shared = lax.all_gather(own, FEAT, axis=0, tiled=False)
+    across = swap(far, 0, 1)
+    jobs = (((0, 1), (0, 1, 2)),)
+    n0, n1, n3, n2 = call(here, squares, [(noise,), (near,)], [data, u, w], jobs)
+    n1, n3 = along_x(n1, 1), along_x(n3, -1)
+    far_squares = jnp.concatenate([row_squares(n) for n in (far, across)], axis=0)
+    f0, f1, f3, f2 = call(here, far_squares, [(far,), (across,)], [data, u, w], jobs)
+    n2 = along_x(n2, 2)
+    f1, f3 = along_x(f1, 1), along_x(f3, -1)
+    u3, w3, n0, n1, n2, n3, f1, f2, f3 = hold((u3, w3, n0, n1, n2, n3, f1, f2, f3))
+
+    squares = jnp.concatenate([squares, far_squares], axis=0)
+    everyone = [(noise,), (near,), (far,), (across,)]
+    c0, c1, c3, c2 = call(here, squares, everyone, [u3, w3], (((0, 1, 2, 3), (0, 1)),))
+    f2 = along_x(f2, 2)
+    c1, c3, c2 = along_x(c1, 1), along_x(c3, -1), along_x(c2, 2)
+    f2, c1, c2, c3, other = hold((f2, c1, c2, c3, other))
+    n, f, c = n0 + n1 + n2 + n3, f0 + f1 + f2 + f3, c0 + c1 + c2 + c3
+
+    def quarters(z):
+        wide, thin = 3 * 256, 256
+        return jnp.stack([
+            jnp.concatenate([
+                (n if i < 2 else f)[z][:, i % 2 * wide:(i % 2 + 1) * wide],
+                c[z][:, i * thin:(i + 1) * thin],
+            ], axis=1)
+            for i in range(4)
+        ])
+
+    own = quarters(0) + lax.ppermute(quarters(1), "zl", [(0, 1), (1, 0)])
+    own = jnp.stack([swap(own[i], *q) for i, q in enumerate(QUARTERS)])
+    own, other = hold((own, other))
     others = lax.all_gather(other, ("y", "core"), axis=0, tiled=True)
-    gathered = blocks + [swap(b, 0, 1) for b in blocks] + [others]
-
-    c = jnp.zeros((1, SAMPLES), jnp.float32)
-    for i in range(ITERS):
-        out = jax.ShapeDtypeStruct((2, SAMPLES), jnp.float32)
-        if i < SPREAD:
-            c = column_update(row_call(sinkhorn_kernel, out, where, [own[None]], c), SAMP_STEPS + FEAT_STEPS)
-        else:
-            c = column_update(row_call(sinkhorn_kernel, out, where, [shared], c), SAMP_STEPS)
+    out = jax.ShapeDtypeStruct((2, SAMPLES), jnp.float32)
+
+    def spread(_, c):
+        return column_update(row_call(sinkhorn_kernel, out, where, [own[None]], c), SAMP_STEPS + FEAT_STEPS)
+
+    c = lax.fori_loop(0, lax.axis_index("x") // 8 + 1, spread, jnp.zeros((1, SAMPLES), jnp.float32))
+    out = jax.ShapeDtypeStruct(own.shape, jnp.bfloat16)
+    mine = row_call(exponentials_kernel, out, where, [own[None]], c)
+    mine = jnp.stack([mine, lax.ppermute(mine, "zl", [(0, 1), (1, 0)])])
+    kernels = [mine] + [along_x(mine, -d) for d in ALONG_X[1:]]
+
+    blocks = [data, u, w, u3, w3]
+    kernels, blocks = hold((kernels, blocks))
+    swapped = [swap(b, 0, 1) for b in blocks]
+    v = jnp.ones((1, SAMPLES), jnp.float32)
+    for i in range(1, ITERS):
+        out = jax.ShapeDtypeStruct((1, SAMPLES), jnp.float32)
+        v = 1.0 / column_sum(balance_call(balance_kernel, out, where, kernels, v))
+        if i == 1:
+            v, swapped = hold((v, swapped))
     out = jax.ShapeDtypeStruct((noise.shape[0], SAMPLES), jnp.bfloat16)
-    weights = row_call(weights_kernel, out, where, [shared], c)
+    weights = balance_call(weights_kernel, out, where, kernels, v)
+    c = c + jnp.log(v)
     share = SAMPLES // parts
     start = (lax.axis_index("zl") * 4 + lax.axis_index("x")) * share
     column_out = lax.dynamic_slice_in_dim(c[0] * temper, start, share, 0)
-    return (targets_call(weights, gathered), column_out)
+    return (targets_call(weights, [*blocks, *swapped, others]), column_out)
 
 
 def solution(mesh):

time: 419 us -> 308 us (0.74)
  waiting for transfers between devices: 249 us -> 150 us
  starting transfers between devices: 71.5 us -> 61.4 us
  local copies, waits for them, and re-layouts: 12.6 us -> 18.2 us
  Pallas kernels: 56.7 us -> 51.2 us
    ppermute x13 -> x11, waiting for transfers between devices: 137 us -> 9.22 us  [swap(): return lax.ppermute(x, 'zh' if dz else 'core', [(0, 1), (1, 0)])]
    ppermute x12 -> x22, waiting for transfers between devices: 27.7 us -> 78.9 us  [the longest x12 42.6 us: along_x(): return lax.ppermute(x, 'x', [(i, (i + step) % 4) for i in range(4)])]
    ppermute x18 -> x7, waiting for transfers between devices: 45.2 us -> 20.7 us  [column_update(): stats = combine(stats, lax.ppermute(stats, axis, pairs))]
    ppermute x18 -> x7, starting transfers between devices: 30.8 us -> 9.01 us  [column_update(): stats = combine(stats, lax.ppermute(stats, axis, pairs))]
    ppermute x12 -> x22, starting transfers between devices: 19.2 us -> 34.5 us  [the longest x12 19.3 us: along_x(): return lax.ppermute(x, 'x', [(i, (i + step) % 4) for i in range(4)])]
    pallas_call x4 -> x2, Pallas kernels: 9.82 us -> 1.86 us  [row_call(): pl.pallas_call(functools.partial(kernel, shapes), out_shape=out_shape, in...]
    pallas_call x3 -> x6, Pallas kernels: 27.7 us -> 31.7 us  [the longest x3 26.9 us: partial_call(): pl.pallas_call(functools.partial(partial_kernel, noise_parts, jobs, scale...]
    unnamed x22 -> x40, local copies, waits for them, and re-layouts: 7.35 us -> 10.4 us
  transfers between devices with their start and end apart: 52 -> 46, of which waited for: 29 -> 32; matrix products, arithmetic and copies ran while one was open for 4% -> 5% of each run, Pallas kernels for 9% -> 11%
where the time goes in v4:
time: 308 us
  waiting for transfers between devices  150 us (49%)
  starting transfers between devices  61.4 us (20%)
  Pallas kernels  51.2 us (17%)
  local copies, waits for them, and re-layouts  18.2 us (6%)
  between operations  14.4 us (5%)
  other arithmetic  12.1 us (4%)
    ppermute x12, waiting for transfers between devices, along_x(): return lax.ppermute(x, 'x', [(i, (i + step) % 4) for i in range(4)])  42.6 us
    ppermute x4, waiting for transfers between devices, ring(): return lax.ppermute(x, 'y', [(i, (i + shift) % 4) for i in range(4)])  38.5 us
    pallas_call x3, Pallas kernels, partial_call(): pl.pallas_call(functools.partial(partial_kernel, noise_parts, jobs, scale...  26.9 us
    ppermute x7, waiting for transfers between devices, column_update(): stats = combine(stats, lax.ppermute(stats, axis, pairs))  20.7 us
    ppermute x8, waiting for transfers between devices, column_sum(): x = x + lax.ppermute(x, axis, [(i, i ^ step) for i in range(n)])  20.4 us
    ppermute x12, starting transfers between devices, along_x(): return lax.ppermute(x, 'x', [(i, (i + step) % 4) for i in range(4)])  19.3 us
    pallas_call x1, Pallas kernels, targets_call(): pl.pallas_call(functools.partial(targets_kernel, widths), out_shape=jax.S...  17.6 us
    ppermute x8, starting transfers between devices, column_sum(): x = x + lax.ppermute(x, axis, [(i, i ^ step) for i in range(n)])  12.6 us
  transfers between devices with their start and end apart: 46, of which 32 were waited for; matrix products, arithmetic and copies ran while one was open for 5% of the time, Pallas kernels for 11%

profile of v4, /device:TPU:0, one launch (start us, length us, event | category | flops | bytes accessed | tf_op | source)
XLA Modules:
  0.0 307.7 jit_solution(14122951457447173396)
XLA Ops:
  10.6 4.0 %collective-permute-start.9 = (bf16[256,4096]{1,0:T(8,128)(2,1)}, bf16[256,4096]{1,0:T(8,128)(2,1)}, u32[]{:S(2)}, u32[]{:S(2)}) collective-permute-start(bf16[256,4096]{1,0:T(8,128)(2,1)} %refs_2_.3), channel_id=1, source_target_pairs={{0,64},{64,0},{1,65},{65,1},{2,66},{66,2},{3,67},{67,3},{4,68},{68... | collective-permute-start | bytes 6291464 | tf_op jit(solution)/shard_map/ppermute | solution.py:325
  18.5 38.5 %collective-permute-done.7.refs_5_.refs_1_ = bf16[256,4096]{1,0:T(8,128)(2,1)} collective-permute-done((bf16[256,4096]{1,0:T(8,128)(2,1)}, bf16[256,4096]{1,0:T(8,128)(2,1)}, u32[]{:S(2)}, u32[]{:S(2)}) %collective-permute-start.7) | collective-permute-done | bytes 2097184 | tf_op jit(solution)/shard_map/ppermute | solution.py:318
  57.1 3.6 %collective-permute-done.9.refs_2_.refs_4_ = bf16[256,4096]{1,0:T(8,128)(2,1)} collective-permute-done((bf16[256,4096]{1,0:T(8,128)(2,1)}, bf16[256,4096]{1,0:T(8,128)(2,1)}, u32[]{:S(2)}, u32[]{:S(2)}) %collective-permute-start.9) | collective-permute-done | bytes 2097184 | tf_op jit(solution)/shard_map/ppermute | solution.py:325
  62.4 8.8 %shard_map.41 = (f32[2,32,1536]{2,1,0:T(8,128)S(1)}, f32[2,32,1536]{2,1,0:T(8,128)S(1)}, f32[2,32,1536]{2,1,0:T(8,128)}, f32[2,32,1536]{2,1,0:T(8,128)}) custom-call(s32[2]{0:T(128)S(1)} %pad_add_fusion.1.refs_0_, f32[512,1]{1,0:T(8,128)S(1)} %copy.10.refs_1_, bf16[256,4096]{1,0:T(8,128)(2,1)S(1)} %copy-done, bf16[256,4096]{1,0:T(8,128)(2,1)S(1)} %copy-done.2, ...), custom_call_target="tpu_custom_call" | custom-call | tf_op jit(solution)/shard_map/pallas_call | solution.py:275
  77.8 2.9 collective-permute-start.12
  80.7 3.2 %collective-permute-start.23 = (bf16[256,4096]{1,0:T(8,128)(2,1)}, bf16[256,4096]{1,0:T(8,128)(2,1)}, u32[]{:S(2)}, u32[]{:S(2)}) collective-permute-start(bf16[256,4096]{1,0:T(8,128)(2,1)} %refs_0_), channel_id=1, source_target_pairs={{0,64},{64,0},{1,65},{65,1},{2,66},{66,2},{3,67},{67,3},{4,68},{68... | collective-permute-start | bytes 6291464 | tf_op jit(solution)/shard_map/ppermute | solution.py:325
  92.5 9.5 %shard_map.42 = (f32[2,32,1536]{2,1,0:T(8,128)S(1)}, f32[2,32,1536]{2,1,0:T(8,128)}, f32[2,32,1536]{2,1,0:T(8,128)}, f32[2,32,1536]{2,1,0:T(8,128)}) custom-call(s32[2]{0:T(128)S(1)} %pad_add_fusion.1.refs_0_, f32[512,1]{1,0:T(8,128)S(1)} %copy.11.refs_1_, bf16[256,4096]{1,0:T(8,128)(2,1)} %collective-permute-done.9.refs_2_.refs_4_, ...), custom_call_target="tpu_custom_call" | custom-call | tf_op jit(solution)/shard_map/pallas_call | solution.py:275
  107.7 6.4 %collective-permute-done.17 = f32[2,32,1536]{2,1,0:T(8,128)} collective-permute-done((f32[2,32,1536]{2,1,0:T(8,128)}, f32[2,32,1536]{2,1,0:T(8,128)}, u32[]{:S(2)}, u32[]{:S(2)}) %collective-permute-start.17) | collective-permute-done | bytes 393248 | tf_op jit(solution)/shard_map/ppermute | solution.py:335
  116.6 8.5 %shard_map.43 = (f32[2,32,1024]{2,1,0:T(8,128)S(1)}, f32[2,32,1024]{2,1,0:T(8,128)}, f32[2,32,1024]{2,1,0:T(8,128)}, f32[2,32,1024]{2,1,0:T(8,128)}) custom-call(s32[2]{0:T(128)S(1)} %pad_add_fusion.1.refs_0_, f32[1024,1]{1,0:T(8,128)S(1)} %copy-done.4, bf16[256,4096]{1,0:T(8,128)(2,1)S(1)} %copy-done, bf16[256,4096]{1,0:T(8,128)(2,1)} %copy-done.1, ...), custom_call_target="tpu_custom_call" | custom-call | tf_op jit(solution)/shard_map/pallas_call | solution.py:275
  126.2 4.0 %collective-permute-start.21 = (f32[2,32,1024]{2,1,0:T(8,128)}, f32[2,32,1024]{2,1,0:T(8,128)S(1)}, u32[]{:S(2)}, u32[]{:S(2)}) collective-permute-start(f32[2,32,1024]{2,1,0:T(8,128)} %get-tuple-element.99), channel_id=1, source_target_pairs={{0,2},{1,3},{2,0},{3,1},{4,6},{5,7},{6,4},{7,5},{8,10},{9,11},{10,... | collective-permute-start | bytes 786440 | tf_op jit(solution)/shard_map/ppermute | solution.py:335
  135.3 8.0 %collective-permute-done.21 = f32[2,32,1024]{2,1,0:T(8,128)S(1)} collective-permute-done((f32[2,32,1024]{2,1,0:T(8,128)}, f32[2,32,1024]{2,1,0:T(8,128)S(1)}, u32[]{:S(2)}, u32[]{:S(2)}) %collective-permute-start.21) | collective-permute-done | bytes 262176 | tf_op jit(solution)/shard_map/ppermute | solution.py:335
  143.3 6.7 %collective-permute-done.19 = f32[2,32,1536]{2,1,0:T(8,128)} collective-permute-done((f32[2,32,1536]{2,1,0:T(8,128)}, f32[2,32,1536]{2,1,0:T(8,128)}, u32[]{:S(2)}, u32[]{:S(2)}) %collective-permute-start.19) | collective-permute-done | bytes 393248 | tf_op jit(solution)/shard_map/ppermute | solution.py:335
  154.8 10.6 %collective-permute-done.24 = f32[4,32,1024]{2,1,0:T(8,128)S(1)} collective-permute-done((f32[4,32,1024]{2,1,0:T(8,128)S(1)}, f32[4,32,1024]{2,1,0:T(8,128)S(1)}, u32[]{:S(2)}, u32[]{:S(2)}) %collective-permute-start.24) | collective-permute-done | bytes 524320 | tf_op jit(solution)/shard_map/ppermute | solution.py:402
  165.6 3.3 %collective-permute-start.26 = (f32[32,1024]{1,0:T(8,128)S(1)}, f32[32,1024]{1,0:T(8,128)S(1)}, u32[]{:S(2)}, u32[]{:S(2)}) collective-permute-start(f32[32,1024]{1,0:T(8,128)S(1)} %get-tuple-element.151), channel_id=1, source_target_pairs={{0,64},{64,0},{1,65},{65,1},{2,66},{66,2},{3,67},{67,3},{4,68},{68... | collective-permute-start | bytes 393224 | tf_op jit(solution)/shard_map/ppermute | solution.py:325
  169.2 3.8 %collective-permute-done.26 = f32[32,1024]{1,0:T(8,128)S(1)} collective-permute-done((f32[32,1024]{1,0:T(8,128)S(1)}, f32[32,1024]{1,0:T(8,128)S(1)}, u32[]{:S(2)}, u32[]{:S(2)}) %collective-permute-start.26) | collective-permute-done | bytes 131104 | tf_op jit(solution)/shard_map/ppermute | solution.py:325
  173.0 2.9 collective-permute-done.27
  176.0 31.6 %while.10 = (s32[]{:T(128)}, f32[1,4096]{1,0:T(1,128)S(1)}, s32[]{:T(128)}, f32[4,32,1024]{2,1,0:T(8,128)S(1)}, s32[3,32]{1,0:T(4,128)S(1)}, /*index=5*/s32[]{:T(128)}) while((s32[]{:T(128)}, f32[1,4096]{1,0:T(1,128)S(1)}, s32[]{:T(128)}, f32[4,32,1024]{2,1,0:T(8,128)S(1)}, s32[3,32]{1,0:T(4,128)S(1)}, /*index=5*/s32[]{:T(128)}) %tuple.76), condition=%wide.region_5.6_spmd, body=%wide.region_4.5_spmd.sunk | while | flops 229378 | bytes 1982813 | solution.py:411
  178.9 3.6 %collective-permute-done.1 = f32[2,4096]{1,0:T(2,128)S(1)} collective-permute-done((f32[2,4096]{1,0:T(2,128)S(1)}, f32[2,4096]{1,0:T(2,128)S(1)}, u32[]{:S(2)}, u32[]{:S(2)}) %collective-permute-start.1) | collective-permute-done | bytes 32800 | tf_op jit(solution)/shard_map/while/body/ppermute | solution.py:200
  184.6 3.5 %collective-permute-done.2 = f32[2,4096]{1,0:T(2,128)S(1)} collective-permute-done((f32[2,4096]{1,0:T(2,128)S(1)}, f32[2,4096]{1,0:T(2,128)S(1)}, u32[]{:S(2)}, u32[]{:S(2)}) %collective-permute-start.2) | collective-permute-done | bytes 32800 | tf_op jit(solution)/shard_map/while/body/ppermute | solution.py:200
  194.9 2.9 collective-permute-done.4
  198.6 3.3 %collective-permute-done.5 = f32[2,4096]{1,0:T(2,128)S(1)} collective-permute-done((f32[2,4096]{1,0:T(2,128)S(1)}, f32[2,4096]{1,0:T(2,128)S(1)}, u32[]{:S(2)}, u32[]{:S(2)}) %collective-permute-start.5) | collective-permute-done | bytes 32800 | tf_op jit(solution)/shard_map/while/body/ppermute | solution.py:200
  203.7 3.8 %collective-permute-done.6 = f32[2,4096]{1,0:T(2,128)S(1)} collective-permute-done((f32[2,4096]{1,0:T(2,128)S(1)}, f32[2,4096]{1,0:T(2,128)S(1)}, u32[]{:S(2)}, u32[]{:S(2)}) %collective-permute-start.6) | collective-permute-done | bytes 32800 | tf_op jit(solution)/shard_map/while/body/ppermute | solution.py:200
  209.5 5.3 %collective-permute-done.28 = bf16[4,32,1024]{2,1,0:T(8,128)(2,1)S(1)} collective-permute-done((bf16[4,32,1024]{2,1,0:T(8,128)(2,1)S(1)}, bf16[4,32,1024]{2,1,0:T(8,128)(2,1)S(1)}, u32[]{:S(2)}, u32[]{:S(2)}) %collective-permute-start.28) | collective-permute-done | bytes 262176 | tf_op jit(solution)/shard_map/ppermute | solution.py:414
  218.6 14.4 %collective-permute-done.29.refs_1_ = bf16[2,4,32,1024]{3,2,1,0:T(8,128)(2,1)S(1)} collective-permute-done((bf16[2,4,32,1024]{3,2,1,0:T(8,128)(2,1)S(1)}, bf16[2,4,32,1024]{3,2,1,0:T(8,128)(2,1)S(1)}, u32[]{:S(2)}, u32[]{:S(2)}) %collective-permute-start.29) | collective-permute-done | bytes 524320 | tf_op jit(solution)/shard_map/ppermute | solution.py:335
  233.0 3.4 %collective-permute-done.30.refs_2_ = bf16[2,4,32,1024]{3,2,1,0:T(8,128)(2,1)S(1)} collective-permute-done((bf16[2,4,32,1024]{3,2,1,0:T(8,128)(2,1)S(1)}, bf16[2,4,32,1024]{3,2,1,0:T(8,128)(2,1)S(1)}, u32[]{:S(2)}, u32[]{:S(2)}) %collective-permute-start.30) | collective-permute-done | bytes 524320 | tf_op jit(solution)/shard_map/ppermute | solution.py:335
  241.4 3.5 %collective-permute-done.33 = f32[1,4096]{1,0:T(1,128)S(1)} collective-permute-done((f32[1,4096]{1,0:T(1,128)S(1)}, f32[1,4096]{1,0:T(1,128)S(1)}, u32[]{:S(2)}, u32[]{:S(2)}) %collective-permute-start.33) | collective-permute-done | bytes 16416 | tf_op jit(solution)/shard_map/ppermute | solution.py:193
  246.8 3.7 %collective-permute-done.34 = f32[1,4096]{1,0:T(1,128)S(1)} collective-permute-done((f32[1,4096]{1,0:T(1,128)S(1)}, f32[1,4096]{1,0:T(1,128)S(1)}, u32[]{:S(2)}, u32[]{:S(2)}) %collective-permute-start.34) | collective-permute-done | bytes 16416 | tf_op jit(solution)/shard_map/ppermute | solution.py:193
  250.6 3.2 %collective-permute-start.35 = (f32[1,4096]{1,0:T(1,128)S(1)}, f32[1,4096]{1,0:T(1,128)S(1)}, u32[]{:S(2)}, u32[]{:S(2)}) collective-permute-start(f32[1,4096]{1,0:T(1,128)S(1)} %add.794), channel_id=1, source_target_pairs={{0,64},{64,0},{1,65},{65,1},{2,66},{66,2},{3,67},{67,3},{4,68},{68... | collective-permute-start | bytes 49160 | tf_op jit(solution)/shard_map/ppermute | solution.py:193
  263.3 3.2 %collective-permute-done.42 = f32[1,4096]{1,0:T(1,128)S(1)} collective-permute-done((f32[1,4096]{1,0:T(1,128)S(1)}, f32[1,4096]{1,0:T(1,128)S(1)}, u32[]{:S(2)}, u32[]{:S(2)}) %collective-permute-start.42) | collective-permute-done | bytes 16416 | tf_op jit(solution)/shard_map/ppermute | solution.py:193
  268.4 3.4 %collective-permute-done.43 = f32[1,4096]{1,0:T(1,128)S(1)} collective-permute-done((f32[1,4096]{1,0:T(1,128)S(1)}, f32[1,4096]{1,0:T(1,128)S(1)}, u32[]{:S(2)}, u32[]{:S(2)}) %collective-permute-start.43) | collective-permute-done | bytes 16416 | tf_op jit(solution)/shard_map/ppermute | solution.py:193
  271.8 3.2 %collective-permute-start.44 = (f32[1,4096]{1,0:T(1,128)S(1)}, f32[1,4096]{1,0:T(1,128)S(1)}, u32[]{:S(2)}, u32[]{:S(2)}) collective-permute-start(f32[1,4096]{1,0:T(1,128)S(1)} %add.798), channel_id=1, source_target_pairs={{0,64},{64,0},{1,65},{65,1},{2,66},{66,2},{3,67},{67,3},{4,68},{68... | collective-permute-start | bytes 49160 | tf_op jit(solution)/shard_map/ppermute | solution.py:193
  283.3 17.6 %shard_map.48 = bf16[256,4096]{1,0:T(8,128)(2,1)} custom-call(bf16[256,4096]{1,0:T(8,128)(2,1)} %copy-done.3, bf16[256,4096]{1,0:T(8,128)(2,1)} %refs_0_, bf16[256,4096]{1,0:T(8,128)(2,1)} %collective-permute-done.7.refs_5_.refs_1_, bf16[256,4096]{1,0:T(8,128)(2,1)} %collective-permute-done.8.refs_6_.refs_2_, ...), custom_call_target="tpu_custom_call" | custom-call | tf_op jit(solution)/shard_map/pallas_call | solution.py:306
  (175 shorter events, 90.6 us)
Async XLA Ops:
  7.2 273.6 %all-gather.2.cloned.1.call-start = ((), (), s32[]{:S(2)}) async-start(), calls=%async_computation | async-start | bytes 18874368 | tf_op jit(solution)/shard_map/all_gather | solution.py:405
  7.2 9.5 %collective-permute-start.10 = (bf16[256,4096]{1,0:T(8,128)(2,1)}, bf16[256,4096]{1,0:T(8,128)(2,1)S(1)}, u32[]{:S(2)}, u32[]{:S(2)}) collective-permute-start(bf16[256,4096]{1,0:T(8,128)(2,1)} %refs_2_.3), channel_id=1, source_target_pairs={{0,8},{8,0},{1,9},{9,1},{2,10},{10,2},{3,11},{11,3},{4,12},{12,4},... | collective-permute-start | bytes 6291464 | tf_op jit(solution)/shard_map/ppermute | solution.py:325
  7.3 49.7 %collective-permute-start.7 = (bf16[256,4096]{1,0:T(8,128)(2,1)}, bf16[256,4096]{1,0:T(8,128)(2,1)}, u32[]{:S(2)}, u32[]{:S(2)}) collective-permute-start(bf16[256,4096]{1,0:T(8,128)(2,1)} %refs_0_), channel_id=1, source_target_pairs={{0,16},{16,32},{32,48},{48,0},{1,17},{17,33},{33,49},{49,1},{2,18}... | collective-permute-start | bytes 6291464 | tf_op jit(solution)/shard_map/ppermute | solution.py:318
  9.0 48.0 %collective-permute-start.8 = (bf16[256,4096]{1,0:T(8,128)(2,1)}, bf16[256,4096]{1,0:T(8,128)(2,1)}, u32[]{:S(2)}, u32[]{:S(2)}) collective-permute-start(bf16[256,4096]{1,0:T(8,128)(2,1)} %refs_0_), channel_id=1, source_target_pairs={{0,48},{16,0},{32,16},{48,32},{1,49},{17,1},{33,17},{49,33},{2,50}... | collective-permute-start | bytes 6291464 | tf_op jit(solution)/shard_map/ppermute | solution.py:318
  10.6 50.0 %collective-permute-start.9 = (bf16[256,4096]{1,0:T(8,128)(2,1)}, bf16[256,4096]{1,0:T(8,128)(2,1)}, u32[]{:S(2)}, u32[]{:S(2)}) collective-permute-start(bf16[256,4096]{1,0:T(8,128)(2,1)} %refs_2_.3), channel_id=1, source_target_pairs={{0,64},{64,0},{1,65},{65,1},{2,66},{66,2},{3,67},{67,3},{4,68},{68... | collective-permute-start | bytes 6291464 | tf_op jit(solution)/shard_map/ppermute | solution.py:325
  60.6 26.1 %collective-permute-start.16 = (bf16[256,4096]{1,0:T(8,128)(2,1)}, bf16[256,4096]{1,0:T(8,128)(2,1)}, u32[]{:S(2)}, u32[]{:S(2)}) collective-permute-start(bf16[256,4096]{1,0:T(8,128)(2,1)} %collective-permute-done.9.refs_2_.refs_4_), channel_id=1, source_target_pairs={{0,8},{8,0},{1,9},{9,1},{2,10},{10,2},{3,11},{11,3},{4,12},{12,4},... | collective-permute-start | bytes 6291464 | tf_op jit(solution)/shard_map/ppermute | solution.py:325
  71.3 12.7 %collective-permute-start.13 = (f32[2,32,1536]{2,1,0:T(8,128)S(1)}, f32[2,32,1536]{2,1,0:T(8,128)S(1)}, u32[]{:S(2)}, u32[]{:S(2)}) collective-permute-start(f32[2,32,1536]{2,1,0:T(8,128)S(1)} %get-tuple-element.83), channel_id=1, source_target_pairs={{0,1},{1,2},{2,3},{3,0},{4,5},{5,6},{6,7},{7,4},{8,9},{9,10},{10,1... | collective-permute-start | bytes 1179656 | tf_op jit(solution)/shard_map/ppermute | solution.py:335
  77.5 30.2 %collective-permute-start.11 = (bf16[128,4096]{1,0:T(8,128)(2,1)}, bf16[128,4096]{1,0:T(8,128)(2,1)S(1)}, u32[]{:S(2)}, u32[]{:S(2)}) collective-permute-start(bf16[128,4096]{1,0:T(8,128)(2,1)} %slice.150), channel_id=1, source_target_pairs={{0,16},{16,32},{32,48},{48,0},{1,17},{17,33},{33,49},{49,1},{2,18}... | collective-permute-start | bytes 3145736 | tf_op jit(solution)/shard_map/ppermute | solution.py:318
  77.8 29.9 %collective-permute-start.12 = (bf16[128,4096]{1,0:T(8,128)(2,1)}, bf16[128,4096]{1,0:T(8,128)(2,1)}, u32[]{:S(2)}, u32[]{:S(2)}) collective-permute-start(bf16[128,4096]{1,0:T(8,128)(2,1)} %slice.151), channel_id=1, source_target_pairs={{0,48},{16,0},{32,16},{48,32},{1,49},{17,1},{33,17},{49,33},{2,50}... | collective-permute-start | bytes 3145736 | tf_op jit(solution)/shard_map/ppermute | solution.py:318
  80.7 53.1 %collective-permute-start.23 = (bf16[256,4096]{1,0:T(8,128)(2,1)}, bf16[256,4096]{1,0:T(8,128)(2,1)}, u32[]{:S(2)}, u32[]{:S(2)}) collective-permute-start(bf16[256,4096]{1,0:T(8,128)(2,1)} %refs_0_), channel_id=1, source_target_pairs={{0,64},{64,0},{1,65},{65,1},{2,66},{66,2},{3,67},{67,3},{4,68},{68... | collective-permute-start | bytes 6291464 | tf_op jit(solution)/shard_map/ppermute | solution.py:325
  84.0 18.7 %collective-permute-start.14 = (f32[2,32,1536]{2,1,0:T(8,128)}, f32[2,32,1536]{2,1,0:T(8,128)}, u32[]{:S(2)}, u32[]{:S(2)}) collective-permute-start(f32[2,32,1536]{2,1,0:T(8,128)} %get-tuple-element.84), channel_id=1, source_target_pairs={{0,2},{1,3},{2,0},{3,1},{4,6},{5,7},{6,4},{7,5},{8,10},{9,11},{10,... | collective-permute-start | bytes 1179656 | tf_op jit(solution)/shard_map/ppermute | solution.py:335
  86.7 17.3 %collective-permute-start.15 = (f32[2,32,1536]{2,1,0:T(8,128)}, f32[2,32,1536]{2,1,0:T(8,128)}, u32[]{:S(2)}, u32[]{:S(2)}) collective-permute-start(f32[2,32,1536]{2,1,0:T(8,128)} %get-tuple-element.85), channel_id=1, source_target_pairs={{0,3},{1,0},{2,1},{3,2},{4,7},{5,4},{6,5},{7,6},{8,11},{9,8},{10,9... | collective-permute-start | bytes 1179656 | tf_op jit(solution)/shard_map/ppermute | solution.py:335
  102.7 11.4 %collective-permute-start.17 = (f32[2,32,1536]{2,1,0:T(8,128)}, f32[2,32,1536]{2,1,0:T(8,128)}, u32[]{:S(2)}, u32[]{:S(2)}) collective-permute-start(f32[2,32,1536]{2,1,0:T(8,128)} %get-tuple-element.87), channel_id=1, source_target_pairs={{0,1},{1,2},{2,3},{3,0},{4,5},{5,6},{6,7},{7,4},{8,9},{9,10},{10,1... | collective-permute-start | bytes 1179656 | tf_op jit(solution)/shard_map/ppermute | solution.py:335
  104.0 11.5 %collective-permute-start.18 = (f32[2,32,1536]{2,1,0:T(8,128)}, f32[2,32,1536]{2,1,0:T(8,128)}, u32[]{:S(2)}, u32[]{:S(2)}) collective-permute-start(f32[2,32,1536]{2,1,0:T(8,128)} %get-tuple-element.89), channel_id=1, source_target_pairs={{0,3},{1,0},{2,1},{3,2},{4,7},{5,4},{6,5},{7,6},{8,11},{9,8},{10,9... | collective-permute-start | bytes 1179656 | tf_op jit(solution)/shard_map/ppermute | solution.py:335
  125.1 10.2 %collective-permute-start.20 = (f32[2,32,1024]{2,1,0:T(8,128)}, f32[2,32,1024]{2,1,0:T(8,128)S(1)}, u32[]{:S(2)}, u32[]{:S(2)}) collective-permute-start(f32[2,32,1024]{2,1,0:T(8,128)} %get-tuple-element.98), channel_id=1, source_target_pairs={{0,1},{1,2},{2,3},{3,0},{4,5},{5,6},{6,7},{7,4},{8,9},{9,10},{10,1... | collective-permute-start | bytes 786440 | tf_op jit(solution)/shard_map/ppermute | solution.py:335
  126.2 17.1 %collective-permute-start.21 = (f32[2,32,1024]{2,1,0:T(8,128)}, f32[2,32,1024]{2,1,0:T(8,128)S(1)}, u32[]{:S(2)}, u32[]{:S(2)}) collective-permute-start(f32[2,32,1024]{2,1,0:T(8,128)} %get-tuple-element.99), channel_id=1, source_target_pairs={{0,2},{1,3},{2,0},{3,1},{4,6},{5,7},{6,4},{7,5},{8,10},{9,11},{10,... | collective-permute-start | bytes 786440 | tf_op jit(solution)/shard_map/ppermute | solution.py:335
  130.3 13.1 %collective-permute-start.22 = (f32[2,32,1024]{2,1,0:T(8,128)}, f32[2,32,1024]{2,1,0:T(8,128)}, u32[]{:S(2)}, u32[]{:S(2)}) collective-permute-start(f32[2,32,1024]{2,1,0:T(8,128)} %get-tuple-element.100), channel_id=1, source_target_pairs={{0,3},{1,0},{2,1},{3,2},{4,7},{5,4},{6,5},{7,6},{8,11},{9,8},{10,9... | collective-permute-start | bytes 786440 | tf_op jit(solution)/shard_map/ppermute | solution.py:335
  131.5 18.5 %collective-permute-start.19 = (f32[2,32,1536]{2,1,0:T(8,128)}, f32[2,32,1536]{2,1,0:T(8,128)}, u32[]{:S(2)}, u32[]{:S(2)}) collective-permute-start(f32[2,32,1536]{2,1,0:T(8,128)} %get-tuple-element.97), channel_id=1, source_target_pairs={{0,2},{1,3},{2,0},{3,1},{4,6},{5,7},{6,4},{7,5},{8,10},{9,11},{10,... | collective-permute-start | bytes 1179656 | tf_op jit(solution)/shard_map/ppermute | solution.py:335
  153.2 12.2 %collective-permute-start.24 = (f32[4,32,1024]{2,1,0:T(8,128)S(1)}, f32[4,32,1024]{2,1,0:T(8,128)S(1)}, u32[]{:S(2)}, u32[]{:S(2)}) collective-permute-start(f32[4,32,1024]{2,1,0:T(8,128)S(1)} %pad_maximum_fusion.6), channel_id=1, source_target_pairs={{0,4},{4,0},{1,5},{5,1},{2,6},{6,2},{3,7},{7,3},{8,12},{12,8},{9,1... | collective-permute-start | bytes 1572872 | tf_op jit(solution)/shard_map/ppermute | solution.py:402
  165.6 7.4 %collective-permute-start.26 = (f32[32,1024]{1,0:T(8,128)S(1)}, f32[32,1024]{1,0:T(8,128)S(1)}, u32[]{:S(2)}, u32[]{:S(2)}) collective-permute-start(f32[32,1024]{1,0:T(8,128)S(1)} %get-tuple-element.151), channel_id=1, source_target_pairs={{0,64},{64,0},{1,65},{65,1},{2,66},{66,2},{3,67},{67,3},{4,68},{68... | collective-permute-start | bytes 393224 | tf_op jit(solution)/shard_map/ppermute | solution.py:325
  168.9 7.0 %collective-permute-start.27 = (f32[32,1024]{1,0:T(8,128)S(1)}, f32[32,1024]{1,0:T(8,128)S(1)}, u32[]{:S(2)}, u32[]{:S(2)}) collective-permute-start(f32[32,1024]{1,0:T(8,128)S(1)} %get-tuple-element.150), channel_id=1, source_target_pairs={{0,72},{8,64},{64,8},{72,0},{1,73},{9,65},{65,9},{73,1},{2,74},{10... | collective-permute-start | bytes 393224 | tf_op jit(solution)/shard_map/ppermute | solution.py:323
  182.6 5.5 %collective-permute-start.2 = (f32[2,4096]{1,0:T(2,128)S(1)}, f32[2,4096]{1,0:T(2,128)S(1)}, u32[]{:S(2)}, u32[]{:S(2)}) collective-permute-start(f32[2,4096]{1,0:T(2,128)S(1)} %pad_maximum_fusion.19), channel_id=1, source_target_pairs={{0,32},{16,48},{32,0},{48,16},{1,33},{17,49},{33,1},{49,17},{2,34}... | collective-permute-start | bytes 98312 | tf_op jit(solution)/shard_map/while/body/ppermute | solution.py:200
  188.2 5.5 %collective-permute-start.3 = (f32[2,4096]{1,0:T(2,128)S(1)}, f32[2,4096]{1,0:T(2,128)S(1)}, u32[]{:S(2)}, u32[]{:S(2)}) collective-permute-start(f32[2,4096]{1,0:T(2,128)S(1)} %pad_maximum_fusion.20), channel_id=1, source_target_pairs={{0,64},{64,0},{1,65},{65,1},{2,66},{66,2},{3,67},{67,3},{4,68},{68... | collective-permute-start | bytes 98312 | tf_op jit(solution)/shard_map/while/body/ppermute | solution.py:200
  202.0 5.5 %collective-permute-start.6 = (f32[2,4096]{1,0:T(2,128)S(1)}, f32[2,4096]{1,0:T(2,128)S(1)}, u32[]{:S(2)}, u32[]{:S(2)}) collective-permute-start(f32[2,4096]{1,0:T(2,128)S(1)} %pad_maximum_fusion.23), channel_id=1, source_target_pairs={{0,2},{1,3},{2,0},{3,1},{4,6},{5,7},{6,4},{7,5},{8,10},{9,11},{10,... | collective-permute-start | bytes 98312 | tf_op jit(solution)/shard_map/while/body/ppermute | solution.py:200
  208.3 6.5 %collective-permute-start.28 = (bf16[4,32,1024]{2,1,0:T(8,128)(2,1)S(1)}, bf16[4,32,1024]{2,1,0:T(8,128)(2,1)S(1)}, u32[]{:S(2)}, u32[]{:S(2)}) collective-permute-start(bf16[4,32,1024]{2,1,0:T(8,128)(2,1)S(1)} %shard_map.44), channel_id=1, source_target_pairs={{0,4},{4,0},{1,5},{5,1},{2,6},{6,2},{3,7},{7,3},{8,12},{12,8},{9,1... | collective-permute-start | bytes 786440 | tf_op jit(solution)/shard_map/ppermute | solution.py:414
  214.8 18.2 %collective-permute-start.29 = (bf16[2,4,32,1024]{3,2,1,0:T(8,128)(2,1)S(1)}, bf16[2,4,32,1024]{3,2,1,0:T(8,128)(2,1)S(1)}, u32[]{:S(2)}, u32[]{:S(2)}) collective-permute-start(bf16[2,4,32,1024]{3,2,1,0:T(8,128)(2,1)S(1)} %pad_maximum_fusion.8.refs_0_), channel_id=1, source_target_pairs={{0,3},{1,0},{2,1},{3,2},{4,7},{5,4},{6,5},{7,6},{8,11},{9,8},{10,9... | collective-permute-start | bytes 1572872 | tf_op jit(solution)/shard_map/ppermute | solution.py:335
  217.1 19.4 %collective-permute-start.30 = (bf16[2,4,32,1024]{3,2,1,0:T(8,128)(2,1)S(1)}, bf16[2,4,32,1024]{3,2,1,0:T(8,128)(2,1)S(1)}, u32[]{:S(2)}, u32[]{:S(2)}) collective-permute-start(bf16[2,4,32,1024]{3,2,1,0:T(8,128)(2,1)S(1)} %pad_maximum_fusion.8.refs_0_), channel_id=1, source_target_pairs={{0,1},{1,2},{2,3},{3,0},{4,5},{5,6},{6,7},{7,4},{8,9},{9,10},{10,1... | collective-permute-start | bytes 1572872 | tf_op jit(solution)/shard_map/ppermute | solution.py:335
  217.1 19.4 %collective-permute-start.31 = (bf16[2,4,32,1024]{3,2,1,0:T(8,128)(2,1)S(1)}, bf16[2,4,32,1024]{3,2,1,0:T(8,128)(2,1)S(1)}, u32[]{:S(2)}, u32[]{:S(2)}) collective-permute-start(bf16[2,4,32,1024]{3,2,1,0:T(8,128)(2,1)S(1)} %pad_maximum_fusion.8.refs_0_), channel_id=1, source_target_pairs={{0,2},{1,3},{2,0},{3,1},{4,6},{5,7},{6,4},{7,5},{8,10},{9,11},{10,... | collective-permute-start | bytes 1572872 | tf_op jit(solution)/shard_map/ppermute | solution.py:335
  236.4 23.3 %collective-permute-start.36 = (bf16[256,4096]{1,0:T(8,128)(2,1)}, bf16[256,4096]{1,0:T(8,128)(2,1)S(1)}, u32[]{:S(2)}, u32[]{:S(2)}) collective-permute-start(bf16[256,4096]{1,0:T(8,128)(2,1)} %refs_0_), channel_id=1, source_target_pairs={{0,8},{8,0},{1,9},{9,1},{2,10},{10,2},{3,11},{11,3},{4,12},{12,4},... | collective-permute-start | bytes 6291464 | tf_op jit(solution)/shard_map/ppermute | solution.py:325
  236.4 23.3 %collective-permute-start.37 = (bf16[256,4096]{1,0:T(8,128)(2,1)}, bf16[256,4096]{1,0:T(8,128)(2,1)S(1)}, u32[]{:S(2)}, u32[]{:S(2)}) collective-permute-start(bf16[256,4096]{1,0:T(8,128)(2,1)} %collective-permute-done.7.refs_5_.refs_1_), channel_id=1, source_target_pairs={{0,8},{8,0},{1,9},{9,1},{2,10},{10,2},{3,11},{11,3},{4,12},{12,4},... | collective-permute-start | bytes 6291464 | tf_op jit(solution)/shard_map/ppermute | solution.py:325
  236.9 22.8 %collective-permute-start.38 = (bf16[256,4096]{1,0:T(8,128)(2,1)}, bf16[256,4096]{1,0:T(8,128)(2,1)S(1)}, u32[]{:S(2)}, u32[]{:S(2)}) collective-permute-start(bf16[256,4096]{1,0:T(8,128)(2,1)} %collective-permute-done.8.refs_6_.refs_2_), channel_id=1, source_target_pairs={{0,8},{8,0},{1,9},{9,1},{2,10},{10,2},{3,11},{11,3},{4,12},{12,4},... | collective-permute-start | bytes 6291464 | tf_op jit(solution)/shard_map/ppermute | solution.py:325
  244.9 5.7 %collective-permute-start.34 = (f32[1,4096]{1,0:T(1,128)S(1)}, f32[1,4096]{1,0:T(1,128)S(1)}, u32[]{:S(2)}, u32[]{:S(2)}) collective-permute-start(f32[1,4096]{1,0:T(1,128)S(1)} %add.793), channel_id=1, source_target_pairs={{0,32},{16,48},{32,0},{48,16},{1,33},{17,49},{33,1},{49,17},{2,34}... | collective-permute-start | bytes 49160 | tf_op jit(solution)/shard_map/ppermute | solution.py:193
  (34 other events, 192.4 us)
Sparse Core Ops, SparseCore 0:
  176.1 84.4 all-gather.1

commit v5 on v4

v5 whole, which is shorter than its diff:
```python
import functools
import math

import jax
import jax.numpy as jnp
from jax import lax
from jax.experimental import pallas as pl
from jax.experimental.pallas import tpu as pltpu
from jax.sharding import Mesh, PartitionSpec as P

F = 32768
ITERS = 3
SAMPLES = 4096
LANES = 128
ROWS = 32
GROUP = 4
DEPTH = 2048
FEAT = ("zl", "x")


def tile_list(shapes):
    return [
        (k, g, n)
        for k, (_, groups, _, width) in enumerate(shapes)
        for g in range(groups)
        for n in range(0, width, LANES)
    ]


def row_pass(tiles, blocks, logits, where, c_ref, peak_ref, row_ref):
    def tile(f, t):
        k, g, n = tiles[t]
        return logits[k][f, g, :, n:n + LANES] + c_ref[:, lanes(where[0, t])]

    def maxima(f, _):
        acc = tile(f, 0)
        for t in range(1, len(tiles)):
            acc = jnp.maximum(acc, tile(f, t))
        peak_ref[pl.ds(f * ROWS, ROWS), :] = acc
        return 0

    lax.fori_loop(0, blocks, maxima, 0)
    peak = jnp.max(peak_ref[...], axis=1, keepdims=True)
    peak_ref[...] = jnp.broadcast_to(peak, peak_ref.shape)

    def totals(f, _):
        top = peak_ref[pl.ds(f * ROWS, ROWS), :]
        acc = jnp.exp(tile(f, 0) - top)
        for t in range(1, len(tiles)):
            acc = acc + jnp.exp(tile(f, t) - top)
        row_ref[pl.ds(f * ROWS, ROWS), :] = acc
        return 0

    lax.fori_loop(0, blocks, totals, 0)
    return jnp.sum(row_ref[...], axis=1, keepdims=True)


def lanes(tile):
    return pl.ds(pl.multiple_of(tile * LANES, LANES), LANES)


def sinkhorn_kernel(shapes, where, *refs):
    logits, (c_ref, out_ref, peak_ref, row_ref) = refs[:len(shapes)], refs[len(shapes):]
    tiles = tile_list(shapes)
    blocks = shapes[0][0]
    total = row_pass(tiles, blocks, logits, where, c_ref, peak_ref, row_ref)
    row_ref[...] = jnp.broadcast_to(-(peak_ref[:, 0:1] + jnp.log(total)), row_ref.shape)
    for first in range(0, len(tiles), GROUP):
        group = range(first, first + GROUP)

        def values(f, r, t):
            k, g, n = tiles[t]
            rows = row_ref[pl.ds(f * ROWS + r * 8, 8), :]
            return logits[k][f, g, r * 8:(r + 1) * 8, n:n + LANES] + rows

        def maxima(f, acc):
            for r in range(ROWS // 8):
                acc = [jnp.maximum(a, values(f, r, t)) for a, t in zip(acc, group)]
            return acc

        start = [jnp.full((8, LANES), -jnp.inf, jnp.float32) for _ in group]
        acc = lax.fori_loop(0, blocks, maxima, start)
        peaks = [jnp.max(a, axis=0, keepdims=True) for a in acc]

        def totals(f, acc):
            for r in range(ROWS // 8):
                acc = [a + jnp.exp(values(f, r, t) - p) for a, p, t in zip(acc, peaks, group)]
            return acc

        start = [jnp.zeros((8, LANES), jnp.float32) for _ in group]
        acc = lax.fori_loop(0, blocks, totals, start)
        for a, p, t in zip(acc, peaks, group):
            out_ref[0:1, lanes(where[0, t])] = p
            out_ref[1:2, lanes(where[0, t])] = jnp.sum(a, axis=0, keepdims=True)


def exponentials_kernel(shapes, where, *refs):
    logits, (c_ref, out_ref, peak_ref, _) = refs[:len(shapes)], refs[len(shapes):]
    tiles = tile_list(shapes)
    acc = None
    for t, (k, g, n) in enumerate(tiles):
        x = logits[k][0, g, :, n:n + LANES] + c_ref[:, lanes(where[0, t])]
        acc = x if acc is None else jnp.maximum(acc, x)
    peak_ref[...] = jnp.broadcast_to(jnp.max(acc, axis=1, keepdims=True), peak_ref.shape)
    top = peak_ref[...]
    for t, (k, g, n) in enumerate(tiles):
        x = logits[k][0, g, :, n:n + LANES] + c_ref[:, lanes(where[0, t])]
        out_ref[g, :, n:n + LANES] = jnp.exp(x - top).astype(jnp.bfloat16)


def scaled_rows(tiles, kernels, where, v_ref, row_ref):
    for d, k_ref in enumerate(kernels):
        for z in range(k_ref.shape[0]):
            acc = None
            for t, (_, g, n) in enumerate(tiles):
                x = k_ref[z, g, :, n:n + LANES].astype(jnp.float32) * v_ref[:, lanes(where[0, t])]
                acc = x if acc is None else acc + x
            first = (d * k_ref.shape[0] + z) * ROWS
            row_ref[first:first + ROWS, :] = acc
    return jnp.sum(row_ref[...], axis=1, keepdims=True)


def balance_kernel(shapes, where, *refs):
    kernels, (v_ref, out_ref, row_ref) = refs[:len(shapes)], refs[len(shapes):]
    tiles = tile_list(((1,) + shapes[0][1:],))
    total = scaled_rows(tiles, kernels, where, v_ref, row_ref)
    row_ref[...] = jnp.broadcast_to(1.0 / total, row_ref.shape)
    for t, (_, g, n) in enumerate(tiles):
        acc = jnp.zeros((ROWS, LANES), jnp.float32)
        for d, k_ref in enumerate(kernels):
            for z in range(k_ref.shape[0]):
                first = (d * k_ref.shape[0] + z) * ROWS
                acc = acc + k_ref[z, g, :, n:n + LANES].astype(jnp.float32) * row_ref[first:first + ROWS, :]
        out_ref[0:1, lanes(where[0, t])] = jnp.sum(acc, axis=0, keepdims=True)


def targets_kernel(shapes, widths, where, *refs):
    n = len(shapes)
    kernels, v_ref, x_refs, (out_ref, row_ref, w_ref) = refs[:n], refs[n], refs[n + 1:-3], refs[-3:]

    @pl.when(pl.program_id(0) == 0)
    def _():
        tiles = tile_list(((1,) + shapes[0][1:],))
        total = scaled_rows(tiles, kernels, where, v_ref, row_ref)
        row_ref[...] = jnp.broadcast_to(1.0 / total, row_ref.shape)
        for d, k_ref in enumerate(kernels):
            for z in range(k_ref.shape[0]):
                first = (d * k_ref.shape[0] + z) * ROWS
                scale = row_ref[first:first + ROWS, :]
                rows = pl.ds(pl.multiple_of(where[2, d * k_ref.shape[0] + z] * ROWS, ROWS), ROWS)
                for t, (_, g, n) in enumerate(tiles):
                    x = k_ref[z, g, :, n:n + LANES].astype(jnp.float32) * v_ref[:, lanes(where[0, t])]
                    w_ref[rows, lanes(where[1, t])] = (x * scale).astype(jnp.bfloat16)

    first, acc = 0, None
    for x, width in zip(x_refs, widths):
        part = jnp.dot(w_ref[:, first:first + width], x[...], preferred_element_type=jnp.float32)
        acc = part if acc is None else acc + part
        first += width
    out_ref[...] = acc.astype(out_ref.dtype)


def targets_call(where, kernels, v, datas):
    shapes = tuple(a.shape for a in kernels)
    rows = sum(s[0] for s in shapes) * ROWS
    widths = tuple(d.shape[0] for d in datas)
    depth, block = datas[0].shape[1], 1024
    vmem = pl.BlockSpec(memory_space=pltpu.VMEM)
    return pl.pallas_call(
        functools.partial(targets_kernel, shapes, widths),
        out_shape=jax.ShapeDtypeStruct((rows, depth), jnp.bfloat16),
        grid=(depth // block,),
        in_specs=[pl.BlockSpec(memory_space=pltpu.SMEM)] + [vmem] * (len(kernels) + 1)
        + [pl.BlockSpec((w, block), lambda n: (0, n)) for w in widths],
        out_specs=pl.BlockSpec((rows, block), lambda n: (0, n)),
        scratch_shapes=[
            pltpu.VMEM((rows, LANES), jnp.float32),
            pltpu.VMEM((rows, sum(widths)), jnp.bfloat16),
        ],
        compiler_params=pltpu.CompilerParams(vmem_limit_bytes=48 * 2**20),
    )(where, *kernels, v, *datas)


def balance_call(kernel, out_shape, where, kernels, v):
    shapes = tuple(a.shape for a in kernels)
    rows = sum(s[0] for s in shapes) * ROWS
    vmem = pl.BlockSpec(memory_space=pltpu.VMEM)
    return pl.pallas_call(
        functools.partial(kernel, shapes),
        out_shape=out_shape,
        in_specs=[pl.BlockSpec(memory_space=pltpu.SMEM)] + [vmem] * (len(kernels) + 1),
        out_specs=vmem,
        scratch_shapes=[pltpu.VMEM((rows, LANES), jnp.float32)],
        compiler_params=pltpu.CompilerParams(vmem_limit_bytes=32 * 2**20),
    )(where, *kernels, v)


def row_call(kernel, out_shape, where, logits, c):
    shapes = tuple(a.shape for a in logits)
    rows = shapes[0][0] * ROWS
    vmem = pl.BlockSpec(memory_space=pltpu.VMEM)
    return pl.pallas_call(
        functools.partial(kernel, shapes),
        out_shape=out_shape,
        in_specs=[pl.BlockSpec(memory_space=pltpu.SMEM)] + [vmem] * (len(logits) + 1),
        out_specs=vmem,
        scratch_shapes=[pltpu.VMEM((rows, LANES), jnp.float32)] * 2,
        compiler_params=pltpu.CompilerParams(vmem_limit_bytes=32 * 2**20),
    )(where, *logits, c)


def combine(a, b):
    peak = jnp.maximum(a[0], b[0])
    total = a[1] * jnp.exp(a[0] - peak) + b[1] * jnp.exp(b[0] - peak)
    return jnp.stack([peak, total])


SAMP_STEPS = (("core", 2, 1), ("y", 4, 1), ("y", 4, 2), ("zh", 2, 1))
FEAT_STEPS = (("zl", 2, 1), ("x", 4, 1), ("x", 4, 2))


def column_sum(x, steps):
    for axis, n, step in steps:
        x = x + lax.ppermute(x, axis, [(i, i ^ step) for i in range(n)])
    return x


def column_update(stats, steps):
    for axis, n, step in steps:
        pairs = [(i, i ^ step) for i in range(n)]
        stats = combine(stats, lax.ppermute(stats, axis, pairs))
    return -(stats[0] + jnp.log(stats[1]))[None, :]


def lane_sums(x):
    acc = None
    for n in range(0, x.shape[1], LANES):
        v = x[:, n:n + LANES].astype(jnp.float32)
        acc = v * v if acc is None else acc + v * v
    return acc


def partial_kernel(noise_parts, jobs, known, scale, *refs):
    n_count = sum(noise_parts)
    x_count = 1 + max(x for _, xs in jobs for x in xs)
    where, old_n, old_x = refs[:3]
    n_refs, x_refs = refs[3:3 + n_count], refs[3 + n_count:3 + n_count + x_count]
    outs, (n_sq, x_row, acc, x_sq) = refs[3 + n_count + x_count:-4], refs[-4:]
    step = pl.program_id(0)
    parts, share, _ = acc.shape
    rows = parts * share
    starts = [sum(noise_parts[:q]) for q in range(len(noise_parts))]

    @pl.when(step == 0)
    def _():
        acc[...] = jnp.zeros_like(acc)
        n_sq[...] = jnp.zeros_like(n_sq)
        x_sq[...] = jnp.zeros_like(x_sq)

    places, first = [], 0
    for qs, xs in jobs:
        widths = [x_refs[x].shape[0] for x in xs]
        block = jnp.concatenate(
            [n_refs[starts[q] + p][...] for q in qs for p in range(noise_parts[q])], axis=0
        )
        others = jnp.concatenate([x_refs[x][...] for x in xs], axis=0)
        inner = lax.dot_general(
            block, others, (((1,), (1,)), ((), ())), preferred_element_type=jnp.float32
        )
        for i, q in enumerate(qs):
            at = first + i * sum(widths)
            part = inner[i * rows:(i + 1) * rows].reshape(parts, share, sum(widths))
            acc[:, :, at:at + sum(widths)] += part
            for x, width in zip(xs, widths):
                places.append((q, x, at))
                at += width
        first += len(qs) * sum(widths)
    x_starts = [sum(r.shape[0] for r in x_refs[:x]) for x in range(x_count)]
    for squares, blocks, seen in ((n_sq, n_refs, known[0]), (x_sq, x_refs, known[1])):
        start = 0
        for r in blocks:
            if start >= seen:
                squares[start:start + r.shape[0], :] += lane_sums(r[...])
            start += r.shape[0]

    @pl.when(step == pl.num_programs(0) - 1)
    def _():
        x_row[...] = lax.dot_general(
            jnp.ones((8, LANES), jnp.float32), x_sq[...], (((1,), (1,)), ((), ())),
            precision=lax.Precision.HIGHEST, preferred_element_type=jnp.float32,
        )[0:1]
        n_sq[...] = jnp.broadcast_to(jnp.sum(n_sq[...], axis=1, keepdims=True), n_sq.shape)
        if known[0]:
            n_sq[0:known[0], :] = old_n[...]
        if known[1]:
            x_row[:, 0:known[1]] = old_x[...]
        for d, out in zip((0, 1, -1, 2), outs):
            for z in range(2):
                f = (where[1] + z) % 2 * 4 + (where[0] + d + 4) % 4
                for q, x, at in places:
                    width = x_refs[x].shape[0]
                    own = n_sq[pl.ds(q * rows + f * share, share), 0:1]
                    other = x_row[:, x_starts[x]:x_starts[x] + width]
                    inner = acc[f, :, at:at + width]
                    out[z, :, at:at + width] = (own + other - 2.0 * inner) * scale


def partial_call(scale, parts, where, noises, datas, jobs, old_n=None, old_x=None):
    known = (0 if old_n is None else old_n.shape[0], 0 if old_x is None else old_x.shape[1])
    old_n = jnp.zeros((8, LANES), jnp.float32) if old_n is None else old_n
    old_x = jnp.zeros((1, LANES), jnp.float32) if old_x is None else old_x
    noise_parts = tuple(len(n) for n in noises)
    flat = [a for n in noises for a in n]
    rows, depth = sum(a.shape[0] for a in noises[0]), flat[0].shape[1]
    total = sum(len(qs) * sum(datas[x].shape[0] for x in xs) for qs, xs in jobs)
    share = rows // parts
    block = DEPTH
    out = (2, share, total)
    n_rows, columns = sum(a.shape[0] for a in flat), sum(d.shape[0] for d in datas)
    squares = [(n_rows, LANES), (1, columns)]
    *pieces, n_sq, x_row = pl.pallas_call(
        functools.partial(partial_kernel, noise_parts, jobs, known, scale),
        cost_estimate=pl.CostEstimate(flops=1, bytes_accessed=1, transcendentals=0),
        out_shape=[jax.ShapeDtypeStruct(o, jnp.float32) for o in [out] * 4 + squares],
        grid=(depth // block,),
        in_specs=[pl.BlockSpec(memory_space=pltpu.SMEM)]
        + [pl.BlockSpec(o.shape, lambda k: (0, 0)) for o in (old_n, old_x)]
        + [pl.BlockSpec((a.shape[0], block), lambda k: (0, k)) for a in (*flat, *datas)],
        out_specs=[pl.BlockSpec(out, lambda k: (0, 0, 0))] * 4
        + [pl.BlockSpec(o, lambda k: (0, 0)) for o in squares],
        scratch_shapes=[
            pltpu.VMEM((parts, share, total), jnp.float32),
            pltpu.VMEM((columns, LANES), jnp.float32),
        ],
        compiler_params=pltpu.CompilerParams(vmem_limit_bytes=48 * 2**20),
    )(where, old_n, old_x, *flat, *datas)
    return pieces, n_sq, x_row


def ring(x, shift):
    return lax.ppermute(x, "y", [(i, (i + shift) % 4) for i in range(4)])


def swap(x, axis):
    return lax.ppermute(x, axis, [(0, 1), (1, 0)])


SOURCES = [(0, 0, 0), (0, 0, 1), (0, 1, 0), (0, 1, 1), (-1, 0, 0), (-1, 0, 1), (1, 0, 0), (1, 0, 1)]
SOURCES += [(-1, 1, 0), (-1, 1, 1), (1, 1, 0), (1, 1, 1), (-2, 0, 0), (2, 0, 1), (-2, 1, 0), (2, 1, 1)]
ALONG_X = (0, 1, -1, 2)


def along_x(x, step):
    return lax.ppermute(x, "x", [(i, (i + step) % 4) for i in range(4)])


def tables(parts):
    zh, y, core = (lax.axis_index(a) for a in ("zh", "y", "core"))
    where, place = [], []
    for dz in range(2):
        for s, (dy, dc, half) in enumerate(SOURCES):
            inside = ((y + dy + 4) % 4 * 2 + (core + dc) % 2) * 2 + half
            where.append((zh + dz) % 2 * 16 + inside)
            place.append(16 + inside if dz else jnp.int32(s))
    x, zl = lax.axis_index("x"), lax.axis_index("zl")
    rows = [(zl + z) % 2 * 4 + (x + d + 4) % 4 for d in ALONG_X for z in range(2)]
    rows = jnp.pad(jnp.stack(rows), (0, len(where) - len(rows)))
    return jnp.stack([jnp.stack(where), jnp.stack(place), rows]).astype(jnp.int32)


def local(noise, data):
    temper = 0.5 / math.sqrt(F)
    scale = -1.0 / (F * temper)
    parts = 8
    half = noise.shape[0] // 2
    call = functools.partial(partial_call, scale, parts)
    where = tables(parts)
    here = jnp.stack([lax.axis_index("x"), lax.axis_index("zl")]).astype(jnp.int32)
    hold = lax.optimization_barrier

    u, w = ring(data, 1), ring(data, -1)
    far = swap(noise, "zh")
    data_c = swap(data, "core")
    u, w, far, data_c, data = hold((u, w, far, data_c, data))

    ua, wb = u[:half], w[half:]
    ua, wb, u, w, data = hold((ua, wb, u, w, data))
    u3, w3 = ring(ua, 1), ring(wb, -1)
    u_c, w_c = swap(u, "core"), swap(w, "core")
    other = swap(data, "zh")
    noises = [(noise,), (far,)]
    (a0, a1, a3, a2), n_sq, _ = call(here, noises, [data, data_c, u, w], (((0, 1), (0, 1, 2, 3)),))
    u_c, w_c, a0, a1, a2, a3 = hold((u_c, w_c, a0, a1, a2, a3))
    a1, a3 = along_x(a1, 1), along_x(a3, -1)
    (b0, b1, b3, b2), _, _ = call(here, noises, [u_c, w_c], (((0, 1), (0, 1)),), n_sq)
    a2 = along_x(a2, 2)
    b1, b3 = along_x(b1, 1), along_x(b3, -1)
    u3, w3, a1, a3, b0, b2 = hold((u3, w3, a1, a3, b0, b2))

    u3_c, w3_c = swap(u3, "core"), swap(w3, "core")
    (c0, c1, c3, c2), _, _ = call(here, noises, [u3, w3, u3_c, w3_c], (((0, 1), (0, 1, 2, 3)),), n_sq)
    b2 = along_x(b2, 2)
    c1, c3, c2 = along_x(c1, 1), along_x(c3, -1), along_x(c2, 2)
    b2, c1, c2, c3, other = hold((b2, c1, c2, c3, other))
    a, b, c = a0 + a1 + a2 + a3, b0 + b1 + b2 + b3, c0 + c1 + c2 + c3

    def halves(z):
        return jnp.stack([
            jnp.concatenate([p[z][:, i * n:(i + 1) * n] for p, n in ((a, 1024), (b, 512), (c, 512))], axis=1)
            for i in range(2)
        ])

    own = halves(0) + lax.ppermute(halves(1), "zl", [(0, 1), (1, 0)])
    own = jnp.stack([own[0], swap(own[1], "zh")])
    own, other = hold((own, other))
    others = lax.all_gather(other, ("y", "core"), axis=0, tiled=True)
    out = jax.ShapeDtypeStruct((2, SAMPLES), jnp.float32)

    steps = SAMP_STEPS + FEAT_STEPS
    once = lax.axis_index("x") // 8 + 1

    def spread(_, c):
        return column_update(row_call(sinkhorn_kernel, out, where, [own[None]], c), steps)

    c = lax.fori_loop(0, once, spread, jnp.zeros((1, SAMPLES), jnp.float32))
    shape = jax.ShapeDtypeStruct(own.shape, jnp.bfloat16)
    mine = row_call(exponentials_kernel, shape, where, [own[None]], c)
    both = jnp.stack([mine, lax.ppermute(mine, "zl", [(0, 1), (1, 0)])])
    mine, both = hold((mine, both))
    kernels = [both] + [along_x(both, -d) for d in ALONG_X[1:]]

    sums = jax.ShapeDtypeStruct((1, SAMPLES), jnp.float32)

    def balance(_, v):
        return 1.0 / column_sum(balance_call(balance_kernel, sums, where, [mine[None]], v), steps)

    v = lax.fori_loop(0, once, balance, jnp.ones((1, SAMPLES), jnp.float32))
    blocks = [data, data_c, u, w, u_c, w_c, u3, w3, u3_c, w3_c]
    for _ in range(2, ITERS):
        v = 1.0 / column_sum(balance_call(balance_kernel, sums, where, kernels, v), SAMP_STEPS)
    c = c + jnp.log(v)
    share = SAMPLES // parts
    start = (lax.axis_index("zl") * 4 + lax.axis_index("x")) * share
    column_out = lax.dynamic_slice_in_dim(c[0] * temper, start, share, 0)
    return (targets_call(where, kernels, v, [*blocks, others]), column_out)


def solution(mesh):
    fine = Mesh(mesh.devices.reshape(2, 4, 2, 2, 4), ("zh", "y", "core", "zl", "x"))
    samp, feat = ("zh", "y", "core"), FEAT
    in_specs = (P(samp, feat), P(samp, feat))
    out_specs = (P(samp, feat), P(feat))
    return jax.shard_map(local, mesh=fine, in_specs=in_specs, out_specs=out_specs, check_vma=False)
```

time: 308 us -> 280 us (0.909)
  starting transfers between devices: 61.4 us -> 48.9 us
  local copies, waits for them, and re-layouts: 18.2 us -> 6.15 us
  other arithmetic: 12.1 us -> 4.09 us
  waiting for transfers between devices: 150 us -> 157 us
  Pallas kernels: 51.2 us -> 47.9 us
    ppermute x12, waiting for transfers between devices: 42.6 us -> 24.8 us  [along_x(): return lax.ppermute(x, 'x', [(i, (i + step) % 4) for i in range(4)])]
    ppermute x8 -> x11, waiting for transfers between devices: 20.4 us -> 37.9 us  [column_sum(): x = x + lax.ppermute(x, axis, [(i, i ^ step) for i in range(n)])]
    unnamed x40 -> x4, local copies, waits for them, and re-layouts: 10.4 us -> 0.01 us
    reduce_sum x4 -> x0, other arithmetic: 6.78 us -> none  [row_squares(): return jnp.sum(jnp.square(x.astype(jnp.float32)), axis=1, keepdims=True)]
    ppermute x8 -> x11, starting transfers between devices: 12.6 us -> 7.69 us  [column_sum(): x = x + lax.ppermute(x, axis, [(i, i ^ step) for i in range(n)])]
    ppermute x14 -> x10, starting transfers between devices: 13.8 us -> 9.76 us  [the longest x8 8.32 us: swap(): return lax.ppermute(x, axis, [(0, 1), (1, 0)])]
    ppermute x4, waiting for transfers between devices: 38.5 us -> 41.9 us  [ring(): return lax.ppermute(x, 'y', [(i, (i + shift) % 4) for i in range(4)])]
    ppermute x7, waiting for transfers between devices: 20.7 us -> 24.1 us  [column_update(): stats = combine(stats, lax.ppermute(stats, axis, pairs))]
  transfers between devices with their start and end apart: 46 -> 45, of which waited for: 32 -> 28; matrix products, arithmetic and copies ran while one was open for 5% -> 1% of each run, Pallas kernels for 11% -> 11%
where the time goes in v5:
time: 280 us; the launch traced here: 279 us
  waiting for transfers between devices  157 us (56%)
  starting transfers between devices  48.9 us (17%)
  Pallas kernels  47.9 us (17%)
  between operations  14.5 us (5%)
  local copies, waits for them, and re-layouts  6.15 us (2%)
  other arithmetic  4.09 us (1%)
    ppermute x4, waiting for transfers between devices, ring(): return lax.ppermute(x, 'y', [(i, (i + shift) % 4) for i in range(4)])  41.9 us
    ppermute x11, waiting for transfers between devices, column_sum(): x = x + lax.ppermute(x, axis, [(i, i ^ step) for i in range(n)])  37.9 us
    pallas_call x3, Pallas kernels, partial_call(): pl.pallas_call(functools.partial(partial_kernel, noise_parts, jobs, known...  25.9 us
    ppermute x12, waiting for transfers between devices, along_x(): return lax.ppermute(x, 'x', [(i, (i + step) % 4) for i in range(4)])  24.8 us
    ppermute x7, waiting for transfers between devices, column_update(): stats = combine(stats, lax.ppermute(stats, axis, pairs))  24.1 us
    ppermute x12, starting transfers between devices, along_x(): return lax.ppermute(x, 'x', [(i, (i + step) % 4) for i in range(4)])  19.1 us
    pallas_call x1, Pallas kernels, targets_call(): pl.pallas_call(functools.partial(targets_kernel, shapes, widths), out_sha...  17.1 us
    ppermute x1, waiting for transfers between devices, local(): own = halves(0) + lax.ppermute(halves(1), 'zl', [(0, 1), (1, 0)])  11.4 us
  transfers between devices with their start and end apart: 45, of which 28 were waited for; matrix products, arithmetic and copies ran while one was open for 1% of the time, Pallas kernels for 11%

profile of v5, /device:TPU:0, one launch (start us, length us, event | category | flops | bytes accessed | tf_op | source)
XLA Modules:
  0.0 279.0 jit_solution(13570209478586011185)
XLA Ops:
  10.5 4.0 %collective-permute-start.16 = (bf16[256,4096]{1,0:T(8,128)(2,1)}, bf16[256,4096]{1,0:T(8,128)(2,1)}, u32[]{:S(2)}, u32[]{:S(2)}) collective-permute-start(bf16[256,4096]{1,0:T(8,128)(2,1)} %refs_3_.5), channel_id=1, source_target_pairs={{0,64},{64,0},{1,65},{65,1},{2,66},{66,2},{3,67},{67,3},{4,68},{68... | collective-permute-start | bytes 6291464 | tf_op jit(solution)/shard_map/ppermute | solution.py:345
  14.5 41.8 %collective-permute-done.14.refs_7_ = bf16[256,4096]{1,0:T(8,128)(2,1)} collective-permute-done((bf16[256,4096]{1,0:T(8,128)(2,1)}, bf16[256,4096]{1,0:T(8,128)(2,1)}, u32[]{:S(2)}, u32[]{:S(2)}) %collective-permute-start.14) | collective-permute-done | bytes 2097184 | tf_op jit(solution)/shard_map/ppermute | solution.py:341
  56.4 3.7 %collective-permute-done.16.refs_4_ = bf16[256,4096]{1,0:T(8,128)(2,1)} collective-permute-done((bf16[256,4096]{1,0:T(8,128)(2,1)}, bf16[256,4096]{1,0:T(8,128)(2,1)}, u32[]{:S(2)}, u32[]{:S(2)}) %collective-permute-start.16) | collective-permute-done | bytes 2097184 | tf_op jit(solution)/shard_map/ppermute | solution.py:345
  65.3 3.0 %collective-permute-start.21 = (bf16[128,4096]{1,0:T(8,128)(2,1)}, bf16[128,4096]{1,0:T(8,128)(2,1)}, u32[]{:S(2)}, u32[]{:S(2)}) collective-permute-start(bf16[128,4096]{1,0:T(8,128)(2,1)} %slice.129), channel_id=1, source_target_pairs={{0,48},{16,0},{32,16},{48,32},{1,49},{17,1},{33,17},{49,33},{2,50}... | collective-permute-start | bytes 3145736 | tf_op jit(solution)/shard_map/ppermute | solution.py:341
  68.3 3.2 %collective-permute-start.32 = (bf16[256,4096]{1,0:T(8,128)(2,1)}, bf16[256,4096]{1,0:T(8,128)(2,1)}, u32[]{:S(2)}, u32[]{:S(2)}) collective-permute-start(bf16[256,4096]{1,0:T(8,128)(2,1)} %refs_5_.1), channel_id=1, source_target_pairs={{0,64},{64,0},{1,65},{65,1},{2,66},{66,2},{3,67},{67,3},{4,68},{68... | collective-permute-start | bytes 6291464 | tf_op jit(solution)/shard_map/ppermute | solution.py:345
  71.7 12.1 %shard_map.41 = (f32[2,32,2048]{2,1,0:T(8,128)S(1)}, f32[2,32,2048]{2,1,0:T(8,128)S(1)}, f32[2,32,2048]{2,1,0:T(8,128)S(1)}, f32[2,32,2048]{2,1,0:T(8,128)S(1)},...) custom-call(s32[2]{0:T(128)S(1)} %pad_add_fusion.1.refs_0_, f32[8,128]{1,0:T(8,128)S(1)} %broadcast_in_dim.16.refs_1_, ...), custom_call_target="tpu_custom_call" | custom-call | flops 1 | bytes 1 | tf_op jit(solution)/shard_map/pallas_call | solution.py:321
  87.1 7.1 %shard_map.42 = (f32[2,32,1024]{2,1,0:T(8,128)S(1)}, f32[2,32,1024]{2,1,0:T(8,128)}, f32[2,32,1024]{2,1,0:T(8,128)}, f32[2,32,1024]{2,1,0:T(8,128)}, f32[512,128]{1,0:T(8,128)}, /*index=5*/f32[1,512]{1,0:T(1,128)}) custom-call(s32[2]{0:T(128)S(1)} %pad_add_fusion.1.refs_0_, f32[512,128]{1,0:T(8,128)S(1)} %get-tuple-element.119.refs_1_, ...), custom_call_target="tpu_custom_call" | custom-call | flops 1 | bytes 1 | tf_op jit(solution)/shard_map/pallas_call | solution.py:321
  94.2 3.8 %collective-permute-done.22 = f32[2,32,2048]{2,1,0:T(8,128)S(1)} collective-permute-done((f32[2,32,2048]{2,1,0:T(8,128)S(1)}, f32[2,32,2048]{2,1,0:T(8,128)S(1)}, u32[]{:S(2)}, u32[]{:S(2)}) %collective-permute-start.22) | collective-permute-done | bytes 524320 | tf_op jit(solution)/shard_map/ppermute | solution.py:354
  102.1 12.8 %collective-permute-done.24 = f32[2,32,2048]{2,1,0:T(8,128)S(1)} collective-permute-done((f32[2,32,2048]{2,1,0:T(8,128)S(1)}, f32[2,32,2048]{2,1,0:T(8,128)S(1)}, u32[]{:S(2)}, u32[]{:S(2)}) %collective-permute-start.24) | collective-permute-done | bytes 524320 | tf_op jit(solution)/shard_map/ppermute | solution.py:354
  119.0 6.7 %shard_map.43 = (f32[2,32,1024]{2,1,0:T(8,128)S(1)}, f32[2,32,1024]{2,1,0:T(8,128)S(1)}, f32[2,32,1024]{2,1,0:T(8,128)S(1)}, f32[2,32,1024]{2,1,0:T(8,128)S(1)}, f32[512,128]{1,0:T(8,128)}, /*index=5*/f32[1,512]{1,0:T(1,128)}) custom-call(s32[2]{0:T(128)S(1)} %pad_add_fusion.1.refs_0_, f32[512,128]{1,0:T(8,128)S(1)} %get-tuple-element.119.refs_1_, ...), custom_call_target="tpu_custom_call" | custom-call | flops 1 | bytes 1 | tf_op jit(solution)/shard_map/pallas_call | solution.py:321
  126.1 2.9 %collective-permute-start.30 = (f32[2,32,1024]{2,1,0:T(8,128)S(1)}, f32[2,32,1024]{2,1,0:T(8,128)S(1)}, u32[]{:S(2)}, u32[]{:S(2)}) collective-permute-start(f32[2,32,1024]{2,1,0:T(8,128)S(1)} %get-tuple-element.133), channel_id=1, source_target_pairs={{0,2},{1,3},{2,0},{3,1},{4,6},{5,7},{6,4},{7,5},{8,10},{9,11},{10,... | collective-permute-start | bytes 786440 | tf_op jit(solution)/shard_map/ppermute | solution.py:354
  131.0 5.1 %collective-permute-done.29 = f32[2,32,1024]{2,1,0:T(8,128)} collective-permute-done((f32[2,32,1024]{2,1,0:T(8,128)S(1)}, f32[2,32,1024]{2,1,0:T(8,128)}, u32[]{:S(2)}, u32[]{:S(2)}) %collective-permute-start.29) | collective-permute-done | bytes 262176 | tf_op jit(solution)/shard_map/ppermute | solution.py:354
  141.8 11.4 %collective-permute-done.34 = f32[2,32,2048]{2,1,0:T(8,128)S(1)} collective-permute-done((f32[2,32,2048]{2,1,0:T(8,128)S(1)}, f32[2,32,2048]{2,1,0:T(8,128)S(1)}, u32[]{:S(2)}, u32[]{:S(2)}) %collective-permute-start.34) | collective-permute-done | bytes 524320 | tf_op jit(solution)/shard_map/ppermute | solution.py:413
  153.9 7.3 %collective-permute-done.35 = f32[32,2048]{1,0:T(8,128)S(1)} collective-permute-done((f32[32,2048]{1,0:T(8,128)S(1)}, f32[32,2048]{1,0:T(8,128)S(1)}, u32[]{:S(2)}, u32[]{:S(2)}) %collective-permute-start.35) | collective-permute-done | bytes 262176 | tf_op jit(solution)/shard_map/ppermute | solution.py:345
  161.3 31.7 %while.20 = (s32[]{:T(128)}, f32[1,4096]{1,0:T(1,128)S(1)}, s32[]{:T(128)}, f32[2,32,2048]{2,1,0:T(8,128)S(1)}, s32[3,32]{1,0:T(4,128)S(1)}, /*index=5*/s32[]{:T(128)}) while((s32[]{:T(128)}, f32[1,4096]{1,0:T(1,128)S(1)}, s32[]{:T(128)}, f32[2,32,2048]{2,1,0:T(8,128)S(1)}, s32[3,32]{1,0:T(4,128)S(1)}, /*index=5*/s32[]{:T(128)}) %tuple.80), condition=%wide.region_1.2_spmd, body=%wide.region_0.1_spmd.sunk | while | flops 229378 | bytes 1982813 | solution.py:425
  163.9 3.9 %collective-permute-done.1 = f32[2,4096]{1,0:T(2,128)S(1)} collective-permute-done((f32[2,4096]{1,0:T(2,128)S(1)}, f32[2,4096]{1,0:T(2,128)S(1)}, u32[]{:S(2)}, u32[]{:S(2)}) %collective-permute-start.1) | collective-permute-done | bytes 32800 | tf_op jit(solution)/shard_map/while/body/ppermute | solution.py:231
  168.6 4.8 %collective-permute-done.2 = f32[2,4096]{1,0:T(2,128)S(1)} collective-permute-done((f32[2,4096]{1,0:T(2,128)S(1)}, f32[2,4096]{1,0:T(2,128)S(1)}, u32[]{:S(2)}, u32[]{:S(2)}) %collective-permute-start.2) | collective-permute-done | bytes 32800 | tf_op jit(solution)/shard_map/while/body/ppermute | solution.py:231
  173.6 5.4 %collective-permute-done.3 = f32[2,4096]{1,0:T(2,128)S(1)} collective-permute-done((f32[2,4096]{1,0:T(2,128)S(1)}, f32[2,4096]{1,0:T(2,128)S(1)}, u32[]{:S(2)}, u32[]{:S(2)}) %collective-permute-start.3) | collective-permute-done | bytes 32800 | tf_op jit(solution)/shard_map/while/body/ppermute | solution.py:231
  179.7 3.5 %collective-permute-done.4 = f32[2,4096]{1,0:T(2,128)S(1)} collective-permute-done((f32[2,4096]{1,0:T(2,128)S(1)}, f32[2,4096]{1,0:T(2,128)S(1)}, u32[]{:S(2)}, u32[]{:S(2)}) %collective-permute-start.4) | collective-permute-done | bytes 32800 | tf_op jit(solution)/shard_map/while/body/ppermute | solution.py:231
  187.4 2.8 %collective-permute-start.6 = (f32[2,4096]{1,0:T(2,128)S(1)}, f32[2,4096]{1,0:T(2,128)S(1)}, u32[]{:S(2)}, u32[]{:S(2)}) collective-permute-start(f32[2,4096]{1,0:T(2,128)S(1)} %pad_maximum_fusion.20), channel_id=1, source_target_pairs={{0,2},{1,3},{2,0},{3,1},{4,6},{5,7},{6,4},{7,5},{8,10},{9,11},{10,... | collective-permute-start | bytes 98312 | tf_op jit(solution)/shard_map/while/body/ppermute | solution.py:231
  194.3 6.0 %collective-permute-done.36 = bf16[2,32,2048]{2,1,0:T(8,128)(2,1)S(1)} collective-permute-done((bf16[2,32,2048]{2,1,0:T(8,128)(2,1)S(1)}, bf16[2,32,2048]{2,1,0:T(8,128)(2,1)S(1)}, u32[]{:S(2)}, u32[]{:S(2)}) %collective-permute-start.36) | collective-permute-done | bytes 262176 | tf_op jit(solution)/shard_map/ppermute | solution.py:428
  200.3 3.4 %collective-permute-start.37 = (bf16[2,2,32,2048]{3,2,1,0:T(8,128)(2,1)S(1)}, bf16[2,2,32,2048]{3,2,1,0:T(8,128)(2,1)S(1)}, u32[]{:S(2)}, u32[]{:S(2)}) collective-permute-start(bf16[2,2,32,2048]{3,2,1,0:T(8,128)(2,1)S(1)} %pad_maximum_fusion.8.refs_0_), channel_id=1, source_target_pairs={{0,3},{1,0},{2,1},{3,2},{4,7},{5,4},{6,5},{7,6},{8,11},{9,8},{10,9... | collective-permute-start | bytes 1572872 | tf_op jit(solution)/shard_map/ppermute | solution.py:354
  205.2 31.1 %while.21 = (s32[]{:T(128)}, f32[1,4096]{1,0:T(1,128)S(1)}, s32[]{:T(128)}, bf16[2,32,2048]{2,1,0:T(8,128)(2,1)S(1)}, s32[3,32]{1,0:T(4,128)S(1)}, /*index=5*/s32[]{:T(128)}) while((s32[]{:T(128)}, f32[1,4096]{1,0:T(1,128)S(1)}, s32[]{:T(128)}, bf16[2,32,2048]{2,1,0:T(8,128)(2,1)S(1)}, s32[3,32]{1,0:T(4,128)S(1)}, /*index=5*/s32[]{:T(128)}) %tuple.88), condition=%wide.region_3.4_spmd, body=%wide.region_2.3_spmd.sunk | while | flops 32770 | bytes 803165 | solution.py:437
  207.4 4.0 %collective-permute-done.8 = f32[1,4096]{1,0:T(1,128)S(1)} collective-permute-done((f32[1,4096]{1,0:T(1,128)S(1)}, f32[1,4096]{1,0:T(1,128)S(1)}, u32[]{:S(2)}, u32[]{:S(2)}) %collective-permute-start.8) | collective-permute-done | bytes 16416 | tf_op jit(solution)/shard_map/while/body/ppermute | solution.py:224
  212.3 4.9 %collective-permute-done.9 = f32[1,4096]{1,0:T(1,128)S(1)} collective-permute-done((f32[1,4096]{1,0:T(1,128)S(1)}, f32[1,4096]{1,0:T(1,128)S(1)}, u32[]{:S(2)}, u32[]{:S(2)}) %collective-permute-start.9) | collective-permute-done | bytes 16416 | tf_op jit(solution)/shard_map/while/body/ppermute | solution.py:224
  217.5 5.0 %collective-permute-done.10 = f32[1,4096]{1,0:T(1,128)S(1)} collective-permute-done((f32[1,4096]{1,0:T(1,128)S(1)}, f32[1,4096]{1,0:T(1,128)S(1)}, u32[]{:S(2)}, u32[]{:S(2)}) %collective-permute-start.10) | collective-permute-done | bytes 16416 | tf_op jit(solution)/shard_map/while/body/ppermute | solution.py:224
  223.1 3.3 %collective-permute-done.11 = f32[1,4096]{1,0:T(1,128)S(1)} collective-permute-done((f32[1,4096]{1,0:T(1,128)S(1)}, f32[1,4096]{1,0:T(1,128)S(1)}, u32[]{:S(2)}, u32[]{:S(2)}) %collective-permute-start.11) | collective-permute-done | bytes 16416 | tf_op jit(solution)/shard_map/while/body/ppermute | solution.py:224
  232.3 3.8 %collective-permute-done.13 = f32[1,4096]{1,0:T(1,128)S(1)} collective-permute-done((f32[1,4096]{1,0:T(1,128)S(1)}, f32[1,4096]{1,0:T(1,128)S(1)}, u32[]{:S(2)}, u32[]{:S(2)}) %collective-permute-start.13) | collective-permute-done | bytes 16416 | tf_op jit(solution)/shard_map/while/body/ppermute | solution.py:224
  240.0 3.7 %collective-permute-done.41 = f32[1,4096]{1,0:T(1,128)S(1)} collective-permute-done((f32[1,4096]{1,0:T(1,128)S(1)}, f32[1,4096]{1,0:T(1,128)S(1)}, u32[]{:S(2)}, u32[]{:S(2)}) %collective-permute-start.41) | collective-permute-done | bytes 16416 | tf_op jit(solution)/shard_map/ppermute | solution.py:224
  244.7 4.4 %collective-permute-done.42 = f32[1,4096]{1,0:T(1,128)S(1)} collective-permute-done((f32[1,4096]{1,0:T(1,128)S(1)}, f32[1,4096]{1,0:T(1,128)S(1)}, u32[]{:S(2)}, u32[]{:S(2)}) %collective-permute-start.42) | collective-permute-done | bytes 16416 | tf_op jit(solution)/shard_map/ppermute | solution.py:224
  249.7 4.8 %collective-permute-done.43 = f32[1,4096]{1,0:T(1,128)S(1)} collective-permute-done((f32[1,4096]{1,0:T(1,128)S(1)}, f32[1,4096]{1,0:T(1,128)S(1)}, u32[]{:S(2)}, u32[]{:S(2)}) %collective-permute-start.43) | collective-permute-done | bytes 16416 | tf_op jit(solution)/shard_map/ppermute | solution.py:224
  255.1 17.1 %shard_map.46 = bf16[256,4096]{1,0:T(8,128)(2,1)} custom-call(s32[3,32]{1,0:T(4,128)S(1)} %get-tuple-element.382, bf16[2,2,32,2048]{3,2,1,0:T(8,128)(2,1)S(1)} %pad_maximum_fusion.8.refs_0_, bf16[2,2,32,2048]{3,2,1,0:T(8,128)(2,1)S(1)} %collective-permute-done.37.refs_1_, bf16[2,2,32,2048]{3,2,1,0:T(8,128)(2,1)} %collective-permute-done.38.refs_2_, ...), custom_call_target="tpu_custom_call" | custom-call | tf_op jit(solution)/shard_map/pallas_call | solution.py:169
  (129 shorter events, 58.4 us)
Async XLA Ops:
  7.2 247.9 %all-gather.2.cloned.1.call-start = ((), (), s32[]{:S(2)}) async-start(), calls=%async_computation | async-start | bytes 18874368 | tf_op jit(solution)/shard_map/all_gather | solution.py:416
  7.2 49.1 %collective-permute-start.14 = (bf16[256,4096]{1,0:T(8,128)(2,1)}, bf16[256,4096]{1,0:T(8,128)(2,1)}, u32[]{:S(2)}, u32[]{:S(2)}) collective-permute-start(bf16[256,4096]{1,0:T(8,128)(2,1)} %refs_5_.1), channel_id=1, source_target_pairs={{0,16},{16,32},{32,48},{48,0},{1,17},{17,33},{33,49},{49,1},{2,18}... | collective-permute-start | bytes 6291464 | tf_op jit(solution)/shard_map/ppermute | solution.py:341
  8.9 47.4 %collective-permute-start.15 = (bf16[256,4096]{1,0:T(8,128)(2,1)}, bf16[256,4096]{1,0:T(8,128)(2,1)}, u32[]{:S(2)}, u32[]{:S(2)}) collective-permute-start(bf16[256,4096]{1,0:T(8,128)(2,1)} %refs_5_.1), channel_id=1, source_target_pairs={{0,48},{16,0},{32,16},{48,32},{1,49},{17,1},{33,17},{49,33},{2,50}... | collective-permute-start | bytes 6291464 | tf_op jit(solution)/shard_map/ppermute | solution.py:341
  10.5 49.5 %collective-permute-start.16 = (bf16[256,4096]{1,0:T(8,128)(2,1)}, bf16[256,4096]{1,0:T(8,128)(2,1)}, u32[]{:S(2)}, u32[]{:S(2)}) collective-permute-start(bf16[256,4096]{1,0:T(8,128)(2,1)} %refs_3_.5), channel_id=1, source_target_pairs={{0,64},{64,0},{1,65},{65,1},{2,66},{66,2},{3,67},{67,3},{4,68},{68... | collective-permute-start | bytes 6291464 | tf_op jit(solution)/shard_map/ppermute | solution.py:345
  14.5 45.5 %collective-permute-start.17 = (bf16[256,4096]{1,0:T(8,128)(2,1)}, bf16[256,4096]{1,0:T(8,128)(2,1)}, u32[]{:S(2)}, u32[]{:S(2)}) collective-permute-start(bf16[256,4096]{1,0:T(8,128)(2,1)} %refs_5_.1), channel_id=1, source_target_pairs={{0,8},{8,0},{1,9},{9,1},{2,10},{10,2},{3,11},{11,3},{4,12},{12,4},... | collective-permute-start | bytes 6291464 | tf_op jit(solution)/shard_map/ppermute | solution.py:345
  64.6 19.1 %collective-permute-start.18 = (bf16[256,4096]{1,0:T(8,128)(2,1)}, bf16[256,4096]{1,0:T(8,128)(2,1)}, u32[]{:S(2)}, u32[]{:S(2)}) collective-permute-start(bf16[256,4096]{1,0:T(8,128)(2,1)} %collective-permute-done.14.refs_7_), channel_id=1, source_target_pairs={{0,8},{8,0},{1,9},{9,1},{2,10},{10,2},{3,11},{11,3},{4,12},{12,4},... | collective-permute-start | bytes 6291464 | tf_op jit(solution)/shard_map/ppermute | solution.py:345
  64.6 19.1 %collective-permute-start.19 = (bf16[256,4096]{1,0:T(8,128)(2,1)}, bf16[256,4096]{1,0:T(8,128)(2,1)}, u32[]{:S(2)}, u32[]{:S(2)}) collective-permute-start(bf16[256,4096]{1,0:T(8,128)(2,1)} %collective-permute-done.15.refs_8_), channel_id=1, source_target_pairs={{0,8},{8,0},{1,9},{9,1},{2,10},{10,2},{3,11},{11,3},{4,12},{12,4},... | collective-permute-start | bytes 6291464 | tf_op jit(solution)/shard_map/ppermute | solution.py:345
  65.1 29.1 %collective-permute-start.20 = (bf16[128,4096]{1,0:T(8,128)(2,1)}, bf16[128,4096]{1,0:T(8,128)(2,1)S(1)}, u32[]{:S(2)}, u32[]{:S(2)}) collective-permute-start(bf16[128,4096]{1,0:T(8,128)(2,1)} %slice.128), channel_id=1, source_target_pairs={{0,16},{16,32},{32,48},{48,0},{1,17},{17,33},{33,49},{49,1},{2,18}... | collective-permute-start | bytes 3145736 | tf_op jit(solution)/shard_map/ppermute | solution.py:341
  65.3 28.8 %collective-permute-start.21 = (bf16[128,4096]{1,0:T(8,128)(2,1)}, bf16[128,4096]{1,0:T(8,128)(2,1)}, u32[]{:S(2)}, u32[]{:S(2)}) collective-permute-start(bf16[128,4096]{1,0:T(8,128)(2,1)} %slice.129), channel_id=1, source_target_pairs={{0,48},{16,0},{32,16},{48,32},{1,49},{17,1},{33,17},{49,33},{2,50}... | collective-permute-start | bytes 3145736 | tf_op jit(solution)/shard_map/ppermute | solution.py:341
  68.3 57.7 %collective-permute-start.32 = (bf16[256,4096]{1,0:T(8,128)(2,1)}, bf16[256,4096]{1,0:T(8,128)(2,1)}, u32[]{:S(2)}, u32[]{:S(2)}) collective-permute-start(bf16[256,4096]{1,0:T(8,128)(2,1)} %refs_5_.1), channel_id=1, source_target_pairs={{0,64},{64,0},{1,65},{65,1},{2,66},{66,2},{3,67},{67,3},{4,68},{68... | collective-permute-start | bytes 6291464 | tf_op jit(solution)/shard_map/ppermute | solution.py:345
  83.8 14.3 %collective-permute-start.22 = (f32[2,32,2048]{2,1,0:T(8,128)S(1)}, f32[2,32,2048]{2,1,0:T(8,128)S(1)}, u32[]{:S(2)}, u32[]{:S(2)}) collective-permute-start(f32[2,32,2048]{2,1,0:T(8,128)S(1)} %get-tuple-element.117), channel_id=1, source_target_pairs={{0,1},{1,2},{2,3},{3,0},{4,5},{5,6},{6,7},{7,4},{8,9},{9,10},{10,1... | collective-permute-start | bytes 1572872 | tf_op jit(solution)/shard_map/ppermute | solution.py:354
  85.3 12.7 %collective-permute-start.23 = (f32[2,32,2048]{2,1,0:T(8,128)S(1)}, f32[2,32,2048]{2,1,0:T(8,128)S(1)}, u32[]{:S(2)}, u32[]{:S(2)}) collective-permute-start(f32[2,32,2048]{2,1,0:T(8,128)S(1)} %get-tuple-element.118), channel_id=1, source_target_pairs={{0,3},{1,0},{2,1},{3,2},{4,7},{5,4},{6,5},{7,6},{8,11},{9,8},{10,9... | collective-permute-start | bytes 1572872 | tf_op jit(solution)/shard_map/ppermute | solution.py:354
  98.0 19.2 %collective-permute-start.27 = (bf16[128,4096]{1,0:T(8,128)(2,1)S(1)}, bf16[128,4096]{1,0:T(8,128)(2,1)S(1)}, u32[]{:S(2)}, u32[]{:S(2)}) collective-permute-start(bf16[128,4096]{1,0:T(8,128)(2,1)S(1)} %collective-permute-done.20.refs_5_.refs_11_), channel_id=1, source_target_pairs={{0,8},{8,0},{1,9},{9,1},{2,10},{10,2},{3,11},{11,3},{4,12},{12,4},... | collective-permute-start | bytes 3145736 | tf_op jit(solution)/shard_map/ppermute | solution.py:345
  98.0 21.0 %collective-permute-start.28 = (bf16[128,4096]{1,0:T(8,128)(2,1)}, bf16[128,4096]{1,0:T(8,128)(2,1)S(1)}, u32[]{:S(2)}, u32[]{:S(2)}) collective-permute-start(bf16[128,4096]{1,0:T(8,128)(2,1)} %collective-permute-done.21.refs_6_.refs_12_), channel_id=1, source_target_pairs={{0,8},{8,0},{1,9},{9,1},{2,10},{10,2},{3,11},{11,3},{4,12},{12,4},... | collective-permute-start | bytes 3145736 | tf_op jit(solution)/shard_map/ppermute | solution.py:345
  98.5 16.3 %collective-permute-start.24 = (f32[2,32,2048]{2,1,0:T(8,128)S(1)}, f32[2,32,2048]{2,1,0:T(8,128)S(1)}, u32[]{:S(2)}, u32[]{:S(2)}) collective-permute-start(f32[2,32,2048]{2,1,0:T(8,128)S(1)} %get-tuple-element.125), channel_id=1, source_target_pairs={{0,2},{1,3},{2,0},{3,1},{4,6},{5,7},{6,4},{7,5},{8,10},{9,11},{10,... | collective-permute-start | bytes 1572872 | tf_op jit(solution)/shard_map/ppermute | solution.py:354
  101.3 27.7 %collective-permute-start.26 = (f32[2,32,1024]{2,1,0:T(8,128)}, f32[2,32,1024]{2,1,0:T(8,128)}, u32[]{:S(2)}, u32[]{:S(2)}) collective-permute-start(f32[2,32,1024]{2,1,0:T(8,128)} %get-tuple-element.129), channel_id=1, source_target_pairs={{0,2},{1,3},{2,0},{3,1},{4,6},{5,7},{6,4},{7,5},{8,10},{9,11},{10,... | collective-permute-start | bytes 786440 | tf_op jit(solution)/shard_map/ppermute | solution.py:354
  115.8 23.4 %collective-permute-start.25 = (f32[2,32,1024]{2,1,0:T(8,128)}, f32[2,32,1024]{2,1,0:T(8,128)}, u32[]{:S(2)}, u32[]{:S(2)}) collective-permute-start(f32[2,32,1024]{2,1,0:T(8,128)} %get-tuple-element.128), channel_id=1, source_target_pairs={{0,1},{1,2},{2,3},{3,0},{4,5},{5,6},{6,7},{7,4},{8,9},{9,10},{10,1... | collective-permute-start | bytes 786440 | tf_op jit(solution)/shard_map/ppermute | solution.py:354
  117.3 21.9 %collective-permute-start.33 = (f32[2,32,1024]{2,1,0:T(8,128)}, f32[2,32,1024]{2,1,0:T(8,128)}, u32[]{:S(2)}, u32[]{:S(2)}) collective-permute-start(f32[2,32,1024]{2,1,0:T(8,128)} %get-tuple-element.136), channel_id=1, source_target_pairs={{0,3},{1,0},{2,1},{3,2},{4,7},{5,4},{6,5},{7,6},{8,11},{9,8},{10,9... | collective-permute-start | bytes 786440 | tf_op jit(solution)/shard_map/ppermute | solution.py:354
  125.8 10.4 %collective-permute-start.29 = (f32[2,32,1024]{2,1,0:T(8,128)S(1)}, f32[2,32,1024]{2,1,0:T(8,128)}, u32[]{:S(2)}, u32[]{:S(2)}) collective-permute-start(f32[2,32,1024]{2,1,0:T(8,128)S(1)} %get-tuple-element.132), channel_id=1, source_target_pairs={{0,1},{1,2},{2,3},{3,0},{4,5},{5,6},{6,7},{7,4},{8,9},{9,10},{10,1... | collective-permute-start | bytes 786440 | tf_op jit(solution)/shard_map/ppermute | solution.py:354
  126.1 12.5 %collective-permute-start.30 = (f32[2,32,1024]{2,1,0:T(8,128)S(1)}, f32[2,32,1024]{2,1,0:T(8,128)S(1)}, u32[]{:S(2)}, u32[]{:S(2)}) collective-permute-start(f32[2,32,1024]{2,1,0:T(8,128)S(1)} %get-tuple-element.133), channel_id=1, source_target_pairs={{0,2},{1,3},{2,0},{3,1},{4,6},{5,7},{6,4},{7,5},{8,10},{9,11},{10,... | collective-permute-start | bytes 786440 | tf_op jit(solution)/shard_map/ppermute | solution.py:354
  129.0 10.2 %collective-permute-start.31 = (f32[2,32,1024]{2,1,0:T(8,128)S(1)}, f32[2,32,1024]{2,1,0:T(8,128)S(1)}, u32[]{:S(2)}, u32[]{:S(2)}) collective-permute-start(f32[2,32,1024]{2,1,0:T(8,128)S(1)} %get-tuple-element.134), channel_id=1, source_target_pairs={{0,3},{1,0},{2,1},{3,2},{4,7},{5,4},{6,5},{7,6},{8,11},{9,8},{10,9... | collective-permute-start | bytes 786440 | tf_op jit(solution)/shard_map/ppermute | solution.py:354
  140.7 12.5 %collective-permute-start.34 = (f32[2,32,2048]{2,1,0:T(8,128)S(1)}, f32[2,32,2048]{2,1,0:T(8,128)S(1)}, u32[]{:S(2)}, u32[]{:S(2)}) collective-permute-start(f32[2,32,2048]{2,1,0:T(8,128)S(1)} %pad_maximum_fusion.6), channel_id=1, source_target_pairs={{0,4},{4,0},{1,5},{5,1},{2,6},{6,2},{3,7},{7,3},{8,12},{12,8},{9,1... | collective-permute-start | bytes 1572872 | tf_op jit(solution)/shard_map/ppermute | solution.py:413
  153.3 8.0 %collective-permute-start.35 = (f32[32,2048]{1,0:T(8,128)S(1)}, f32[32,2048]{1,0:T(8,128)S(1)}, u32[]{:S(2)}, u32[]{:S(2)}) collective-permute-start(f32[32,2048]{1,0:T(8,128)S(1)} %get-tuple-element.181), channel_id=1, source_target_pairs={{0,64},{64,0},{1,65},{65,1},{2,66},{66,2},{3,67},{67,3},{4,68},{68... | collective-permute-start | bytes 786440 | tf_op jit(solution)/shard_map/ppermute | solution.py:345
  167.9 5.5 %collective-permute-start.2 = (f32[2,4096]{1,0:T(2,128)S(1)}, f32[2,4096]{1,0:T(2,128)S(1)}, u32[]{:S(2)}, u32[]{:S(2)}) collective-permute-start(f32[2,4096]{1,0:T(2,128)S(1)} %pad_maximum_fusion.16), channel_id=1, source_target_pairs={{0,32},{16,48},{32,0},{48,16},{1,33},{17,49},{33,1},{49,17},{2,34}... | collective-permute-start | bytes 98312 | tf_op jit(solution)/shard_map/while/body/ppermute | solution.py:231
  173.6 5.5 %collective-permute-start.3 = (f32[2,4096]{1,0:T(2,128)S(1)}, f32[2,4096]{1,0:T(2,128)S(1)}, u32[]{:S(2)}, u32[]{:S(2)}) collective-permute-start(f32[2,4096]{1,0:T(2,128)S(1)} %pad_maximum_fusion.17), channel_id=1, source_target_pairs={{0,64},{64,0},{1,65},{65,1},{2,66},{66,2},{3,67},{67,3},{4,68},{68... | collective-permute-start | bytes 98312 | tf_op jit(solution)/shard_map/while/body/ppermute | solution.py:231
  187.4 5.5 %collective-permute-start.6 = (f32[2,4096]{1,0:T(2,128)S(1)}, f32[2,4096]{1,0:T(2,128)S(1)}, u32[]{:S(2)}, u32[]{:S(2)}) collective-permute-start(f32[2,4096]{1,0:T(2,128)S(1)} %pad_maximum_fusion.20), channel_id=1, source_target_pairs={{0,2},{1,3},{2,0},{3,1},{4,6},{5,7},{6,4},{7,5},{8,10},{9,11},{10,... | collective-permute-start | bytes 98312 | tf_op jit(solution)/shard_map/while/body/ppermute | solution.py:231
  193.8 6.5 %collective-permute-start.36 = (bf16[2,32,2048]{2,1,0:T(8,128)(2,1)S(1)}, bf16[2,32,2048]{2,1,0:T(8,128)(2,1)S(1)}, u32[]{:S(2)}, u32[]{:S(2)}) collective-permute-start(bf16[2,32,2048]{2,1,0:T(8,128)(2,1)S(1)} %shard_map.44), channel_id=1, source_target_pairs={{0,4},{4,0},{1,5},{5,1},{2,6},{6,2},{3,7},{7,3},{8,12},{12,8},{9,1... | collective-permute-start | bytes 786440 | tf_op jit(solution)/shard_map/ppermute | solution.py:428
  200.3 36.0 %collective-permute-start.37 = (bf16[2,2,32,2048]{3,2,1,0:T(8,128)(2,1)S(1)}, bf16[2,2,32,2048]{3,2,1,0:T(8,128)(2,1)S(1)}, u32[]{:S(2)}, u32[]{:S(2)}) collective-permute-start(bf16[2,2,32,2048]{3,2,1,0:T(8,128)(2,1)S(1)} %pad_maximum_fusion.8.refs_0_), channel_id=1, source_target_pairs={{0,3},{1,0},{2,1},{3,2},{4,7},{5,4},{6,5},{7,6},{8,11},{9,8},{10,9... | collective-permute-start | bytes 1572872 | tf_op jit(solution)/shard_map/ppermute | solution.py:354
  203.7 32.7 %collective-permute-start.38 = (bf16[2,2,32,2048]{3,2,1,0:T(8,128)(2,1)S(1)}, bf16[2,2,32,2048]{3,2,1,0:T(8,128)(2,1)}, u32[]{:S(2)}, u32[]{:S(2)}) collective-permute-start(bf16[2,2,32,2048]{3,2,1,0:T(8,128)(2,1)S(1)} %pad_maximum_fusion.8.refs_0_), channel_id=1, source_target_pairs={{0,1},{1,2},{2,3},{3,0},{4,5},{5,6},{6,7},{7,4},{8,9},{9,10},{10,1... | collective-permute-start | bytes 1572872 | tf_op jit(solution)/shard_map/ppermute | solution.py:354
  203.7 32.7 %collective-permute-start.39 = (bf16[2,2,32,2048]{3,2,1,0:T(8,128)(2,1)S(1)}, bf16[2,2,32,2048]{3,2,1,0:T(8,128)(2,1)}, u32[]{:S(2)}, u32[]{:S(2)}) collective-permute-start(bf16[2,2,32,2048]{3,2,1,0:T(8,128)(2,1)S(1)} %pad_maximum_fusion.8.refs_0_), channel_id=1, source_target_pairs={{0,2},{1,3},{2,0},{3,1},{4,6},{5,7},{6,4},{7,5},{8,10},{9,11},{10,... | collective-permute-start | bytes 1572872 | tf_op jit(solution)/shard_map/ppermute | solution.py:354
  211.5 5.7 %collective-permute-start.9 = (f32[1,4096]{1,0:T(1,128)S(1)}, f32[1,4096]{1,0:T(1,128)S(1)}, u32[]{:S(2)}, u32[]{:S(2)}) collective-permute-start(f32[1,4096]{1,0:T(1,128)S(1)} %add.871), channel_id=1, source_target_pairs={{0,32},{16,48},{32,0},{48,16},{1,33},{17,49},{33,1},{49,17},{2,34}... | collective-permute-start | bytes 49160 | tf_op jit(solution)/shard_map/while/body/ppermute | solution.py:224
  217.2 5.3 %collective-permute-start.10 = (f32[1,4096]{1,0:T(1,128)S(1)}, f32[1,4096]{1,0:T(1,128)S(1)}, u32[]{:S(2)}, u32[]{:S(2)}) collective-permute-start(f32[1,4096]{1,0:T(1,128)S(1)} %add.872), channel_id=1, source_target_pairs={{0,64},{64,0},{1,65},{65,1},{2,66},{66,2},{3,67},{67,3},{4,68},{68... | collective-permute-start | bytes 49160 | tf_op jit(solution)/shard_map/while/body/ppermute | solution.py:224
  (15 other events, 119.3 us)
Sparse Core Ops, SparseCore 0:
  161.4 81.8 all-gather.1

commit v6 on v5

--- a/solution.py
+++ b/solution.py
@@ -96,16 +96,17 @@
 
 def exponentials_kernel(shapes, where, *refs):
     logits, (c_ref, out_ref, peak_ref, _) = refs[:len(shapes)], refs[len(shapes):]
-    tiles = tile_list(shapes)
-    acc = None
-    for t, (k, g, n) in enumerate(tiles):
-        x = logits[k][0, g, :, n:n + LANES] + c_ref[:, lanes(where[0, t])]
-        acc = x if acc is None else jnp.maximum(acc, x)
-    peak_ref[...] = jnp.broadcast_to(jnp.max(acc, axis=1, keepdims=True), peak_ref.shape)
-    top = peak_ref[...]
-    for t, (k, g, n) in enumerate(tiles):
-        x = logits[k][0, g, :, n:n + LANES] + c_ref[:, lanes(where[0, t])]
-        out_ref[g, :, n:n + LANES] = jnp.exp(x - top).astype(jnp.bfloat16)
+    tiles = tile_list(shapes[:1])
+    for k, ref in enumerate(logits):
+        acc = None
+        for t, (_, g, n) in enumerate(tiles):
+            x = ref[0, g, :, n:n + LANES] + c_ref[:, lanes(where[0, t])]
+            acc = x if acc is None else jnp.maximum(acc, x)
+        peak_ref[...] = jnp.broadcast_to(jnp.max(acc, axis=1, keepdims=True), peak_ref.shape)
+        top = peak_ref[...]
+        for t, (_, g, n) in enumerate(tiles):
+            x = ref[0, g, :, n:n + LANES] + c_ref[:, lanes(where[0, t])]
+            out_ref[k, g, :, n:n + LANES] = jnp.exp(x - top).astype(jnp.bfloat16)
 
 
 def scaled_rows(tiles, kernels, where, v_ref, row_ref):
@@ -209,26 +210,42 @@
     )(where, *logits, c)
 
 
-def combine(a, b):
-    peak = jnp.maximum(a[0], b[0])
-    total = a[1] * jnp.exp(a[0] - peak) + b[1] * jnp.exp(b[0] - peak)
-    return jnp.stack([peak, total])
-
-
-SAMP_STEPS = (("core", 2, 1), ("y", 4, 1), ("y", 4, 2), ("zh", 2, 1))
-FEAT_STEPS = (("zl", 2, 1), ("x", 4, 1), ("x", 4, 2))
-
-
-def column_sum(x, steps):
+SAMP_RINGS = (("core", 2), ("y", 4), ("zh", 2))
+ALL_RINGS = (("core", 2), ("y", 4), (("zh", "zl"), 4), ("x", 4))
+
+
+def around(x, axis, n):
+    def shift(k):
+        return lax.ppermute(x, axis, [(i, (i + k) % n) for i in range(n)])
+
+    if n == 2:
+        return [(x, shift(1))]
+    left, right, across = shift(1), shift(-1), shift(2)
+    return [(x, across), (left, right)]
+
+
+def combine(pairs):
+    peak = functools.reduce(jnp.maximum, [p[0] for pair in pairs for p in pair])
+    totals = [sum(p[1] * jnp.exp(p[0] - peak) for p in pair) for pair in pairs]
+    return jnp.stack([peak, sum(totals)])
+
+
+def column_sum(x, rings):
+    for axis, n in rings:
+        x = sum(a + b for a, b in around(x, axis, n))
+    return x
+
+
+def column_sum_in_pairs(x):
+    steps = (("core", 2, 1), ("y", 4, 1), ("y", 4, 2), ("zh", 2, 1), ("zl", 2, 1), ("x", 4, 1), ("x", 4, 2))
     for axis, n, step in steps:
         x = x + lax.ppermute(x, axis, [(i, i ^ step) for i in range(n)])
     return x
 
 
-def column_update(stats, steps):
-    for axis, n, step in steps:
-        pairs = [(i, i ^ step) for i in range(n)]
-        stats = combine(stats, lax.ppermute(stats, axis, pairs))
+def column_update(stats, rings):
+    for axis, n in rings:
+        stats = combine(around(stats, axis, n))
     return -(stats[0] + jnp.log(stats[1]))[None, :]
 
 
@@ -337,6 +354,24 @@
     return pieces, n_sq, x_row
 
 
+def halves_kernel(u_ref, w_ref, a_ref, b_ref):
+    a_ref[...] = u_ref[...]
+    b_ref[...] = w_ref[...]
+
+
+def halves_call(u, w):
+    half, block = u.shape[0] // 2, 2048
+    out = jax.ShapeDtypeStruct((half, u.shape[1]), u.dtype)
+    return pl.pallas_call(
+        halves_kernel,
+        cost_estimate=pl.CostEstimate(flops=1, bytes_accessed=1, transcendentals=0),
+        out_shape=[out, out],
+        grid=(u.shape[1] // block,),
+        in_specs=[pl.BlockSpec((half, block), lambda n: (0, n)), pl.BlockSpec((half, block), lambda n: (1, n))],
+        out_specs=[pl.BlockSpec((half, block), lambda n: (0, n))] * 2,
+    )(u, w)
+
+
 def ring(x, shift):
     return lax.ppermute(x, "y", [(i, (i + shift) % 4) for i in range(4)])
 
@@ -381,15 +416,18 @@
     u, w = ring(data, 1), ring(data, -1)
     far = swap(noise, "zh")
     data_c = swap(data, "core")
-    u, w, far, data_c, data = hold((u, w, far, data_c, data))
-
-    ua, wb = u[:half], w[half:]
+    (k0, k1, k3, k2), n_sq, x_row = call(here, [(noise,)], [data, data_c], (((0,), (0, 1)),))
+    k1, k3, k2 = along_x(k1, 1), along_x(k3, -1), along_x(k2, 2)
+    u, w, far, data_c, data, k0, k1, k2, k3 = hold((u, w, far, data_c, data, k0, k1, k2, k3))
+
+    ua, wb = halves_call(u, w)
     ua, wb, u, w, data = hold((ua, wb, u, w, data))
     u3, w3 = ring(ua, 1), ring(wb, -1)
     u_c, w_c = swap(u, "core"), swap(w, "core")
     other = swap(data, "zh")
     noises = [(noise,), (far,)]
-    (a0, a1, a3, a2), n_sq, _ = call(here, noises, [data, data_c, u, w], (((0, 1), (0, 1, 2, 3)),))
+    jobs = (((0, 1), (2, 3)), ((1,), (0, 1)))
+    (a0, a1, a3, a2), n_sq, _ = call(here, noises, [data, data_c, u, w], jobs, n_sq, x_row)
     u_c, w_c, a0, a1, a2, a3 = hold((u_c, w_c, a0, a1, a2, a3))
     a1, a3 = along_x(a1, 1), along_x(a3, -1)
     (b0, b1, b3, b2), _, _ = call(here, noises, [u_c, w_c], (((0, 1), (0, 1)),), n_sq)
@@ -401,43 +439,54 @@
     (c0, c1, c3, c2), _, _ = call(here, noises, [u3, w3, u3_c, w3_c], (((0, 1), (0, 1, 2, 3)),), n_sq)
     b2 = along_x(b2, 2)
     c1, c3, c2 = along_x(c1, 1), along_x(c3, -1), along_x(c2, 2)
+    k, a = k0 + k1 + k2 + k3, a0 + a1 + a2 + a3
+
+    def early(z):
+        return jnp.stack([
+            jnp.concatenate([k[z], a[z][:, :512]], axis=1),
+            jnp.concatenate([a[z][:, 1024:], a[z][:, 512:1024]], axis=1),
+        ])
+
     b2, c1, c2, c3, other = hold((b2, c1, c2, c3, other))
-    a, b, c = a0 + a1 + a2 + a3, b0 + b1 + b2 + b3, c0 + c1 + c2 + c3
-
-    def halves(z):
+    b, c = b0 + b1 + b2 + b3, c0 + c1 + c2 + c3
+
+    def late(z):
         return jnp.stack([
-            jnp.concatenate([p[z][:, i * n:(i + 1) * n] for p, n in ((a, 1024), (b, 512), (c, 512))], axis=1)
-            for i in range(2)
+            jnp.concatenate([p[z][:, i * 512:(i + 1) * 512] for p in (b, c)], axis=1) for i in range(2)
         ])
 
-    own = halves(0) + lax.ppermute(halves(1), "zl", [(0, 1), (1, 0)])
-    own = jnp.stack([own[0], swap(own[1], "zh")])
+    def across_z(x, step):
+        return lax.ppermute(x, ("zh", "zl"), [(i, i ^ step) for i in range(4)])
+
+    mine, theirs = (jnp.concatenate([early(z), late(z)], axis=2) for z in range(2))
+    own = jnp.stack([
+        mine[0] + across_z(theirs[0], 1), across_z(mine[1], 2) + across_z(theirs[1], 3)
+    ])
     own, other = hold((own, other))
     others = lax.all_gather(other, ("y", "core"), axis=0, tiled=True)
     out = jax.ShapeDtypeStruct((2, SAMPLES), jnp.float32)
 
-    steps = SAMP_STEPS + FEAT_STEPS
     once = lax.axis_index("x") // 8 + 1
 
     def spread(_, c):
-        return column_update(row_call(sinkhorn_kernel, out, where, [own[None]], c), steps)
-
+        return column_update(row_call(sinkhorn_kernel, out, where, [own[None]], c), ALL_RINGS)
+
+    pair = lax.ppermute(own, "zl", [(0, 1), (1, 0)])
     c = lax.fori_loop(0, once, spread, jnp.zeros((1, SAMPLES), jnp.float32))
-    shape = jax.ShapeDtypeStruct(own.shape, jnp.bfloat16)
-    mine = row_call(exponentials_kernel, shape, where, [own[None]], c)
-    both = jnp.stack([mine, lax.ppermute(mine, "zl", [(0, 1), (1, 0)])])
-    mine, both = hold((mine, both))
+    c, pair = hold((c, pair))
+    shape = jax.ShapeDtypeStruct((2,) + own.shape, jnp.bfloat16)
+    both = row_call(exponentials_kernel, shape, where, [own[None], pair[None]], c)
     kernels = [both] + [along_x(both, -d) for d in ALONG_X[1:]]
 
     sums = jax.ShapeDtypeStruct((1, SAMPLES), jnp.float32)
 
     def balance(_, v):
-        return 1.0 / column_sum(balance_call(balance_kernel, sums, where, [mine[None]], v), steps)
+        return 1.0 / column_sum_in_pairs(balance_call(balance_kernel, sums, where, [both[:1]], v))
 
     v = lax.fori_loop(0, once, balance, jnp.ones((1, SAMPLES), jnp.float32))
     blocks = [data, data_c, u, w, u_c, w_c, u3, w3, u3_c, w3_c]
     for _ in range(2, ITERS):
-        v = 1.0 / column_sum(balance_call(balance_kernel, sums, where, kernels, v), SAMP_STEPS)
+        v = 1.0 / column_sum(balance_call(balance_kernel, sums, where, kernels, v), SAMP_RINGS)
     c = c + jnp.log(v)
     share = SAMPLES // parts
     start = (lax.axis_index("zl") * 4 + lax.axis_index("x")) * share

time: 280 us -> 263 us (0.939)
  waiting for transfers between devices: 157 us -> 96 us
  starting transfers between devices: 48.9 us -> 78.9 us
  Pallas kernels: 47.9 us -> 54.2 us
  local copies, waits for them, and re-layouts: 6.15 us -> 10.2 us
    ppermute x20 -> x26, waiting for transfers between devices: 79.4 us -> 47.2 us  [the longest x7 19.5 us: column_sum_in_pairs(): x = x + lax.ppermute(x, axis, [(i, i ^ step) for i in range(n)])]
    ppermute x20 -> x26, starting transfers between devices: 14.9 us -> 36.9 us  [the longest x15 21.5 us: shift(): return lax.ppermute(x, axis, [(i, (i + k) % n) for i in range(n)])]
    ppermute x12 -> x15, waiting for transfers between devices: 24.8 us -> 10.7 us  [along_x(): return lax.ppermute(x, 'x', [(i, (i + step) % 4) for i in range(4)])]
    ppermute x8 -> x7, waiting for transfers between devices: 11 us -> 2.95 us  [swap(): return lax.ppermute(x, axis, [(0, 1), (1, 0)])]
    unnamed x4 -> x30, local copies, waits for them, and re-layouts: 0.01 us -> 7.35 us
    ppermute x12 -> x15, starting transfers between devices: 19.1 us -> 26.3 us  [along_x(): return lax.ppermute(x, 'x', [(i, (i + step) % 4) for i in range(4)])]
    ppermute x4, waiting for transfers between devices: 41.9 us -> 35 us  [ring(): return lax.ppermute(x, 'y', [(i, (i + shift) % 4) for i in range(4)])]
    another operation x13 -> x14, other arithmetic: 0.41 us -> 3.69 us  [the longest x4 2.66 us: early(): jnp.stack([jnp.concatenate([k[z], a[z][:, :512]], axis=1), jnp.concatenat...]
  transfers between devices with their start and end apart: 45 -> 53, of which waited for: 28 -> 33; matrix products, arithmetic and copies ran while one was open for 1% -> 3% of each run, Pallas kernels for 11% -> 13%
where the time goes in v6:
time: 263 us; the launch traced here: 261 us
  waiting for transfers between devices  96 us (37%)
  starting transfers between devices  78.9 us (30%)
  Pallas kernels  54.2 us (21%)
  between operations  14.6 us (6%)
  local copies, waits for them, and re-layouts  10.2 us (4%)
  other arithmetic  6.62 us (3%)
    ppermute x4, waiting for transfers between devices, ring(): return lax.ppermute(x, 'y', [(i, (i + shift) % 4) for i in range(4)])  35 us
    pallas_call x4, Pallas kernels, partial_call(): pl.pallas_call(functools.partial(partial_kernel, noise_parts, jobs, known...  27.3 us
    ppermute x15, starting transfers between devices, along_x(): return lax.ppermute(x, 'x', [(i, (i + step) % 4) for i in range(4)])  26.3 us
    ppermute x15, starting transfers between devices, shift(): return lax.ppermute(x, axis, [(i, (i + k) % n) for i in range(n)])  21.5 us
    ppermute x7, waiting for transfers between devices, column_sum_in_pairs(): x = x + lax.ppermute(x, axis, [(i, i ^ step) for i in range(n)])  19.5 us
    ppermute x15, waiting for transfers between devices, shift(): return lax.ppermute(x, axis, [(i, (i + k) % n) for i in range(n)])  17.9 us
    pallas_call x1, Pallas kernels, targets_call(): pl.pallas_call(functools.partial(targets_kernel, shapes, widths), out_sha...  17.1 us
    ppermute x15, waiting for transfers between devices, along_x(): return lax.ppermute(x, 'x', [(i, (i + step) % 4) for i in range(4)])  10.7 us
  transfers between devices with their start and end apart: 53, of which 33 were waited for; matrix products, arithmetic and copies ran while one was open for 3% of the time, Pallas kernels for 13%

profile of v6, /device:TPU:0, one launch (start us, length us, event | category | flops | bytes accessed | tf_op | source)
XLA Modules:
  0.0 260.9 jit_solution(8081825316418097904)
XLA Ops:
  10.6 4.0 %collective-permute-start.19 = (bf16[256,4096]{1,0:T(8,128)(2,1)}, bf16[256,4096]{1,0:T(8,128)(2,1)S(1)}, u32[]{:S(2)}, u32[]{:S(2)}) collective-permute-start(bf16[256,4096]{1,0:T(8,128)(2,1)} %refs_3_.7), channel_id=1, source_target_pairs={{0,64},{64,0},{1,65},{65,1},{2,66},{66,2},{3,67},{67,3},{4,68},{68... | collective-permute-start | bytes 6291464 | tf_op jit(solution)/shard_map/ppermute | solution.py:380
  17.8 4.8 %shard_map.41 = (f32[2,32,512]{2,1,0:T(8,128)S(1)}, f32[2,32,512]{2,1,0:T(8,128)S(1)}, f32[2,32,512]{2,1,0:T(8,128)S(1)}, f32[2,32,512]{2,1,0:T(8,128)S(1)}, f32...) custom-call(s32[2]{0:T(128)S(1)} %pad_add_fusion.1.refs_0_, f32[8,128]{1,0:T(8,128)S(1)} %broadcast_in_dim.16.refs_1_, ...), custom_call_target="tpu_custom_call" | custom-call | flops 1 | bytes 1 | tf_op jit(solution)/shard_map/pallas_call | solution.py:338
  24.2 2.7 %collective-permute-start.22 = (f32[2,32,512]{2,1,0:T(8,128)S(1)}, f32[2,32,512]{2,1,0:T(8,128)S(1)}, u32[]{:S(2)}, u32[]{:S(2)}) collective-permute-start(f32[2,32,512]{2,1,0:T(8,128)S(1)} %get-tuple-element.116), channel_id=1, source_target_pairs={{0,2},{1,3},{2,0},{3,1},{4,6},{5,7},{6,4},{7,5},{8,10},{9,11},{10,... | collective-permute-start | bytes 393224 | tf_op jit(solution)/shard_map/ppermute | solution.py:389
  27.0 30.0 %collective-permute-done.17.u_ref.refs_7_ = bf16[256,4096]{1,0:T(8,128)(2,1)} collective-permute-done((bf16[256,4096]{1,0:T(8,128)(2,1)}, bf16[256,4096]{1,0:T(8,128)(2,1)}, u32[]{:S(2)}, u32[]{:S(2)}) %collective-permute-start.17) | collective-permute-done | bytes 2097184 | tf_op jit(solution)/shard_map/ppermute | solution.py:376
  57.0 2.8 %collective-permute-start.23 = (f32[2,32,512]{2,1,0:T(8,128)S(1)}, f32[2,32,512]{2,1,0:T(8,128)S(1)}, u32[]{:S(2)}, u32[]{:S(2)}) collective-permute-start(f32[2,32,512]{2,1,0:T(8,128)S(1)} %get-tuple-element.117), channel_id=1, source_target_pairs={{0,3},{1,0},{2,1},{3,2},{4,7},{5,4},{6,5},{7,6},{8,11},{9,8},{10,9... | collective-permute-start | bytes 393224 | tf_op jit(solution)/shard_map/ppermute | solution.py:389
  62.4 2.8 %shard_map.42 = (bf16[128,4096]{1,0:T(8,128)(2,1)}, bf16[128,4096]{1,0:T(8,128)(2,1)}) custom-call(bf16[256,4096]{1,0:T(8,128)(2,1)} %collective-permute-done.17.u_ref.refs_7_, bf16[256,4096]{1,0:T(8,128)(2,1)} %collective-permute-done.18.w_ref.refs_8_), custom_call_target="tpu_custom_call" | custom-call | flops 1 | bytes 1 | tf_op jit(solution)/shard_map/pallas_call | solution.py:365
  66.0 3.0 %collective-permute-start.27 = (bf16[128,4096]{1,0:T(8,128)(2,1)}, bf16[128,4096]{1,0:T(8,128)(2,1)S(1)}, u32[]{:S(2)}, u32[]{:S(2)}) collective-permute-start(bf16[128,4096]{1,0:T(8,128)(2,1)} %get-tuple-element.140), channel_id=1, source_target_pairs={{0,48},{16,0},{32,16},{48,32},{1,49},{17,1},{33,17},{49,33},{2,50}... | collective-permute-start | bytes 3145736 | tf_op jit(solution)/shard_map/ppermute | solution.py:376
  69.0 3.9 %collective-permute-start.38 = (bf16[256,4096]{1,0:T(8,128)(2,1)}, bf16[256,4096]{1,0:T(8,128)(2,1)}, u32[]{:S(2)}, u32[]{:S(2)}) collective-permute-start(bf16[256,4096]{1,0:T(8,128)(2,1)} %refs_5_.1), channel_id=1, source_target_pairs={{0,64},{64,0},{1,65},{65,1},{2,66},{66,2},{3,67},{67,3},{4,68},{68... | collective-permute-start | bytes 6291464 | tf_op jit(solution)/shard_map/ppermute | solution.py:380
  74.5 9.0 %shard_map.43 = (f32[2,32,1536]{2,1,0:T(8,128)S(1)}, f32[2,32,1536]{2,1,0:T(8,128)S(1)}, f32[2,32,1536]{2,1,0:T(8,128)S(1)}, f32[2,32,1536]{2,1,0:T(8,128)S(1)},...) custom-call(s32[2]{0:T(128)S(1)} %pad_add_fusion.1.refs_0_, f32[256,128]{1,0:T(8,128)S(1)} %get-tuple-element.129.refs_1_, ...), custom_call_target="tpu_custom_call" | custom-call | flops 1 | bytes 1 | tf_op jit(solution)/shard_map/pallas_call | solution.py:338
  87.4 5.0 %collective-permute-done.26.refs_5_.refs_11_ = bf16[128,4096]{1,0:T(8,128)(2,1)S(1)} collective-permute-done((bf16[128,4096]{1,0:T(8,128)(2,1)}, bf16[128,4096]{1,0:T(8,128)(2,1)S(1)}, u32[]{:S(2)}, u32[]{:S(2)}) %collective-permute-start.26) | collective-permute-done | bytes 1048608 | tf_op jit(solution)/shard_map/ppermute | solution.py:376
  92.4 2.7 %collective-permute-start.30 = (f32[2,32,1536]{2,1,0:T(8,128)S(1)}, f32[2,32,1536]{2,1,0:T(8,128)S(1)}, u32[]{:S(2)}, u32[]{:S(2)}) collective-permute-start(f32[2,32,1536]{2,1,0:T(8,128)S(1)} %get-tuple-element.149), channel_id=1, source_target_pairs={{0,2},{1,3},{2,0},{3,1},{4,6},{5,7},{6,4},{7,5},{8,10},{9,11},{10,... | collective-permute-start | bytes 1179656 | tf_op jit(solution)/shard_map/ppermute | solution.py:389
  95.8 6.9 %shard_map.44 = (f32[2,32,1024]{2,1,0:T(8,128)S(1)}, f32[2,32,1024]{2,1,0:T(8,128)}, f32[2,32,1024]{2,1,0:T(8,128)}, f32[2,32,1024]{2,1,0:T(8,128)}, f32[512,128]{1,0:T(8,128)}, /*index=5*/f32[1,512]{1,0:T(1,128)}) custom-call(s32[2]{0:T(128)S(1)} %pad_add_fusion.1.refs_0_, f32[512,128]{1,0:T(8,128)S(1)} %get-tuple-element.143.refs_1_, ...), custom_call_target="tpu_custom_call" | custom-call | flops 1 | bytes 1 | tf_op jit(solution)/shard_map/pallas_call | solution.py:338
  109.6 6.6 %shard_map.45 = (f32[2,32,1024]{2,1,0:T(8,128)S(1)}, f32[2,32,1024]{2,1,0:T(8,128)S(1)}, f32[2,32,1024]{2,1,0:T(8,128)S(1)}, f32[2,32,1024]{2,1,0:T(8,128)S(1)}, f32[512,128]{1,0:T(8,128)}, /*index=5*/f32[1,512]{1,0:T(1,128)}) custom-call(s32[2]{0:T(128)S(1)} %pad_add_fusion.1.refs_0_, f32[512,128]{1,0:T(8,128)S(1)} %get-tuple-element.143.refs_1_, ...), custom_call_target="tpu_custom_call" | custom-call | flops 1 | bytes 1 | tf_op jit(solution)/shard_map/pallas_call | solution.py:338
  118.5 2.7 %collective-permute-start.36 = (f32[2,32,1024]{2,1,0:T(8,128)S(1)}, f32[2,32,1024]{2,1,0:T(8,128)S(1)}, u32[]{:S(2)}, u32[]{:S(2)}) collective-permute-start(f32[2,32,1024]{2,1,0:T(8,128)S(1)} %get-tuple-element.157), channel_id=1, source_target_pairs={{0,2},{1,3},{2,0},{3,1},{4,6},{5,7},{6,4},{7,5},{8,10},{9,11},{10,... | collective-permute-start | bytes 786440 | tf_op jit(solution)/shard_map/ppermute | solution.py:389
  126.3 3.9 %collective-permute-done.36 = f32[2,32,1024]{2,1,0:T(8,128)S(1)} collective-permute-done((f32[2,32,1024]{2,1,0:T(8,128)S(1)}, f32[2,32,1024]{2,1,0:T(8,128)S(1)}, u32[]{:S(2)}, u32[]{:S(2)}) %collective-permute-start.36) | collective-permute-done | bytes 262176 | tf_op jit(solution)/shard_map/ppermute | solution.py:389
  130.2 3.7 %collective-permute-done.37 = f32[2,32,1024]{2,1,0:T(8,128)S(1)} collective-permute-done((f32[2,32,1024]{2,1,0:T(8,128)S(1)}, f32[2,32,1024]{2,1,0:T(8,128)S(1)}, u32[]{:S(2)}, u32[]{:S(2)}) %collective-permute-start.37) | collective-permute-done | bytes 262176 | tf_op jit(solution)/shard_map/ppermute | solution.py:389
  136.5 2.6 collective-permute-start.42
  140.4 4.4 %collective-permute-done.40 = f32[32,2048]{1,0:T(8,128)S(1)} collective-permute-done((f32[32,2048]{1,0:T(8,128)S(1)}, f32[32,2048]{1,0:T(8,128)S(1)}, u32[]{:S(2)}, u32[]{:S(2)}) %collective-permute-start.40) | collective-permute-done | bytes 262176 | tf_op jit(solution)/shard_map/ppermute | solution.py:459
  144.8 3.7 %collective-permute-done.42 = f32[32,2048]{1,0:T(8,128)S(1)} collective-permute-done((f32[32,2048]{1,0:T(8,128)S(1)}, f32[32,2048]{1,0:T(8,128)S(1)}, u32[]{:S(2)}, u32[]{:S(2)}) %collective-permute-start.42) | collective-permute-done | bytes 262176 | tf_op jit(solution)/shard_map/ppermute | solution.py:459
  151.8 28.3 %while.20 = (s32[]{:T(128)}, f32[1,4096]{1,0:T(1,128)S(1)}, s32[]{:T(128)}, f32[2,32,2048]{2,1,0:T(8,128)}, s32[3,32]{1,0:T(4,128)S(1)}, /*index=5*/s32[]{:T(128)}) while((s32[]{:T(128)}, f32[1,4096]{1,0:T(1,128)S(1)}, s32[]{:T(128)}, f32[2,32,2048]{2,1,0:T(8,128)}, s32[3,32]{1,0:T(4,128)S(1)}, /*index=5*/s32[]{:T(128)}) %tuple.75), condition=%wide.region_1.2_spmd, body=%wide.region_0.1_spmd.sunk | while | flops 229378 | bytes 2081237 | solution.py:475
  165.1 3.1 %collective-permute-start.6 = (f32[2,4096]{1,0:T(2,128)S(1)}, f32[2,4096]{1,0:T(2,128)S(1)}, u32[]{:S(2)}, u32[]{:S(2)}) collective-permute-start(f32[2,4096]{1,0:T(2,128)S(1)} %pad_maximum_fusion.8), channel_id=1, source_target_pairs={{0,64},{4,68},{64,0},{68,4},{1,65},{5,69},{65,1},{69,5},{2,66},{6,... | collective-permute-start | bytes 98312 | tf_op jit(solution)/shard_map/while/body/ppermute | solution.py:219
  170.7 3.8 %collective-permute-start.7 = (f32[2,4096]{1,0:T(2,128)S(1)}, f32[2,4096]{1,0:T(2,128)S(1)}, u32[]{:S(2)}, u32[]{:S(2)}) collective-permute-start(f32[2,4096]{1,0:T(2,128)S(1)} %pad_maximum_fusion.9), channel_id=1, source_target_pairs={{0,3},{1,0},{2,1},{3,2},{4,7},{5,4},{6,5},{7,6},{8,11},{9,8},{10,9... | collective-permute-start | bytes 98312 | tf_op jit(solution)/shard_map/while/body/ppermute | solution.py:219
  176.1 3.5 %collective-permute-done.8 = f32[2,4096]{1,0:T(2,128)S(1)} collective-permute-done((f32[2,4096]{1,0:T(2,128)S(1)}, f32[2,4096]{1,0:T(2,128)S(1)}, u32[]{:S(2)}, u32[]{:S(2)}) %collective-permute-start.8) | collective-permute-done | bytes 32800 | tf_op jit(solution)/shard_map/while/body/ppermute | solution.py:219
  182.3 3.2 %collective-permute-start.44 = (bf16[2,2,32,2048]{3,2,1,0:T(8,128)(2,1)}, bf16[2,2,32,2048]{3,2,1,0:T(8,128)(2,1)}, u32[]{:S(2)}, u32[]{:S(2)}) collective-permute-start(bf16[2,2,32,2048]{3,2,1,0:T(8,128)(2,1)} %shard_map.46.refs_0_), channel_id=1, source_target_pairs={{0,3},{1,0},{2,1},{3,2},{4,7},{5,4},{6,5},{7,6},{8,11},{9,8},{10,9... | collective-permute-start | bytes 1572872 | tf_op jit(solution)/shard_map/ppermute | solution.py:389
  187.0 31.9 %while.21 = (s32[]{:T(128)}, f32[1,4096]{1,0:T(1,128)S(1)}, s32[]{:T(128)}, bf16[2,2,32,2048]{3,2,1,0:T(8,128)(2,1)}, s32[3,32]{1,0:T(4,128)S(1)}, /*index=5*/s32[]{:T(128)}) while((s32[]{:T(128)}, f32[1,4096]{1,0:T(1,128)S(1)}, s32[]{:T(128)}, bf16[2,2,32,2048]{3,2,1,0:T(8,128)(2,1)}, s32[3,32]{1,0:T(4,128)S(1)}, /*index=5*/s32[]{:T(128)}) %tuple.83), condition=%wide.region_3.4_spmd, body=%wide.region_2.3_spmd.sunk | while | flops 32770 | bytes 1327453 | solution.py:486
  190.1 4.0 %collective-permute-done.11 = f32[1,4096]{1,0:T(1,128)S(1)} collective-permute-done((f32[1,4096]{1,0:T(1,128)S(1)}, f32[1,4096]{1,0:T(1,128)S(1)}, u32[]{:S(2)}, u32[]{:S(2)}) %collective-permute-start.11) | collective-permute-done | bytes 16416 | tf_op jit(solution)/shard_map/while/body/ppermute | solution.py:242
  195.4 4.4 %collective-permute-done.12 = f32[1,4096]{1,0:T(1,128)S(1)} collective-permute-done((f32[1,4096]{1,0:T(1,128)S(1)}, f32[1,4096]{1,0:T(1,128)S(1)}, u32[]{:S(2)}, u32[]{:S(2)}) %collective-permute-start.12) | collective-permute-done | bytes 16416 | tf_op jit(solution)/shard_map/while/body/ppermute | solution.py:242
  199.9 3.1 %collective-permute-start.13 = (f32[1,4096]{1,0:T(1,128)S(1)}, f32[1,4096]{1,0:T(1,128)S(1)}, u32[]{:S(2)}, u32[]{:S(2)}) collective-permute-start(f32[1,4096]{1,0:T(1,128)S(1)} %add.929), channel_id=1, source_target_pairs={{0,64},{64,0},{1,65},{65,1},{2,66},{66,2},{3,67},{67,3},{4,68},{68... | collective-permute-start | bytes 49160 | tf_op jit(solution)/shard_map/while/body/ppermute | solution.py:242
  209.0 2.7 %collective-permute-start.15 = (f32[1,4096]{1,0:T(1,128)S(1)}, f32[1,4096]{1,0:T(1,128)S(1)}, u32[]{:S(2)}, u32[]{:S(2)}) collective-permute-start(f32[1,4096]{1,0:T(1,128)S(1)} %add.931), channel_id=1, source_target_pairs={{0,1},{1,0},{2,3},{3,2},{4,5},{5,4},{6,7},{7,6},{8,9},{9,8},{10,11... | collective-permute-start | bytes 49160 | tf_op jit(solution)/shard_map/while/body/ppermute | solution.py:242
  215.1 3.8 %collective-permute-done.16 = f32[1,4096]{1,0:T(1,128)S(1)} collective-permute-done((f32[1,4096]{1,0:T(1,128)S(1)}, f32[1,4096]{1,0:T(1,128)S(1)}, u32[]{:S(2)}, u32[]{:S(2)}) %collective-permute-start.16) | collective-permute-done | bytes 16416 | tf_op jit(solution)/shard_map/while/body/ppermute | solution.py:242
  229.5 3.4 %collective-permute-start.51 = (f32[1,4096]{1,0:T(1,128)S(1)}, f32[1,4096]{1,0:T(1,128)S(1)}, u32[]{:S(2)}, u32[]{:S(2)}) collective-permute-start(f32[1,4096]{1,0:T(1,128)S(1)} %add_add_fusion.4), channel_id=1, source_target_pairs={{0,64},{64,0},{1,65},{65,1},{2,66},{66,2},{3,67},{67,3},{4,68},{68... | collective-permute-start | bytes 49160 | tf_op jit(solution)/shard_map/ppermute | solution.py:219
  237.0 17.1 %shard_map.48 = bf16[256,4096]{1,0:T(8,128)(2,1)} custom-call(s32[3,32]{1,0:T(4,128)S(1)} %get-tuple-element.401, bf16[2,2,32,2048]{3,2,1,0:T(8,128)(2,1)} %shard_map.46.refs_0_, bf16[2,2,32,2048]{3,2,1,0:T(8,128)(2,1)} %collective-permute-done.44.refs_1_, bf16[2,2,32,2048]{3,2,1,0:T(8,128)(2,1)} %collective-permute-done.45.refs_2_, ...), custom_call_target="tpu_custom_call" | custom-call | tf_op jit(solution)/shard_map/pallas_call | solution.py:170
  (173 shorter events, 88.7 us)
Async XLA Ops:
  7.2 228.6 %all-gather.2.cloned.1.call-start = ((), (), s32[]{:S(2)}) async-start(), calls=%async_computation | async-start | bytes 18874368 | tf_op jit(solution)/shard_map/all_gather | solution.py:466
  7.2 7.4 %collective-permute-start.20 = (bf16[256,4096]{1,0:T(8,128)(2,1)}, bf16[256,4096]{1,0:T(8,128)(2,1)}, u32[]{:S(2)}, u32[]{:S(2)}) collective-permute-start(bf16[256,4096]{1,0:T(8,128)(2,1)} %refs_5_.1), channel_id=1, source_target_pairs={{0,8},{8,0},{1,9},{9,1},{2,10},{10,2},{3,11},{11,3},{4,12},{12,4},... | collective-permute-start | bytes 6291464 | tf_op jit(solution)/shard_map/ppermute | solution.py:380
  7.3 49.7 %collective-permute-start.17 = (bf16[256,4096]{1,0:T(8,128)(2,1)}, bf16[256,4096]{1,0:T(8,128)(2,1)}, u32[]{:S(2)}, u32[]{:S(2)}) collective-permute-start(bf16[256,4096]{1,0:T(8,128)(2,1)} %refs_5_.1), channel_id=1, source_target_pairs={{0,16},{16,32},{32,48},{48,0},{1,17},{17,33},{33,49},{49,1},{2,18}... | collective-permute-start | bytes 6291464 | tf_op jit(solution)/shard_map/ppermute | solution.py:376
  9.0 50.7 %collective-permute-start.18 = (bf16[256,4096]{1,0:T(8,128)(2,1)}, bf16[256,4096]{1,0:T(8,128)(2,1)}, u32[]{:S(2)}, u32[]{:S(2)}) collective-permute-start(bf16[256,4096]{1,0:T(8,128)(2,1)} %refs_5_.1), channel_id=1, source_target_pairs={{0,48},{16,0},{32,16},{48,32},{1,49},{17,1},{33,17},{49,33},{2,50}... | collective-permute-start | bytes 6291464 | tf_op jit(solution)/shard_map/ppermute | solution.py:376
  10.6 49.9 %collective-permute-start.19 = (bf16[256,4096]{1,0:T(8,128)(2,1)}, bf16[256,4096]{1,0:T(8,128)(2,1)S(1)}, u32[]{:S(2)}, u32[]{:S(2)}) collective-permute-start(bf16[256,4096]{1,0:T(8,128)(2,1)} %refs_3_.7), channel_id=1, source_target_pairs={{0,64},{64,0},{1,65},{65,1},{2,66},{66,2},{3,67},{67,3},{4,68},{68... | collective-permute-start | bytes 6291464 | tf_op jit(solution)/shard_map/ppermute | solution.py:380
  22.7 39.1 %collective-permute-start.21 = (f32[2,32,512]{2,1,0:T(8,128)S(1)}, f32[2,32,512]{2,1,0:T(8,128)S(1)}, u32[]{:S(2)}, u32[]{:S(2)}) collective-permute-start(f32[2,32,512]{2,1,0:T(8,128)S(1)} %get-tuple-element.115), channel_id=1, source_target_pairs={{0,1},{1,2},{2,3},{3,0},{4,5},{5,6},{6,7},{7,4},{8,9},{9,10},{10,1... | collective-permute-start | bytes 393224 | tf_op jit(solution)/shard_map/ppermute | solution.py:389
  24.2 37.6 %collective-permute-start.22 = (f32[2,32,512]{2,1,0:T(8,128)S(1)}, f32[2,32,512]{2,1,0:T(8,128)S(1)}, u32[]{:S(2)}, u32[]{:S(2)}) collective-permute-start(f32[2,32,512]{2,1,0:T(8,128)S(1)} %get-tuple-element.116), channel_id=1, source_target_pairs={{0,2},{1,3},{2,0},{3,1},{4,6},{5,7},{6,4},{7,5},{8,10},{9,11},{10,... | collective-permute-start | bytes 393224 | tf_op jit(solution)/shard_map/ppermute | solution.py:389
  65.2 18.3 %collective-permute-start.24 = (bf16[256,4096]{1,0:T(8,128)(2,1)}, bf16[256,4096]{1,0:T(8,128)(2,1)S(1)}, u32[]{:S(2)}, u32[]{:S(2)}) collective-permute-start(bf16[256,4096]{1,0:T(8,128)(2,1)} %collective-permute-done.17.u_ref.refs_7_), channel_id=1, source_target_pairs={{0,8},{8,0},{1,9},{9,1},{2,10},{10,2},{3,11},{11,3},{4,12},{12,4},... | collective-permute-start | bytes 6291464 | tf_op jit(solution)/shard_map/ppermute | solution.py:380
  65.3 18.2 %collective-permute-start.25 = (bf16[256,4096]{1,0:T(8,128)(2,1)}, bf16[256,4096]{1,0:T(8,128)(2,1)S(1)}, u32[]{:S(2)}, u32[]{:S(2)}) collective-permute-start(bf16[256,4096]{1,0:T(8,128)(2,1)} %collective-permute-done.18.w_ref.refs_8_), channel_id=1, source_target_pairs={{0,8},{8,0},{1,9},{9,1},{2,10},{10,2},{3,11},{11,3},{4,12},{12,4},... | collective-permute-start | bytes 6291464 | tf_op jit(solution)/shard_map/ppermute | solution.py:380
  65.8 26.6 %collective-permute-start.26 = (bf16[128,4096]{1,0:T(8,128)(2,1)}, bf16[128,4096]{1,0:T(8,128)(2,1)S(1)}, u32[]{:S(2)}, u32[]{:S(2)}) collective-permute-start(bf16[128,4096]{1,0:T(8,128)(2,1)} %get-tuple-element.139), channel_id=1, source_target_pairs={{0,16},{16,32},{32,48},{48,0},{1,17},{17,33},{33,49},{49,1},{2,18}... | collective-permute-start | bytes 3145736 | tf_op jit(solution)/shard_map/ppermute | solution.py:376
  66.0 36.6 %collective-permute-start.27 = (bf16[128,4096]{1,0:T(8,128)(2,1)}, bf16[128,4096]{1,0:T(8,128)(2,1)S(1)}, u32[]{:S(2)}, u32[]{:S(2)}) collective-permute-start(bf16[128,4096]{1,0:T(8,128)(2,1)} %get-tuple-element.140), channel_id=1, source_target_pairs={{0,48},{16,0},{32,16},{48,32},{1,49},{17,1},{33,17},{49,33},{2,50}... | collective-permute-start | bytes 3145736 | tf_op jit(solution)/shard_map/ppermute | solution.py:376
  69.0 49.5 %collective-permute-start.38 = (bf16[256,4096]{1,0:T(8,128)(2,1)}, bf16[256,4096]{1,0:T(8,128)(2,1)}, u32[]{:S(2)}, u32[]{:S(2)}) collective-permute-start(bf16[256,4096]{1,0:T(8,128)(2,1)} %refs_5_.1), channel_id=1, source_target_pairs={{0,64},{64,0},{1,65},{65,1},{2,66},{66,2},{3,67},{67,3},{4,68},{68... | collective-permute-start | bytes 6291464 | tf_op jit(solution)/shard_map/ppermute | solution.py:380
  83.5 19.1 %collective-permute-start.28 = (f32[2,32,1536]{2,1,0:T(8,128)S(1)}, f32[2,32,1536]{2,1,0:T(8,128)S(1)}, u32[]{:S(2)}, u32[]{:S(2)}) collective-permute-start(f32[2,32,1536]{2,1,0:T(8,128)S(1)} %get-tuple-element.141), channel_id=1, source_target_pairs={{0,1},{1,2},{2,3},{3,0},{4,5},{5,6},{6,7},{7,4},{8,9},{9,10},{10,1... | collective-permute-start | bytes 1179656 | tf_op jit(solution)/shard_map/ppermute | solution.py:389
  84.8 17.9 %collective-permute-start.29 = (f32[2,32,1536]{2,1,0:T(8,128)S(1)}, f32[2,32,1536]{2,1,0:T(8,128)S(1)}, u32[]{:S(2)}, u32[]{:S(2)}) collective-permute-start(f32[2,32,1536]{2,1,0:T(8,128)S(1)} %get-tuple-element.142), channel_id=1, source_target_pairs={{0,3},{1,0},{2,1},{3,2},{4,7},{5,4},{6,5},{7,6},{8,11},{9,8},{10,9... | collective-permute-start | bytes 1179656 | tf_op jit(solution)/shard_map/ppermute | solution.py:389
  92.4 13.1 %collective-permute-start.30 = (f32[2,32,1536]{2,1,0:T(8,128)S(1)}, f32[2,32,1536]{2,1,0:T(8,128)S(1)}, u32[]{:S(2)}, u32[]{:S(2)}) collective-permute-start(f32[2,32,1536]{2,1,0:T(8,128)S(1)} %get-tuple-element.149), channel_id=1, source_target_pairs={{0,2},{1,3},{2,0},{3,1},{4,6},{5,7},{6,4},{7,5},{8,10},{9,11},{10,... | collective-permute-start | bytes 1179656 | tf_op jit(solution)/shard_map/ppermute | solution.py:389
  102.8 6.8 %collective-permute-start.34 = (bf16[128,4096]{1,0:T(8,128)(2,1)S(1)}, bf16[128,4096]{1,0:T(8,128)(2,1)S(1)}, u32[]{:S(2)}, u32[]{:S(2)}) collective-permute-start(bf16[128,4096]{1,0:T(8,128)(2,1)S(1)} %collective-permute-done.27.refs_6_.refs_12_), channel_id=1, source_target_pairs={{0,8},{8,0},{1,9},{9,1},{2,10},{10,2},{3,11},{11,3},{4,12},{12,4},... | collective-permute-start | bytes 3145736 | tf_op jit(solution)/shard_map/ppermute | solution.py:380
  103.3 18.0 %collective-permute-start.32 = (f32[2,32,1024]{2,1,0:T(8,128)}, f32[2,32,1024]{2,1,0:T(8,128)}, u32[]{:S(2)}, u32[]{:S(2)}) collective-permute-start(f32[2,32,1024]{2,1,0:T(8,128)} %get-tuple-element.153), channel_id=1, source_target_pairs={{0,2},{1,3},{2,0},{3,1},{4,6},{5,7},{6,4},{7,5},{8,10},{9,11},{10,... | collective-permute-start | bytes 786440 | tf_op jit(solution)/shard_map/ppermute | solution.py:389
  106.3 27.6 %collective-permute-start.31 = (f32[2,32,1024]{2,1,0:T(8,128)}, f32[2,32,1024]{2,1,0:T(8,128)}, u32[]{:S(2)}, u32[]{:S(2)}) collective-permute-start(f32[2,32,1024]{2,1,0:T(8,128)} %get-tuple-element.152), channel_id=1, source_target_pairs={{0,1},{1,2},{2,3},{3,0},{4,5},{5,6},{6,7},{7,4},{8,9},{9,10},{10,1... | collective-permute-start | bytes 786440 | tf_op jit(solution)/shard_map/ppermute | solution.py:389
  107.5 26.4 %collective-permute-start.39 = (f32[2,32,1024]{2,1,0:T(8,128)}, f32[2,32,1024]{2,1,0:T(8,128)}, u32[]{:S(2)}, u32[]{:S(2)}) collective-permute-start(f32[2,32,1024]{2,1,0:T(8,128)} %get-tuple-element.160), channel_id=1, source_target_pairs={{0,3},{1,0},{2,1},{3,2},{4,7},{5,4},{6,5},{7,6},{8,11},{9,8},{10,9... | collective-permute-start | bytes 786440 | tf_op jit(solution)/shard_map/ppermute | solution.py:389
  116.2 10.1 %collective-permute-start.35 = (f32[2,32,1024]{2,1,0:T(8,128)S(1)}, f32[2,32,1024]{2,1,0:T(8,128)}, u32[]{:S(2)}, u32[]{:S(2)}) collective-permute-start(f32[2,32,1024]{2,1,0:T(8,128)S(1)} %get-tuple-element.156), channel_id=1, source_target_pairs={{0,1},{1,2},{2,3},{3,0},{4,5},{5,6},{6,7},{7,4},{8,9},{9,10},{10,1... | collective-permute-start | bytes 786440 | tf_op jit(solution)/shard_map/ppermute | solution.py:389
  118.5 11.7 %collective-permute-start.36 = (f32[2,32,1024]{2,1,0:T(8,128)S(1)}, f32[2,32,1024]{2,1,0:T(8,128)S(1)}, u32[]{:S(2)}, u32[]{:S(2)}) collective-permute-start(f32[2,32,1024]{2,1,0:T(8,128)S(1)} %get-tuple-element.157), channel_id=1, source_target_pairs={{0,2},{1,3},{2,0},{3,1},{4,6},{5,7},{6,4},{7,5},{8,10},{9,11},{10,... | collective-permute-start | bytes 786440 | tf_op jit(solution)/shard_map/ppermute | solution.py:389
  121.3 12.6 %collective-permute-start.37 = (f32[2,32,1024]{2,1,0:T(8,128)S(1)}, f32[2,32,1024]{2,1,0:T(8,128)S(1)}, u32[]{:S(2)}, u32[]{:S(2)}) collective-permute-start(f32[2,32,1024]{2,1,0:T(8,128)S(1)} %get-tuple-element.158), channel_id=1, source_target_pairs={{0,3},{1,0},{2,1},{3,2},{4,7},{5,4},{6,5},{7,6},{8,11},{9,8},{10,9... | collective-permute-start | bytes 786440 | tf_op jit(solution)/shard_map/ppermute | solution.py:389
  135.4 9.3 %collective-permute-start.40 = (f32[32,2048]{1,0:T(8,128)S(1)}, f32[32,2048]{1,0:T(8,128)S(1)}, u32[]{:S(2)}, u32[]{:S(2)}) collective-permute-start(f32[32,2048]{1,0:T(8,128)S(1)} %get-tuple-element.198), channel_id=1, source_target_pairs={{0,4},{4,0},{64,68},{68,64},{1,5},{5,1},{65,69},{69,65},{2,6},{6,2... | collective-permute-start | bytes 786440 | tf_op jit(solution)/shard_map/ppermute | solution.py:459
  136.5 12.0 %collective-permute-start.42 = (f32[32,2048]{1,0:T(8,128)S(1)}, f32[32,2048]{1,0:T(8,128)S(1)}, u32[]{:S(2)}, u32[]{:S(2)}) collective-permute-start(f32[32,2048]{1,0:T(8,128)S(1)} %get-tuple-element.199), channel_id=1, source_target_pairs={{0,68},{4,64},{64,4},{68,0},{1,69},{5,65},{65,5},{69,1},{2,70},{6,... | collective-permute-start | bytes 786440 | tf_op jit(solution)/shard_map/ppermute | solution.py:459
  139.2 11.0 %collective-permute-start.41 = (f32[32,2048]{1,0:T(8,128)S(1)}, f32[32,2048]{1,0:T(8,128)S(1)}, u32[]{:S(2)}, u32[]{:S(2)}) collective-permute-start(f32[32,2048]{1,0:T(8,128)S(1)} %slice_bitcast_fusion.1), channel_id=1, source_target_pairs={{0,64},{4,68},{64,0},{68,4},{1,65},{5,69},{65,1},{69,5},{2,66},{6,... | collective-permute-start | bytes 786440 | tf_op jit(solution)/shard_map/ppermute | solution.py:459
  151.6 28.5 %collective-permute-start.43 = (f32[2,32,2048]{2,1,0:T(8,128)}, f32[2,32,2048]{2,1,0:T(8,128)S(1)}, u32[]{:S(2)}, u32[]{:S(2)}) collective-permute-start(f32[2,32,2048]{2,1,0:T(8,128)} %pad_maximum_fusion.3), channel_id=1, source_target_pairs={{0,4},{4,0},{1,5},{5,1},{2,6},{6,2},{3,7},{7,3},{8,12},{12,8},{9,1... | collective-permute-start | bytes 1572872 | tf_op jit(solution)/shard_map/ppermute | solution.py:474
  182.3 36.6 %collective-permute-start.44 = (bf16[2,2,32,2048]{3,2,1,0:T(8,128)(2,1)}, bf16[2,2,32,2048]{3,2,1,0:T(8,128)(2,1)}, u32[]{:S(2)}, u32[]{:S(2)}) collective-permute-start(bf16[2,2,32,2048]{3,2,1,0:T(8,128)(2,1)} %shard_map.46.refs_0_), channel_id=1, source_target_pairs={{0,3},{1,0},{2,1},{3,2},{4,7},{5,4},{6,5},{7,6},{8,11},{9,8},{10,9... | collective-permute-start | bytes 1572872 | tf_op jit(solution)/shard_map/ppermute | solution.py:389
  185.5 33.4 %collective-permute-start.45 = (bf16[2,2,32,2048]{3,2,1,0:T(8,128)(2,1)}, bf16[2,2,32,2048]{3,2,1,0:T(8,128)(2,1)}, u32[]{:S(2)}, u32[]{:S(2)}) collective-permute-start(bf16[2,2,32,2048]{3,2,1,0:T(8,128)(2,1)} %shard_map.46.refs_0_), channel_id=1, source_target_pairs={{0,1},{1,2},{2,3},{3,0},{4,5},{5,6},{6,7},{7,4},{8,9},{9,10},{10,1... | collective-permute-start | bytes 1572872 | tf_op jit(solution)/shard_map/ppermute | solution.py:389
  185.5 33.4 %collective-permute-start.46 = (bf16[2,2,32,2048]{3,2,1,0:T(8,128)(2,1)}, bf16[2,2,32,2048]{3,2,1,0:T(8,128)(2,1)}, u32[]{:S(2)}, u32[]{:S(2)}) collective-permute-start(bf16[2,2,32,2048]{3,2,1,0:T(8,128)(2,1)} %shard_map.46.refs_0_), channel_id=1, source_target_pairs={{0,2},{1,3},{2,0},{3,1},{4,6},{5,7},{6,4},{7,5},{8,10},{9,11},{10,... | collective-permute-start | bytes 1572872 | tf_op jit(solution)/shard_map/ppermute | solution.py:389
  194.2 5.7 %collective-permute-start.12 = (f32[1,4096]{1,0:T(1,128)S(1)}, f32[1,4096]{1,0:T(1,128)S(1)}, u32[]{:S(2)}, u32[]{:S(2)}) collective-permute-start(f32[1,4096]{1,0:T(1,128)S(1)} %add.928), channel_id=1, source_target_pairs={{0,32},{16,48},{32,0},{48,16},{1,33},{17,49},{33,1},{49,17},{2,34}... | collective-permute-start | bytes 49160 | tf_op jit(solution)/shard_map/while/body/ppermute | solution.py:242
  222.8 5.7 %collective-permute-start.48 = (f32[1,4096]{1,0:T(1,128)S(1)}, f32[1,4096]{1,0:T(1,128)S(1)}, u32[]{:S(2)}, u32[]{:S(2)}) collective-permute-start(f32[1,4096]{1,0:T(1,128)S(1)} %add.826), channel_id=1, source_target_pairs={{0,32},{16,48},{32,0},{48,16},{1,33},{17,49},{33,1},{49,17},{2,34}... | collective-permute-start | bytes 49160 | tf_op jit(solution)/shard_map/ppermute | solution.py:219
  229.5 5.6 %collective-permute-start.51 = (f32[1,4096]{1,0:T(1,128)S(1)}, f32[1,4096]{1,0:T(1,128)S(1)}, u32[]{:S(2)}, u32[]{:S(2)}) collective-permute-start(f32[1,4096]{1,0:T(1,128)S(1)} %add_add_fusion.4), channel_id=1, source_target_pairs={{0,64},{64,0},{1,65},{65,1},{2,66},{66,2},{3,67},{67,3},{4,68},{68... | collective-permute-start | bytes 49160 | tf_op jit(solution)/shard_map/ppermute | solution.py:219
  (36 other events, 219.9 us)
Sparse Core Ops, SparseCore 0:
  151.2 84.5 all-gather.1

commit v7 on v6

--- a/solution.py
+++ b/solution.py
@@ -153,11 +153,10 @@
                     x = k_ref[z, g, :, n:n + LANES].astype(jnp.float32) * v_ref[:, lanes(where[0, t])]
                     w_ref[rows, lanes(where[1, t])] = (x * scale).astype(jnp.bfloat16)
 
-    first, acc = 0, None
-    for x, width in zip(x_refs, widths):
-        part = jnp.dot(w_ref[:, first:first + width], x[...], preferred_element_type=jnp.float32)
-        acc = part if acc is None else acc + part
-        first += width
+    most = jnp.concatenate([x[...] for x in x_refs[:-1]], axis=0)
+    first = sum(widths[:-1])
+    acc = jnp.dot(w_ref[:, :first], most, preferred_element_type=jnp.float32)
+    acc += jnp.dot(w_ref[:, first:], x_refs[-1][...], preferred_element_type=jnp.float32)
     out_ref[...] = acc.astype(out_ref.dtype)
 
 
@@ -237,7 +236,7 @@
 
 
 def column_sum_in_pairs(x):
-    steps = (("core", 2, 1), ("y", 4, 1), ("y", 4, 2), ("zh", 2, 1), ("zl", 2, 1), ("x", 4, 1), ("x", 4, 2))
+    steps = (("core", 2, 1), ("y", 4, 1), ("y", 4, 2), ("zh", 2, 1), ("x", 4, 1), ("x", 4, 2))
     for axis, n, step in steps:
         x = x + lax.ppermute(x, axis, [(i, i ^ step) for i in range(n)])
     return x
@@ -459,18 +458,23 @@
         return lax.ppermute(x, ("zh", "zl"), [(i, i ^ step) for i in range(4)])
 
     mine, theirs = (jnp.concatenate([early(z), late(z)], axis=2) for z in range(2))
-    own = jnp.stack([
-        mine[0] + across_z(theirs[0], 1), across_z(mine[1], 2) + across_z(theirs[1], 3)
-    ])
-    own, other = hold((own, other))
+    mine, theirs, other = hold((mine, theirs, other))
     others = lax.all_gather(other, ("y", "core"), axis=0, tiled=True)
     out = jax.ShapeDtypeStruct((2, SAMPLES), jnp.float32)
 
     once = lax.axis_index("x") // 8 + 1
 
+    once = lax.axis_index("x") // 8 + 1
+
+    def to_owners(_, acc):
+        return acc + jnp.stack([
+            mine[0] + across_z(theirs[0], 1), across_z(mine[1], 2) + across_z(theirs[1], 3)
+        ])
+
     def spread(_, c):
         return column_update(row_call(sinkhorn_kernel, out, where, [own[None]], c), ALL_RINGS)
 
+    own = lax.fori_loop(0, once, to_owners, jnp.zeros(mine.shape, jnp.float32))
     pair = lax.ppermute(own, "zl", [(0, 1), (1, 0)])
     c = lax.fori_loop(0, once, spread, jnp.zeros((1, SAMPLES), jnp.float32))
     c, pair = hold((c, pair))
@@ -481,7 +485,7 @@
     sums = jax.ShapeDtypeStruct((1, SAMPLES), jnp.float32)
 
     def balance(_, v):
-        return 1.0 / column_sum_in_pairs(balance_call(balance_kernel, sums, where, [both[:1]], v))
+        return 1.0 / column_sum_in_pairs(balance_call(balance_kernel, sums, where, [both], v))
 
     v = lax.fori_loop(0, once, balance, jnp.ones((1, SAMPLES), jnp.float32))
     blocks = [data, data_c, u, w, u_c, w_c, u3, w3, u3_c, w3_c]

time: 263 us -> 260 us (0.989)
    ppermute x7 -> x6, waiting for transfers between devices: 19.5 us -> 17.2 us  [column_sum_in_pairs(): x = x + lax.ppermute(x, axis, [(i, i ^ step) for i in range(n)])]
    ppermute x7 -> x6, starting transfers between devices: 10.4 us -> 9 us  [column_sum_in_pairs(): x = x + lax.ppermute(x, axis, [(i, i ^ step) for i in range(n)])]
  transfers between devices with their start and end apart: 53 -> 52, of which waited for: 33 -> 31; matrix products, arithmetic and copies ran while one was open for 3% -> 3% of each run, Pallas kernels for 13% -> 14%
where the time goes in v7:
time: 260 us; the launch traced here: 258 us
  waiting for transfers between devices  94 us (36%)
  starting transfers between devices  77.4 us (30%)
  Pallas kernels  54.1 us (21%)
  between operations  14.6 us (6%)
  local copies, waits for them, and re-layouts  10.1 us (4%)
  other arithmetic  7.71 us (3%)
    ppermute x4, waiting for transfers between devices, ring(): return lax.ppermute(x, 'y', [(i, (i + shift) % 4) for i in range(4)])  35 us
    pallas_call x4, Pallas kernels, partial_call(): pl.pallas_call(functools.partial(partial_kernel, noise_parts, jobs, known...  27.3 us
    ppermute x15, starting transfers between devices, along_x(): return lax.ppermute(x, 'x', [(i, (i + step) % 4) for i in range(4)])  26.3 us
    ppermute x15, starting transfers between devices, shift(): return lax.ppermute(x, axis, [(i, (i + k) % n) for i in range(n)])  21.7 us
    ppermute x15, waiting for transfers between devices, shift(): return lax.ppermute(x, axis, [(i, (i + k) % n) for i in range(n)])  18 us
    ppermute x6, waiting for transfers between devices, column_sum_in_pairs(): x = x + lax.ppermute(x, axis, [(i, i ^ step) for i in range(n)])  17.2 us
    pallas_call x1, Pallas kernels, targets_call(): pl.pallas_call(functools.partial(targets_kernel, shapes, widths), out_sha...  16.3 us
    ppermute x15, waiting for transfers between devices, along_x(): return lax.ppermute(x, 'x', [(i, (i + step) % 4) for i in range(4)])  10.7 us
  transfers between devices with their start and end apart: 52, of which 31 were waited for; matrix products, arithmetic and copies ran while one was open for 3% of the time, Pallas kernels for 14%

profile of v7, /device:TPU:0, one launch (start us, length us, event | category | flops | bytes accessed | tf_op | source)
XLA Modules:
  0.0 258.2 jit_solution(2172424171997621484)
XLA Ops:
  10.6 4.0 %collective-permute-start.18 = (bf16[256,4096]{1,0:T(8,128)(2,1)}, bf16[256,4096]{1,0:T(8,128)(2,1)S(1)}, u32[]{:S(2)}, u32[]{:S(2)}) collective-permute-start(bf16[256,4096]{1,0:T(8,128)(2,1)} %refs_3_.7), channel_id=1, source_target_pairs={{0,64},{64,0},{1,65},{65,1},{2,66},{66,2},{3,67},{67,3},{4,68},{68... | collective-permute-start | bytes 6291464 | tf_op jit(solution)/shard_map/ppermute | solution.py:379
  17.8 4.8 %shard_map.41 = (f32[2,32,512]{2,1,0:T(8,128)S(1)}, f32[2,32,512]{2,1,0:T(8,128)S(1)}, f32[2,32,512]{2,1,0:T(8,128)S(1)}, f32[2,32,512]{2,1,0:T(8,128)S(1)}, f32...) custom-call(s32[2]{0:T(128)S(1)} %pad_add_fusion.1.refs_0_, f32[8,128]{1,0:T(8,128)S(1)} %broadcast_in_dim.20.refs_1_, ...), custom_call_target="tpu_custom_call" | custom-call | flops 1 | bytes 1 | tf_op jit(solution)/shard_map/pallas_call | solution.py:337
  24.2 2.7 %collective-permute-start.21 = (f32[2,32,512]{2,1,0:T(8,128)S(1)}, f32[2,32,512]{2,1,0:T(8,128)S(1)}, u32[]{:S(2)}, u32[]{:S(2)}) collective-permute-start(f32[2,32,512]{2,1,0:T(8,128)S(1)} %get-tuple-element.183), channel_id=1, source_target_pairs={{0,2},{1,3},{2,0},{3,1},{4,6},{5,7},{6,4},{7,5},{8,10},{9,11},{10,... | collective-permute-start | bytes 393224 | tf_op jit(solution)/shard_map/ppermute | solution.py:388
  27.0 30.0 %collective-permute-done.16.u_ref.refs_7_ = bf16[256,4096]{1,0:T(8,128)(2,1)} collective-permute-done((bf16[256,4096]{1,0:T(8,128)(2,1)}, bf16[256,4096]{1,0:T(8,128)(2,1)}, u32[]{:S(2)}, u32[]{:S(2)}) %collective-permute-start.16) | collective-permute-done | bytes 2097184 | tf_op jit(solution)/shard_map/ppermute | solution.py:375
  57.0 2.8 %collective-permute-start.22 = (f32[2,32,512]{2,1,0:T(8,128)S(1)}, f32[2,32,512]{2,1,0:T(8,128)S(1)}, u32[]{:S(2)}, u32[]{:S(2)}) collective-permute-start(f32[2,32,512]{2,1,0:T(8,128)S(1)} %get-tuple-element.184), channel_id=1, source_target_pairs={{0,3},{1,0},{2,1},{3,2},{4,7},{5,4},{6,5},{7,6},{8,11},{9,8},{10,9... | collective-permute-start | bytes 393224 | tf_op jit(solution)/shard_map/ppermute | solution.py:388
  62.4 2.8 %shard_map.42 = (bf16[128,4096]{1,0:T(8,128)(2,1)}, bf16[128,4096]{1,0:T(8,128)(2,1)}) custom-call(bf16[256,4096]{1,0:T(8,128)(2,1)} %collective-permute-done.16.u_ref.refs_7_, bf16[256,4096]{1,0:T(8,128)(2,1)} %collective-permute-done.17.w_ref.refs_8_), custom_call_target="tpu_custom_call" | custom-call | flops 1 | bytes 1 | tf_op jit(solution)/shard_map/pallas_call | solution.py:364
  66.0 3.0 %collective-permute-start.26 = (bf16[128,4096]{1,0:T(8,128)(2,1)}, bf16[128,4096]{1,0:T(8,128)(2,1)S(1)}, u32[]{:S(2)}, u32[]{:S(2)}) collective-permute-start(bf16[128,4096]{1,0:T(8,128)(2,1)} %get-tuple-element.207), channel_id=1, source_target_pairs={{0,48},{16,0},{32,16},{48,32},{1,49},{17,1},{33,17},{49,33},{2,50}... | collective-permute-start | bytes 3145736 | tf_op jit(solution)/shard_map/ppermute | solution.py:375
  69.0 3.9 %collective-permute-start.37 = (bf16[256,4096]{1,0:T(8,128)(2,1)}, bf16[256,4096]{1,0:T(8,128)(2,1)}, u32[]{:S(2)}, u32[]{:S(2)}) collective-permute-start(bf16[256,4096]{1,0:T(8,128)(2,1)} %refs_5_.1), channel_id=1, source_target_pairs={{0,64},{64,0},{1,65},{65,1},{2,66},{66,2},{3,67},{67,3},{4,68},{68... | collective-permute-start | bytes 6291464 | tf_op jit(solution)/shard_map/ppermute | solution.py:379
  74.5 9.0 %shard_map.43 = (f32[2,32,1536]{2,1,0:T(8,128)S(1)}, f32[2,32,1536]{2,1,0:T(8,128)S(1)}, f32[2,32,1536]{2,1,0:T(8,128)S(1)}, f32[2,32,1536]{2,1,0:T(8,128)S(1)},...) custom-call(s32[2]{0:T(128)S(1)} %pad_add_fusion.1.refs_0_, f32[256,128]{1,0:T(8,128)S(1)} %get-tuple-element.196.refs_1_, ...), custom_call_target="tpu_custom_call" | custom-call | flops 1 | bytes 1 | tf_op jit(solution)/shard_map/pallas_call | solution.py:337
  87.4 5.0 %collective-permute-done.25.refs_5_.refs_11_ = bf16[128,4096]{1,0:T(8,128)(2,1)S(1)} collective-permute-done((bf16[128,4096]{1,0:T(8,128)(2,1)}, bf16[128,4096]{1,0:T(8,128)(2,1)S(1)}, u32[]{:S(2)}, u32[]{:S(2)}) %collective-permute-start.25) | collective-permute-done | bytes 1048608 | tf_op jit(solution)/shard_map/ppermute | solution.py:375
  92.4 2.7 %collective-permute-start.29 = (f32[2,32,1536]{2,1,0:T(8,128)S(1)}, f32[2,32,1536]{2,1,0:T(8,128)S(1)}, u32[]{:S(2)}, u32[]{:S(2)}) collective-permute-start(f32[2,32,1536]{2,1,0:T(8,128)S(1)} %get-tuple-element.216), channel_id=1, source_target_pairs={{0,2},{1,3},{2,0},{3,1},{4,6},{5,7},{6,4},{7,5},{8,10},{9,11},{10,... | collective-permute-start | bytes 1179656 | tf_op jit(solution)/shard_map/ppermute | solution.py:388
  95.8 6.9 %shard_map.44 = (f32[2,32,1024]{2,1,0:T(8,128)S(1)}, f32[2,32,1024]{2,1,0:T(8,128)}, f32[2,32,1024]{2,1,0:T(8,128)}, f32[2,32,1024]{2,1,0:T(8,128)}, f32[512,128]{1,0:T(8,128)}, /*index=5*/f32[1,512]{1,0:T(1,128)}) custom-call(s32[2]{0:T(128)S(1)} %pad_add_fusion.1.refs_0_, f32[512,128]{1,0:T(8,128)S(1)} %get-tuple-element.210.refs_1_, ...), custom_call_target="tpu_custom_call" | custom-call | flops 1 | bytes 1 | tf_op jit(solution)/shard_map/pallas_call | solution.py:337
  109.6 6.6 %shard_map.45 = (f32[2,32,1024]{2,1,0:T(8,128)S(1)}, f32[2,32,1024]{2,1,0:T(8,128)S(1)}, f32[2,32,1024]{2,1,0:T(8,128)S(1)}, f32[2,32,1024]{2,1,0:T(8,128)S(1)}, f32[512,128]{1,0:T(8,128)}, /*index=5*/f32[1,512]{1,0:T(1,128)}) custom-call(s32[2]{0:T(128)S(1)} %pad_add_fusion.1.refs_0_, f32[512,128]{1,0:T(8,128)S(1)} %get-tuple-element.210.refs_1_, ...), custom_call_target="tpu_custom_call" | custom-call | flops 1 | bytes 1 | tf_op jit(solution)/shard_map/pallas_call | solution.py:337
  118.5 2.7 %collective-permute-start.35 = (f32[2,32,1024]{2,1,0:T(8,128)S(1)}, f32[2,32,1024]{2,1,0:T(8,128)S(1)}, u32[]{:S(2)}, u32[]{:S(2)}) collective-permute-start(f32[2,32,1024]{2,1,0:T(8,128)S(1)} %get-tuple-element.224), channel_id=1, source_target_pairs={{0,2},{1,3},{2,0},{3,1},{4,6},{5,7},{6,4},{7,5},{8,10},{9,11},{10,... | collective-permute-start | bytes 786440 | tf_op jit(solution)/shard_map/ppermute | solution.py:388
  126.3 3.9 %collective-permute-done.35 = f32[2,32,1024]{2,1,0:T(8,128)S(1)} collective-permute-done((f32[2,32,1024]{2,1,0:T(8,128)S(1)}, f32[2,32,1024]{2,1,0:T(8,128)S(1)}, u32[]{:S(2)}, u32[]{:S(2)}) %collective-permute-start.35) | collective-permute-done | bytes 262176 | tf_op jit(solution)/shard_map/ppermute | solution.py:388
  130.2 3.7 %collective-permute-done.36 = f32[2,32,1024]{2,1,0:T(8,128)S(1)} collective-permute-done((f32[2,32,1024]{2,1,0:T(8,128)S(1)}, f32[2,32,1024]{2,1,0:T(8,128)S(1)}, u32[]{:S(2)}, u32[]{:S(2)}) %collective-permute-start.36) | collective-permute-done | bytes 262176 | tf_op jit(solution)/shard_map/ppermute | solution.py:388
  140.9 4.6 %collective-permute-done.39 = f32[32,2048]{1,0:T(8,128)S(1)} collective-permute-done((f32[32,2048]{1,0:T(8,128)S(1)}, f32[32,2048]{1,0:T(8,128)S(1)}, u32[]{:S(2)}, u32[]{:S(2)}) %collective-permute-start.39) | collective-permute-done | bytes 262176 | tf_op jit(solution)/shard_map/while/body/ppermute | solution.py:458
  145.5 3.6 %collective-permute-done.41 = f32[32,2048]{1,0:T(8,128)S(1)} collective-permute-done((f32[32,2048]{1,0:T(8,128)S(1)}, f32[32,2048]{1,0:T(8,128)S(1)}, u32[]{:S(2)}, u32[]{:S(2)}) %collective-permute-start.41) | collective-permute-done | bytes 262176 | tf_op jit(solution)/shard_map/while/body/ppermute | solution.py:458
  153.7 29.0 %while.33 = (s32[]{:T(128)}, f32[1,4096]{1,0:T(1,128)S(1)}, s32[]{:T(128)}, f32[2,32,2048]{2,1,0:T(8,128)}, s32[3,32]{1,0:T(4,128)S(1)}, /*index=5*/s32[]{:T(128)}) while((s32[]{:T(128)}, f32[1,4096]{1,0:T(1,128)S(1)}, s32[]{:T(128)}, f32[2,32,2048]{2,1,0:T(8,128)}, s32[3,32]{1,0:T(4,128)S(1)}, /*index=5*/s32[]{:T(128)}) %tuple.98), condition=%wide.region_3.4_spmd, body=%wide.region_2.3_spmd.sunk | while | flops 229378 | bytes 2081237 | solution.py:479
  167.7 3.0 %collective-permute-start.6 = (f32[2,4096]{1,0:T(2,128)S(1)}, f32[2,4096]{1,0:T(2,128)S(1)}, u32[]{:S(2)}, u32[]{:S(2)}) collective-permute-start(f32[2,4096]{1,0:T(2,128)S(1)} %pad_maximum_fusion.8), channel_id=1, source_target_pairs={{0,64},{4,68},{64,0},{68,4},{1,65},{5,69},{65,1},{69,5},{2,66},{6,... | collective-permute-start | bytes 98312 | tf_op jit(solution)/shard_map/while/body/ppermute | solution.py:218
  173.3 3.7 %collective-permute-start.7 = (f32[2,4096]{1,0:T(2,128)S(1)}, f32[2,4096]{1,0:T(2,128)S(1)}, u32[]{:S(2)}, u32[]{:S(2)}) collective-permute-start(f32[2,4096]{1,0:T(2,128)S(1)} %pad_maximum_fusion.9), channel_id=1, source_target_pairs={{0,3},{1,0},{2,1},{3,2},{4,7},{5,4},{6,5},{7,6},{8,11},{9,8},{10,9... | collective-permute-start | bytes 98312 | tf_op jit(solution)/shard_map/while/body/ppermute | solution.py:218
  178.6 3.5 %collective-permute-done.8 = f32[2,4096]{1,0:T(2,128)S(1)} collective-permute-done((f32[2,4096]{1,0:T(2,128)S(1)}, f32[2,4096]{1,0:T(2,128)S(1)}, u32[]{:S(2)}, u32[]{:S(2)}) %collective-permute-start.8) | collective-permute-done | bytes 32800 | tf_op jit(solution)/shard_map/while/body/ppermute | solution.py:218
  184.9 3.2 %collective-permute-start.43 = (bf16[2,2,32,2048]{3,2,1,0:T(8,128)(2,1)}, bf16[2,2,32,2048]{3,2,1,0:T(8,128)(2,1)}, u32[]{:S(2)}, u32[]{:S(2)}) collective-permute-start(bf16[2,2,32,2048]{3,2,1,0:T(8,128)(2,1)} %shard_map.46.refs_0_), channel_id=1, source_target_pairs={{0,3},{1,0},{2,1},{3,2},{4,7},{5,4},{6,5},{7,6},{8,11},{9,8},{10,9... | collective-permute-start | bytes 1572872 | tf_op jit(solution)/shard_map/ppermute | solution.py:388
  189.5 27.8 %while.34 = (s32[]{:T(128)}, f32[1,4096]{1,0:T(1,128)S(1)}, s32[]{:T(128)}, s32[3,32]{1,0:T(4,128)S(1)}, bf16[2,2,32,2048]{3,2,1,0:T(8,128)(2,1)}, /*index=5*/s32[]{:T(128)}) while((s32[]{:T(128)}, f32[1,4096]{1,0:T(1,128)S(1)}, s32[]{:T(128)}, s32[3,32]{1,0:T(4,128)S(1)}, bf16[2,2,32,2048]{3,2,1,0:T(8,128)(2,1)}, /*index=5*/s32[]{:T(128)}) %tuple.106), condition=%wide.region_5.6_spmd, body=%wide.region_4.5_spmd.sunk | while | flops 28674 | bytes 688437 | solution.py:490
  192.3 4.0 %collective-permute-done.11 = f32[1,4096]{1,0:T(1,128)S(1)} collective-permute-done((f32[1,4096]{1,0:T(1,128)S(1)}, f32[1,4096]{1,0:T(1,128)S(1)}, u32[]{:S(2)}, u32[]{:S(2)}) %collective-permute-start.11) | collective-permute-done | bytes 16416 | tf_op jit(solution)/shard_map/while/body/ppermute | solution.py:241
  197.8 4.2 %collective-permute-done.12 = f32[1,4096]{1,0:T(1,128)S(1)} collective-permute-done((f32[1,4096]{1,0:T(1,128)S(1)}, f32[1,4096]{1,0:T(1,128)S(1)}, u32[]{:S(2)}, u32[]{:S(2)}) %collective-permute-start.12) | collective-permute-done | bytes 16416 | tf_op jit(solution)/shard_map/while/body/ppermute | solution.py:241
  202.0 3.1 %collective-permute-start.13 = (f32[1,4096]{1,0:T(1,128)S(1)}, f32[1,4096]{1,0:T(1,128)S(1)}, u32[]{:S(2)}, u32[]{:S(2)}) collective-permute-start(f32[1,4096]{1,0:T(1,128)S(1)} %add.943), channel_id=1, source_target_pairs={{0,64},{64,0},{1,65},{65,1},{2,66},{66,2},{3,67},{67,3},{4,68},{68... | collective-permute-start | bytes 49160 | tf_op jit(solution)/shard_map/while/body/ppermute | solution.py:241
  207.4 2.8 %collective-permute-start.14 = (f32[1,4096]{1,0:T(1,128)S(1)}, f32[1,4096]{1,0:T(1,128)S(1)}, u32[]{:S(2)}, u32[]{:S(2)}) collective-permute-start(f32[1,4096]{1,0:T(1,128)S(1)} %add.944), channel_id=1, source_target_pairs={{0,1},{1,0},{2,3},{3,2},{4,5},{5,4},{6,7},{7,6},{8,9},{9,8},{10,11... | collective-permute-start | bytes 49160 | tf_op jit(solution)/shard_map/while/body/ppermute | solution.py:241
  213.4 3.9 %collective-permute-done.15 = f32[1,4096]{1,0:T(1,128)S(1)} collective-permute-done((f32[1,4096]{1,0:T(1,128)S(1)}, f32[1,4096]{1,0:T(1,128)S(1)}, u32[]{:S(2)}, u32[]{:S(2)}) %collective-permute-start.15) | collective-permute-done | bytes 16416 | tf_op jit(solution)/shard_map/while/body/ppermute | solution.py:241
  217.3 2.6 shard_map.47
  227.6 3.4 %collective-permute-start.50 = (f32[1,4096]{1,0:T(1,128)S(1)}, f32[1,4096]{1,0:T(1,128)S(1)}, u32[]{:S(2)}, u32[]{:S(2)}) collective-permute-start(f32[1,4096]{1,0:T(1,128)S(1)} %add_add_fusion.4), channel_id=1, source_target_pairs={{0,64},{64,0},{1,65},{65,1},{2,66},{66,2},{3,67},{67,3},{4,68},{68... | collective-permute-start | bytes 49160 | tf_op jit(solution)/shard_map/ppermute | solution.py:218
  235.1 16.3 %shard_map.48 = bf16[256,4096]{1,0:T(8,128)(2,1)} custom-call(s32[3,32]{1,0:T(4,128)S(1)} %get-tuple-element.517, bf16[2,2,32,2048]{3,2,1,0:T(8,128)(2,1)} %shard_map.46.refs_0_, bf16[2,2,32,2048]{3,2,1,0:T(8,128)(2,1)} %collective-permute-done.43.refs_1_, bf16[2,2,32,2048]{3,2,1,0:T(8,128)(2,1)} %collective-permute-done.44.refs_2_, ...), custom_call_target="tpu_custom_call" | custom-call | tf_op jit(solution)/shard_map/pallas_call | solution.py:169
  (172 shorter events, 88.7 us)
Async XLA Ops:
  7.2 226.7 %all-gather.2.cloned.1.call-start = ((), (), s32[]{:S(2)}) async-start(), calls=%async_computation | async-start | bytes 18874368 | tf_op jit(solution)/shard_map/all_gather | solution.py:462
  7.2 7.4 %collective-permute-start.19 = (bf16[256,4096]{1,0:T(8,128)(2,1)}, bf16[256,4096]{1,0:T(8,128)(2,1)}, u32[]{:S(2)}, u32[]{:S(2)}) collective-permute-start(bf16[256,4096]{1,0:T(8,128)(2,1)} %refs_5_.1), channel_id=1, source_target_pairs={{0,8},{8,0},{1,9},{9,1},{2,10},{10,2},{3,11},{11,3},{4,12},{12,4},... | collective-permute-start | bytes 6291464 | tf_op jit(solution)/shard_map/ppermute | solution.py:379
  7.3 49.7 %collective-permute-start.16 = (bf16[256,4096]{1,0:T(8,128)(2,1)}, bf16[256,4096]{1,0:T(8,128)(2,1)}, u32[]{:S(2)}, u32[]{:S(2)}) collective-permute-start(bf16[256,4096]{1,0:T(8,128)(2,1)} %refs_5_.1), channel_id=1, source_target_pairs={{0,16},{16,32},{32,48},{48,0},{1,17},{17,33},{33,49},{49,1},{2,18}... | collective-permute-start | bytes 6291464 | tf_op jit(solution)/shard_map/ppermute | solution.py:375
  9.0 50.7 %collective-permute-start.17 = (bf16[256,4096]{1,0:T(8,128)(2,1)}, bf16[256,4096]{1,0:T(8,128)(2,1)}, u32[]{:S(2)}, u32[]{:S(2)}) collective-permute-start(bf16[256,4096]{1,0:T(8,128)(2,1)} %refs_5_.1), channel_id=1, source_target_pairs={{0,48},{16,0},{32,16},{48,32},{1,49},{17,1},{33,17},{49,33},{2,50}... | collective-permute-start | bytes 6291464 | tf_op jit(solution)/shard_map/ppermute | solution.py:375
  10.6 49.9 %collective-permute-start.18 = (bf16[256,4096]{1,0:T(8,128)(2,1)}, bf16[256,4096]{1,0:T(8,128)(2,1)S(1)}, u32[]{:S(2)}, u32[]{:S(2)}) collective-permute-start(bf16[256,4096]{1,0:T(8,128)(2,1)} %refs_3_.7), channel_id=1, source_target_pairs={{0,64},{64,0},{1,65},{65,1},{2,66},{66,2},{3,67},{67,3},{4,68},{68... | collective-permute-start | bytes 6291464 | tf_op jit(solution)/shard_map/ppermute | solution.py:379
  22.7 39.1 %collective-permute-start.20 = (f32[2,32,512]{2,1,0:T(8,128)S(1)}, f32[2,32,512]{2,1,0:T(8,128)S(1)}, u32[]{:S(2)}, u32[]{:S(2)}) collective-permute-start(f32[2,32,512]{2,1,0:T(8,128)S(1)} %get-tuple-element.182), channel_id=1, source_target_pairs={{0,1},{1,2},{2,3},{3,0},{4,5},{5,6},{6,7},{7,4},{8,9},{9,10},{10,1... | collective-permute-start | bytes 393224 | tf_op jit(solution)/shard_map/ppermute | solution.py:388
  24.2 37.6 %collective-permute-start.21 = (f32[2,32,512]{2,1,0:T(8,128)S(1)}, f32[2,32,512]{2,1,0:T(8,128)S(1)}, u32[]{:S(2)}, u32[]{:S(2)}) collective-permute-start(f32[2,32,512]{2,1,0:T(8,128)S(1)} %get-tuple-element.183), channel_id=1, source_target_pairs={{0,2},{1,3},{2,0},{3,1},{4,6},{5,7},{6,4},{7,5},{8,10},{9,11},{10,... | collective-permute-start | bytes 393224 | tf_op jit(solution)/shard_map/ppermute | solution.py:388
  65.2 18.3 %collective-permute-start.23 = (bf16[256,4096]{1,0:T(8,128)(2,1)}, bf16[256,4096]{1,0:T(8,128)(2,1)S(1)}, u32[]{:S(2)}, u32[]{:S(2)}) collective-permute-start(bf16[256,4096]{1,0:T(8,128)(2,1)} %collective-permute-done.16.u_ref.refs_7_), channel_id=1, source_target_pairs={{0,8},{8,0},{1,9},{9,1},{2,10},{10,2},{3,11},{11,3},{4,12},{12,4},... | collective-permute-start | bytes 6291464 | tf_op jit(solution)/shard_map/ppermute | solution.py:379
  65.3 18.2 %collective-permute-start.24 = (bf16[256,4096]{1,0:T(8,128)(2,1)}, bf16[256,4096]{1,0:T(8,128)(2,1)S(1)}, u32[]{:S(2)}, u32[]{:S(2)}) collective-permute-start(bf16[256,4096]{1,0:T(8,128)(2,1)} %collective-permute-done.17.w_ref.refs_8_), channel_id=1, source_target_pairs={{0,8},{8,0},{1,9},{9,1},{2,10},{10,2},{3,11},{11,3},{4,12},{12,4},... | collective-permute-start | bytes 6291464 | tf_op jit(solution)/shard_map/ppermute | solution.py:379
  65.8 26.6 %collective-permute-start.25 = (bf16[128,4096]{1,0:T(8,128)(2,1)}, bf16[128,4096]{1,0:T(8,128)(2,1)S(1)}, u32[]{:S(2)}, u32[]{:S(2)}) collective-permute-start(bf16[128,4096]{1,0:T(8,128)(2,1)} %get-tuple-element.206), channel_id=1, source_target_pairs={{0,16},{16,32},{32,48},{48,0},{1,17},{17,33},{33,49},{49,1},{2,18}... | collective-permute-start | bytes 3145736 | tf_op jit(solution)/shard_map/ppermute | solution.py:375
  66.0 36.6 %collective-permute-start.26 = (bf16[128,4096]{1,0:T(8,128)(2,1)}, bf16[128,4096]{1,0:T(8,128)(2,1)S(1)}, u32[]{:S(2)}, u32[]{:S(2)}) collective-permute-start(bf16[128,4096]{1,0:T(8,128)(2,1)} %get-tuple-element.207), channel_id=1, source_target_pairs={{0,48},{16,0},{32,16},{48,32},{1,49},{17,1},{33,17},{49,33},{2,50}... | collective-permute-start | bytes 3145736 | tf_op jit(solution)/shard_map/ppermute | solution.py:375
  69.0 49.5 %collective-permute-start.37 = (bf16[256,4096]{1,0:T(8,128)(2,1)}, bf16[256,4096]{1,0:T(8,128)(2,1)}, u32[]{:S(2)}, u32[]{:S(2)}) collective-permute-start(bf16[256,4096]{1,0:T(8,128)(2,1)} %refs_5_.1), channel_id=1, source_target_pairs={{0,64},{64,0},{1,65},{65,1},{2,66},{66,2},{3,67},{67,3},{4,68},{68... | collective-permute-start | bytes 6291464 | tf_op jit(solution)/shard_map/ppermute | solution.py:379
  83.5 19.1 %collective-permute-start.27 = (f32[2,32,1536]{2,1,0:T(8,128)S(1)}, f32[2,32,1536]{2,1,0:T(8,128)S(1)}, u32[]{:S(2)}, u32[]{:S(2)}) collective-permute-start(f32[2,32,1536]{2,1,0:T(8,128)S(1)} %get-tuple-element.208), channel_id=1, source_target_pairs={{0,1},{1,2},{2,3},{3,0},{4,5},{5,6},{6,7},{7,4},{8,9},{9,10},{10,1... | collective-permute-start | bytes 1179656 | tf_op jit(solution)/shard_map/ppermute | solution.py:388
  84.8 17.9 %collective-permute-start.28 = (f32[2,32,1536]{2,1,0:T(8,128)S(1)}, f32[2,32,1536]{2,1,0:T(8,128)S(1)}, u32[]{:S(2)}, u32[]{:S(2)}) collective-permute-start(f32[2,32,1536]{2,1,0:T(8,128)S(1)} %get-tuple-element.209), channel_id=1, source_target_pairs={{0,3},{1,0},{2,1},{3,2},{4,7},{5,4},{6,5},{7,6},{8,11},{9,8},{10,9... | collective-permute-start | bytes 1179656 | tf_op jit(solution)/shard_map/ppermute | solution.py:388
  92.4 13.1 %collective-permute-start.29 = (f32[2,32,1536]{2,1,0:T(8,128)S(1)}, f32[2,32,1536]{2,1,0:T(8,128)S(1)}, u32[]{:S(2)}, u32[]{:S(2)}) collective-permute-start(f32[2,32,1536]{2,1,0:T(8,128)S(1)} %get-tuple-element.216), channel_id=1, source_target_pairs={{0,2},{1,3},{2,0},{3,1},{4,6},{5,7},{6,4},{7,5},{8,10},{9,11},{10,... | collective-permute-start | bytes 1179656 | tf_op jit(solution)/shard_map/ppermute | solution.py:388
  102.8 6.8 %collective-permute-start.33 = (bf16[128,4096]{1,0:T(8,128)(2,1)S(1)}, bf16[128,4096]{1,0:T(8,128)(2,1)S(1)}, u32[]{:S(2)}, u32[]{:S(2)}) collective-permute-start(bf16[128,4096]{1,0:T(8,128)(2,1)S(1)} %collective-permute-done.26.refs_6_.refs_12_), channel_id=1, source_target_pairs={{0,8},{8,0},{1,9},{9,1},{2,10},{10,2},{3,11},{11,3},{4,12},{12,4},... | collective-permute-start | bytes 3145736 | tf_op jit(solution)/shard_map/ppermute | solution.py:379
  103.3 18.0 %collective-permute-start.31 = (f32[2,32,1024]{2,1,0:T(8,128)}, f32[2,32,1024]{2,1,0:T(8,128)}, u32[]{:S(2)}, u32[]{:S(2)}) collective-permute-start(f32[2,32,1024]{2,1,0:T(8,128)} %get-tuple-element.220), channel_id=1, source_target_pairs={{0,2},{1,3},{2,0},{3,1},{4,6},{5,7},{6,4},{7,5},{8,10},{9,11},{10,... | collective-permute-start | bytes 786440 | tf_op jit(solution)/shard_map/ppermute | solution.py:388
  106.3 27.6 %collective-permute-start.30 = (f32[2,32,1024]{2,1,0:T(8,128)}, f32[2,32,1024]{2,1,0:T(8,128)}, u32[]{:S(2)}, u32[]{:S(2)}) collective-permute-start(f32[2,32,1024]{2,1,0:T(8,128)} %get-tuple-element.219), channel_id=1, source_target_pairs={{0,1},{1,2},{2,3},{3,0},{4,5},{5,6},{6,7},{7,4},{8,9},{9,10},{10,1... | collective-permute-start | bytes 786440 | tf_op jit(solution)/shard_map/ppermute | solution.py:388
  107.5 26.4 %collective-permute-start.38 = (f32[2,32,1024]{2,1,0:T(8,128)}, f32[2,32,1024]{2,1,0:T(8,128)}, u32[]{:S(2)}, u32[]{:S(2)}) collective-permute-start(f32[2,32,1024]{2,1,0:T(8,128)} %get-tuple-element.227), channel_id=1, source_target_pairs={{0,3},{1,0},{2,1},{3,2},{4,7},{5,4},{6,5},{7,6},{8,11},{9,8},{10,9... | collective-permute-start | bytes 786440 | tf_op jit(solution)/shard_map/ppermute | solution.py:388
  116.2 10.1 %collective-permute-start.34 = (f32[2,32,1024]{2,1,0:T(8,128)S(1)}, f32[2,32,1024]{2,1,0:T(8,128)}, u32[]{:S(2)}, u32[]{:S(2)}) collective-permute-start(f32[2,32,1024]{2,1,0:T(8,128)S(1)} %get-tuple-element.223), channel_id=1, source_target_pairs={{0,1},{1,2},{2,3},{3,0},{4,5},{5,6},{6,7},{7,4},{8,9},{9,10},{10,1... | collective-permute-start | bytes 786440 | tf_op jit(solution)/shard_map/ppermute | solution.py:388
  118.5 11.7 %collective-permute-start.35 = (f32[2,32,1024]{2,1,0:T(8,128)S(1)}, f32[2,32,1024]{2,1,0:T(8,128)S(1)}, u32[]{:S(2)}, u32[]{:S(2)}) collective-permute-start(f32[2,32,1024]{2,1,0:T(8,128)S(1)} %get-tuple-element.224), channel_id=1, source_target_pairs={{0,2},{1,3},{2,0},{3,1},{4,6},{5,7},{6,4},{7,5},{8,10},{9,11},{10,... | collective-permute-start | bytes 786440 | tf_op jit(solution)/shard_map/ppermute | solution.py:388
  121.3 12.6 %collective-permute-start.36 = (f32[2,32,1024]{2,1,0:T(8,128)S(1)}, f32[2,32,1024]{2,1,0:T(8,128)S(1)}, u32[]{:S(2)}, u32[]{:S(2)}) collective-permute-start(f32[2,32,1024]{2,1,0:T(8,128)S(1)} %get-tuple-element.225), channel_id=1, source_target_pairs={{0,3},{1,0},{2,1},{3,2},{4,7},{5,4},{6,5},{7,6},{8,11},{9,8},{10,9... | collective-permute-start | bytes 786440 | tf_op jit(solution)/shard_map/ppermute | solution.py:388
  136.1 9.3 %collective-permute-start.39 = (f32[32,2048]{1,0:T(8,128)S(1)}, f32[32,2048]{1,0:T(8,128)S(1)}, u32[]{:S(2)}, u32[]{:S(2)}) collective-permute-start(f32[32,2048]{1,0:T(8,128)S(1)} %get-tuple-element.275), channel_id=1, source_target_pairs={{0,4},{4,0},{64,68},{68,64},{1,5},{5,1},{65,69},{69,65},{2,6},{6,2... | collective-permute-start | bytes 786440 | tf_op jit(solution)/shard_map/while/body/ppermute | solution.py:458
  137.2 11.9 %collective-permute-start.41 = (f32[32,2048]{1,0:T(8,128)S(1)}, f32[32,2048]{1,0:T(8,128)S(1)}, u32[]{:S(2)}, u32[]{:S(2)}) collective-permute-start(f32[32,2048]{1,0:T(8,128)S(1)} %get-tuple-element.276), channel_id=1, source_target_pairs={{0,68},{4,64},{64,4},{68,0},{1,69},{5,65},{65,5},{69,1},{2,70},{6,... | collective-permute-start | bytes 786440 | tf_op jit(solution)/shard_map/while/body/ppermute | solution.py:458
  139.7 11.1 %collective-permute-start.40 = (f32[32,2048]{1,0:T(8,128)S(1)}, f32[32,2048]{1,0:T(8,128)S(1)}, u32[]{:S(2)}, u32[]{:S(2)}) collective-permute-start(f32[32,2048]{1,0:T(8,128)S(1)} %slice_bitcast_fusion.1), channel_id=1, source_target_pairs={{0,64},{4,68},{64,0},{68,4},{1,65},{5,69},{65,1},{69,5},{2,66},{6,... | collective-permute-start | bytes 786440 | tf_op jit(solution)/shard_map/while/body/ppermute | solution.py:458
  153.7 29.0 %collective-permute-start.42 = (f32[2,32,2048]{2,1,0:T(8,128)}, f32[2,32,2048]{2,1,0:T(8,128)S(1)}, u32[]{:S(2)}, u32[]{:S(2)}) collective-permute-start(f32[2,32,2048]{2,1,0:T(8,128)} %get-tuple-element.424), channel_id=1, source_target_pairs={{0,4},{4,0},{1,5},{5,1},{2,6},{6,2},{3,7},{7,3},{8,12},{12,8},{9,1... | collective-permute-start | bytes 1572872 | tf_op jit(solution)/shard_map/ppermute | solution.py:478
  157.5 6.1 %collective-permute-start.2 = (f32[2,4096]{1,0:T(2,128)S(1)}, f32[2,4096]{1,0:T(2,128)S(1)}, u32[]{:S(2)}, u32[]{:S(2)}) collective-permute-start(f32[2,4096]{1,0:T(2,128)S(1)} %pad_maximum_fusion.7), channel_id=1, source_target_pairs={{0,16},{16,32},{32,48},{48,0},{1,17},{17,33},{33,49},{49,1},{2,18}... | collective-permute-start | bytes 98312 | tf_op jit(solution)/shard_map/while/body/ppermute | solution.py:218
  159.0 6.1 %collective-permute-start.3 = (f32[2,4096]{1,0:T(2,128)S(1)}, f32[2,4096]{1,0:T(2,128)S(1)}, u32[]{:S(2)}, u32[]{:S(2)}) collective-permute-start(f32[2,4096]{1,0:T(2,128)S(1)} %pad_maximum_fusion.7), channel_id=1, source_target_pairs={{0,32},{16,48},{32,0},{48,16},{1,33},{17,49},{33,1},{49,17},{2,34}... | collective-permute-start | bytes 98312 | tf_op jit(solution)/shard_map/while/body/ppermute | solution.py:218
  184.9 32.4 %collective-permute-start.43 = (bf16[2,2,32,2048]{3,2,1,0:T(8,128)(2,1)}, bf16[2,2,32,2048]{3,2,1,0:T(8,128)(2,1)}, u32[]{:S(2)}, u32[]{:S(2)}) collective-permute-start(bf16[2,2,32,2048]{3,2,1,0:T(8,128)(2,1)} %shard_map.46.refs_0_), channel_id=1, source_target_pairs={{0,3},{1,0},{2,1},{3,2},{4,7},{5,4},{6,5},{7,6},{8,11},{9,8},{10,9... | collective-permute-start | bytes 1572872 | tf_op jit(solution)/shard_map/ppermute | solution.py:388
  188.0 29.3 %collective-permute-start.44 = (bf16[2,2,32,2048]{3,2,1,0:T(8,128)(2,1)}, bf16[2,2,32,2048]{3,2,1,0:T(8,128)(2,1)}, u32[]{:S(2)}, u32[]{:S(2)}) collective-permute-start(bf16[2,2,32,2048]{3,2,1,0:T(8,128)(2,1)} %shard_map.46.refs_0_), channel_id=1, source_target_pairs={{0,1},{1,2},{2,3},{3,0},{4,5},{5,6},{6,7},{7,4},{8,9},{9,10},{10,1... | collective-permute-start | bytes 1572872 | tf_op jit(solution)/shard_map/ppermute | solution.py:388
  188.0 29.3 %collective-permute-start.45 = (bf16[2,2,32,2048]{3,2,1,0:T(8,128)(2,1)}, bf16[2,2,32,2048]{3,2,1,0:T(8,128)(2,1)}, u32[]{:S(2)}, u32[]{:S(2)}) collective-permute-start(bf16[2,2,32,2048]{3,2,1,0:T(8,128)(2,1)} %shard_map.46.refs_0_), channel_id=1, source_target_pairs={{0,2},{1,3},{2,0},{3,1},{4,6},{5,7},{6,4},{7,5},{8,10},{9,11},{10,... | collective-permute-start | bytes 1572872 | tf_op jit(solution)/shard_map/ppermute | solution.py:388
  196.4 5.6 %collective-permute-start.12 = (f32[1,4096]{1,0:T(1,128)S(1)}, f32[1,4096]{1,0:T(1,128)S(1)}, u32[]{:S(2)}, u32[]{:S(2)}) collective-permute-start(f32[1,4096]{1,0:T(1,128)S(1)} %add.942), channel_id=1, source_target_pairs={{0,32},{16,48},{32,0},{48,16},{1,33},{17,49},{33,1},{49,17},{2,34}... | collective-permute-start | bytes 49160 | tf_op jit(solution)/shard_map/while/body/ppermute | solution.py:241
  (35 other events, 216.3 us)
Sparse Core Ops, SparseCore 0:
  135.7 84.9 all-gather.1

commit v8 on v7

--- a/solution.py
+++ b/solution.py
@@ -416,8 +416,10 @@
     far = swap(noise, "zh")
     data_c = swap(data, "core")
     (k0, k1, k3, k2), n_sq, x_row = call(here, [(noise,)], [data, data_c], (((0,), (0, 1)),))
-    k1, k3, k2 = along_x(k1, 1), along_x(k3, -1), along_x(k2, 2)
-    u, w, far, data_c, data, k0, k1, k2, k3 = hold((u, w, far, data_c, data, k0, k1, k2, k3))
+    k1, k3 = along_x(k1, 1), along_x(k3, -1)
+    k1, k2, k3 = hold((k1, k2, k3))
+    k2 = along_x(k2, 2)
+    u, w, data_c, data, k0, k1, k2, k3 = hold((u, w, data_c, data, k0, k1, k2, k3))
 
     ua, wb = halves_call(u, w)
     ua, wb, u, w, data = hold((ua, wb, u, w, data))

time: 260 us -> 255 us (0.981)
  waiting for transfers between devices: 94 us -> 87.9 us
    ppermute x4, waiting for transfers between devices: 35 us -> 30.5 us  [ring(): return lax.ppermute(x, 'y', [(i, (i + shift) % 4) for i in range(4)])]
    unnamed x30 -> x28, local copies, waits for them, and re-layouts: 7.35 us -> 6.42 us
  transfers between devices with their start and end apart: 52 -> 52, of which waited for: 31 -> 30; matrix products, arithmetic and copies ran while one was open for 3% -> 4% of each run, Pallas kernels for 14% -> 15%
where the time goes in v8:
time: 255 us; the launch traced here: 254 us
  waiting for transfers between devices  87.9 us (34%)
  starting transfers between devices  79.7 us (31%)
  Pallas kernels  54.5 us (21%)
  between operations  14.6 us (6%)
  local copies, waits for them, and re-layouts  9.17 us (4%)
  other arithmetic  7.73 us (3%)
    ppermute x4, waiting for transfers between devices, ring(): return lax.ppermute(x, 'y', [(i, (i + shift) % 4) for i in range(4)])  30.5 us
    pallas_call x4, Pallas kernels, partial_call(): pl.pallas_call(functools.partial(partial_kernel, noise_parts, jobs, known...  27.8 us
    ppermute x15, starting transfers between devices, along_x(): return lax.ppermute(x, 'x', [(i, (i + step) % 4) for i in range(4)])  25.3 us
    ppermute x15, starting transfers between devices, shift(): return lax.ppermute(x, axis, [(i, (i + k) % n) for i in range(n)])  23.9 us
    ppermute x15, waiting for transfers between devices, shift(): return lax.ppermute(x, axis, [(i, (i + k) % n) for i in range(n)])  17.1 us
    pallas_call x1, Pallas kernels, targets_call(): pl.pallas_call(functools.partial(targets_kernel, shapes, widths), out_sha...  16.3 us
    ppermute x6, waiting for transfers between devices, column_sum_in_pairs(): x = x + lax.ppermute(x, axis, [(i, i ^ step) for i in range(n)])  15.9 us
    ppermute x15, waiting for transfers between devices, along_x(): return lax.ppermute(x, 'x', [(i, (i + step) % 4) for i in range(4)])  10.7 us
  transfers between devices with their start and end apart: 52, of which 30 were waited for; matrix products, arithmetic and copies ran while one was open for 4% of the time, Pallas kernels for 15%

profile of v8, /device:TPU:0, one launch (start us, length us, event | category | flops | bytes accessed | tf_op | source)
XLA Modules:
  0.0 253.9 jit_solution(8370218121293448618)
XLA Ops:
  10.6 4.0 %collective-permute-start.24 = (bf16[256,4096]{1,0:T(8,128)(2,1)}, bf16[256,4096]{1,0:T(8,128)(2,1)}, u32[]{:S(2)}, u32[]{:S(2)}) collective-permute-start(bf16[256,4096]{1,0:T(8,128)(2,1)} %refs_3_.7), channel_id=1, source_target_pairs={{0,64},{64,0},{1,65},{65,1},{2,66},{66,2},{3,67},{67,3},{4,68},{68... | collective-permute-start | bytes 6291464 | tf_op jit(solution)/shard_map/ppermute | solution.py:379
  19.2 4.8 %shard_map.41 = (f32[2,32,512]{2,1,0:T(8,128)S(1)}, f32[2,32,512]{2,1,0:T(8,128)S(1)}, f32[2,32,512]{2,1,0:T(8,128)S(1)}, f32[2,32,512]{2,1,0:T(8,128)S(1)}, f32...) custom-call(s32[2]{0:T(128)S(1)} %pad_add_fusion.1.refs_0_, f32[8,128]{1,0:T(8,128)S(1)} %broadcast_in_dim.20.refs_1_, ...), custom_call_target="tpu_custom_call" | custom-call | flops 1 | bytes 1 | tf_op jit(solution)/shard_map/pallas_call | solution.py:337
  27.3 3.0 %collective-permute-done.19 = f32[2,32,512]{2,1,0:T(8,128)S(1)} collective-permute-done((f32[2,32,512]{2,1,0:T(8,128)S(1)}, f32[2,32,512]{2,1,0:T(8,128)S(1)}, u32[]{:S(2)}, u32[]{:S(2)}) %collective-permute-start.19) | collective-permute-done | bytes 131104 | tf_op jit(solution)/shard_map/ppermute | solution.py:388
  30.5 2.7 %collective-permute-start.21 = (f32[2,32,512]{2,1,0:T(8,128)S(1)}, f32[2,32,512]{2,1,0:T(8,128)S(1)}, u32[]{:S(2)}, u32[]{:S(2)}) collective-permute-start(f32[2,32,512]{2,1,0:T(8,128)S(1)} %get-tuple-element.188), channel_id=1, source_target_pairs={{0,2},{1,3},{2,0},{3,1},{4,6},{5,7},{6,4},{7,5},{8,10},{9,11},{10,... | collective-permute-start | bytes 393224 | tf_op jit(solution)/shard_map/ppermute | solution.py:388
  33.3 23.7 %collective-permute-done.16.u_ref.refs_7_ = bf16[256,4096]{1,0:T(8,128)(2,1)} collective-permute-done((bf16[256,4096]{1,0:T(8,128)(2,1)}, bf16[256,4096]{1,0:T(8,128)(2,1)}, u32[]{:S(2)}, u32[]{:S(2)}) %collective-permute-start.16) | collective-permute-done | bytes 2097184 | tf_op jit(solution)/shard_map/ppermute | solution.py:375
  57.7 2.7 %shard_map.42 = (bf16[128,4096]{1,0:T(8,128)(2,1)}, bf16[128,4096]{1,0:T(8,128)(2,1)}) custom-call(bf16[256,4096]{1,0:T(8,128)(2,1)} %collective-permute-done.16.u_ref.refs_7_, bf16[256,4096]{1,0:T(8,128)(2,1)} %collective-permute-done.17.w_ref.refs_8_), custom_call_target="tpu_custom_call" | custom-call | flops 1 | bytes 1 | tf_op jit(solution)/shard_map/pallas_call | solution.py:364
  64.2 3.9 %collective-permute-start.37 = (bf16[256,4096]{1,0:T(8,128)(2,1)}, bf16[256,4096]{1,0:T(8,128)(2,1)}, u32[]{:S(2)}, u32[]{:S(2)}) collective-permute-start(bf16[256,4096]{1,0:T(8,128)(2,1)} %refs_5_.1), channel_id=1, source_target_pairs={{0,64},{64,0},{1,65},{65,1},{2,66},{66,2},{3,67},{67,3},{4,68},{68... | collective-permute-start | bytes 6291464 | tf_op jit(solution)/shard_map/ppermute | solution.py:379
  68.1 9.3 %shard_map.43 = (f32[2,32,1536]{2,1,0:T(8,128)S(1)}, f32[2,32,1536]{2,1,0:T(8,128)S(1)}, f32[2,32,1536]{2,1,0:T(8,128)S(1)}, f32[2,32,1536]{2,1,0:T(8,128)S(1)},...) custom-call(s32[2]{0:T(128)S(1)} %pad_add_fusion.1.refs_0_, f32[256,128]{1,0:T(8,128)S(1)} %get-tuple-element.201.refs_1_, ...), custom_call_target="tpu_custom_call" | custom-call | flops 1 | bytes 1 | tf_op jit(solution)/shard_map/pallas_call | solution.py:337
  80.7 6.8 %collective-permute-done.25.refs_5_.refs_11_ = bf16[128,4096]{1,0:T(8,128)(2,1)S(1)} collective-permute-done((bf16[128,4096]{1,0:T(8,128)(2,1)}, bf16[128,4096]{1,0:T(8,128)(2,1)S(1)}, u32[]{:S(2)}, u32[]{:S(2)}) %collective-permute-start.25) | collective-permute-done | bytes 1048608 | tf_op jit(solution)/shard_map/ppermute | solution.py:375
  87.4 3.0 %collective-permute-start.29 = (f32[2,32,1536]{2,1,0:T(8,128)S(1)}, f32[2,32,1536]{2,1,0:T(8,128)S(1)}, u32[]{:S(2)}, u32[]{:S(2)}) collective-permute-start(f32[2,32,1536]{2,1,0:T(8,128)S(1)} %get-tuple-element.220), channel_id=1, source_target_pairs={{0,2},{1,3},{2,0},{3,1},{4,6},{5,7},{6,4},{7,5},{8,10},{9,11},{10,... | collective-permute-start | bytes 1179656 | tf_op jit(solution)/shard_map/ppermute | solution.py:388
  91.1 7.1 %shard_map.44 = (f32[2,32,1024]{2,1,0:T(8,128)S(1)}, f32[2,32,1024]{2,1,0:T(8,128)}, f32[2,32,1024]{2,1,0:T(8,128)}, f32[2,32,1024]{2,1,0:T(8,128)}, f32[512,128]{1,0:T(8,128)}, /*index=5*/f32[1,512]{1,0:T(1,128)}) custom-call(s32[2]{0:T(128)S(1)} %pad_add_fusion.1.refs_0_, f32[512,128]{1,0:T(8,128)S(1)} %get-tuple-element.214.refs_1_, ...), custom_call_target="tpu_custom_call" | custom-call | flops 1 | bytes 1 | tf_op jit(solution)/shard_map/pallas_call | solution.py:337
  103.6 6.6 %shard_map.45 = (f32[2,32,1024]{2,1,0:T(8,128)S(1)}, f32[2,32,1024]{2,1,0:T(8,128)S(1)}, f32[2,32,1024]{2,1,0:T(8,128)S(1)}, f32[2,32,1024]{2,1,0:T(8,128)S(1)}, f32[512,128]{1,0:T(8,128)}, /*index=5*/f32[1,512]{1,0:T(1,128)}) custom-call(s32[2]{0:T(128)S(1)} %pad_add_fusion.1.refs_0_, f32[512,128]{1,0:T(8,128)S(1)} %get-tuple-element.214.refs_1_, ...), custom_call_target="tpu_custom_call" | custom-call | flops 1 | bytes 1 | tf_op jit(solution)/shard_map/pallas_call | solution.py:337
  110.5 3.1 %collective-permute-done.37 = bf16[256,4096]{1,0:T(8,128)(2,1)} collective-permute-done((bf16[256,4096]{1,0:T(8,128)(2,1)}, bf16[256,4096]{1,0:T(8,128)(2,1)}, u32[]{:S(2)}, u32[]{:S(2)}) %collective-permute-start.37) | collective-permute-done | bytes 2097184 | tf_op jit(solution)/shard_map/ppermute | solution.py:379
  113.6 3.0 %collective-permute-start.35 = (f32[2,32,1024]{2,1,0:T(8,128)S(1)}, f32[2,32,1024]{2,1,0:T(8,128)S(1)}, u32[]{:S(2)}, u32[]{:S(2)}) collective-permute-start(f32[2,32,1024]{2,1,0:T(8,128)S(1)} %get-tuple-element.228), channel_id=1, source_target_pairs={{0,2},{1,3},{2,0},{3,1},{4,6},{5,7},{6,4},{7,5},{8,10},{9,11},{10,... | collective-permute-start | bytes 786440 | tf_op jit(solution)/shard_map/ppermute | solution.py:388
  121.0 4.7 %collective-permute-done.35 = f32[2,32,1024]{2,1,0:T(8,128)S(1)} collective-permute-done((f32[2,32,1024]{2,1,0:T(8,128)S(1)}, f32[2,32,1024]{2,1,0:T(8,128)S(1)}, u32[]{:S(2)}, u32[]{:S(2)}) %collective-permute-start.35) | collective-permute-done | bytes 262176 | tf_op jit(solution)/shard_map/ppermute | solution.py:388
  134.9 4.6 %collective-permute-done.39 = f32[32,2048]{1,0:T(8,128)S(1)} collective-permute-done((f32[32,2048]{1,0:T(8,128)S(1)}, f32[32,2048]{1,0:T(8,128)S(1)}, u32[]{:S(2)}, u32[]{:S(2)}) %collective-permute-start.39) | collective-permute-done | bytes 262176 | tf_op jit(solution)/shard_map/while/body/ppermute | solution.py:460
  139.5 4.1 %collective-permute-done.41 = f32[32,2048]{1,0:T(8,128)S(1)} collective-permute-done((f32[32,2048]{1,0:T(8,128)S(1)}, f32[32,2048]{1,0:T(8,128)S(1)}, u32[]{:S(2)}, u32[]{:S(2)}) %collective-permute-start.41) | collective-permute-done | bytes 262176 | tf_op jit(solution)/shard_map/while/body/ppermute | solution.py:460
  148.3 29.0 %while.33 = (s32[]{:T(128)}, f32[1,4096]{1,0:T(1,128)S(1)}, s32[]{:T(128)}, f32[2,32,2048]{2,1,0:T(8,128)}, s32[3,32]{1,0:T(4,128)S(1)}, /*index=5*/s32[]{:T(128)}) while((s32[]{:T(128)}, f32[1,4096]{1,0:T(1,128)S(1)}, s32[]{:T(128)}, f32[2,32,2048]{2,1,0:T(8,128)}, s32[3,32]{1,0:T(4,128)S(1)}, /*index=5*/s32[]{:T(128)}) %tuple.100), condition=%wide.region_3.4_spmd, body=%wide.region_2.3_spmd.sunk | while | flops 229378 | bytes 2081237 | solution.py:481
  156.2 3.3 %collective-permute-done.2 = f32[2,4096]{1,0:T(2,128)S(1)} collective-permute-done((f32[2,4096]{1,0:T(2,128)S(1)}, f32[2,4096]{1,0:T(2,128)S(1)}, u32[]{:S(2)}, u32[]{:S(2)}) %collective-permute-start.2) | collective-permute-done | bytes 32800 | tf_op jit(solution)/shard_map/while/body/ppermute | solution.py:218
  162.2 3.1 %collective-permute-start.6 = (f32[2,4096]{1,0:T(2,128)S(1)}, f32[2,4096]{1,0:T(2,128)S(1)}, u32[]{:S(2)}, u32[]{:S(2)}) collective-permute-start(f32[2,4096]{1,0:T(2,128)S(1)} %pad_maximum_fusion.8), channel_id=1, source_target_pairs={{0,64},{4,68},{64,0},{68,4},{1,65},{5,69},{65,1},{69,5},{2,66},{6,... | collective-permute-start | bytes 98312 | tf_op jit(solution)/shard_map/while/body/ppermute | solution.py:218
  167.9 3.8 %collective-permute-start.7 = (f32[2,4096]{1,0:T(2,128)S(1)}, f32[2,4096]{1,0:T(2,128)S(1)}, u32[]{:S(2)}, u32[]{:S(2)}) collective-permute-start(f32[2,4096]{1,0:T(2,128)S(1)} %pad_maximum_fusion.9), channel_id=1, source_target_pairs={{0,3},{1,0},{2,1},{3,2},{4,7},{5,4},{6,5},{7,6},{8,11},{9,8},{10,9... | collective-permute-start | bytes 98312 | tf_op jit(solution)/shard_map/while/body/ppermute | solution.py:218
  173.3 3.5 %collective-permute-done.8 = f32[2,4096]{1,0:T(2,128)S(1)} collective-permute-done((f32[2,4096]{1,0:T(2,128)S(1)}, f32[2,4096]{1,0:T(2,128)S(1)}, u32[]{:S(2)}, u32[]{:S(2)}) %collective-permute-start.8) | collective-permute-done | bytes 32800 | tf_op jit(solution)/shard_map/while/body/ppermute | solution.py:218
  179.5 3.2 %collective-permute-start.43 = (bf16[2,2,32,2048]{3,2,1,0:T(8,128)(2,1)}, bf16[2,2,32,2048]{3,2,1,0:T(8,128)(2,1)}, u32[]{:S(2)}, u32[]{:S(2)}) collective-permute-start(bf16[2,2,32,2048]{3,2,1,0:T(8,128)(2,1)} %shard_map.46.refs_0_), channel_id=1, source_target_pairs={{0,3},{1,0},{2,1},{3,2},{4,7},{5,4},{6,5},{7,6},{8,11},{9,8},{10,9... | collective-permute-start | bytes 1572872 | tf_op jit(solution)/shard_map/ppermute | solution.py:388
  184.1 27.7 %while.34 = (s32[]{:T(128)}, f32[1,4096]{1,0:T(1,128)S(1)}, s32[]{:T(128)}, s32[3,32]{1,0:T(4,128)S(1)}, bf16[2,2,32,2048]{3,2,1,0:T(8,128)(2,1)}, /*index=5*/s32[]{:T(128)}) while((s32[]{:T(128)}, f32[1,4096]{1,0:T(1,128)S(1)}, s32[]{:T(128)}, s32[3,32]{1,0:T(4,128)S(1)}, bf16[2,2,32,2048]{3,2,1,0:T(8,128)(2,1)}, /*index=5*/s32[]{:T(128)}) %tuple.108), condition=%wide.region_5.6_spmd, body=%wide.region_4.5_spmd.sunk | while | flops 28674 | bytes 688437 | solution.py:492
  187.2 3.7 %collective-permute-done.11 = f32[1,4096]{1,0:T(1,128)S(1)} collective-permute-done((f32[1,4096]{1,0:T(1,128)S(1)}, f32[1,4096]{1,0:T(1,128)S(1)}, u32[]{:S(2)}, u32[]{:S(2)}) %collective-permute-start.11) | collective-permute-done | bytes 16416 | tf_op jit(solution)/shard_map/while/body/ppermute | solution.py:241
  193.4 3.3 %collective-permute-done.12 = f32[1,4096]{1,0:T(1,128)S(1)} collective-permute-done((f32[1,4096]{1,0:T(1,128)S(1)}, f32[1,4096]{1,0:T(1,128)S(1)}, u32[]{:S(2)}, u32[]{:S(2)}) %collective-permute-start.12) | collective-permute-done | bytes 16416 | tf_op jit(solution)/shard_map/while/body/ppermute | solution.py:241
  196.7 3.1 %collective-permute-start.13 = (f32[1,4096]{1,0:T(1,128)S(1)}, f32[1,4096]{1,0:T(1,128)S(1)}, u32[]{:S(2)}, u32[]{:S(2)}) collective-permute-start(f32[1,4096]{1,0:T(1,128)S(1)} %add.943), channel_id=1, source_target_pairs={{0,64},{64,0},{1,65},{65,1},{2,66},{66,2},{3,67},{67,3},{4,68},{68... | collective-permute-start | bytes 49160 | tf_op jit(solution)/shard_map/while/body/ppermute | solution.py:241
  202.0 2.7 %collective-permute-start.14 = (f32[1,4096]{1,0:T(1,128)S(1)}, f32[1,4096]{1,0:T(1,128)S(1)}, u32[]{:S(2)}, u32[]{:S(2)}) collective-permute-start(f32[1,4096]{1,0:T(1,128)S(1)} %add.944), channel_id=1, source_target_pairs={{0,1},{1,0},{2,3},{3,2},{4,5},{5,4},{6,7},{7,6},{8,9},{9,8},{10,11... | collective-permute-start | bytes 49160 | tf_op jit(solution)/shard_map/while/body/ppermute | solution.py:241
  208.0 3.8 %collective-permute-done.15 = f32[1,4096]{1,0:T(1,128)S(1)} collective-permute-done((f32[1,4096]{1,0:T(1,128)S(1)}, f32[1,4096]{1,0:T(1,128)S(1)}, u32[]{:S(2)}, u32[]{:S(2)}) %collective-permute-start.15) | collective-permute-done | bytes 16416 | tf_op jit(solution)/shard_map/while/body/ppermute | solution.py:241
  211.8 2.6 %shard_map.47 = f32[1,4096]{1,0:T(1,128)S(1)} custom-call(s32[3,32]{1,0:T(4,128)S(1)} %get-tuple-element.521, bf16[2,2,32,2048]{3,2,1,0:T(8,128)(2,1)} %shard_map.46.refs_0_, bf16[2,2,32,2048]{3,2,1,0:T(8,128)(2,1)} %collective-permute-done.43.refs_1_, bf16[2,2,32,2048]{3,2,1,0:T(8,128)(2,1)} %collective-permute-done.44.refs_2_, ...), custom_call_target="tpu_custom_call" | custom-call | tf_op jit(solution)/shard_map/pallas_call | solution.py:188
  223.3 3.5 %collective-permute-start.50 = (f32[1,4096]{1,0:T(1,128)S(1)}, f32[1,4096]{1,0:T(1,128)S(1)}, u32[]{:S(2)}, u32[]{:S(2)}) collective-permute-start(f32[1,4096]{1,0:T(1,128)S(1)} %add_add_fusion.4), channel_id=1, source_target_pairs={{0,64},{64,0},{1,65},{65,1},{2,66},{66,2},{3,67},{67,3},{4,68},{68... | collective-permute-start | bytes 49160 | tf_op jit(solution)/shard_map/ppermute | solution.py:218
  230.7 16.3 %shard_map.48 = bf16[256,4096]{1,0:T(8,128)(2,1)} custom-call(s32[3,32]{1,0:T(4,128)S(1)} %get-tuple-element.521, bf16[2,2,32,2048]{3,2,1,0:T(8,128)(2,1)} %shard_map.46.refs_0_, bf16[2,2,32,2048]{3,2,1,0:T(8,128)(2,1)} %collective-permute-done.43.refs_1_, bf16[2,2,32,2048]{3,2,1,0:T(8,128)(2,1)} %collective-permute-done.44.refs_2_, ...), custom_call_target="tpu_custom_call" | custom-call | tf_op jit(solution)/shard_map/pallas_call | solution.py:169
  (170 shorter events, 87.9 us)
Async XLA Ops:
  7.2 222.3 %all-gather.2.cloned.1.call-start = ((), (), s32[]{:S(2)}) async-start(), calls=%async_computation | async-start | bytes 18874368 | tf_op jit(solution)/shard_map/all_gather | solution.py:464
  7.2 7.4 %collective-permute-start.18 = (bf16[256,4096]{1,0:T(8,128)(2,1)}, bf16[256,4096]{1,0:T(8,128)(2,1)S(1)}, u32[]{:S(2)}, u32[]{:S(2)}) collective-permute-start(bf16[256,4096]{1,0:T(8,128)(2,1)} %refs_5_.1), channel_id=1, source_target_pairs={{0,8},{8,0},{1,9},{9,1},{2,10},{10,2},{3,11},{11,3},{4,12},{12,4},... | collective-permute-start | bytes 6291464 | tf_op jit(solution)/shard_map/ppermute | solution.py:379
  7.3 49.7 %collective-permute-start.16 = (bf16[256,4096]{1,0:T(8,128)(2,1)}, bf16[256,4096]{1,0:T(8,128)(2,1)}, u32[]{:S(2)}, u32[]{:S(2)}) collective-permute-start(bf16[256,4096]{1,0:T(8,128)(2,1)} %refs_5_.1), channel_id=1, source_target_pairs={{0,16},{16,32},{32,48},{48,0},{1,17},{17,33},{33,49},{49,1},{2,18}... | collective-permute-start | bytes 6291464 | tf_op jit(solution)/shard_map/ppermute | solution.py:375
  9.0 48.0 %collective-permute-start.17 = (bf16[256,4096]{1,0:T(8,128)(2,1)}, bf16[256,4096]{1,0:T(8,128)(2,1)}, u32[]{:S(2)}, u32[]{:S(2)}) collective-permute-start(bf16[256,4096]{1,0:T(8,128)(2,1)} %refs_5_.1), channel_id=1, source_target_pairs={{0,48},{16,0},{32,16},{48,32},{1,49},{17,1},{33,17},{49,33},{2,50}... | collective-permute-start | bytes 6291464 | tf_op jit(solution)/shard_map/ppermute | solution.py:375
  10.6 53.6 %collective-permute-start.24 = (bf16[256,4096]{1,0:T(8,128)(2,1)}, bf16[256,4096]{1,0:T(8,128)(2,1)}, u32[]{:S(2)}, u32[]{:S(2)}) collective-permute-start(bf16[256,4096]{1,0:T(8,128)(2,1)} %refs_3_.7), channel_id=1, source_target_pairs={{0,64},{64,0},{1,65},{65,1},{2,66},{66,2},{3,67},{67,3},{4,68},{68... | collective-permute-start | bytes 6291464 | tf_op jit(solution)/shard_map/ppermute | solution.py:379
  24.0 6.3 %collective-permute-start.19 = (f32[2,32,512]{2,1,0:T(8,128)S(1)}, f32[2,32,512]{2,1,0:T(8,128)S(1)}, u32[]{:S(2)}, u32[]{:S(2)}) collective-permute-start(f32[2,32,512]{2,1,0:T(8,128)S(1)} %get-tuple-element.184), channel_id=1, source_target_pairs={{0,1},{1,2},{2,3},{3,0},{4,5},{5,6},{6,7},{7,4},{8,9},{9,10},{10,1... | collective-permute-start | bytes 393224 | tf_op jit(solution)/shard_map/ppermute | solution.py:388
  30.5 26.5 %collective-permute-start.21 = (f32[2,32,512]{2,1,0:T(8,128)S(1)}, f32[2,32,512]{2,1,0:T(8,128)S(1)}, u32[]{:S(2)}, u32[]{:S(2)}) collective-permute-start(f32[2,32,512]{2,1,0:T(8,128)S(1)} %get-tuple-element.188), channel_id=1, source_target_pairs={{0,2},{1,3},{2,0},{3,1},{4,6},{5,7},{6,4},{7,5},{8,10},{9,11},{10,... | collective-permute-start | bytes 393224 | tf_op jit(solution)/shard_map/ppermute | solution.py:388
  60.4 16.9 %collective-permute-start.22 = (bf16[256,4096]{1,0:T(8,128)(2,1)}, bf16[256,4096]{1,0:T(8,128)(2,1)S(1)}, u32[]{:S(2)}, u32[]{:S(2)}) collective-permute-start(bf16[256,4096]{1,0:T(8,128)(2,1)} %collective-permute-done.16.u_ref.refs_7_), channel_id=1, source_target_pairs={{0,8},{8,0},{1,9},{9,1},{2,10},{10,2},{3,11},{11,3},{4,12},{12,4},... | collective-permute-start | bytes 6291464 | tf_op jit(solution)/shard_map/ppermute | solution.py:379
  60.4 16.9 %collective-permute-start.23 = (bf16[256,4096]{1,0:T(8,128)(2,1)}, bf16[256,4096]{1,0:T(8,128)(2,1)S(1)}, u32[]{:S(2)}, u32[]{:S(2)}) collective-permute-start(bf16[256,4096]{1,0:T(8,128)(2,1)} %collective-permute-done.17.w_ref.refs_8_), channel_id=1, source_target_pairs={{0,8},{8,0},{1,9},{9,1},{2,10},{10,2},{3,11},{11,3},{4,12},{12,4},... | collective-permute-start | bytes 6291464 | tf_op jit(solution)/shard_map/ppermute | solution.py:379
  60.9 26.5 %collective-permute-start.25 = (bf16[128,4096]{1,0:T(8,128)(2,1)}, bf16[128,4096]{1,0:T(8,128)(2,1)S(1)}, u32[]{:S(2)}, u32[]{:S(2)}) collective-permute-start(bf16[128,4096]{1,0:T(8,128)(2,1)} %get-tuple-element.210), channel_id=1, source_target_pairs={{0,16},{16,32},{32,48},{48,0},{1,17},{17,33},{33,49},{49,1},{2,18}... | collective-permute-start | bytes 3145736 | tf_op jit(solution)/shard_map/ppermute | solution.py:375
  62.5 35.7 %collective-permute-start.26 = (bf16[128,4096]{1,0:T(8,128)(2,1)}, bf16[128,4096]{1,0:T(8,128)(2,1)S(1)}, u32[]{:S(2)}, u32[]{:S(2)}) collective-permute-start(bf16[128,4096]{1,0:T(8,128)(2,1)} %get-tuple-element.211), channel_id=1, source_target_pairs={{0,48},{16,0},{32,16},{48,32},{1,49},{17,1},{33,17},{49,33},{2,50}... | collective-permute-start | bytes 3145736 | tf_op jit(solution)/shard_map/ppermute | solution.py:375
  64.2 49.4 %collective-permute-start.37 = (bf16[256,4096]{1,0:T(8,128)(2,1)}, bf16[256,4096]{1,0:T(8,128)(2,1)}, u32[]{:S(2)}, u32[]{:S(2)}) collective-permute-start(bf16[256,4096]{1,0:T(8,128)(2,1)} %refs_5_.1), channel_id=1, source_target_pairs={{0,64},{64,0},{1,65},{65,1},{2,66},{66,2},{3,67},{67,3},{4,68},{68... | collective-permute-start | bytes 6291464 | tf_op jit(solution)/shard_map/ppermute | solution.py:379
  77.4 20.9 %collective-permute-start.27 = (f32[2,32,1536]{2,1,0:T(8,128)S(1)}, f32[2,32,1536]{2,1,0:T(8,128)S(1)}, u32[]{:S(2)}, u32[]{:S(2)}) collective-permute-start(f32[2,32,1536]{2,1,0:T(8,128)S(1)} %get-tuple-element.212), channel_id=1, source_target_pairs={{0,1},{1,2},{2,3},{3,0},{4,5},{5,6},{6,7},{7,4},{8,9},{9,10},{10,1... | collective-permute-start | bytes 1179656 | tf_op jit(solution)/shard_map/ppermute | solution.py:388
  78.9 19.3 %collective-permute-start.28 = (f32[2,32,1536]{2,1,0:T(8,128)S(1)}, f32[2,32,1536]{2,1,0:T(8,128)S(1)}, u32[]{:S(2)}, u32[]{:S(2)}) collective-permute-start(f32[2,32,1536]{2,1,0:T(8,128)S(1)} %get-tuple-element.213), channel_id=1, source_target_pairs={{0,3},{1,0},{2,1},{3,2},{4,7},{5,4},{6,5},{7,6},{8,11},{9,8},{10,9... | collective-permute-start | bytes 1179656 | tf_op jit(solution)/shard_map/ppermute | solution.py:388
  87.4 11.9 %collective-permute-start.29 = (f32[2,32,1536]{2,1,0:T(8,128)S(1)}, f32[2,32,1536]{2,1,0:T(8,128)S(1)}, u32[]{:S(2)}, u32[]{:S(2)}) collective-permute-start(f32[2,32,1536]{2,1,0:T(8,128)S(1)} %get-tuple-element.220), channel_id=1, source_target_pairs={{0,2},{1,3},{2,0},{3,1},{4,6},{5,7},{6,4},{7,5},{8,10},{9,11},{10,... | collective-permute-start | bytes 1179656 | tf_op jit(solution)/shard_map/ppermute | solution.py:388
  98.8 17.8 %collective-permute-start.31 = (f32[2,32,1024]{2,1,0:T(8,128)}, f32[2,32,1024]{2,1,0:T(8,128)}, u32[]{:S(2)}, u32[]{:S(2)}) collective-permute-start(f32[2,32,1024]{2,1,0:T(8,128)} %get-tuple-element.224), channel_id=1, source_target_pairs={{0,2},{1,3},{2,0},{3,1},{4,6},{5,7},{6,4},{7,5},{8,10},{9,11},{10,... | collective-permute-start | bytes 786440 | tf_op jit(solution)/shard_map/ppermute | solution.py:388
  100.2 27.7 %collective-permute-start.30 = (f32[2,32,1024]{2,1,0:T(8,128)}, f32[2,32,1024]{2,1,0:T(8,128)}, u32[]{:S(2)}, u32[]{:S(2)}) collective-permute-start(f32[2,32,1024]{2,1,0:T(8,128)} %get-tuple-element.223), channel_id=1, source_target_pairs={{0,1},{1,2},{2,3},{3,0},{4,5},{5,6},{6,7},{7,4},{8,9},{9,10},{10,1... | collective-permute-start | bytes 786440 | tf_op jit(solution)/shard_map/ppermute | solution.py:388
  101.8 26.1 %collective-permute-start.38 = (f32[2,32,1024]{2,1,0:T(8,128)}, f32[2,32,1024]{2,1,0:T(8,128)}, u32[]{:S(2)}, u32[]{:S(2)}) collective-permute-start(f32[2,32,1024]{2,1,0:T(8,128)} %get-tuple-element.231), channel_id=1, source_target_pairs={{0,3},{1,0},{2,1},{3,2},{4,7},{5,4},{6,5},{7,6},{8,11},{9,8},{10,9... | collective-permute-start | bytes 786440 | tf_op jit(solution)/shard_map/ppermute | solution.py:388
  110.2 10.8 %collective-permute-start.34 = (f32[2,32,1024]{2,1,0:T(8,128)S(1)}, f32[2,32,1024]{2,1,0:T(8,128)}, u32[]{:S(2)}, u32[]{:S(2)}) collective-permute-start(f32[2,32,1024]{2,1,0:T(8,128)S(1)} %get-tuple-element.227), channel_id=1, source_target_pairs={{0,1},{1,2},{2,3},{3,0},{4,5},{5,6},{6,7},{7,4},{8,9},{9,10},{10,1... | collective-permute-start | bytes 786440 | tf_op jit(solution)/shard_map/ppermute | solution.py:388
  113.6 12.2 %collective-permute-start.35 = (f32[2,32,1024]{2,1,0:T(8,128)S(1)}, f32[2,32,1024]{2,1,0:T(8,128)S(1)}, u32[]{:S(2)}, u32[]{:S(2)}) collective-permute-start(f32[2,32,1024]{2,1,0:T(8,128)S(1)} %get-tuple-element.228), channel_id=1, source_target_pairs={{0,2},{1,3},{2,0},{3,1},{4,6},{5,7},{6,4},{7,5},{8,10},{9,11},{10,... | collective-permute-start | bytes 786440 | tf_op jit(solution)/shard_map/ppermute | solution.py:388
  116.6 11.3 %collective-permute-start.36 = (f32[2,32,1024]{2,1,0:T(8,128)S(1)}, f32[2,32,1024]{2,1,0:T(8,128)S(1)}, u32[]{:S(2)}, u32[]{:S(2)}) collective-permute-start(f32[2,32,1024]{2,1,0:T(8,128)S(1)} %get-tuple-element.229), channel_id=1, source_target_pairs={{0,3},{1,0},{2,1},{3,2},{4,7},{5,4},{6,5},{7,6},{8,11},{9,8},{10,9... | collective-permute-start | bytes 786440 | tf_op jit(solution)/shard_map/ppermute | solution.py:388
  130.2 9.3 %collective-permute-start.39 = (f32[32,2048]{1,0:T(8,128)S(1)}, f32[32,2048]{1,0:T(8,128)S(1)}, u32[]{:S(2)}, u32[]{:S(2)}) collective-permute-start(f32[32,2048]{1,0:T(8,128)S(1)} %get-tuple-element.279), channel_id=1, source_target_pairs={{0,4},{4,0},{64,68},{68,64},{1,5},{5,1},{65,69},{69,65},{2,6},{6,2... | collective-permute-start | bytes 786440 | tf_op jit(solution)/shard_map/while/body/ppermute | solution.py:460
  131.2 12.4 %collective-permute-start.41 = (f32[32,2048]{1,0:T(8,128)S(1)}, f32[32,2048]{1,0:T(8,128)S(1)}, u32[]{:S(2)}, u32[]{:S(2)}) collective-permute-start(f32[32,2048]{1,0:T(8,128)S(1)} %get-tuple-element.280), channel_id=1, source_target_pairs={{0,68},{4,64},{64,4},{68,0},{1,69},{5,65},{65,5},{69,1},{2,70},{6,... | collective-permute-start | bytes 786440 | tf_op jit(solution)/shard_map/while/body/ppermute | solution.py:460
  133.8 11.6 %collective-permute-start.40 = (f32[32,2048]{1,0:T(8,128)S(1)}, f32[32,2048]{1,0:T(8,128)S(1)}, u32[]{:S(2)}, u32[]{:S(2)}) collective-permute-start(f32[32,2048]{1,0:T(8,128)S(1)} %slice_bitcast_fusion.1), channel_id=1, source_target_pairs={{0,64},{4,68},{64,0},{68,4},{1,65},{5,69},{65,1},{69,5},{2,66},{6,... | collective-permute-start | bytes 786440 | tf_op jit(solution)/shard_map/while/body/ppermute | solution.py:460
  148.3 29.1 %collective-permute-start.42 = (f32[2,32,2048]{2,1,0:T(8,128)}, f32[2,32,2048]{2,1,0:T(8,128)S(1)}, u32[]{:S(2)}, u32[]{:S(2)}) collective-permute-start(f32[2,32,2048]{2,1,0:T(8,128)} %get-tuple-element.428), channel_id=1, source_target_pairs={{0,4},{4,0},{1,5},{5,1},{2,6},{6,2},{3,7},{7,3},{8,12},{12,8},{9,1... | collective-permute-start | bytes 1572872 | tf_op jit(solution)/shard_map/ppermute | solution.py:480
  153.3 6.3 %collective-permute-start.2 = (f32[2,4096]{1,0:T(2,128)S(1)}, f32[2,4096]{1,0:T(2,128)S(1)}, u32[]{:S(2)}, u32[]{:S(2)}) collective-permute-start(f32[2,4096]{1,0:T(2,128)S(1)} %pad_maximum_fusion.7), channel_id=1, source_target_pairs={{0,16},{16,32},{32,48},{48,0},{1,17},{17,33},{33,49},{49,1},{2,18}... | collective-permute-start | bytes 98312 | tf_op jit(solution)/shard_map/while/body/ppermute | solution.py:218
  153.6 6.1 %collective-permute-start.3 = (f32[2,4096]{1,0:T(2,128)S(1)}, f32[2,4096]{1,0:T(2,128)S(1)}, u32[]{:S(2)}, u32[]{:S(2)}) collective-permute-start(f32[2,4096]{1,0:T(2,128)S(1)} %pad_maximum_fusion.7), channel_id=1, source_target_pairs={{0,32},{16,48},{32,0},{48,16},{1,33},{17,49},{33,1},{49,17},{2,34}... | collective-permute-start | bytes 98312 | tf_op jit(solution)/shard_map/while/body/ppermute | solution.py:218
  179.5 32.3 %collective-permute-start.43 = (bf16[2,2,32,2048]{3,2,1,0:T(8,128)(2,1)}, bf16[2,2,32,2048]{3,2,1,0:T(8,128)(2,1)}, u32[]{:S(2)}, u32[]{:S(2)}) collective-permute-start(bf16[2,2,32,2048]{3,2,1,0:T(8,128)(2,1)} %shard_map.46.refs_0_), channel_id=1, source_target_pairs={{0,3},{1,0},{2,1},{3,2},{4,7},{5,4},{6,5},{7,6},{8,11},{9,8},{10,9... | collective-permute-start | bytes 1572872 | tf_op jit(solution)/shard_map/ppermute | solution.py:388
  182.6 29.2 %collective-permute-start.44 = (bf16[2,2,32,2048]{3,2,1,0:T(8,128)(2,1)}, bf16[2,2,32,2048]{3,2,1,0:T(8,128)(2,1)}, u32[]{:S(2)}, u32[]{:S(2)}) collective-permute-start(bf16[2,2,32,2048]{3,2,1,0:T(8,128)(2,1)} %shard_map.46.refs_0_), channel_id=1, source_target_pairs={{0,1},{1,2},{2,3},{3,0},{4,5},{5,6},{6,7},{7,4},{8,9},{9,10},{10,1... | collective-permute-start | bytes 1572872 | tf_op jit(solution)/shard_map/ppermute | solution.py:388
  182.6 29.2 %collective-permute-start.45 = (bf16[2,2,32,2048]{3,2,1,0:T(8,128)(2,1)}, bf16[2,2,32,2048]{3,2,1,0:T(8,128)(2,1)}, u32[]{:S(2)}, u32[]{:S(2)}) collective-permute-start(bf16[2,2,32,2048]{3,2,1,0:T(8,128)(2,1)} %shard_map.46.refs_0_), channel_id=1, source_target_pairs={{0,2},{1,3},{2,0},{3,1},{4,6},{5,7},{6,4},{7,5},{8,10},{9,11},{10,... | collective-permute-start | bytes 1572872 | tf_op jit(solution)/shard_map/ppermute | solution.py:388
  191.0 5.6 %collective-permute-start.12 = (f32[1,4096]{1,0:T(1,128)S(1)}, f32[1,4096]{1,0:T(1,128)S(1)}, u32[]{:S(2)}, u32[]{:S(2)}) collective-permute-start(f32[1,4096]{1,0:T(1,128)S(1)} %add.942), channel_id=1, source_target_pairs={{0,32},{16,48},{32,0},{48,16},{1,33},{17,49},{33,1},{49,17},{2,34}... | collective-permute-start | bytes 49160 | tf_op jit(solution)/shard_map/while/body/ppermute | solution.py:241
  215.7 5.6 %collective-permute-start.47 = (f32[1,4096]{1,0:T(1,128)S(1)}, f32[1,4096]{1,0:T(1,128)S(1)}, u32[]{:S(2)}, u32[]{:S(2)}) collective-permute-start(f32[1,4096]{1,0:T(1,128)S(1)} %add.837), channel_id=1, source_target_pairs={{0,32},{16,48},{32,0},{48,16},{1,33},{17,49},{33,1},{49,17},{2,34}... | collective-permute-start | bytes 49160 | tf_op jit(solution)/shard_map/ppermute | solution.py:218
  (34 other events, 239.8 us)
Sparse Core Ops, SparseCore 0:
  129.7 86.2 all-gather.1

commit v9 on v8

--- a/solution.py
+++ b/solution.py
@@ -153,10 +153,8 @@
                     x = k_ref[z, g, :, n:n + LANES].astype(jnp.float32) * v_ref[:, lanes(where[0, t])]
                     w_ref[rows, lanes(where[1, t])] = (x * scale).astype(jnp.bfloat16)
 
-    most = jnp.concatenate([x[...] for x in x_refs[:-1]], axis=0)
-    first = sum(widths[:-1])
-    acc = jnp.dot(w_ref[:, :first], most, preferred_element_type=jnp.float32)
-    acc += jnp.dot(w_ref[:, first:], x_refs[-1][...], preferred_element_type=jnp.float32)
+    everything = jnp.concatenate([x[...] for x in x_refs], axis=0)
+    acc = jnp.dot(w_ref[...], everything, preferred_element_type=jnp.float32)
     out_ref[...] = acc.astype(out_ref.dtype)
 
 

time: 255 us -> 255 us (level)
  no operation moved by 1% of the time
where the time goes in v9:
time: 255 us; the launch traced here: 254 us
  waiting for transfers between devices  87.9 us (34%)
  starting transfers between devices  79.7 us (31%)
  Pallas kernels  54.5 us (21%)
  between operations  14.6 us (6%)
  local copies, waits for them, and re-layouts  9.17 us (4%)
  other arithmetic  7.73 us (3%)
    ppermute x4, waiting for transfers between devices, ring(): return lax.ppermute(x, 'y', [(i, (i + shift) % 4) for i in range(4)])  30.5 us
    pallas_call x4, Pallas kernels, partial_call(): pl.pallas_call(functools.partial(partial_kernel, noise_parts, jobs, known...  27.8 us
    ppermute x15, starting transfers between devices, along_x(): return lax.ppermute(x, 'x', [(i, (i + step) % 4) for i in range(4)])  25.3 us
    ppermute x15, starting transfers between devices, shift(): return lax.ppermute(x, axis, [(i, (i + k) % n) for i in range(n)])  23.9 us
    ppermute x15, waiting for transfers between devices, shift(): return lax.ppermute(x, axis, [(i, (i + k) % n) for i in range(n)])  17.1 us
    pallas_call x1, Pallas kernels, targets_call(): pl.pallas_call(functools.partial(targets_kernel, shapes, widths), out_sha...  16.3 us
    ppermute x6, waiting for transfers between devices, column_sum_in_pairs(): x = x + lax.ppermute(x, axis, [(i, i ^ step) for i in range(n)])  15.9 us
    ppermute x15, waiting for transfers between devices, along_x(): return lax.ppermute(x, 'x', [(i, (i + step) % 4) for i in range(4)])  10.7 us
  transfers between devices with their start and end apart: 52, of which 30 were waited for; matrix products, arithmetic and copies ran while one was open for 4% of the time, Pallas kernels for 15%

profile of v9, /device:TPU:0, one launch (start us, length us, event | category | flops | bytes accessed | tf_op | source)
XLA Modules:
  0.0 253.9 jit_solution(15255746031899096258)
XLA Ops:
  10.6 4.0 %collective-permute-start.24 = (bf16[256,4096]{1,0:T(8,128)(2,1)}, bf16[256,4096]{1,0:T(8,128)(2,1)}, u32[]{:S(2)}, u32[]{:S(2)}) collective-permute-start(bf16[256,4096]{1,0:T(8,128)(2,1)} %refs_3_.7), channel_id=1, source_target_pairs={{0,64},{64,0},{1,65},{65,1},{2,66},{66,2},{3,67},{67,3},{4,68},{68... | collective-permute-start | bytes 6291464 | tf_op jit(solution)/shard_map/ppermute | solution.py:377
  19.2 4.8 %shard_map.41 = (f32[2,32,512]{2,1,0:T(8,128)S(1)}, f32[2,32,512]{2,1,0:T(8,128)S(1)}, f32[2,32,512]{2,1,0:T(8,128)S(1)}, f32[2,32,512]{2,1,0:T(8,128)S(1)}, f32...) custom-call(s32[2]{0:T(128)S(1)} %pad_add_fusion.1.refs_0_, f32[8,128]{1,0:T(8,128)S(1)} %broadcast_in_dim.20.refs_1_, ...), custom_call_target="tpu_custom_call" | custom-call | flops 1 | bytes 1 | tf_op jit(solution)/shard_map/pallas_call | solution.py:335
  27.3 3.0 %collective-permute-done.19 = f32[2,32,512]{2,1,0:T(8,128)S(1)} collective-permute-done((f32[2,32,512]{2,1,0:T(8,128)S(1)}, f32[2,32,512]{2,1,0:T(8,128)S(1)}, u32[]{:S(2)}, u32[]{:S(2)}) %collective-permute-start.19) | collective-permute-done | bytes 131104 | tf_op jit(solution)/shard_map/ppermute | solution.py:386
  30.5 2.7 %collective-permute-start.21 = (f32[2,32,512]{2,1,0:T(8,128)S(1)}, f32[2,32,512]{2,1,0:T(8,128)S(1)}, u32[]{:S(2)}, u32[]{:S(2)}) collective-permute-start(f32[2,32,512]{2,1,0:T(8,128)S(1)} %get-tuple-element.188), channel_id=1, source_target_pairs={{0,2},{1,3},{2,0},{3,1},{4,6},{5,7},{6,4},{7,5},{8,10},{9,11},{10,... | collective-permute-start | bytes 393224 | tf_op jit(solution)/shard_map/ppermute | solution.py:386
  33.3 23.7 %collective-permute-done.16.u_ref.refs_7_ = bf16[256,4096]{1,0:T(8,128)(2,1)} collective-permute-done((bf16[256,4096]{1,0:T(8,128)(2,1)}, bf16[256,4096]{1,0:T(8,128)(2,1)}, u32[]{:S(2)}, u32[]{:S(2)}) %collective-permute-start.16) | collective-permute-done | bytes 2097184 | tf_op jit(solution)/shard_map/ppermute | solution.py:373
  57.7 2.7 %shard_map.42 = (bf16[128,4096]{1,0:T(8,128)(2,1)}, bf16[128,4096]{1,0:T(8,128)(2,1)}) custom-call(bf16[256,4096]{1,0:T(8,128)(2,1)} %collective-permute-done.16.u_ref.refs_7_, bf16[256,4096]{1,0:T(8,128)(2,1)} %collective-permute-done.17.w_ref.refs_8_), custom_call_target="tpu_custom_call" | custom-call | flops 1 | bytes 1 | tf_op jit(solution)/shard_map/pallas_call | solution.py:362
  64.2 3.9 %collective-permute-start.37 = (bf16[256,4096]{1,0:T(8,128)(2,1)}, bf16[256,4096]{1,0:T(8,128)(2,1)}, u32[]{:S(2)}, u32[]{:S(2)}) collective-permute-start(bf16[256,4096]{1,0:T(8,128)(2,1)} %refs_5_.1), channel_id=1, source_target_pairs={{0,64},{64,0},{1,65},{65,1},{2,66},{66,2},{3,67},{67,3},{4,68},{68... | collective-permute-start | bytes 6291464 | tf_op jit(solution)/shard_map/ppermute | solution.py:377
  68.1 9.3 %shard_map.43 = (f32[2,32,1536]{2,1,0:T(8,128)S(1)}, f32[2,32,1536]{2,1,0:T(8,128)S(1)}, f32[2,32,1536]{2,1,0:T(8,128)S(1)}, f32[2,32,1536]{2,1,0:T(8,128)S(1)},...) custom-call(s32[2]{0:T(128)S(1)} %pad_add_fusion.1.refs_0_, f32[256,128]{1,0:T(8,128)S(1)} %get-tuple-element.201.refs_1_, ...), custom_call_target="tpu_custom_call" | custom-call | flops 1 | bytes 1 | tf_op jit(solution)/shard_map/pallas_call | solution.py:335
  80.7 6.8 %collective-permute-done.25.refs_5_.refs_11_ = bf16[128,4096]{1,0:T(8,128)(2,1)S(1)} collective-permute-done((bf16[128,4096]{1,0:T(8,128)(2,1)}, bf16[128,4096]{1,0:T(8,128)(2,1)S(1)}, u32[]{:S(2)}, u32[]{:S(2)}) %collective-permute-start.25) | collective-permute-done | bytes 1048608 | tf_op jit(solution)/shard_map/ppermute | solution.py:373
  87.4 3.0 %collective-permute-start.29 = (f32[2,32,1536]{2,1,0:T(8,128)S(1)}, f32[2,32,1536]{2,1,0:T(8,128)S(1)}, u32[]{:S(2)}, u32[]{:S(2)}) collective-permute-start(f32[2,32,1536]{2,1,0:T(8,128)S(1)} %get-tuple-element.220), channel_id=1, source_target_pairs={{0,2},{1,3},{2,0},{3,1},{4,6},{5,7},{6,4},{7,5},{8,10},{9,11},{10,... | collective-permute-start | bytes 1179656 | tf_op jit(solution)/shard_map/ppermute | solution.py:386
  91.1 7.1 %shard_map.44 = (f32[2,32,1024]{2,1,0:T(8,128)S(1)}, f32[2,32,1024]{2,1,0:T(8,128)}, f32[2,32,1024]{2,1,0:T(8,128)}, f32[2,32,1024]{2,1,0:T(8,128)}, f32[512,128]{1,0:T(8,128)}, /*index=5*/f32[1,512]{1,0:T(1,128)}) custom-call(s32[2]{0:T(128)S(1)} %pad_add_fusion.1.refs_0_, f32[512,128]{1,0:T(8,128)S(1)} %get-tuple-element.214.refs_1_, ...), custom_call_target="tpu_custom_call" | custom-call | flops 1 | bytes 1 | tf_op jit(solution)/shard_map/pallas_call | solution.py:335
  103.6 6.6 %shard_map.45 = (f32[2,32,1024]{2,1,0:T(8,128)S(1)}, f32[2,32,1024]{2,1,0:T(8,128)S(1)}, f32[2,32,1024]{2,1,0:T(8,128)S(1)}, f32[2,32,1024]{2,1,0:T(8,128)S(1)}, f32[512,128]{1,0:T(8,128)}, /*index=5*/f32[1,512]{1,0:T(1,128)}) custom-call(s32[2]{0:T(128)S(1)} %pad_add_fusion.1.refs_0_, f32[512,128]{1,0:T(8,128)S(1)} %get-tuple-element.214.refs_1_, ...), custom_call_target="tpu_custom_call" | custom-call | flops 1 | bytes 1 | tf_op jit(solution)/shard_map/pallas_call | solution.py:335
  110.5 3.1 %collective-permute-done.37 = bf16[256,4096]{1,0:T(8,128)(2,1)} collective-permute-done((bf16[256,4096]{1,0:T(8,128)(2,1)}, bf16[256,4096]{1,0:T(8,128)(2,1)}, u32[]{:S(2)}, u32[]{:S(2)}) %collective-permute-start.37) | collective-permute-done | bytes 2097184 | tf_op jit(solution)/shard_map/ppermute | solution.py:377
  113.6 3.0 %collective-permute-start.35 = (f32[2,32,1024]{2,1,0:T(8,128)S(1)}, f32[2,32,1024]{2,1,0:T(8,128)S(1)}, u32[]{:S(2)}, u32[]{:S(2)}) collective-permute-start(f32[2,32,1024]{2,1,0:T(8,128)S(1)} %get-tuple-element.228), channel_id=1, source_target_pairs={{0,2},{1,3},{2,0},{3,1},{4,6},{5,7},{6,4},{7,5},{8,10},{9,11},{10,... | collective-permute-start | bytes 786440 | tf_op jit(solution)/shard_map/ppermute | solution.py:386
  121.0 4.7 %collective-permute-done.35 = f32[2,32,1024]{2,1,0:T(8,128)S(1)} collective-permute-done((f32[2,32,1024]{2,1,0:T(8,128)S(1)}, f32[2,32,1024]{2,1,0:T(8,128)S(1)}, u32[]{:S(2)}, u32[]{:S(2)}) %collective-permute-start.35) | collective-permute-done | bytes 262176 | tf_op jit(solution)/shard_map/ppermute | solution.py:386
  134.9 4.6 %collective-permute-done.39 = f32[32,2048]{1,0:T(8,128)S(1)} collective-permute-done((f32[32,2048]{1,0:T(8,128)S(1)}, f32[32,2048]{1,0:T(8,128)S(1)}, u32[]{:S(2)}, u32[]{:S(2)}) %collective-permute-start.39) | collective-permute-done | bytes 262176 | tf_op jit(solution)/shard_map/while/body/ppermute | solution.py:458
  139.5 4.1 %collective-permute-done.41 = f32[32,2048]{1,0:T(8,128)S(1)} collective-permute-done((f32[32,2048]{1,0:T(8,128)S(1)}, f32[32,2048]{1,0:T(8,128)S(1)}, u32[]{:S(2)}, u32[]{:S(2)}) %collective-permute-start.41) | collective-permute-done | bytes 262176 | tf_op jit(solution)/shard_map/while/body/ppermute | solution.py:458
  148.3 29.0 %while.33 = (s32[]{:T(128)}, f32[1,4096]{1,0:T(1,128)S(1)}, s32[]{:T(128)}, f32[2,32,2048]{2,1,0:T(8,128)}, s32[3,32]{1,0:T(4,128)S(1)}, /*index=5*/s32[]{:T(128)}) while((s32[]{:T(128)}, f32[1,4096]{1,0:T(1,128)S(1)}, s32[]{:T(128)}, f32[2,32,2048]{2,1,0:T(8,128)}, s32[3,32]{1,0:T(4,128)S(1)}, /*index=5*/s32[]{:T(128)}) %tuple.100), condition=%wide.region_3.4_spmd, body=%wide.region_2.3_spmd.sunk | while | flops 229378 | bytes 2081237 | solution.py:479
  156.2 3.3 %collective-permute-done.2 = f32[2,4096]{1,0:T(2,128)S(1)} collective-permute-done((f32[2,4096]{1,0:T(2,128)S(1)}, f32[2,4096]{1,0:T(2,128)S(1)}, u32[]{:S(2)}, u32[]{:S(2)}) %collective-permute-start.2) | collective-permute-done | bytes 32800 | tf_op jit(solution)/shard_map/while/body/ppermute | solution.py:216
  162.2 3.1 %collective-permute-start.6 = (f32[2,4096]{1,0:T(2,128)S(1)}, f32[2,4096]{1,0:T(2,128)S(1)}, u32[]{:S(2)}, u32[]{:S(2)}) collective-permute-start(f32[2,4096]{1,0:T(2,128)S(1)} %pad_maximum_fusion.8), channel_id=1, source_target_pairs={{0,64},{4,68},{64,0},{68,4},{1,65},{5,69},{65,1},{69,5},{2,66},{6,... | collective-permute-start | bytes 98312 | tf_op jit(solution)/shard_map/while/body/ppermute | solution.py:216
  167.9 3.8 %collective-permute-start.7 = (f32[2,4096]{1,0:T(2,128)S(1)}, f32[2,4096]{1,0:T(2,128)S(1)}, u32[]{:S(2)}, u32[]{:S(2)}) collective-permute-start(f32[2,4096]{1,0:T(2,128)S(1)} %pad_maximum_fusion.9), channel_id=1, source_target_pairs={{0,3},{1,0},{2,1},{3,2},{4,7},{5,4},{6,5},{7,6},{8,11},{9,8},{10,9... | collective-permute-start | bytes 98312 | tf_op jit(solution)/shard_map/while/body/ppermute | solution.py:216
  173.3 3.5 %collective-permute-done.8 = f32[2,4096]{1,0:T(2,128)S(1)} collective-permute-done((f32[2,4096]{1,0:T(2,128)S(1)}, f32[2,4096]{1,0:T(2,128)S(1)}, u32[]{:S(2)}, u32[]{:S(2)}) %collective-permute-start.8) | collective-permute-done | bytes 32800 | tf_op jit(solution)/shard_map/while/body/ppermute | solution.py:216
  179.5 3.2 %collective-permute-start.43 = (bf16[2,2,32,2048]{3,2,1,0:T(8,128)(2,1)}, bf16[2,2,32,2048]{3,2,1,0:T(8,128)(2,1)}, u32[]{:S(2)}, u32[]{:S(2)}) collective-permute-start(bf16[2,2,32,2048]{3,2,1,0:T(8,128)(2,1)} %shard_map.46.refs_0_), channel_id=1, source_target_pairs={{0,3},{1,0},{2,1},{3,2},{4,7},{5,4},{6,5},{7,6},{8,11},{9,8},{10,9... | collective-permute-start | bytes 1572872 | tf_op jit(solution)/shard_map/ppermute | solution.py:386
  184.1 27.7 %while.34 = (s32[]{:T(128)}, f32[1,4096]{1,0:T(1,128)S(1)}, s32[]{:T(128)}, s32[3,32]{1,0:T(4,128)S(1)}, bf16[2,2,32,2048]{3,2,1,0:T(8,128)(2,1)}, /*index=5*/s32[]{:T(128)}) while((s32[]{:T(128)}, f32[1,4096]{1,0:T(1,128)S(1)}, s32[]{:T(128)}, s32[3,32]{1,0:T(4,128)S(1)}, bf16[2,2,32,2048]{3,2,1,0:T(8,128)(2,1)}, /*index=5*/s32[]{:T(128)}) %tuple.108), condition=%wide.region_5.6_spmd, body=%wide.region_4.5_spmd.sunk | while | flops 28674 | bytes 688437 | solution.py:490
  187.2 3.7 %collective-permute-done.11 = f32[1,4096]{1,0:T(1,128)S(1)} collective-permute-done((f32[1,4096]{1,0:T(1,128)S(1)}, f32[1,4096]{1,0:T(1,128)S(1)}, u32[]{:S(2)}, u32[]{:S(2)}) %collective-permute-start.11) | collective-permute-done | bytes 16416 | tf_op jit(solution)/shard_map/while/body/ppermute | solution.py:239
  193.4 3.3 %collective-permute-done.12 = f32[1,4096]{1,0:T(1,128)S(1)} collective-permute-done((f32[1,4096]{1,0:T(1,128)S(1)}, f32[1,4096]{1,0:T(1,128)S(1)}, u32[]{:S(2)}, u32[]{:S(2)}) %collective-permute-start.12) | collective-permute-done | bytes 16416 | tf_op jit(solution)/shard_map/while/body/ppermute | solution.py:239
  196.7 3.1 %collective-permute-start.13 = (f32[1,4096]{1,0:T(1,128)S(1)}, f32[1,4096]{1,0:T(1,128)S(1)}, u32[]{:S(2)}, u32[]{:S(2)}) collective-permute-start(f32[1,4096]{1,0:T(1,128)S(1)} %add.943), channel_id=1, source_target_pairs={{0,64},{64,0},{1,65},{65,1},{2,66},{66,2},{3,67},{67,3},{4,68},{68... | collective-permute-start | bytes 49160 | tf_op jit(solution)/shard_map/while/body/ppermute | solution.py:239
  202.0 2.7 %collective-permute-start.14 = (f32[1,4096]{1,0:T(1,128)S(1)}, f32[1,4096]{1,0:T(1,128)S(1)}, u32[]{:S(2)}, u32[]{:S(2)}) collective-permute-start(f32[1,4096]{1,0:T(1,128)S(1)} %add.944), channel_id=1, source_target_pairs={{0,1},{1,0},{2,3},{3,2},{4,5},{5,4},{6,7},{7,6},{8,9},{9,8},{10,11... | collective-permute-start | bytes 49160 | tf_op jit(solution)/shard_map/while/body/ppermute | solution.py:239
  208.0 3.8 %collective-permute-done.15 = f32[1,4096]{1,0:T(1,128)S(1)} collective-permute-done((f32[1,4096]{1,0:T(1,128)S(1)}, f32[1,4096]{1,0:T(1,128)S(1)}, u32[]{:S(2)}, u32[]{:S(2)}) %collective-permute-start.15) | collective-permute-done | bytes 16416 | tf_op jit(solution)/shard_map/while/body/ppermute | solution.py:239
  211.8 2.6 %shard_map.47 = f32[1,4096]{1,0:T(1,128)S(1)} custom-call(s32[3,32]{1,0:T(4,128)S(1)} %get-tuple-element.521, bf16[2,2,32,2048]{3,2,1,0:T(8,128)(2,1)} %shard_map.46.refs_0_, bf16[2,2,32,2048]{3,2,1,0:T(8,128)(2,1)} %collective-permute-done.43.refs_1_, bf16[2,2,32,2048]{3,2,1,0:T(8,128)(2,1)} %collective-permute-done.44.refs_2_, ...), custom_call_target="tpu_custom_call" | custom-call | tf_op jit(solution)/shard_map/pallas_call | solution.py:186
  223.3 3.5 %collective-permute-start.50 = (f32[1,4096]{1,0:T(1,128)S(1)}, f32[1,4096]{1,0:T(1,128)S(1)}, u32[]{:S(2)}, u32[]{:S(2)}) collective-permute-start(f32[1,4096]{1,0:T(1,128)S(1)} %add_add_fusion.4), channel_id=1, source_target_pairs={{0,64},{64,0},{1,65},{65,1},{2,66},{66,2},{3,67},{67,3},{4,68},{68... | collective-permute-start | bytes 49160 | tf_op jit(solution)/shard_map/ppermute | solution.py:216
  230.7 16.3 %shard_map.48 = bf16[256,4096]{1,0:T(8,128)(2,1)} custom-call(s32[3,32]{1,0:T(4,128)S(1)} %get-tuple-element.521, bf16[2,2,32,2048]{3,2,1,0:T(8,128)(2,1)} %shard_map.46.refs_0_, bf16[2,2,32,2048]{3,2,1,0:T(8,128)(2,1)} %collective-permute-done.43.refs_1_, bf16[2,2,32,2048]{3,2,1,0:T(8,128)(2,1)} %collective-permute-done.44.refs_2_, ...), custom_call_target="tpu_custom_call" | custom-call | tf_op jit(solution)/shard_map/pallas_call | solution.py:167
  (170 shorter events, 87.9 us)
Async XLA Ops:
  7.2 222.3 %all-gather.2.cloned.1.call-start = ((), (), s32[]{:S(2)}) async-start(), calls=%async_computation | async-start | bytes 18874368 | tf_op jit(solution)/shard_map/all_gather | solution.py:462
  7.2 7.4 %collective-permute-start.18 = (bf16[256,4096]{1,0:T(8,128)(2,1)}, bf16[256,4096]{1,0:T(8,128)(2,1)S(1)}, u32[]{:S(2)}, u32[]{:S(2)}) collective-permute-start(bf16[256,4096]{1,0:T(8,128)(2,1)} %refs_5_.1), channel_id=1, source_target_pairs={{0,8},{8,0},{1,9},{9,1},{2,10},{10,2},{3,11},{11,3},{4,12},{12,4},... | collective-permute-start | bytes 6291464 | tf_op jit(solution)/shard_map/ppermute | solution.py:377
  7.3 49.7 %collective-permute-start.16 = (bf16[256,4096]{1,0:T(8,128)(2,1)}, bf16[256,4096]{1,0:T(8,128)(2,1)}, u32[]{:S(2)}, u32[]{:S(2)}) collective-permute-start(bf16[256,4096]{1,0:T(8,128)(2,1)} %refs_5_.1), channel_id=1, source_target_pairs={{0,16},{16,32},{32,48},{48,0},{1,17},{17,33},{33,49},{49,1},{2,18}... | collective-permute-start | bytes 6291464 | tf_op jit(solution)/shard_map/ppermute | solution.py:373
  9.0 48.0 %collective-permute-start.17 = (bf16[256,4096]{1,0:T(8,128)(2,1)}, bf16[256,4096]{1,0:T(8,128)(2,1)}, u32[]{:S(2)}, u32[]{:S(2)}) collective-permute-start(bf16[256,4096]{1,0:T(8,128)(2,1)} %refs_5_.1), channel_id=1, source_target_pairs={{0,48},{16,0},{32,16},{48,32},{1,49},{17,1},{33,17},{49,33},{2,50}... | collective-permute-start | bytes 6291464 | tf_op jit(solution)/shard_map/ppermute | solution.py:373
  10.6 53.6 %collective-permute-start.24 = (bf16[256,4096]{1,0:T(8,128)(2,1)}, bf16[256,4096]{1,0:T(8,128)(2,1)}, u32[]{:S(2)}, u32[]{:S(2)}) collective-permute-start(bf16[256,4096]{1,0:T(8,128)(2,1)} %refs_3_.7), channel_id=1, source_target_pairs={{0,64},{64,0},{1,65},{65,1},{2,66},{66,2},{3,67},{67,3},{4,68},{68... | collective-permute-start | bytes 6291464 | tf_op jit(solution)/shard_map/ppermute | solution.py:377
  24.0 6.3 %collective-permute-start.19 = (f32[2,32,512]{2,1,0:T(8,128)S(1)}, f32[2,32,512]{2,1,0:T(8,128)S(1)}, u32[]{:S(2)}, u32[]{:S(2)}) collective-permute-start(f32[2,32,512]{2,1,0:T(8,128)S(1)} %get-tuple-element.184), channel_id=1, source_target_pairs={{0,1},{1,2},{2,3},{3,0},{4,5},{5,6},{6,7},{7,4},{8,9},{9,10},{10,1... | collective-permute-start | bytes 393224 | tf_op jit(solution)/shard_map/ppermute | solution.py:386
  30.5 26.5 %collective-permute-start.21 = (f32[2,32,512]{2,1,0:T(8,128)S(1)}, f32[2,32,512]{2,1,0:T(8,128)S(1)}, u32[]{:S(2)}, u32[]{:S(2)}) collective-permute-start(f32[2,32,512]{2,1,0:T(8,128)S(1)} %get-tuple-element.188), channel_id=1, source_target_pairs={{0,2},{1,3},{2,0},{3,1},{4,6},{5,7},{6,4},{7,5},{8,10},{9,11},{10,... | collective-permute-start | bytes 393224 | tf_op jit(solution)/shard_map/ppermute | solution.py:386
  60.4 16.9 %collective-permute-start.22 = (bf16[256,4096]{1,0:T(8,128)(2,1)}, bf16[256,4096]{1,0:T(8,128)(2,1)S(1)}, u32[]{:S(2)}, u32[]{:S(2)}) collective-permute-start(bf16[256,4096]{1,0:T(8,128)(2,1)} %collective-permute-done.16.u_ref.refs_7_), channel_id=1, source_target_pairs={{0,8},{8,0},{1,9},{9,1},{2,10},{10,2},{3,11},{11,3},{4,12},{12,4},... | collective-permute-start | bytes 6291464 | tf_op jit(solution)/shard_map/ppermute | solution.py:377
  60.4 16.9 %collective-permute-start.23 = (bf16[256,4096]{1,0:T(8,128)(2,1)}, bf16[256,4096]{1,0:T(8,128)(2,1)S(1)}, u32[]{:S(2)}, u32[]{:S(2)}) collective-permute-start(bf16[256,4096]{1,0:T(8,128)(2,1)} %collective-permute-done.17.w_ref.refs_8_), channel_id=1, source_target_pairs={{0,8},{8,0},{1,9},{9,1},{2,10},{10,2},{3,11},{11,3},{4,12},{12,4},... | collective-permute-start | bytes 6291464 | tf_op jit(solution)/shard_map/ppermute | solution.py:377
  60.9 26.5 %collective-permute-start.25 = (bf16[128,4096]{1,0:T(8,128)(2,1)}, bf16[128,4096]{1,0:T(8,128)(2,1)S(1)}, u32[]{:S(2)}, u32[]{:S(2)}) collective-permute-start(bf16[128,4096]{1,0:T(8,128)(2,1)} %get-tuple-element.210), channel_id=1, source_target_pairs={{0,16},{16,32},{32,48},{48,0},{1,17},{17,33},{33,49},{49,1},{2,18}... | collective-permute-start | bytes 3145736 | tf_op jit(solution)/shard_map/ppermute | solution.py:373
  62.5 35.7 %collective-permute-start.26 = (bf16[128,4096]{1,0:T(8,128)(2,1)}, bf16[128,4096]{1,0:T(8,128)(2,1)S(1)}, u32[]{:S(2)}, u32[]{:S(2)}) collective-permute-start(bf16[128,4096]{1,0:T(8,128)(2,1)} %get-tuple-element.211), channel_id=1, source_target_pairs={{0,48},{16,0},{32,16},{48,32},{1,49},{17,1},{33,17},{49,33},{2,50}... | collective-permute-start | bytes 3145736 | tf_op jit(solution)/shard_map/ppermute | solution.py:373
  64.2 49.4 %collective-permute-start.37 = (bf16[256,4096]{1,0:T(8,128)(2,1)}, bf16[256,4096]{1,0:T(8,128)(2,1)}, u32[]{:S(2)}, u32[]{:S(2)}) collective-permute-start(bf16[256,4096]{1,0:T(8,128)(2,1)} %refs_5_.1), channel_id=1, source_target_pairs={{0,64},{64,0},{1,65},{65,1},{2,66},{66,2},{3,67},{67,3},{4,68},{68... | collective-permute-start | bytes 6291464 | tf_op jit(solution)/shard_map/ppermute | solution.py:377
  77.4 20.9 %collective-permute-start.27 = (f32[2,32,1536]{2,1,0:T(8,128)S(1)}, f32[2,32,1536]{2,1,0:T(8,128)S(1)}, u32[]{:S(2)}, u32[]{:S(2)}) collective-permute-start(f32[2,32,1536]{2,1,0:T(8,128)S(1)} %get-tuple-element.212), channel_id=1, source_target_pairs={{0,1},{1,2},{2,3},{3,0},{4,5},{5,6},{6,7},{7,4},{8,9},{9,10},{10,1... | collective-permute-start | bytes 1179656 | tf_op jit(solution)/shard_map/ppermute | solution.py:386
  78.9 19.3 %collective-permute-start.28 = (f32[2,32,1536]{2,1,0:T(8,128)S(1)}, f32[2,32,1536]{2,1,0:T(8,128)S(1)}, u32[]{:S(2)}, u32[]{:S(2)}) collective-permute-start(f32[2,32,1536]{2,1,0:T(8,128)S(1)} %get-tuple-element.213), channel_id=1, source_target_pairs={{0,3},{1,0},{2,1},{3,2},{4,7},{5,4},{6,5},{7,6},{8,11},{9,8},{10,9... | collective-permute-start | bytes 1179656 | tf_op jit(solution)/shard_map/ppermute | solution.py:386
  87.4 11.9 %collective-permute-start.29 = (f32[2,32,1536]{2,1,0:T(8,128)S(1)}, f32[2,32,1536]{2,1,0:T(8,128)S(1)}, u32[]{:S(2)}, u32[]{:S(2)}) collective-permute-start(f32[2,32,1536]{2,1,0:T(8,128)S(1)} %get-tuple-element.220), channel_id=1, source_target_pairs={{0,2},{1,3},{2,0},{3,1},{4,6},{5,7},{6,4},{7,5},{8,10},{9,11},{10,... | collective-permute-start | bytes 1179656 | tf_op jit(solution)/shard_map/ppermute | solution.py:386
  98.8 17.8 %collective-permute-start.31 = (f32[2,32,1024]{2,1,0:T(8,128)}, f32[2,32,1024]{2,1,0:T(8,128)}, u32[]{:S(2)}, u32[]{:S(2)}) collective-permute-start(f32[2,32,1024]{2,1,0:T(8,128)} %get-tuple-element.224), channel_id=1, source_target_pairs={{0,2},{1,3},{2,0},{3,1},{4,6},{5,7},{6,4},{7,5},{8,10},{9,11},{10,... | collective-permute-start | bytes 786440 | tf_op jit(solution)/shard_map/ppermute | solution.py:386
  100.2 27.7 %collective-permute-start.30 = (f32[2,32,1024]{2,1,0:T(8,128)}, f32[2,32,1024]{2,1,0:T(8,128)}, u32[]{:S(2)}, u32[]{:S(2)}) collective-permute-start(f32[2,32,1024]{2,1,0:T(8,128)} %get-tuple-element.223), channel_id=1, source_target_pairs={{0,1},{1,2},{2,3},{3,0},{4,5},{5,6},{6,7},{7,4},{8,9},{9,10},{10,1... | collective-permute-start | bytes 786440 | tf_op jit(solution)/shard_map/ppermute | solution.py:386
  101.8 26.1 %collective-permute-start.38 = (f32[2,32,1024]{2,1,0:T(8,128)}, f32[2,32,1024]{2,1,0:T(8,128)}, u32[]{:S(2)}, u32[]{:S(2)}) collective-permute-start(f32[2,32,1024]{2,1,0:T(8,128)} %get-tuple-element.231), channel_id=1, source_target_pairs={{0,3},{1,0},{2,1},{3,2},{4,7},{5,4},{6,5},{7,6},{8,11},{9,8},{10,9... | collective-permute-start | bytes 786440 | tf_op jit(solution)/shard_map/ppermute | solution.py:386
  110.2 10.8 %collective-permute-start.34 = (f32[2,32,1024]{2,1,0:T(8,128)S(1)}, f32[2,32,1024]{2,1,0:T(8,128)}, u32[]{:S(2)}, u32[]{:S(2)}) collective-permute-start(f32[2,32,1024]{2,1,0:T(8,128)S(1)} %get-tuple-element.227), channel_id=1, source_target_pairs={{0,1},{1,2},{2,3},{3,0},{4,5},{5,6},{6,7},{7,4},{8,9},{9,10},{10,1... | collective-permute-start | bytes 786440 | tf_op jit(solution)/shard_map/ppermute | solution.py:386
  113.6 12.2 %collective-permute-start.35 = (f32[2,32,1024]{2,1,0:T(8,128)S(1)}, f32[2,32,1024]{2,1,0:T(8,128)S(1)}, u32[]{:S(2)}, u32[]{:S(2)}) collective-permute-start(f32[2,32,1024]{2,1,0:T(8,128)S(1)} %get-tuple-element.228), channel_id=1, source_target_pairs={{0,2},{1,3},{2,0},{3,1},{4,6},{5,7},{6,4},{7,5},{8,10},{9,11},{10,... | collective-permute-start | bytes 786440 | tf_op jit(solution)/shard_map/ppermute | solution.py:386
  116.6 11.3 %collective-permute-start.36 = (f32[2,32,1024]{2,1,0:T(8,128)S(1)}, f32[2,32,1024]{2,1,0:T(8,128)S(1)}, u32[]{:S(2)}, u32[]{:S(2)}) collective-permute-start(f32[2,32,1024]{2,1,0:T(8,128)S(1)} %get-tuple-element.229), channel_id=1, source_target_pairs={{0,3},{1,0},{2,1},{3,2},{4,7},{5,4},{6,5},{7,6},{8,11},{9,8},{10,9... | collective-permute-start | bytes 786440 | tf_op jit(solution)/shard_map/ppermute | solution.py:386
  130.2 9.3 %collective-permute-start.39 = (f32[32,2048]{1,0:T(8,128)S(1)}, f32[32,2048]{1,0:T(8,128)S(1)}, u32[]{:S(2)}, u32[]{:S(2)}) collective-permute-start(f32[32,2048]{1,0:T(8,128)S(1)} %get-tuple-element.279), channel_id=1, source_target_pairs={{0,4},{4,0},{64,68},{68,64},{1,5},{5,1},{65,69},{69,65},{2,6},{6,2... | collective-permute-start | bytes 786440 | tf_op jit(solution)/shard_map/while/body/ppermute | solution.py:458
  131.2 12.4 %collective-permute-start.41 = (f32[32,2048]{1,0:T(8,128)S(1)}, f32[32,2048]{1,0:T(8,128)S(1)}, u32[]{:S(2)}, u32[]{:S(2)}) collective-permute-start(f32[32,2048]{1,0:T(8,128)S(1)} %get-tuple-element.280), channel_id=1, source_target_pairs={{0,68},{4,64},{64,4},{68,0},{1,69},{5,65},{65,5},{69,1},{2,70},{6,... | collective-permute-start | bytes 786440 | tf_op jit(solution)/shard_map/while/body/ppermute | solution.py:458
  133.8 11.6 %collective-permute-start.40 = (f32[32,2048]{1,0:T(8,128)S(1)}, f32[32,2048]{1,0:T(8,128)S(1)}, u32[]{:S(2)}, u32[]{:S(2)}) collective-permute-start(f32[32,2048]{1,0:T(8,128)S(1)} %slice_bitcast_fusion.1), channel_id=1, source_target_pairs={{0,64},{4,68},{64,0},{68,4},{1,65},{5,69},{65,1},{69,5},{2,66},{6,... | collective-permute-start | bytes 786440 | tf_op jit(solution)/shard_map/while/body/ppermute | solution.py:458
  148.3 29.1 %collective-permute-start.42 = (f32[2,32,2048]{2,1,0:T(8,128)}, f32[2,32,2048]{2,1,0:T(8,128)S(1)}, u32[]{:S(2)}, u32[]{:S(2)}) collective-permute-start(f32[2,32,2048]{2,1,0:T(8,128)} %get-tuple-element.428), channel_id=1, source_target_pairs={{0,4},{4,0},{1,5},{5,1},{2,6},{6,2},{3,7},{7,3},{8,12},{12,8},{9,1... | collective-permute-start | bytes 1572872 | tf_op jit(solution)/shard_map/ppermute | solution.py:478
  153.3 6.3 %collective-permute-start.2 = (f32[2,4096]{1,0:T(2,128)S(1)}, f32[2,4096]{1,0:T(2,128)S(1)}, u32[]{:S(2)}, u32[]{:S(2)}) collective-permute-start(f32[2,4096]{1,0:T(2,128)S(1)} %pad_maximum_fusion.7), channel_id=1, source_target_pairs={{0,16},{16,32},{32,48},{48,0},{1,17},{17,33},{33,49},{49,1},{2,18}... | collective-permute-start | bytes 98312 | tf_op jit(solution)/shard_map/while/body/ppermute | solution.py:216
  153.6 6.1 %collective-permute-start.3 = (f32[2,4096]{1,0:T(2,128)S(1)}, f32[2,4096]{1,0:T(2,128)S(1)}, u32[]{:S(2)}, u32[]{:S(2)}) collective-permute-start(f32[2,4096]{1,0:T(2,128)S(1)} %pad_maximum_fusion.7), channel_id=1, source_target_pairs={{0,32},{16,48},{32,0},{48,16},{1,33},{17,49},{33,1},{49,17},{2,34}... | collective-permute-start | bytes 98312 | tf_op jit(solution)/shard_map/while/body/ppermute | solution.py:216
  179.5 32.3 %collective-permute-start.43 = (bf16[2,2,32,2048]{3,2,1,0:T(8,128)(2,1)}, bf16[2,2,32,2048]{3,2,1,0:T(8,128)(2,1)}, u32[]{:S(2)}, u32[]{:S(2)}) collective-permute-start(bf16[2,2,32,2048]{3,2,1,0:T(8,128)(2,1)} %shard_map.46.refs_0_), channel_id=1, source_target_pairs={{0,3},{1,0},{2,1},{3,2},{4,7},{5,4},{6,5},{7,6},{8,11},{9,8},{10,9... | collective-permute-start | bytes 1572872 | tf_op jit(solution)/shard_map/ppermute | solution.py:386
  182.6 29.2 %collective-permute-start.44 = (bf16[2,2,32,2048]{3,2,1,0:T(8,128)(2,1)}, bf16[2,2,32,2048]{3,2,1,0:T(8,128)(2,1)}, u32[]{:S(2)}, u32[]{:S(2)}) collective-permute-start(bf16[2,2,32,2048]{3,2,1,0:T(8,128)(2,1)} %shard_map.46.refs_0_), channel_id=1, source_target_pairs={{0,1},{1,2},{2,3},{3,0},{4,5},{5,6},{6,7},{7,4},{8,9},{9,10},{10,1... | collective-permute-start | bytes 1572872 | tf_op jit(solution)/shard_map/ppermute | solution.py:386
  182.6 29.2 %collective-permute-start.45 = (bf16[2,2,32,2048]{3,2,1,0:T(8,128)(2,1)}, bf16[2,2,32,2048]{3,2,1,0:T(8,128)(2,1)}, u32[]{:S(2)}, u32[]{:S(2)}) collective-permute-start(bf16[2,2,32,2048]{3,2,1,0:T(8,128)(2,1)} %shard_map.46.refs_0_), channel_id=1, source_target_pairs={{0,2},{1,3},{2,0},{3,1},{4,6},{5,7},{6,4},{7,5},{8,10},{9,11},{10,... | collective-permute-start | bytes 1572872 | tf_op jit(solution)/shard_map/ppermute | solution.py:386
  191.0 5.6 %collective-permute-start.12 = (f32[1,4096]{1,0:T(1,128)S(1)}, f32[1,4096]{1,0:T(1,128)S(1)}, u32[]{:S(2)}, u32[]{:S(2)}) collective-permute-start(f32[1,4096]{1,0:T(1,128)S(1)} %add.942), channel_id=1, source_target_pairs={{0,32},{16,48},{32,0},{48,16},{1,33},{17,49},{33,1},{49,17},{2,34}... | collective-permute-start | bytes 49160 | tf_op jit(solution)/shard_map/while/body/ppermute | solution.py:239
  215.7 5.6 %collective-permute-start.47 = (f32[1,4096]{1,0:T(1,128)S(1)}, f32[1,4096]{1,0:T(1,128)S(1)}, u32[]{:S(2)}, u32[]{:S(2)}) collective-permute-start(f32[1,4096]{1,0:T(1,128)S(1)} %add.837), channel_id=1, source_target_pairs={{0,32},{16,48},{32,0},{48,16},{1,33},{17,49},{33,1},{49,17},{2,34}... | collective-permute-start | bytes 49160 | tf_op jit(solution)/shard_map/ppermute | solution.py:216
  (34 other events, 239.8 us)
Sparse Core Ops, SparseCore 0:
  129.7 86.2 all-gather.1
